TPU v7x, 32 devices: a whole 2x2x4 slice. The times are simulated.
32 devices in a mesh: dp: 8 (over z, x), head: 4 (over y, core).
Axes of the slice: x: 2, y: 2, z: 4, core: 2. Of those that a mesh axis runs over, the one named last changes fastest.
Arguments:
- tokens: bfloat16 [8, 2048, 1024], P('dp', 'head'), may hold values from -6 to 6
- doc_starts: int32 [8, 4], P('dp'), may hold values from 0 to 2047, as said below
- grad_out: bfloat16 [8, 2048, 1024], P('dp', 'head'), may hold values from -6 to 6
- norm_one: float32 [2, 1024], replicated, may hold values from 0.1 to 1.9
- w_query: bfloat16 [2, 1024, 512], P(None, None, 'head'), may hold values from -0.1875 to 0.1875
- w_key: bfloat16 [2, 1024, 512], P(None, None, 'head'), may hold values from -0.1875 to 0.1875
- w_value: bfloat16 [2, 1024, 1024], P(None, None, 'head'), may hold values from -0.1875 to 0.1875
- w_outgate: bfloat16 [2, 1024, 1024], P(None, None, 'head'), may hold values from -0.1875 to 0.1875
- w_rank: bfloat16 [2, 1024, 16], replicated, may hold values from -0.1875 to 0.1875
- w_decay: bfloat16 [2, 16, 512], P(None, None, 'head'), may hold values from -1.5 to 1.5
- decay_bias: float32 [2, 512], P(None, 'head'), may hold values from 0 to 6
- group_gain: float32 [2, 256], replicated, may hold values from 0.1 to 1.9
- w_out: bfloat16 [2, 1024, 1024], P(None, 'head'), may hold values from -0.1875 to 0.1875
- norm_two: float32 [2, 1024], replicated, may hold values from 0.1 to 1.9
- w_gate: bfloat16 [2, 1024, 2816], P(None, None, 'head'), may hold values from -0.1875 to 0.1875
- w_up: bfloat16 [2, 1024, 2816], P(None, None, 'head'), may hold values from -0.1875 to 0.1875
- w_down: bfloat16 [2, 2816, 1024], P(None, 'head'), may hold values from -0.109375 to 0.109375
Outputs:
- result: bfloat16 [8, 2048, 1024], P('dp', 'head')
- grad_tokens: float32 [8, 2048, 1024], P('dp', 'head')
- grad_norm_one: float32 [2, 1024], replicated
- grad_w_query: float32 [2, 1024, 512], P(None, None, 'head')
- grad_w_key: float32 [2, 1024, 512], P(None, None, 'head')
- grad_w_value: float32 [2, 1024, 1024], P(None, None, 'head')
- grad_w_outgate: float32 [2, 1024, 1024], P(None, None, 'head')
- grad_w_rank: float32 [2, 1024, 16], replicated
- grad_w_decay: float32 [2, 16, 512], P(None, None, 'head')
- grad_decay_bias: float32 [2, 512], P(None, 'head')
- grad_group_gain: float32 [2, 256], replicated
- grad_w_out: float32 [2, 1024, 1024], P(None, 'head')
- grad_norm_two: float32 [2, 1024], replicated
- grad_w_gate: float32 [2, 1024, 2816], P(None, None, 'head')
- grad_w_up: float32 [2, 1024, 2816], P(None, None, 'head')
- grad_w_down: float32 [2, 2816, 1024], P(None, 'head')
Inputs may be any that keep to these rules, and one draw needn't show every extreme that they name: `doc_starts`: each row's entries rise strictly and the first is 0; in the first row the last entry is 2047.
All inputs are finite; a program needn't handle non-finite values.
Results may differ from a plain program's by a relative error of at most 0.024.
Values may be sent and summed in bfloat16 or wider, within the bound.
A program may use at most 256 MiB of HBM per device.

v0:
```python
from functools import partial

import jax
import jax.numpy as jnp
from jax import lax
from jax.sharding import PartitionSpec as P

SPAN = 64
LAYERS = 2
SEQ = 2048
HK = 128


epsilon = 1e-06
highest = lax.Precision.HIGHEST


def rms_norm(hidden, gain):
    return hidden * lax.rsqrt(jnp.mean(hidden * hidden, axis=-1, keepdims=True) + epsilon) * gain


def norm_back(hidden, gain, grad_normed):
    scale = lax.rsqrt(jnp.mean(hidden * hidden, axis=-1, keepdims=True) + epsilon)
    weighted = grad_normed * gain
    grad_hidden = scale * weighted - hidden * (scale * scale * scale) * jnp.mean(
        weighted * hidden, axis=-1, keepdims=True
    )
    grad_gain = jnp.sum((grad_normed * hidden * scale).reshape(-1, hidden.shape[-1]), axis=0)
    return (grad_hidden, grad_gain)


def inner_rows(left, right):
    return lax.dot_general(
        left, right, (((0,), (0,)), ((), ())), preferred_element_type=jnp.float32
    )


def against_cols(left, right):
    return lax.dot_general(
        left, right, (((1,), (1,)), ((), ())), preferred_element_type=jnp.float32
    )


def span_step(state, inputs):
    queries, keys_in, values_in, decays, doc_ids, doc_before = inputs
    running = jnp.cumsum(decays, axis=0)
    scaled_query = queries * jnp.exp(running)
    scaled_key = keys_in * jnp.exp(-running)
    scores = jnp.dot(scaled_query, scaled_key.T, precision=highest)
    places = lax.iota(jnp.int32, queries.shape[0])
    allowed = (places[:, None] >= places[None, :]) & (doc_ids[:, None] == doc_ids[None, :])
    scores = jnp.where(allowed, scores, jnp.zeros_like(scores))
    carried = (doc_ids == doc_before).astype(jnp.float32)
    output = jnp.dot(scores, values_in, precision=highest) + carried[:, None] * jnp.dot(
        scaled_query, state, precision=highest
    )
    ending = running[-1]
    same_doc = (doc_ids == doc_ids[-1]).astype(jnp.float32)
    moved_key = keys_in * jnp.exp(ending[None, :] - running) * same_doc[:, None]
    new_state = state * (jnp.exp(ending)[:, None] * carried[-1]) + jnp.dot(
        moved_key.T, values_in, precision=highest
    )
    return (new_state, output)


def mix_head(queries, keys_in, values_in, decays, doc_ids):
    total = queries.shape[0]
    blocks = total // SPAN
    queries = queries * queries.shape[-1] ** (-0.5)
    block_q = queries.reshape(blocks, SPAN, -1)
    block_k = keys_in.reshape(blocks, SPAN, -1)
    block_v = values_in.reshape(blocks, SPAN, -1)
    block_d = decays.reshape(blocks, SPAN, -1)
    block_ids = doc_ids.reshape(blocks, SPAN)
    doc_before = jnp.concatenate([jnp.full((1,), -1, jnp.int32), block_ids[:-1, -1]])
    start_state = jnp.zeros((queries.shape[-1], values_in.shape[-1]), jnp.float32)
    final_state, outputs = lax.scan(
        jax.checkpoint(span_step),
        start_state,
        (block_q, block_k, block_v, block_d, block_ids, doc_before),
    )
    return outputs.reshape(total, -1)


def mix_local(
    doc_ids, queries, keys_in, values_in, outgate, ranked, decay_weight, bias_local, gain_heads
):
    rows_count = doc_ids.shape[0]
    total = queries.shape[0]
    seq_len = total // rows_count
    local_heads = queries.shape[1] // HK
    before = jnp.dot(ranked, decay_weight, precision=highest) + bias_local
    decays = jax.nn.log_sigmoid(before) / 16.0
    shaped = (seq_len, rows_count, local_heads, -1)
    per_head = jax.vmap(mix_head, in_axes=(1, 1, 1, 1, None), out_axes=1)
    per_row = jax.vmap(per_head, in_axes=(1, 1, 1, 1, 0), out_axes=1)
    mixed = per_row(
        queries.reshape(shaped),
        keys_in.reshape(shaped),
        values_in.reshape(shaped),
        decays.reshape(shaped),
        doc_ids,
    )
    normed_heads = (
        mixed
        * lax.rsqrt(jnp.maximum(jnp.mean(mixed * mixed, axis=-1, keepdims=True), 1.0))
        * gain_heads
    )
    gated = normed_heads * jax.nn.silu(outgate.reshape(shaped))
    return gated.reshape(total, -1)


def per_device(
    tokens,
    doc_starts,
    grad_out,
    norm_one,
    w_query,
    w_key,
    w_value,
    w_outgate,
    w_rank,
    w_decay,
    decay_bias,
    group_gain,
    w_out,
    norm_two,
    w_gate,
    w_up,
    w_down,
):
    rows_count, shard_len, width = tokens.shape
    places = lax.iota(jnp.int32, SEQ)
    doc_ids = (
        jnp.sum((doc_starts[:, :, None] <= places[None, None, :]).astype(jnp.int32), axis=1) - 1
    )
    mixer_fn = partial(mix_local, doc_ids)

    def spread(local):
        return lax.all_gather(local, "head", axis=0, tiled=True).reshape(-1, width)

    def spread_again(local):
        return lax.all_gather(local, "head", axis=0, tiled=True).reshape(-1, width)

    def fetch_grad(local):
        return lax.all_gather(local.astype(jnp.bfloat16), "head", axis=0, tiled=True).reshape(
            -1, width
        )

    def settle(branch, weight):
        return lax.psum_scatter(
            jnp.dot(branch, weight, preferred_element_type=jnp.float32),
            "head",
            scatter_dimension=0,
            tiled=True,
        ).reshape(shard_len, rows_count, width)

    def return_grad(partial_grad):
        return (
            lax.psum_scatter(
                partial_grad.astype(jnp.bfloat16), "head", scatter_dimension=0, tiled=True
            )
            .astype(jnp.float32)
            .reshape(shard_len, rows_count, width)
        )

    hidden = jnp.transpose(tokens.astype(jnp.float32), (1, 0, 2))
    saved_in = []
    saved_mid = []
    for which_layer in range(LAYERS):
        saved_in.append(hidden)
        normed_in = spread(rms_norm(hidden, norm_one[which_layer]).astype(jnp.bfloat16))
        queries = jnp.dot(normed_in, w_query[which_layer], preferred_element_type=jnp.float32)
        keys_in = jnp.dot(normed_in, w_key[which_layer], preferred_element_type=jnp.float32)
        values_in = jnp.dot(normed_in, w_value[which_layer], preferred_element_type=jnp.float32)
        outgate = jnp.dot(normed_in, w_outgate[which_layer], preferred_element_type=jnp.float32)
        ranked = jnp.dot(normed_in, w_rank[which_layer], preferred_element_type=jnp.float32)
        gated = mixer_fn(
            queries,
            keys_in,
            values_in,
            outgate,
            ranked,
            w_decay[which_layer].astype(jnp.float32),
            decay_bias[which_layer],
            group_gain[which_layer],
        )
        hidden = hidden + settle(gated.astype(jnp.bfloat16), w_out[which_layer])
        saved_mid.append(hidden)
        normed_mid = spread(rms_norm(hidden, norm_two[which_layer]).astype(jnp.bfloat16))
        gate_pre = jnp.dot(normed_mid, w_gate[which_layer], preferred_element_type=jnp.float32)
        up_pre = jnp.dot(normed_mid, w_up[which_layer], preferred_element_type=jnp.float32)
        product = (jax.nn.silu(gate_pre) * up_pre).astype(jnp.bfloat16)
        hidden = hidden + settle(product, w_down[which_layer])
    result = jnp.transpose(hidden, (1, 0, 2)).astype(jnp.bfloat16)
    grad_hidden = jnp.transpose(grad_out.astype(jnp.float32), (1, 0, 2))
    split_store = [None] * LAYERS
    shared_store = [None] * LAYERS
    for which_layer in reversed(range(LAYERS)):
        hidden_mid = saved_mid[which_layer]
        hidden_in = saved_in[which_layer]
        normed_mid = spread_again(rms_norm(hidden_mid, norm_two[which_layer]).astype(jnp.bfloat16))
        normed_in = spread_again(rms_norm(hidden_in, norm_one[which_layer]).astype(jnp.bfloat16))
        gate_pre = jnp.dot(normed_mid, w_gate[which_layer], preferred_element_type=jnp.float32)
        up_pre = jnp.dot(normed_mid, w_up[which_layer], preferred_element_type=jnp.float32)
        sigmoid_gate = jax.nn.sigmoid(gate_pre)
        product = (gate_pre * sigmoid_gate * up_pre).astype(jnp.bfloat16)
        grad_branch = fetch_grad(grad_hidden)
        grad_down = inner_rows(product, grad_branch)
        grad_product = against_cols(grad_branch, w_down[which_layer])
        grad_gate = (
            grad_product * up_pre * sigmoid_gate * (1.0 + gate_pre * (1.0 - sigmoid_gate))
        ).astype(jnp.bfloat16)
        grad_up_pre = (grad_product * gate_pre * sigmoid_gate).astype(jnp.bfloat16)
        grad_wgate = inner_rows(normed_mid, grad_gate)
        grad_wup = inner_rows(normed_mid, grad_up_pre)
        grad_normed = against_cols(grad_gate, w_gate[which_layer]) + against_cols(
            grad_up_pre, w_up[which_layer]
        )
        back_mid, grad_gain_two = norm_back(
            hidden_mid, norm_two[which_layer], return_grad(grad_normed)
        )
        grad_hidden = grad_hidden + back_mid
        queries = jnp.dot(normed_in, w_query[which_layer], preferred_element_type=jnp.float32)
        keys_in = jnp.dot(normed_in, w_key[which_layer], preferred_element_type=jnp.float32)
        values_in = jnp.dot(normed_in, w_value[which_layer], preferred_element_type=jnp.float32)
        outgate = jnp.dot(normed_in, w_outgate[which_layer], preferred_element_type=jnp.float32)
        ranked = jnp.dot(normed_in, w_rank[which_layer], preferred_element_type=jnp.float32)
        gated, pullback = jax.vjp(
            mixer_fn,
            queries,
            keys_in,
            values_in,
            outgate,
            ranked,
            w_decay[which_layer].astype(jnp.float32),
            decay_bias[which_layer],
            group_gain[which_layer],
        )
        gated_low = gated.astype(jnp.bfloat16)
        grad_mixbranch = fetch_grad(grad_hidden)
        grad_wout = inner_rows(gated_low, grad_mixbranch)
        grad_gated = against_cols(grad_mixbranch, w_out[which_layer])
        (
            grad_query,
            grad_key,
            grad_value,
            grad_outgate,
            grad_ranked,
            grad_wdecay,
            grad_bias,
            grad_groupgain,
        ) = pullback(grad_gated)
        grad_query = grad_query.astype(jnp.bfloat16)
        grad_key = grad_key.astype(jnp.bfloat16)
        grad_value = grad_value.astype(jnp.bfloat16)
        grad_outgate = grad_outgate.astype(jnp.bfloat16)
        grad_ranked = grad_ranked.astype(jnp.bfloat16)
        grad_wquery = inner_rows(normed_in, grad_query)
        grad_wkey = inner_rows(normed_in, grad_key)
        grad_wvalue = inner_rows(normed_in, grad_value)
        grad_woutgate = inner_rows(normed_in, grad_outgate)
        grad_wrank = inner_rows(normed_in, grad_ranked)
        grad_normed_in = against_cols(grad_query, w_query[which_layer]) + against_cols(
            grad_key, w_key[which_layer]
        )
        grad_normed_in = (
            grad_normed_in
            + against_cols(grad_value, w_value[which_layer])
            + against_cols(grad_outgate, w_outgate[which_layer])
        )
        grad_normed_in = grad_normed_in + against_cols(grad_ranked, w_rank[which_layer])
        back_in, grad_gain_one = norm_back(
            hidden_in, norm_one[which_layer], return_grad(grad_normed_in)
        )
        grad_hidden = grad_hidden + back_in
        split_grads = (
            grad_wquery,
            grad_wkey,
            grad_wvalue,
            grad_woutgate,
            grad_wdecay,
            grad_bias,
            grad_wout,
            grad_wgate,
            grad_wup,
            grad_down,
        )
        split_store[which_layer] = split_grads
        shared_store[which_layer] = (grad_gain_one, grad_wrank, grad_groupgain, grad_gain_two)
    stacked = tuple(
        (
            jnp.stack([split_store[which_layer][member] for which_layer in range(LAYERS)])
            for member in range(10)
        )
    )
    stacked = (
        lax.psum(stacked[0].astype(jnp.bfloat16), "dp").astype(jnp.float32),
        lax.psum(stacked[1].astype(jnp.bfloat16), "dp").astype(jnp.float32),
        lax.psum(stacked[2].astype(jnp.bfloat16), "dp").astype(jnp.float32),
        lax.psum(stacked[3].astype(jnp.bfloat16), "dp").astype(jnp.float32),
        lax.psum(stacked[4].astype(jnp.bfloat16), "dp").astype(jnp.float32),
        lax.psum(stacked[5].astype(jnp.bfloat16), "dp").astype(jnp.float32),
        lax.psum(stacked[6].astype(jnp.bfloat16), "dp").astype(jnp.float32),
        lax.psum(stacked[7].astype(jnp.bfloat16), "dp").astype(jnp.float32),
        lax.psum(stacked[8].astype(jnp.bfloat16), "dp").astype(jnp.float32),
        lax.psum(stacked[9].astype(jnp.bfloat16), "dp").astype(jnp.float32),
    )
    shared = tuple(
        (
            jnp.stack([shared_store[which_layer][member] for which_layer in range(LAYERS)])
            for member in range(4)
        )
    )
    shared = lax.psum((shared[0], shared[1], shared[2], shared[3]), ("dp", "head"))
    grad_tokens = jnp.transpose(grad_hidden, (1, 0, 2))
    return (
        result,
        grad_tokens,
        shared[0],
        stacked[0],
        stacked[1],
        stacked[2],
        stacked[3],
        shared[1],
        stacked[4],
        stacked[5],
        shared[2],
        stacked[6],
        shared[3],
        stacked[7],
        stacked[8],
        stacked[9],
    )


def solution(mesh):
    return jax.shard_map(
        per_device,
        mesh=mesh,
        in_specs=(
            P("dp", "head", None),
            P("dp", None),
            P("dp", "head", None),
            P(),
            P(None, None, "head"),
            P(None, None, "head"),
            P(None, None, "head"),
            P(None, None, "head"),
            P(),
            P(None, None, "head"),
            P(None, "head"),
            P(),
            P(None, "head", None),
            P(),
            P(None, None, "head"),
            P(None, None, "head"),
            P(None, "head", None),
        ),
        out_specs=(
            P("dp", "head", None),
            P("dp", "head", None),
            P(),
            P(None, None, "head"),
            P(None, None, "head"),
            P(None, None, "head"),
            P(None, None, "head"),
            P(),
            P(None, None, "head"),
            P(None, "head"),
            P(),
            P(None, "head", None),
            P(),
            P(None, None, "head"),
            P(None, None, "head"),
            P(None, "head", None),
        ),
        check_vma=False,
    )
```

profile of v0, /device:TPU:0, one launch (start us, length us, event | category | flops | bytes accessed | tf_op | source)
XLA Modules:
  0.0 3490.8 jit_solution(7747792300034795847)
XLA Ops:
  13.4 36.7 %all-gather.16.cloned.1.call-done = bf16[2048,1,1024]{2,0,1:T(8,128)(2,1)} async-done(((bf16[512,1,1024]{2,0,1:T(8,128)(2,1)}), bf16[2048,1,1024]{2,0,1:T(8,128)(2,1)}) %all-gather.16.cloned.1.call-update) | async-done | bytes 4194320 | tf_op jit(solution)/shard_map/all_gather | solution.py:140
  62.7 282.0 %while.104 = (s32[]{:T(128)}, f32[1,1,128,256]{3,2,1,0:T(8,128)S(1)}, f32[32,1,1,64,256]{4,3,2,1,0:T(8,128)S(1)}, f32[32,1,1,64,128]{4,3,2,1,0:T(8,128)}, s32[32...) while((s32[]{:T(128)}, ...), condition=%wide.region_4.5_spmd.clone, body=%wide.region_2.4_spmd.clone.sunk | while | flops 69960128 | bytes 1157893 | solution.py:77
  355.8 71.2 %reduce-scatter.9.cloned.1.call-done = f32[512,1024]{1,0:T(8,128)} async-done(((f32[2048,1024]{1,0:T(8,128)}), f32[512,1024]{1,0:T(8,128)}) %reduce-scatter.9.cloned.1.call-update) | async-done | bytes 2097168 | tf_op jit(solution)/shard_map/reduce_scatter | solution.py:151
  431.2 34.2 all-gather.18.cloned.1.call-done
  484.0 71.8 %reduce-scatter.11.cloned.1.call-done = f32[512,1024]{1,0:T(8,128)} async-done(((f32[2048,1024]{1,0:T(8,128)}), f32[512,1024]{1,0:T(8,128)}) %reduce-scatter.11.cloned.1.call-update) | async-done | bytes 2097168 | tf_op jit(solution)/shard_map/reduce_scatter | solution.py:151
  560.4 34.6 all-gather.20.cloned.1.call-done
  607.5 282.1 %while.105 = (s32[]{:T(128)}, f32[1,1,128,256]{3,2,1,0:T(8,128)S(1)}, f32[32,1,1,64,256]{4,3,2,1,0:T(8,128)S(1)}, f32[32,1,1,64,128]{4,3,2,1,0:T(8,128)}, s32[32...) while((s32[]{:T(128)}, ...), condition=%wide.region_12.13_spmd.clone, body=%wide.region_10.12_spmd.clone.sunk | while | flops 69960128 | bytes 1157893 | solution.py:77
  900.0 71.9 %reduce-scatter.13.cloned.1.call-done = f32[512,1024]{1,0:T(8,128)} async-done(((f32[2048,1024]{1,0:T(8,128)}), f32[512,1024]{1,0:T(8,128)}) %reduce-scatter.13.cloned.1.call-update) | async-done | bytes 2097168 | tf_op jit(solution)/shard_map/reduce_scatter | solution.py:151
  977.3 33.7 all-gather.22.cloned.1.call-done
  1024.9 22.2 all-gather.24.cloned.1.call-done
  1068.9 42.5 %reduce-scatter.17.cloned.1.call-done = bf16[512,1024]{1,0:T(8,128)(2,1)} async-done(((bf16[2048,1024]{1,0:T(8,128)(2,1)}), bf16[512,1024]{1,0:T(8,128)(2,1)}) %reduce-scatter.17.cloned.1.call-update) | async-done | bytes 1048592 | tf_op jit(solution)/shard_map/reduce_scatter | solution.py:160
  1120.0 356.0 %while.106 = (s32[]{:T(128)}, f32[1,1,128,256]{3,2,1,0:T(8,128)S(1)}, f32[32,1,1,64,256]{4,3,2,1,0:T(8,128)}, f32[32,1,1,128,256]{4,3,2,1,0:T(8,128)}, f32[32,1,...) while((s32[]{:T(128)}, ...), condition=%wide.region_21.23_spmd.clone, body=%wide.region_19.22_spmd.clone.sunk | while | flops 69992896 | bytes 1419794 | solution.py:77
  1489.1 368.9 %while.107 = (s32[]{:T(128)}, f32[1,1,128,256]{2,3,1,0:T(8,128)S(1)}, f32[32,1,1,64,128]{4,3,2,1,0:T(8,128)}, bf16[32,1,1,64,128]{4,3,2,1,0:T(8,128)(2,1)}, bf16...) while((s32[]{:T(128)}, ...), condition=%wide.region_29.31_spmd.clone, body=%wide.region_24.30_spmd.clone.sunk | while | flops 146268672 | bytes 4058135 | solution.py:77
  1899.4 35.0 %reduce-scatter.19.cloned.1.call-done = bf16[512,1024]{1,0:T(8,128)(2,1)} async-done(((bf16[2048,1024]{1,0:T(8,128)(2,1)}), bf16[512,1024]{1,0:T(8,128)(2,1)}) %reduce-scatter.19.cloned.1.call-update) | async-done | bytes 1048592 | tf_op jit(solution)/shard_map/reduce_scatter | solution.py:160
  1936.9 71.8 %reduce-scatter.15.cloned.1.call-done = f32[512,1024]{1,0:T(8,128)} async-done(((f32[2048,1024]{1,0:T(8,128)}), f32[512,1024]{1,0:T(8,128)}) %reduce-scatter.15.cloned.1.call-update) | async-done | bytes 2097168 | tf_op jit(solution)/shard_map/reduce_scatter | solution.py:151
  2013.8 34.4 all-gather.28.cloned.1.call-done
  2068.3 44.6 %reduce-scatter.21.cloned.1.call-done = bf16[512,1024]{1,0:T(8,128)(2,1)} async-done(((bf16[2048,1024]{1,0:T(8,128)(2,1)}), bf16[512,1024]{1,0:T(8,128)(2,1)}) %reduce-scatter.21.cloned.1.call-update) | async-done | bytes 1048592 | tf_op jit(solution)/shard_map/reduce_scatter | solution.py:160
  2121.7 348.8 %while.108 = (s32[]{:T(128)}, f32[1,1,128,256]{3,2,1,0:T(8,128)S(1)}, f32[32,1,1,64,256]{4,3,2,1,0:T(8,128)}, f32[32,1,1,128,256]{4,3,2,1,0:T(8,128)}, f32[32,1,...) while((s32[]{:T(128)}, ...), condition=%wide.region_36.38_spmd.clone, body=%wide.region_34.37_spmd.clone.sunk | while | flops 69992896 | bytes 1419794 | solution.py:77
  2494.6 362.9 %while.109 = (s32[]{:T(128)}, f32[1,1,128,256]{2,3,1,0:T(8,128)S(1)}, f32[32,1,1,64,128]{4,3,2,1,0:T(8,128)}, bf16[32,1,1,64,128]{4,3,2,1,0:T(8,128)(2,1)}, bf16...) while((s32[]{:T(128)}, ...), condition=%wide.region_44.46_spmd.clone, body=%wide.region_39.45_spmd.clone.sunk | while | flops 146268672 | bytes 4058135 | solution.py:77
  2876.6 11.6 add_convert_fusion
  2942.5 23.3 all-reduce.3
  2976.0 41.0 %all-reduce.2 = (f32[2,1024]{1,0:T(2,128)}, f32[2,256]{1,0:T(2,128)}, f32[2,1024]{1,0:T(2,128)}) all-reduce(f32[2,1024]{1,0:T(2,128)S(1)} %pad_maximum_fusion.9, f32[2,256]{1,0:T(2,128)S(1)} %pad_maximum_fusion.12, f32[2,1024]{1,0:T(2,128)S(1)} %pad_maximum_fusion.11), channel_id=1, replica_groups=mesh['dp'=8,'head'=4] {'dp','head'}, use_global_device_ids=true, to_apply=%region_49.51 | all-reduce | flops 4608 | bytes 36864 | tf_op jit(solution)/shard_map/psum | solution.py:315
  3017.0 336.8 %all-reduce.10.cloned.1.call-done = (bf16[2,1024,128]{2,1,0:T(8,128)(2,1)}, bf16[2,1024,128]{2,1,0:T(8,128)(2,1)}, bf16[2,1024,256]{2,1,0:T(8,128)(2,1)}, bf16[2...) async-done(((bf16[2,1024,128]{2,1,0:T(8,128)(2,1)}, ...) | async-done | bytes 12845072 | tf_op jit(solution)/shard_map/psum | solution.py:298
  3373.5 108.5 %all-reduce.8.cloned.1.call-done = f32[2,1024,16]{1,2,0:T(8,128)} async-done(((f32[2,1024,16]{1,2,0:T(8,128)}), f32[2,1024,16]{1,2,0:T(8,128)}) %all-reduce.8.cloned.1.call-update) | async-done | bytes 131088 | tf_op jit(solution)/shard_map/psum | solution.py:315
  (4119 shorter events, 2249.0 us)
Async XLA Ops:
  7.2 42.9 %all-gather.16.cloned.1.call-start = ((), (), s32[]{:S(2)}) async-start(), calls=%async_computation.8 | async-start | bytes 5242880 | tf_op jit(solution)/shard_map/all_gather | solution.py:140
  10.2 548.1 %copy-start.80 = (f32[1,1024]{1,0:T(1,128)}, f32[1,1024]{1,0:T(1,128)S(1)}, u32[]{:S(2)}) copy-start(f32[1,1024]{1,0:T(1,128)S(1)} %get-tuple-element.1629) | copy-start | bytes 12292
  12.8 414.2 %reduce-scatter.9.cloned.1.call-start = ((), (), s32[]{:S(2)}) async-start(), calls=%async_computation.9 | async-start | bytes 10485760 | tf_op jit(solution)/shard_map/reduce_scatter | solution.py:151
  13.4 331.8 %copy-start.99 = (f32[1,256]{1,0:T(1,128)}, f32[1,256]{1,0:T(1,128)S(1)}, u32[]{:S(2)}) copy-start(f32[1,256]{1,0:T(1,128)S(1)} %get-tuple-element.1640) | copy-start | bytes 3076
  355.1 110.3 %all-gather.18.cloned.1.call-start = ((), (), s32[]{:S(2)}) async-start(), calls=%async_computation.18 | async-start | bytes 5242880 | tf_op jit(solution)/shard_map/all_gather | solution.py:140
  355.7 73.8 %copy-start.82 = (f32[1,1024]{1,0:T(1,128)}, f32[1,1024]{1,0:T(1,128)S(1)}, u32[]{:S(2)}) copy-start(f32[1,1024]{1,0:T(1,128)S(1)} %get-tuple-element.1628) | copy-start | bytes 12292
  428.9 126.9 %copy-start.4 = (f32[512,1024]{1,0:T(8,128)}, f32[512,1024]{1,0:T(8,128)S(1)}, u32[]{:S(2)}) copy-start(f32[512,1024]{1,0:T(8,128)S(1)} %get-tuple-element.1584) | copy-start | bytes 6291460
  430.8 125.1 %reduce-scatter.11.cloned.1.call-start = ((), (), s32[]{:S(2)}) async-start(), calls=%async_computation.10 | async-start | bytes 10485760 | tf_op jit(solution)/shard_map/reduce_scatter | solution.py:151
  483.9 111.0 %all-gather.20.cloned.1.call-start = ((), (), s32[]{:S(2)}) async-start(), calls=%async_computation.19 | async-start | bytes 5242880 | tf_op jit(solution)/shard_map/all_gather | solution.py:140
  560.3 411.5 %reduce-scatter.13.cloned.1.call-start = ((), (), s32[]{:S(2)}) async-start(), calls=%async_computation.11 | async-start | bytes 10485760 | tf_op jit(solution)/shard_map/reduce_scatter | solution.py:151
  899.9 111.0 %all-gather.22.cloned.1.call-start = ((), (), s32[]{:S(2)}) async-start(), calls=%async_computation.20 | async-start | bytes 5242880 | tf_op jit(solution)/shard_map/all_gather | solution.py:140
  976.3 70.8 %all-gather.24.cloned.1.call-start = ((), (), s32[]{:S(2)}) async-start(), calls=%async_computation.21 | async-start | bytes 5242880 | tf_op jit(solution)/shard_map/all_gather | solution.py:146
  977.1 134.4 %reduce-scatter.17.cloned.1.call-start = ((), (), s32[]{:S(2)}) async-start(), calls=%async_computation.13 | async-start | bytes 5242880 | tf_op jit(solution)/shard_map/reduce_scatter | solution.py:160
  1066.8 411.4 %all-gather.26.cloned.1.call-start = ((), (), s32[]{:S(2)}) async-start(), calls=%async_computation.22 | async-start | bytes 5242880 | tf_op jit(solution)/shard_map/all_gather | solution.py:146
  1115.8 818.5 %reduce-scatter.19.cloned.1.call-start = ((), (), s32[]{:S(2)}) async-start(), calls=%async_computation.14 | async-start | bytes 5242880 | tf_op jit(solution)/shard_map/reduce_scatter | solution.py:160
  1889.7 119.0 %reduce-scatter.15.cloned.1.call-start = ((), (), s32[]{:S(2)}) async-start(), calls=%async_computation.12 | async-start | bytes 10485760 | tf_op jit(solution)/shard_map/reduce_scatter | solution.py:151
  1899.3 109.4 %copy-start.21 = (bf16[1,512,1024]{2,1,0:T(8,128)(2,1)S(1)}, bf16[1,512,1024]{2,1,0:T(8,128)(2,1)}, u32[]{:S(2)}) copy-start(bf16[1,512,1024]{2,1,0:T(8,128)(2,1)} %param.32) | copy-start | bytes 3145732
  1899.3 109.4 %copy-start.96 = (f32[512]{0:T(512)S(1)}, f32[512]{0:T(512)}, u32[]{:S(2)}) copy-start(f32[512]{0:T(512)} %get-tuple-element.1635) | copy-start | bytes 6148
  1899.3 148.9 %all-gather.28.cloned.1.call-start = ((), (), s32[]{:S(2)}) async-start(), calls=%async_computation.23 | async-start | bytes 5242880 | tf_op jit(solution)/shard_map/all_gather | solution.py:146
  2013.6 99.3 %reduce-scatter.21.cloned.1.call-start = ((), (), s32[]{:S(2)}) async-start(), calls=%async_computation.15 | async-start | bytes 5242880 | tf_op jit(solution)/shard_map/reduce_scatter | solution.py:160
  2068.3 416.1 %all-gather.30.cloned.1.call-start = ((), (), s32[]{:S(2)}) async-start(), calls=%async_computation.24 | async-start | bytes 5242880 | tf_op jit(solution)/shard_map/all_gather | solution.py:146
  2117.3 853.3 %reduce-scatter.23.cloned.1.call-start = ((), (), s32[]{:S(2)}) async-start(), calls=%async_computation.16 | async-start | bytes 5242880 | tf_op jit(solution)/shard_map/reduce_scatter | solution.py:160
  2888.2 465.7 %all-reduce.10.cloned.1.call-start = ((), (), s32[]{:S(2)}) async-start(), calls=%async_computation.25 | async-start | bytes 25690112 | tf_op jit(solution)/shard_map/psum | solution.py:298
  2936.9 545.1 %all-reduce.8.cloned.1.call-start = ((), (), s32[]{:S(2)}) async-start(), calls=%async_computation.17 | async-start | bytes 262144 | tf_op jit(solution)/shard_map/psum | solution.py:315
  (128 other events, 1195.3 us)
Sparse Core Ops, SparseCore 0:
  12.9 37.1 all-gather.15
  355.2 71.7 reduce-scatter.8
  430.9 34.4 all-gather.17
  484.1 71.7 reduce-scatter.10
  560.4 34.4 all-gather.19
  900.0 71.7 reduce-scatter.12
  976.4 34.4 all-gather.21
  1012.6 34.4 all-gather.23
  1066.9 44.5 reduce-scatter.16
  1116.0 34.4 all-gather.25
  1889.8 44.4 reduce-scatter.18
  1937.0 71.6 reduce-scatter.14
  2013.7 34.4 all-gather.27
  2068.4 44.4 reduce-scatter.20
  2117.5 34.4 all-gather.29
  2888.3 44.5 reduce-scatter.22
  2939.5 414.3 all-reduce.9
  3360.7 121.2 all-reduce.7
where the time goes:
time: 3550 us; the launch traced here: 3490 us
  waiting for transfers between devices  1050 us (30%)
  matrix products  962 us (27%)
  local copies, waits for them, and re-layouts  703 us (20%)
  other arithmetic  592 us (17%)
  loops' own time  99.8 us (3%)
  blocking collectives  64.3 us (2%)
    psum x1, waiting for transfers between devices, per_device(): lax.psum(stacked[0].astype(jnp.bfloat16), 'dp').astype(jnp.float32)  337 us
    reduce_scatter x4, waiting for transfers between devices, settle(): lax.psum_scatter(jnp.dot(branch, weight, preferred_element_type=jnp.float...  287 us
    squeeze x384, local copies, waits for them, and re-layouts, mix_head(): lax.scan(jax.checkpoint(span_step), start_state, (block_q, block_k, block...  254 us
    dot_general x320, matrix products, span_step(): scores = jnp.dot(scaled_query, scaled_key.T, precision=highest)  201 us
    dot_general x256, matrix products, span_step(): jnp.dot(moved_key.T, values_in, precision=highest)  200 us
    dynamic_slice x320, local copies, waits for them, and re-layouts, mix_head(): lax.scan(jax.checkpoint(span_step), start_state, (block_q, block_k, block...  179 us
    dot_general x256, matrix products, span_step(): jnp.dot(scaled_query, state, precision=highest)  163 us
    dot_general x256, matrix products, span_step(): jnp.dot(scores, values_in, precision=highest)  162 us

commit v1 on v0

v1 whole, which is shorter than its diff:
```python
import jax
import jax.numpy as jnp
from jax import lax
from jax.experimental import pallas as pl
from jax.experimental.pallas import tpu as pltpu
from jax.sharding import PartitionSpec as P

LAYERS = 2
HK = 128
HV = 256
HEAD_COLS = 2 * HK + 2 * HV
BLK = 128
MID = BLK // 2 - 1
epsilon = 1e-06
highest = lax.Precision.HIGHEST
VMEM_LIMIT = 48 * 1024 * 1024

f32 = jnp.float32
bf16 = jnp.bfloat16


def nn(left, right):
    return lax.dot_general(left, right, (((1,), (0,)), ((), ())), preferred_element_type=f32)


def nt(left, right):
    return lax.dot_general(left, right, (((1,), (1,)), ((), ())), preferred_element_type=f32)


def tn(left, right):
    return lax.dot_general(left, right, (((0,), (0,)), ((), ())), preferred_element_type=f32)


def doc_count(meta, ndoc, place):
    total = (meta[0] <= place).astype(jnp.int32)
    for which in range(1, ndoc):
        total = total + (meta[which] <= place).astype(jnp.int32)
    return total


def block_masks(meta, ndoc, start):
    rows = lax.broadcasted_iota(jnp.int32, (BLK, BLK), 0) + start
    cols = lax.broadcasted_iota(jnp.int32, (BLK, BLK), 1) + start
    row_ids = doc_count(meta, ndoc, rows)
    col_ids = doc_count(meta, ndoc, cols)
    id_prev = doc_count(meta, ndoc, start - 1)
    id_last = doc_count(meta, ndoc, start + BLK - 1)
    allowed = (rows >= cols) & (row_ids == col_ids)
    carried = jnp.where(row_ids == id_prev, 1.0, 0.0)
    same = jnp.where(row_ids == id_last, 1.0, 0.0)
    keep = jnp.where(id_last == id_prev, 1.0, 0.0)
    return allowed, carried, same, keep


def split_dot(ones_mat, value, dot):
    high = value.astype(bf16)
    low = (value - high.astype(f32)).astype(bf16)
    return dot(ones_mat, high) + dot(ones_mat, low)


def tri_ones():
    rows = lax.broadcasted_iota(jnp.int32, (BLK, BLK), 0)
    cols = lax.broadcasted_iota(jnp.int32, (BLK, BLK), 1)
    return jnp.where(rows >= cols, 1.0, 0.0).astype(bf16)


def head_parts(x_ref, slot):
    at = slot * HEAD_COLS
    query = x_ref[:, at : at + HK] * (HK**-0.5)
    key = x_ref[:, at + HK : at + 2 * HK]
    value = x_ref[:, at + 2 * HK : at + 2 * HK + HV]
    outgate = x_ref[:, at + 2 * HK + HV : at + HEAD_COLS]
    return query, key, value, outgate


def decay_before(x_ref, wdec_ref, bias_ref):
    ranked = x_ref[:, 2 * HEAD_COLS :]
    return jnp.dot(ranked, wdec_ref[...], precision=highest, preferred_element_type=f32) + bias_ref[...]


def states_kernel(ndoc, meta, x_ref, wdec_ref, bias_ref, run_ref, state_ref, cum_ref, final_ref, state, cum):
    block = pl.program_id(0)

    @pl.when(block == 0)
    def _():
        state[...] = jnp.zeros_like(state)
        cum[...] = jnp.ones_like(cum)

    start = meta[ndoc] + block * BLK
    _, _, same, keep = block_masks(meta, ndoc, start)
    before = decay_before(x_ref, wdec_ref, bias_ref)
    decays = (jnp.minimum(before, 0.0) - jnp.log1p(jnp.exp(-jnp.abs(before)))) * (1.0 / 16.0)
    running = split_dot(tri_ones(), decays, nn)
    run_ref[...] = running
    ending = running[BLK - 1 :, :]
    factor = jnp.exp(ending) * keep
    cum_ref[0] = cum[...]
    cum[...] = cum[...] * factor
    for slot in range(2):
        lanes = slice(slot * HK, slot * HK + HK)
        _, key, value, _ = head_parts(x_ref, slot)
        moved = (key * jnp.exp(ending[:, lanes] - running[:, lanes]) * same).astype(bf16)
        old = state[slot]
        state_ref[0, slot] = old.astype(bf16)
        new = old * factor[:, lanes] + tn(value.astype(bf16), moved)
        state[slot] = new
        final_ref[slot] = new.astype(bf16)


def mix_kernel(ndoc, meta, x_ref, run_ref, state_ref, cum_ref, first_ref, gain_ref, gated_ref, mixed_ref):
    block = pl.program_id(0)
    start = meta[ndoc] + block * BLK
    allowed, carried, _, _ = block_masks(meta, ndoc, start)
    gain = gain_ref[...]
    for slot in range(2):
        lanes = slice(slot * HK, slot * HK + HK)
        cols = slice(slot * HV, slot * HV + HV)
        query, key, value, outgate = head_parts(x_ref, slot)
        running = run_ref[:, lanes]
        middle = running[MID : MID + 1, :]
        rel_query = (query * jnp.exp(running - middle)).astype(bf16)
        rel_key = (key * jnp.exp(middle - running)).astype(bf16)
        scores = jnp.where(allowed, nt(rel_query, rel_key), 0.0).astype(bf16)
        far_query = (query * jnp.exp(running) * carried).astype(bf16)
        state = (state_ref[0, slot].astype(f32) + first_ref[slot].astype(f32) * cum_ref[0][:, lanes]).astype(bf16)
        mixed = nn(scores, value.astype(bf16)) + nt(far_query, state)
        scale = lax.rsqrt(jnp.maximum(jnp.mean(mixed * mixed, axis=-1, keepdims=True), 1.0))
        gated_ref[:, cols] = (mixed * scale * gain * outgate * jax.nn.sigmoid(outgate)).astype(bf16)
        mixed_ref[:, cols] = mixed.astype(bf16)


def back_states_kernel(
    ndoc, nblk, meta, x_ref, run_ref, mixed_ref, dgated_ref, gain_ref,
    dmixed_ref, doutgate_ref, dstate_ref, cum_ref, final_ref, dgain_ref, state, cum,
):
    step = pl.program_id(0)

    @pl.when(step == 0)
    def _():
        state[...] = jnp.zeros_like(state)
        cum[...] = jnp.ones_like(cum)
        dgain_ref[...] = jnp.zeros_like(dgain_ref)

    start = meta[ndoc] + (nblk - 1 - step) * BLK
    _, carried, _, keep = block_masks(meta, ndoc, start)
    gain = gain_ref[...]
    running = run_ref[...]
    factor = jnp.exp(running[BLK - 1 :, :]) * keep
    cum_ref[0] = cum[...]
    cum[...] = cum[...] * factor
    for slot in range(2):
        lanes = slice(slot * HK, slot * HK + HK)
        cols = slice(slot * HV, slot * HV + HV)
        query, _, _, outgate = head_parts(x_ref, slot)
        mixed = mixed_ref[:, cols].astype(f32)
        dgated = dgated_ref[:, cols].astype(f32)
        mean = jnp.mean(mixed * mixed, axis=-1, keepdims=True)
        scale = lax.rsqrt(jnp.maximum(mean, 1.0))
        sig = jax.nn.sigmoid(outgate)
        silu = outgate * sig
        dnormed = dgated * silu
        plain = mixed * scale
        doutgate_ref[:, cols] = (dgated * plain * gain * (sig + silu * (1.0 - sig))).astype(bf16)
        dgain_ref[...] += jnp.sum(dnormed * plain, axis=0, keepdims=True)
        weighted = dnormed * gain
        inner = jnp.where(mean > 1.0, jnp.mean(weighted * plain, axis=-1, keepdims=True), 0.0)
        dmixed = (scale * (weighted - plain * inner)).astype(bf16)
        dmixed_ref[:, cols] = dmixed
        far_query = (query * jnp.exp(running[:, lanes]) * carried).astype(bf16)
        old = state[slot]
        dstate_ref[0, slot] = old.astype(bf16)
        new = old * factor[:, lanes] + tn(dmixed, far_query)
        state[slot] = new
        final_ref[slot] = new.astype(bf16)


def back_kernel(
    ndoc, meta, x_ref, run_ref, state_ref, cum_ref, first_ref, dmixed_ref, doutgate_ref,
    dstate_ref, dcum_ref, dlast_ref, wdec_ref, bias_ref, dx_ref, dwdec_ref, dbias_ref,
):
    block = pl.program_id(0)

    @pl.when(block == 0)
    def _():
        dwdec_ref[...] = jnp.zeros_like(dwdec_ref)
        dbias_ref[...] = jnp.zeros_like(dbias_ref)

    start = meta[ndoc] + block * BLK
    allowed, carried, same, keep = block_masks(meta, ndoc, start)
    last_row = lax.broadcasted_iota(jnp.int32, (BLK, HK), 0) == BLK - 1
    drunning = []
    for slot in range(2):
        lanes = slice(slot * HK, slot * HK + HK)
        cols = slice(slot * HV, slot * HV + HV)
        at = slot * HEAD_COLS
        query, key, value, _ = head_parts(x_ref, slot)
        running = run_ref[:, lanes]
        middle = running[MID : MID + 1, :]
        ending = running[BLK - 1 :, :]
        up = jnp.exp(running - middle)
        down = jnp.exp(middle - running)
        far = jnp.exp(running) * carried
        near = jnp.exp(ending - running) * same
        rel_query = (query * up).astype(bf16)
        rel_key = (key * down).astype(bf16)
        far_query = (query * far).astype(bf16)
        moved = (key * near).astype(bf16)
        value = value.astype(bf16)
        scores = jnp.where(allowed, nt(rel_query, rel_key), 0.0).astype(bf16)
        state = state_ref[0, slot].astype(f32) + first_ref[slot].astype(f32) * cum_ref[0][:, lanes]
        dstate = dstate_ref[0, slot].astype(f32) + dlast_ref[slot].astype(f32) * dcum_ref[0][:, lanes]
        state_low = state.astype(bf16)
        dstate_low = dstate.astype(bf16)
        dmixed = dmixed_ref[:, cols]
        dvalue = tn(scores, dmixed) + nt(moved, dstate_low)
        dscores = jnp.where(allowed, nt(dmixed, value), 0.0).astype(bf16)
        drel_query = nn(dscores, rel_key)
        drel_key = tn(dscores, rel_query)
        dfar = nn(dmixed, state_low)
        dmoved = nn(value, dstate_low)
        dquery = drel_query * up + dfar * far
        dkey = drel_key * down + dmoved * near
        moved_grad = dmoved * moved.astype(f32)
        dending = jnp.sum(moved_grad, axis=0, keepdims=True) + jnp.sum(
            state * dstate, axis=0, keepdims=True
        ) * (jnp.exp(ending) * keep)
        drun = (
            drel_query * rel_query.astype(f32)
            - drel_key * rel_key.astype(f32)
            + dfar * far_query.astype(f32)
            - moved_grad
        )
        drunning.append(drun + jnp.where(last_row, dending, 0.0))
        dx_ref[:, at : at + HK] = (dquery * (HK**-0.5)).astype(bf16)
        dx_ref[:, at + HK : at + 2 * HK] = dkey.astype(bf16)
        dx_ref[:, at + 2 * HK : at + 2 * HK + HV] = dvalue.astype(bf16)
        dx_ref[:, at + 2 * HK + HV : at + HEAD_COLS] = doutgate_ref[:, cols]
    drun_both = jnp.concatenate(drunning, axis=1)
    ddecay = split_dot(tri_ones(), drun_both, tn)
    before = decay_before(x_ref, wdec_ref, bias_ref)
    dbefore = ddecay * (1.0 / 16.0) * jax.nn.sigmoid(-before)
    dbias_ref[...] += jnp.sum(dbefore, axis=0, keepdims=True)
    ranked = x_ref[:, 2 * HEAD_COLS :]
    dlow = dbefore.astype(bf16)
    dwdec_ref[...] += tn(ranked.astype(bf16), dlow)
    dx_ref[:, 2 * HEAD_COLS :] = nt(dlow, wdec_ref[...].astype(bf16)).astype(bf16)


def kernel_params():
    return pltpu.CompilerParams(dimension_semantics=("arbitrary",), vmem_limit_bytes=VMEM_LIMIT)


class Mixer:
    def __init__(self, meta, ndoc, tokens):
        self.meta = meta
        self.ndoc = ndoc
        self.tokens = tokens
        self.nblk = tokens // BLK
        self.half = self.nblk // 2

    def rows(self, width, reverse=False):
        nblk, half, core = self.nblk, self.half, self.ndoc + 1

        def place(step, meta):
            time = nblk - 1 - step if reverse else step
            return (lax.rem(time + meta[core] * half, nblk), 0)

        return pl.BlockSpec((BLK, width), place)

    def per_block(self, shape, reverse=False):
        nblk = self.nblk
        zeros = (0,) * len(shape)
        return pl.BlockSpec(
            (1,) + shape, lambda step, meta: ((nblk - 1 - step if reverse else step),) + zeros
        )

    def whole(self, shape):
        zeros = (0,) * len(shape)
        return pl.BlockSpec(shape, lambda step, meta: zeros)

    def call(self, body, in_specs, out_specs, out_shape, scratch, *args):
        return pl.pallas_call(
            body,
            grid_spec=pltpu.PrefetchScalarGridSpec(
                num_scalar_prefetch=1,
                grid=(self.nblk,),
                in_specs=in_specs,
                out_specs=out_specs,
                scratch_shapes=scratch,
            ),
            out_shape=[jax.ShapeDtypeStruct(s, d) for s, d in out_shape],
            compiler_params=kernel_params(),
        )(self.meta, *args)

    def state_scratch(self):
        return [pltpu.VMEM((2, HV, HK), f32), pltpu.VMEM((1, 2 * HK), f32)]

    def states(self, x, wdec, bias):
        ndoc, n = self.ndoc, self.nblk

        def body(*refs):
            states_kernel(ndoc, *refs)

        return self.call(
            body,
            [self.rows(x.shape[1]), self.whole(wdec.shape), self.whole(bias.shape)],
            [
                self.rows(2 * HK),
                self.per_block((2, HV, HK)),
                self.per_block((1, 2 * HK)),
                self.whole((2, HV, HK)),
            ],
            [
                ((self.tokens, 2 * HK), f32),
                ((n, 2, HV, HK), bf16),
                ((n, 1, 2 * HK), f32),
                ((2, HV, HK), bf16),
            ],
            self.state_scratch(),
            x, wdec, bias,
        )

    def mix(self, x, run, states, cum, first, gain):
        ndoc = self.ndoc

        def body(*refs):
            mix_kernel(ndoc, *refs)

        return self.call(
            body,
            [
                self.rows(x.shape[1]),
                self.rows(2 * HK),
                self.per_block((2, HV, HK)),
                self.per_block((1, 2 * HK)),
                self.whole((2, HV, HK)),
                self.whole(gain.shape),
            ],
            [self.rows(2 * HV), self.rows(2 * HV)],
            [((self.tokens, 2 * HV), bf16), ((self.tokens, 2 * HV), bf16)],
            [],
            x, run, states, cum, first, gain,
        )

    def back_states(self, x, run, mixed, dgated, gain):
        ndoc, n = self.ndoc, self.nblk

        def body(*refs):
            back_states_kernel(ndoc, n, *refs)

        return self.call(
            body,
            [
                self.rows(x.shape[1], True),
                self.rows(2 * HK, True),
                self.rows(2 * HV, True),
                self.rows(2 * HV, True),
                self.whole(gain.shape),
            ],
            [
                self.rows(2 * HV, True),
                self.rows(2 * HV, True),
                self.per_block((2, HV, HK), True),
                self.per_block((1, 2 * HK), True),
                self.whole((2, HV, HK)),
                self.whole((1, HV)),
            ],
            [
                ((self.tokens, 2 * HV), bf16),
                ((self.tokens, 2 * HV), bf16),
                ((n, 2, HV, HK), bf16),
                ((n, 1, 2 * HK), f32),
                ((2, HV, HK), bf16),
                ((1, HV), f32),
            ],
            self.state_scratch(),
            x, run, mixed, dgated, gain,
        )

    def back(self, x, run, states, cum, first, dmixed, doutgate, dstates, dcum, dlast, wdec, bias):
        ndoc = self.ndoc
        rank = wdec.shape[0]

        def body(*refs):
            back_kernel(ndoc, *refs)

        return self.call(
            body,
            [
                self.rows(x.shape[1]),
                self.rows(2 * HK),
                self.per_block((2, HV, HK)),
                self.per_block((1, 2 * HK)),
                self.whole((2, HV, HK)),
                self.rows(2 * HV),
                self.rows(2 * HV),
                self.per_block((2, HV, HK)),
                self.per_block((1, 2 * HK)),
                self.whole((2, HV, HK)),
                self.whole(wdec.shape),
                self.whole(bias.shape),
            ],
            [self.rows(x.shape[1]), self.whole((rank, 2 * HK)), self.whole((1, 2 * HK))],
            [
                ((self.tokens, x.shape[1]), bf16),
                ((rank, 2 * HK), f32),
                ((1, 2 * HK), f32),
            ],
            [],
            x, run, states, cum, first, dmixed, doutgate, dstates, dcum, dlast, wdec, bias,
        )


def norm_scale(hidden):
    return lax.rsqrt(jnp.mean(hidden * hidden, axis=-1, keepdims=True) + epsilon)


def norm_low(hidden, gain):
    return (hidden * norm_scale(hidden) * gain).astype(bf16)


def norm_back(hidden, gain, grad_normed):
    scale = norm_scale(hidden)
    weighted = grad_normed * gain
    grad_hidden = scale * weighted - hidden * (scale * scale * scale) * jnp.mean(
        weighted * hidden, axis=-1, keepdims=True
    )
    return grad_hidden, jnp.sum(grad_normed * hidden * scale, axis=0)


def core_swap(value):
    return lax.ppermute(value, "head", [(i, i ^ 1) for i in range(4)])


def chip_swap(value):
    return lax.ppermute(value, "head", [(i, i ^ 2) for i in range(4)])


def pad_cols(value, width):
    return jnp.pad(value, ((0, 0), (0, width - value.shape[1])))


def pad_rows(value, height):
    return jnp.pad(value, ((0, height - value.shape[0]), (0, 0)))


def per_device(
    tokens, doc_starts, grad_out, norm_one, w_query, w_key, w_value, w_outgate, w_rank, w_decay,
    decay_bias, group_gain, w_out, norm_two, w_gate, w_up, w_down,
):
    shard_len, width = tokens.shape[1:]
    ndoc = doc_starts.shape[1]
    ff = w_gate.shape[2]
    ffp = -(-ff // 128) * 128
    member = lax.axis_index("head")
    core = member % 2
    chip = member // 2
    meta = jnp.concatenate(
        [doc_starts[0], jnp.stack([chip * (2 * shard_len), core]).astype(jnp.int32)]
    )
    mixer = Mixer(meta, ndoc, 2 * shard_len)

    small = jnp.concatenate([w_decay.astype(f32), decay_bias[:, None, :]], axis=1)
    small = jnp.concatenate([small, chip_swap(small)], axis=2)
    rank = w_decay.shape[1]

    mix_w, out_w, in_w, down_w = [], [], [], []
    for layer in range(LAYERS):
        own = jnp.concatenate([w_query[layer], w_key[layer], w_value[layer], w_outgate[layer]], axis=1)
        mix_w.append(jnp.concatenate([own, chip_swap(own), w_rank[layer]], axis=1))
        out_w.append(jnp.concatenate([w_out[layer], chip_swap(w_out[layer])], axis=0))
        own = jnp.concatenate([w_gate[layer], w_up[layer]], axis=1)
        far = chip_swap(own)
        in_w.append(
            jnp.concatenate(
                [
                    pad_cols(part, ffp)
                    for part in (own[:, :ff], far[:, :ff], own[:, ff:], far[:, ff:])
                ],
                axis=1,
            )
        )
        far = chip_swap(w_down[layer])
        down_w.append(jnp.concatenate([pad_rows(w_down[layer], ffp), pad_rows(far, ffp)], axis=0))

    def with_partner(local):
        return jnp.concatenate([local, core_swap(local)], axis=0)

    def settle(dot, branch, weight):
        sent = core_swap(dot(branch[shard_len:], weight).astype(bf16))
        return dot(branch[:shard_len], weight) + sent.astype(f32)

    hidden = tokens[0].astype(f32)
    saved = []
    for layer in range(LAYERS):
        hidden_in = hidden
        a = with_partner(norm_low(hidden, norm_one[layer]))
        x = nn(a, mix_w[layer])
        wdec, bias = small[layer, :rank], small[layer, rank:]
        run, states, cum, final = mixer.states(x, wdec, bias)
        first = chip_swap(final)[::-1] * chip.astype(bf16)
        gain = group_gain[layer][None]
        gated, mixed = mixer.mix(x, run, states, cum, first, gain)
        hidden_mid = hidden + settle(nn, gated, out_w[layer])
        m = with_partner(norm_low(hidden_mid, norm_two[layer]))
        both = nn(m, in_w[layer])
        gate, up = both[:, : 2 * ffp], both[:, 2 * ffp :]
        product = (jax.nn.silu(gate) * up).astype(bf16)
        gate, up = gate.astype(bf16), up.astype(bf16)
        hidden = hidden_mid + settle(nn, product, down_w[layer])
        saved.append(
            (hidden_in, hidden_mid, a, m, x, run, states, cum, first, mixed, gated, gate, up, product)
        )
    result = hidden.astype(bf16)[None]

    grad = grad_out[0].astype(f32)
    split_grads = [None] * LAYERS
    shared_grads = [None] * LAYERS

    def gather_grad(own, far):
        total = own.astype(f32) + chip_swap(far.astype(bf16)).astype(f32)
        return lax.psum(total.astype(bf16), "dp")

    for layer in reversed(range(LAYERS)):
        (
            hidden_in, hidden_mid, a, m, x, run, states, cum, first, mixed, gated, gate, up, product,
        ) = saved[layer]
        gain = group_gain[layer][None]
        wdec, bias = small[layer, :rank], small[layer, rank:]
        g_out = with_partner(grad.astype(bf16))
        dproduct = nt(g_out, down_w[layer])
        gate, up = gate.astype(f32), up.astype(f32)
        sig = jax.nn.sigmoid(gate)
        dgate = (dproduct * up * sig * (1.0 + gate * (1.0 - sig))).astype(bf16)
        dup = (dproduct * gate * sig).astype(bf16)
        dboth = jnp.concatenate([dgate, dup], axis=1)
        g_down = tn(product, g_out).astype(bf16)
        down_grad = gather_grad(g_down[:ff], g_down[ffp : ffp + ff])
        g_in = tn(m, dboth).astype(bf16)
        in_grad = gather_grad(
            jnp.concatenate([g_in[:, :ff], g_in[:, 2 * ffp : 2 * ffp + ff]], axis=1),
            jnp.concatenate([g_in[:, ffp : ffp + ff], g_in[:, 3 * ffp : 3 * ffp + ff]], axis=1),
        )
        back_mid, gain_two = norm_back(hidden_mid, norm_two[layer], settle(nt, dboth, in_w[layer]))
        grad = grad + back_mid
        g_mix = with_partner(grad.astype(bf16))
        dgated = nt(g_mix, out_w[layer])
        g_wout = tn(gated, g_mix).astype(bf16)
        out_grad = gather_grad(g_wout[:HV], g_wout[HV:])
        dmixed, doutgate, dstates, dcum, dfinal, dgain = mixer.back_states(x, run, mixed, dgated, gain)
        dlast = chip_swap(dfinal)[::-1] * (1 - chip).astype(bf16)
        dx, dwdec, dbias = mixer.back(
            x, run, states, cum, first, dmixed, doutgate, dstates, dcum, dlast, wdec, bias
        )
        g_wmix = tn(a, dx)
        mix_grad = gather_grad(g_wmix[:, :HEAD_COLS], g_wmix[:, HEAD_COLS : 2 * HEAD_COLS])
        back_in, gain_one = norm_back(hidden_in, norm_one[layer], settle(nt, dx, mix_w[layer]))
        grad = grad + back_in
        split_grads[layer] = (mix_grad, out_grad, in_grad, down_grad)
        shared_grads[layer] = (
            gain_one,
            g_wmix[:, 2 * HEAD_COLS :],
            dgain[0],
            gain_two,
            jnp.concatenate([dwdec, dbias], axis=0),
        )

    def stacked(group, pick=lambda v: v):
        return jnp.stack([pick(split_grads[layer][group]).astype(f32) for layer in range(LAYERS)])

    shared = [jnp.stack([shared_grads[layer][i] for layer in range(LAYERS)]) for i in range(5)]
    far_small = chip_swap(shared[4][:, :, HK:])
    own_small = lax.psum(shared[4][:, :, :HK] + far_small, "dp")
    shared = lax.psum(tuple(shared[:4]), ("dp", "head"))
    return (
        result,
        grad[None],
        shared[0],
        stacked(0, lambda v: v[:, :HK]),
        stacked(0, lambda v: v[:, HK : 2 * HK]),
        stacked(0, lambda v: v[:, 2 * HK : 2 * HK + HV]),
        stacked(0, lambda v: v[:, 2 * HK + HV :]),
        shared[1],
        own_small[:, :rank],
        own_small[:, rank],
        shared[2],
        stacked(1),
        shared[3],
        stacked(2, lambda v: v[:, :ff]),
        stacked(2, lambda v: v[:, ff:]),
        stacked(3),
    )


def solution(mesh):
    cols = P(None, None, "head")
    rows = P(None, "head", None)
    place = P("dp", "head", None)
    return jax.shard_map(
        per_device,
        mesh=mesh,
        in_specs=(
            place, P("dp", None), place, P(), cols, cols, cols, cols, P(), cols,
            P(None, "head"), P(), rows, P(), cols, cols, rows,
        ),
        out_specs=(
            place, place, P(), cols, cols, cols, cols, P(), cols, P(None, "head"), P(), rows,
            P(), cols, cols, rows,
        ),
        check_vma=False,
    )
```

time: 3550 us -> 1290 us (0.36); the launches traced: 3490 us -> 1290 us
  matrix products: 962 us -> 199 us
  local copies, waits for them, and re-layouts: 703 us -> 71.2 us
  other arithmetic: 592 us -> 77.1 us
  waiting for transfers between devices: 1050 us -> 744 us
  loops' own time: 99.8 us -> 0 us
  Pallas kernels: 0 us -> 75 us
    dot_general x1148 -> x32, matrix products: 962 us -> 199 us  [the longest x12 76.9 us: nt(): lax.dot_general(left, right, (((1,), (1,)), ((), ())), preferred_element_...]
    reduce_scatter x8 -> x0, waiting for transfers between devices: 409 us -> none  [the longest x4 287 us: settle(): lax.psum_scatter(jnp.dot(branch, weight, preferred_element_type=jnp.float...]
    ppermute x0 -> x38, waiting for transfers between devices: none -> 356 us  [the longest x22 343 us: chip_swap(): return lax.ppermute(value, 'head', [(i, i ^ 2) for i in range(4)])]
    squeeze x576 -> x9, local copies, waits for them, and re-layouts: 254 us -> 8.7 us  [the longest x1 2.36 us: per_device(): w_out[layer]]
    slice x388 -> x15, local copies, waits for them, and re-layouts: 234 us -> 8.99 us  [the longest x2 2.69 us: per_device(): far[:, ff:]]
    all_gather x8 -> x0, waiting for transfers between devices: 196 us -> none  [the longest x4 139 us: spread(): return lax.all_gather(local, 'head', axis=0, tiled=True).reshape(-1, width)]
    dynamic_slice x320 -> x0, local copies, waits for them, and re-layouts: 179 us -> none  [mix_head(): lax.scan(jax.checkpoint(span_step), start_state, (block_q, block_k, block...]
    convert_element_type x274 -> x13, other arithmetic: 204 us -> 28.9 us  [the longest x4 13.4 us: gather_grad(): return lax.psum(total.astype(bf16), 'dp')]
where the time goes in v1:
time: 1290 us
  waiting for transfers between devices  744 us (58%)
  matrix products  199 us (15%)
  blocking collectives  82.1 us (6%)
  other arithmetic  77.1 us (6%)
  Pallas kernels  75 us (6%)
  local copies, waits for them, and re-layouts  71.2 us (6%)
  starting transfers between devices  20.5 us (2%)
  between operations  15.9 us (1%)
    ppermute x22, waiting for transfers between devices, chip_swap(): return lax.ppermute(value, 'head', [(i, i ^ 2) for i in range(4)])  343 us
    psum x1, waiting for transfers between devices, gather_grad(): return lax.psum(total.astype(bf16), 'dp')  301 us
    psum x1, waiting for transfers between devices, per_device(): shared = lax.psum(tuple(shared[:4]), ('dp', 'head'))  87 us
    dot_general x12, matrix products, nt(): lax.dot_general(left, right, (((1,), (1,)), ((), ())), preferred_element_...  76.9 us
    pallas_call x8, Pallas kernels, call(): pl.pallas_call(body, grid_spec=pltpu.PrefetchScalarGridSpec(num_scalar_pr...  75 us
    dot_general x12, matrix products, nn(): lax.dot_general(left, right, (((1,), (0,)), ((), ())), preferred_element_...  74.5 us
    dot_general x8, matrix products, tn(): lax.dot_general(left, right, (((0,), (0,)), ((), ())), preferred_element_...  47.8 us
    unnamed x247, local copies, waits for them, and re-layouts  45.9 us
  transfers between devices with their start and end apart: 40, of which 19 were waited for; matrix products, arithmetic and copies ran while one was open for 23% of the time, Pallas kernels for 6%

profile of v1, /device:TPU:0, one launch (start us, length us, event | category | flops | bytes accessed | tf_op | source)
XLA Modules:
  0.0 1285.4 jit_solution(11812598466741294302)
XLA Ops:
  39.9 23.1 %collective-permute-done.1 = bf16[1024,768]{1,0:T(8,128)(2,1)} collective-permute-done((bf16[1024,768]{1,0:T(8,128)(2,1)}, bf16[1024,768]{1,0:T(8,128)(2,1)}, u32[]{:S(2)}, u32[]{:S(2)}) %collective-permute-start.1) | collective-permute-done | bytes 1572896 | tf_op jit(solution)/shard_map/ppermute | solution.py:436
  66.4 9.3 fusion.118.refs_1_
  75.7 9.5 shard_map.288
  85.3 102.5 %collective-permute-done.3 = bf16[2,256,128]{2,1,0:T(8,128)(2,1)S(1)} collective-permute-done((bf16[2,256,128]{2,1,0:T(8,128)(2,1)S(1)}, bf16[2,256,128]{2,1,0:T(8,128)(2,1)S(1)}, u32[]{:S(2)}, u32[]{:S(2)}) %collective-permute-start.3) | collective-permute-done | bytes 131104 | tf_op jit(solution)/shard_map/ppermute | solution.py:436
  214.7 15.8 %fusion.116 = f32[1024,3072]{1,0:T(8,128)} fusion(bf16[512,1024]{1,0:T(8,128)(2,1)} %copy-done.105, bf16[512,1024]{1,0:T(8,128)(2,1)S(1)} %multiply_convert_fusion.4, bf16[1024,704]{0,1:T(8,128)(2,1)S(1)} %slice.380, bf16[1024,704]{0,1:T(8,128)(2,1)S(1)} %copy-done.32, bf16[1024,704]{0,1:T(8,128)(2,1)S(1)} %copy-done.36, ...), kind=kOutput, calls=%fused_computation.189 | convolution fusion | flops 6496976896 | bytes 20578304 | tf_op jit(solution)/shard_map/dot_general | solution.py:23
  254.9 27.8 %collective-permute-done.11 = bf16[1024,768]{1,0:T(8,128)(2,1)} collective-permute-done((bf16[1024,768]{1,0:T(8,128)(2,1)S(1)}, bf16[1024,768]{1,0:T(8,128)(2,1)}, u32[]{:S(2)}, u32[]{:S(2)}) %collective-permute-start.11) | collective-permute-done | bytes 1572896 | tf_op jit(solution)/shard_map/ppermute | solution.py:436
  286.1 9.3 fusion.115.refs_1_
  295.4 9.3 shard_map.290
  328.6 14.1 %fusion.113 = f32[1024,3072]{1,0:T(8,128)} fusion(bf16[512,1024]{1,0:T(8,128)(2,1)S(1)} %collective-permute-done.15, bf16[512,1024]{1,0:T(8,128)(2,1)S(1)} %multiply_convert_fusion.2, bf16[1024,704]{0,1:T(8,128)(2,1)} %slice.387, bf16[1024,704]{0,1:T(8,128)(2,1)S(1)} %copy-done.39, bf16[1024,704]{0,1:T(8,128)(2,1)S(1)} %copy-done.40, ...), kind=kOutput, calls=%fused_computation.186 | convolution fusion | flops 6496976896 | bytes 20578304 | tf_op jit(solution)/shard_map/dot_general | solution.py:23
  342.8 17.2 %collective-permute-done.17 = bf16[704,1024]{1,0:T(8,128)(2,1)} collective-permute-done((bf16[704,1024]{1,0:T(8,128)(2,1)}, bf16[704,1024]{1,0:T(8,128)(2,1)}, u32[]{:S(2)}, u32[]{:S(2)}) %collective-permute-start.17) | collective-permute-done | bytes 1441824 | tf_op jit(solution)/shard_map/ppermute | solution.py:436
  360.0 16.0 %fusion.16 = (bf16[1024,1536]{1,0:T(8,128)(2,1)}, bf16[1024,1536]{1,0:T(8,128)(2,1)}, bf16[1024,1536]{1,0:T(8,128)(2,1)}) fusion(f32[1024,3072]{1,0:T(8,128)} %fusion.113, bf16[704,1024]{1,0:T(8,128)(2,1)} %collective-permute-done.17, bf16[704,1024]{1,0:T(8,128)(2,1)} %get-tuple-element.134, bf16[512,1024]{1,0:T(8,128)(2,1)} %collective-permute-done.19, ...), kind=kOutput, calls=%fused_computation.36 | convolution fusion | flops 3271032832 | bytes 33292288 | tf_op jit(solution)/shard_map/dot_general | solution.py:27
  415.7 10.3 fusion.35
  426.0 11.8 collective-permute-done.22
  437.8 12.1 shard_map.293
  479.9 54.2 %collective-permute-done.33 = bf16[256,1024]{1,0:T(8,128)(2,1)S(1)} collective-permute-done((bf16[256,1024]{1,0:T(8,128)(2,1)S(1)}, bf16[256,1024]{1,0:T(8,128)(2,1)S(1)}, u32[]{:S(2)}, u32[]{:S(2)}) %collective-permute-start.33) | collective-permute-done | bytes 524320 | tf_op jit(solution)/shard_map/ppermute | solution.py:436
  538.4 9.8 fusion.24
  555.6 9.3 fusion.36
  604.6 73.7 %collective-permute-done.27 = bf16[2,256,128]{2,1,0:T(8,128)(2,1)S(1)} collective-permute-done((bf16[2,256,128]{2,1,0:T(8,128)(2,1)S(1)}, bf16[2,256,128]{2,1,0:T(8,128)(2,1)S(1)}, u32[]{:S(2)}, u32[]{:S(2)}) %collective-permute-start.27) | collective-permute-done | bytes 131104 | tf_op jit(solution)/shard_map/ppermute | solution.py:436
  678.4 12.4 shard_map.295
  711.1 20.9 %collective-permute-done.29 = bf16[1024,768]{0,1:T(8,128)(2,1)S(1)} collective-permute-done((bf16[1024,768]{0,1:T(8,128)(2,1)S(1)}, bf16[1024,768]{0,1:T(8,128)(2,1)S(1)}, u32[]{:S(2)}, u32[]{:S(2)}) %collective-permute-start.29) | collective-permute-done | bytes 1572896 | tf_op jit(solution)/shard_map/ppermute | solution.py:436
  753.6 40.2 %psum.95 = f32[2,17,128]{2,1,0:T(8,128)S(1)} all-reduce(f32[2,17,128]{2,1,0:T(8,128)S(1)} %fusion.131), channel_id=1, replica_groups=mesh['dp'=8,'head'=4] {'dp'}, use_global_device_ids=true, to_apply=%region_14.15 | all-reduce | flops 4352 | bytes 34816 | tf_op jit(solution)/shard_map/psum | solution.py:573
  801.3 41.9 %all-reduce.10 = (f32[2,1024]{1,0:T(2,128)}, f32[2,256]{1,0:T(2,128)}, f32[2,1024]{1,0:T(2,128)}) all-reduce(f32[2,1024]{1,0:T(2,128)S(1)} %pad_maximum_fusion.50, f32[2,256]{1,0:T(2,128)S(1)} %pad_maximum_fusion.52, f32[2,1024]{1,0:T(2,128)S(1)} %pad_maximum_fusion.51), channel_id=1, replica_groups=mesh['dp'=8,'head'=4] {'dp','head'}, use_global_device_ids=true, to_apply=%region_10.11 | all-reduce | flops 4608 | bytes 36864 | tf_op jit(solution)/shard_map/psum | solution.py:574
  847.3 301.3 %all-reduce.17.cloned.1.call-done = (bf16[1024,768]{0,1:T(8,128)(2,1)}, bf16[1024,768]{0,1:T(8,128)(2,1)}, bf16[1,256,1024]{2,1,0:T(8,128)(2,1)}, bf16[1,256,102...) async-done(((bf16[1024,768]{0,1:T(8,128)(2,1)}, ...) | async-done | bytes 12845072 | tf_op jit(solution)/shard_map/psum | solution.py:522
  1189.8 87.0 %all-reduce.15.cloned.1.call-done = f32[2,1024,16]{1,2,0:T(8,128)} async-done(((f32[2,1024,16]{1,2,0:T(8,128)}), f32[2,1024,16]{1,2,0:T(8,128)}) %all-reduce.15.cloned.1.call-update) | async-done | bytes 131088 | tf_op jit(solution)/shard_map/psum | solution.py:574
  (440 shorter events, 330.7 us)
Async XLA Ops:
  7.2 1141.5 %all-reduce.17.cloned.1.call-start = ((), (), s32[]{:S(2)}) async-start(), calls=%async_computation.1 | async-start | bytes 25690112 | tf_op jit(solution)/shard_map/psum | solution.py:522
  14.1 181.5 %collective-permute-start.4 = (bf16[256,1024]{1,0:T(8,128)(2,1)}, bf16[256,1024]{1,0:T(8,128)(2,1)}, u32[]{:S(2)}, u32[]{:S(2)}) collective-permute-start(bf16[256,1024]{1,0:T(8,128)(2,1)} %get-tuple-element.149), channel_id=1, source_target_pairs={{0,2},{1,3},{2,0},{3,1},{4,6},{5,7},{6,4},{7,5},{8,10},{9,11},{10,... | collective-permute-start | bytes 1572872 | tf_op jit(solution)/shard_map/ppermute | solution.py:436
  17.7 48.7 %collective-permute-start = (bf16[512,1024]{1,0:T(8,128)(2,1)}, bf16[512,1024]{1,0:T(8,128)(2,1)}, u32[]{:S(2)}, u32[]{:S(2)}) collective-permute-start(bf16[512,1024]{1,0:T(8,128)(2,1)} %fusion.55), channel_id=1, source_target_pairs={{0,1},{1,0},{2,3},{3,2},{4,5},{5,4},{6,7},{7,6},{8,9},{9,8},{10,11... | collective-permute-start | bytes 3145736 | tf_op jit(solution)/shard_map/ppermute | solution.py:432
  20.8 42.1 %collective-permute-start.1 = (bf16[1024,768]{1,0:T(8,128)(2,1)}, bf16[1024,768]{1,0:T(8,128)(2,1)}, u32[]{:S(2)}, u32[]{:S(2)}) collective-permute-start(bf16[1024,768]{1,0:T(8,128)(2,1)} %pad_maximum_fusion.20), channel_id=1, source_target_pairs={{0,2},{1,3},{2,0},{3,1},{4,6},{5,7},{6,4},{7,5},{8,10},{9,11},{10,... | collective-permute-start | bytes 4718600 | tf_op jit(solution)/shard_map/ppermute | solution.py:436
  28.0 179.8 %collective-permute-start.7 = (bf16[1024,1408]{0,1:T(8,128)(2,1)}, bf16[1024,1408]{0,1:T(8,128)(2,1)}, u32[]{:S(2)}, u32[]{:S(2)}) collective-permute-start(bf16[1024,1408]{0,1:T(8,128)(2,1)} %pad_maximum_fusion.8), channel_id=1, source_target_pairs={{0,2},{1,3},{2,0},{3,1},{4,6},{5,7},{6,4},{7,5},{8,10},{9,11},{10,... | collective-permute-start | bytes 8650760 | tf_op jit(solution)/shard_map/ppermute | solution.py:436
  39.0 170.3 %collective-permute-start.16 = (bf16[1024,1408]{0,1:T(8,128)(2,1)}, bf16[1024,1408]{0,1:T(8,128)(2,1)S(1)}, u32[]{:S(2)}, u32[]{:S(2)}) collective-permute-start(bf16[1024,1408]{0,1:T(8,128)(2,1)} %pad_maximum_fusion.9), channel_id=1, source_target_pairs={{0,2},{1,3},{2,0},{3,1},{4,6},{5,7},{6,4},{7,5},{8,10},{9,11},{10,... | collective-permute-start | bytes 8650760 | tf_op jit(solution)/shard_map/ppermute | solution.py:436
  85.2 102.6 %collective-permute-start.3 = (bf16[2,256,128]{2,1,0:T(8,128)(2,1)S(1)}, bf16[2,256,128]{2,1,0:T(8,128)(2,1)S(1)}, u32[]{:S(2)}, u32[]{:S(2)}) collective-permute-start(bf16[2,256,128]{2,1,0:T(8,128)(2,1)S(1)} %get-tuple-element.49), channel_id=1, source_target_pairs={{0,2},{1,3},{2,0},{3,1},{4,6},{5,7},{6,4},{7,5},{8,10},{9,11},{10,... | collective-permute-start | bytes 393224 | tf_op jit(solution)/shard_map/ppermute | solution.py:436
  207.6 33.9 %collective-permute-start.8 = (bf16[704,1024]{1,0:T(8,128)(2,1)}, bf16[704,1024]{1,0:T(8,128)(2,1)}, u32[]{:S(2)}, u32[]{:S(2)}) collective-permute-start(bf16[704,1024]{1,0:T(8,128)(2,1)} %get-tuple-element.135), channel_id=1, source_target_pairs={{0,2},{1,3},{2,0},{3,1},{4,6},{5,7},{6,4},{7,5},{8,10},{9,11},{10,... | collective-permute-start | bytes 4325384 | tf_op jit(solution)/shard_map/ppermute | solution.py:436
  245.3 37.4 %collective-permute-start.11 = (bf16[1024,768]{1,0:T(8,128)(2,1)S(1)}, bf16[1024,768]{1,0:T(8,128)(2,1)}, u32[]{:S(2)}, u32[]{:S(2)}) collective-permute-start(bf16[1024,768]{1,0:T(8,128)(2,1)S(1)} %pad_maximum_fusion.21), channel_id=1, source_target_pairs={{0,2},{1,3},{2,0},{3,1},{4,6},{5,7},{6,4},{7,5},{8,10},{9,11},{10,... | collective-permute-start | bytes 4718600 | tf_op jit(solution)/shard_map/ppermute | solution.py:436
  254.3 31.8 %collective-permute-start.10 = (bf16[512,1024]{1,0:T(8,128)(2,1)}, bf16[512,1024]{1,0:T(8,128)(2,1)}, u32[]{:S(2)}, u32[]{:S(2)}) collective-permute-start(bf16[512,1024]{1,0:T(8,128)(2,1)} %multiply_convert_fusion.3), channel_id=1, source_target_pairs={{0,1},{1,0},{2,3},{3,2},{4,5},{5,4},{6,7},{7,6},{8,9},{9,8},{10,11... | collective-permute-start | bytes 3145736 | tf_op jit(solution)/shard_map/ppermute | solution.py:432
  254.5 63.0 %collective-permute-start.13 = (bf16[256,1024]{1,0:T(8,128)(2,1)}, bf16[256,1024]{1,0:T(8,128)(2,1)}, u32[]{:S(2)}, u32[]{:S(2)}) collective-permute-start(bf16[256,1024]{1,0:T(8,128)(2,1)} %get-tuple-element.148), channel_id=1, source_target_pairs={{0,2},{1,3},{2,0},{3,1},{4,6},{5,7},{6,4},{7,5},{8,10},{9,11},{10,... | collective-permute-start | bytes 1572872 | tf_op jit(solution)/shard_map/ppermute | solution.py:436
  326.0 33.9 %collective-permute-start.17 = (bf16[704,1024]{1,0:T(8,128)(2,1)}, bf16[704,1024]{1,0:T(8,128)(2,1)}, u32[]{:S(2)}, u32[]{:S(2)}) collective-permute-start(bf16[704,1024]{1,0:T(8,128)(2,1)} %get-tuple-element.134), channel_id=1, source_target_pairs={{0,2},{1,3},{2,0},{3,1},{4,6},{5,7},{6,4},{7,5},{8,10},{9,11},{10,... | collective-permute-start | bytes 4325384 | tf_op jit(solution)/shard_map/ppermute | solution.py:436
  400.9 56.8 %collective-permute-start.37 = (bf16[704,1024]{1,0:T(8,128)(2,1)}, bf16[704,1024]{1,0:T(8,128)(2,1)}, u32[]{:S(2)}, u32[]{:S(2)}) collective-permute-start(bf16[704,1024]{1,0:T(8,128)(2,1)} %slice.437), channel_id=1, source_target_pairs={{0,2},{1,3},{2,0},{3,1},{4,6},{5,7},{6,4},{7,5},{8,10},{9,11},{10,... | collective-permute-start | bytes 4325384 | tf_op jit(solution)/shard_map/ppermute | solution.py:436
  457.4 77.9 %collective-permute-start.35 = (bf16[1024,1408]{1,0:T(8,128)(2,1)}, bf16[1024,1408]{1,0:T(8,128)(2,1)S(1)}, u32[]{:S(2)}, u32[]{:S(2)}) collective-permute-start(bf16[1024,1408]{1,0:T(8,128)(2,1)} %pad_maximum_fusion.11), channel_id=1, source_target_pairs={{0,2},{1,3},{2,0},{3,1},{4,6},{5,7},{6,4},{7,5},{8,10},{9,11},{10,... | collective-permute-start | bytes 8650760 | tf_op jit(solution)/shard_map/ppermute | solution.py:436
  464.5 69.7 %collective-permute-start.33 = (bf16[256,1024]{1,0:T(8,128)(2,1)S(1)}, bf16[256,1024]{1,0:T(8,128)(2,1)S(1)}, u32[]{:S(2)}, u32[]{:S(2)}) collective-permute-start(bf16[256,1024]{1,0:T(8,128)(2,1)S(1)} %slice.421), channel_id=1, source_target_pairs={{0,2},{1,3},{2,0},{3,1},{4,6},{5,7},{6,4},{7,5},{8,10},{9,11},{10,... | collective-permute-start | bytes 1572872 | tf_op jit(solution)/shard_map/ppermute | solution.py:436
  469.9 68.4 %collective-permute-start.24 = (bf16[512,1024]{1,0:T(8,128)(2,1)S(1)}, bf16[512,1024]{1,0:T(8,128)(2,1)}, u32[]{:S(2)}, u32[]{:S(2)}) collective-permute-start(bf16[512,1024]{1,0:T(8,128)(2,1)S(1)} %get-tuple-element.113), channel_id=1, source_target_pairs={{0,1},{1,0},{2,3},{3,2},{4,5},{5,4},{6,7},{7,6},{8,9},{9,8},{10,11... | collective-permute-start | bytes 3145736 | tf_op jit(solution)/shard_map/ppermute | solution.py:432
  479.6 218.2 %collective-permute-start.30 = (bf16[1024,768]{0,1:T(8,128)(2,1)}, bf16[1024,768]{0,1:T(8,128)(2,1)}, u32[]{:S(2)}, u32[]{:S(2)}) collective-permute-start(bf16[1024,768]{0,1:T(8,128)(2,1)} %slice.620), channel_id=1, source_target_pairs={{0,2},{1,3},{2,0},{3,1},{4,6},{5,7},{6,4},{7,5},{8,10},{9,11},{10,... | collective-permute-start | bytes 4718600 | tf_op jit(solution)/shard_map/ppermute | solution.py:436
  579.1 129.0 %collective-permute-start.34 = (bf16[1024,1408]{1,0:T(8,128)(2,1)}, bf16[1024,1408]{1,0:T(8,128)(2,1)S(1)}, u32[]{:S(2)}, u32[]{:S(2)}) collective-permute-start(bf16[1024,1408]{1,0:T(8,128)(2,1)} %pad_maximum_fusion.10), channel_id=1, source_target_pairs={{0,2},{1,3},{2,0},{3,1},{4,6},{5,7},{6,4},{7,5},{8,10},{9,11},{10,... | collective-permute-start | bytes 8650760 | tf_op jit(solution)/shard_map/ppermute | solution.py:436
  585.7 117.8 %collective-permute-start.36 = (bf16[704,1024]{1,0:T(8,128)(2,1)}, bf16[704,1024]{1,0:T(8,128)(2,1)}, u32[]{:S(2)}, u32[]{:S(2)}) collective-permute-start(bf16[704,1024]{1,0:T(8,128)(2,1)} %slice.435), channel_id=1, source_target_pairs={{0,2},{1,3},{2,0},{3,1},{4,6},{5,7},{6,4},{7,5},{8,10},{9,11},{10,... | collective-permute-start | bytes 4325384 | tf_op jit(solution)/shard_map/ppermute | solution.py:436
  599.9 78.4 %collective-permute-start.27 = (bf16[2,256,128]{2,1,0:T(8,128)(2,1)S(1)}, bf16[2,256,128]{2,1,0:T(8,128)(2,1)S(1)}, u32[]{:S(2)}, u32[]{:S(2)}) collective-permute-start(bf16[2,256,128]{2,1,0:T(8,128)(2,1)S(1)} %get-tuple-element.68), channel_id=1, source_target_pairs={{0,2},{1,3},{2,0},{3,1},{4,6},{5,7},{6,4},{7,5},{8,10},{9,11},{10,... | collective-permute-start | bytes 393224 | tf_op jit(solution)/shard_map/ppermute | solution.py:436
  603.1 104.0 %collective-permute-start.32 = (bf16[256,1024]{1,0:T(8,128)(2,1)S(1)}, bf16[256,1024]{1,0:T(8,128)(2,1)S(1)}, u32[]{:S(2)}, u32[]{:S(2)}) collective-permute-start(bf16[256,1024]{1,0:T(8,128)(2,1)S(1)} %slice.419), channel_id=1, source_target_pairs={{0,2},{1,3},{2,0},{3,1},{4,6},{5,7},{6,4},{7,5},{8,10},{9,11},{10,... | collective-permute-start | bytes 1572872 | tf_op jit(solution)/shard_map/ppermute | solution.py:436
  697.4 34.6 %collective-permute-start.29 = (bf16[1024,768]{0,1:T(8,128)(2,1)S(1)}, bf16[1024,768]{0,1:T(8,128)(2,1)S(1)}, u32[]{:S(2)}, u32[]{:S(2)}) collective-permute-start(bf16[1024,768]{0,1:T(8,128)(2,1)S(1)} %slice.621), channel_id=1, source_target_pairs={{0,2},{1,3},{2,0},{3,1},{4,6},{5,7},{6,4},{7,5},{8,10},{9,11},{10,... | collective-permute-start | bytes 4718600 | tf_op jit(solution)/shard_map/ppermute | solution.py:436
  733.8 543.0 %all-reduce.15.cloned.1.call-start = ((), (), s32[]{:S(2)}) async-start(), calls=%async_computation | async-start | bytes 262144 | tf_op jit(solution)/shard_map/psum | solution.py:574
  749.6 45.3 %collective-permute-start.28 = (bf16[512,1024]{1,0:T(8,128)(2,1)}, bf16[512,1024]{1,0:T(8,128)(2,1)S(1)}, u32[]{:S(2)}, u32[]{:S(2)}) collective-permute-start(bf16[512,1024]{1,0:T(8,128)(2,1)} %fusion.96), channel_id=1, source_target_pairs={{0,1},{1,0},{2,3},{3,2},{4,5},{5,4},{6,7},{7,6},{8,9},{9,8},{10,11... | collective-permute-start | bytes 3145736 | tf_op jit(solution)/shard_map/ppermute | solution.py:432
  (133 other events, 2213.4 us)
Sparse Core Ops, SparseCore 0:
  733.9 414.7 all-reduce.16
  1155.7 121.0 all-reduce.14

commit v2 on v1

--- a/solution.py
+++ b/solution.py
@@ -130,7 +130,7 @@
 
 
 def back_states_kernel(
-    ndoc, nblk, meta, x_ref, run_ref, mixed_ref, dgated_ref, gain_ref,
+    ndoc, nblk, meta, x_ref, run_ref, mixed_ref, grad_ref, own_out_ref, far_out_ref, gain_ref,
     dmixed_ref, doutgate_ref, dstate_ref, cum_ref, final_ref, dgain_ref, state, cum,
 ):
     step = pl.program_id(0)
@@ -153,7 +153,7 @@
         cols = slice(slot * HV, slot * HV + HV)
         query, _, _, outgate = head_parts(x_ref, slot)
         mixed = mixed_ref[:, cols].astype(f32)
-        dgated = dgated_ref[:, cols].astype(f32)
+        dgated = nt(grad_ref[...], (own_out_ref, far_out_ref)[slot][...])
         mean = jnp.mean(mixed * mixed, axis=-1, keepdims=True)
         scale = lax.rsqrt(jnp.maximum(mean, 1.0))
         sig = jax.nn.sigmoid(outgate)
@@ -342,7 +342,7 @@
             x, run, states, cum, first, gain,
         )
 
-    def back_states(self, x, run, mixed, dgated, gain):
+    def back_states(self, x, run, mixed, grad, own_out, far_out, gain):
         ndoc, n = self.ndoc, self.nblk
 
         def body(*refs):
@@ -354,7 +354,9 @@
                 self.rows(x.shape[1], True),
                 self.rows(2 * HK, True),
                 self.rows(2 * HV, True),
-                self.rows(2 * HV, True),
+                self.rows(grad.shape[1], True),
+                self.whole(own_out.shape),
+                self.whole(far_out.shape),
                 self.whole(gain.shape),
             ],
             [
@@ -374,7 +376,7 @@
                 ((1, HV), f32),
             ],
             self.state_scratch(),
-            x, run, mixed, dgated, gain,
+            x, run, mixed, grad, own_out, far_out, gain,
         )
 
     def back(self, x, run, states, cum, first, dmixed, doutgate, dstates, dcum, dlast, wdec, bias):
@@ -411,6 +413,290 @@
         )
 
 
+ROWS_BLK = 256
+
+
+def layer_spec(array, layer):
+    if array.ndim == 3:
+        return pl.BlockSpec((None,) + array.shape[1:], lambda i: (layer, 0, 0))
+    return pl.BlockSpec(array.shape, lambda i: (0, 0))
+
+
+def row_spec(array, first=0, last=None):
+    def place(i):
+        at = i + first
+        return (at if last is None else jnp.minimum(at, last), 0)
+
+    return pl.BlockSpec((ROWS_BLK, array.shape[1]), place)
+
+
+def grid_params():
+    return pltpu.CompilerParams(dimension_semantics=("arbitrary",), vmem_limit_bytes=VMEM_LIMIT)
+
+
+def sum_of_dots(terms, layer, first_row, rows, out_type):
+    lefts = []
+    for left, _, _, _ in terms:
+        if not any(left is seen for seen in lefts):
+            lefts.append(left)
+    which = [next(i for i, seen in enumerate(lefts) if seen is left) for left, _, _, _ in terms]
+    rights = [right for _, _, right, _ in terms]
+    width = rights[0].shape[-2] if terms[0][3] else rights[0].shape[-1]
+
+    def body(*refs):
+        left_refs, right_refs, out = refs[: len(lefts)], refs[len(lefts) : -1], refs[-1]
+        total = None
+        for (_, at, _, turned), index, right in zip(terms, which, right_refs):
+            depth = right.shape[1] if turned else right.shape[0]
+            part = (nt if turned else nn)(left_refs[index][:, at : at + depth], right[...])
+            total = part if total is None else total + part
+        out[...] = total.astype(out_type)
+
+    return pl.pallas_call(
+        body,
+        grid=(rows // ROWS_BLK,),
+        in_specs=[row_spec(v, first_row // ROWS_BLK) for v in lefts] + [layer_spec(v, layer) for v in rights],
+        out_specs=pl.BlockSpec((ROWS_BLK, width), lambda i: (i, 0)),
+        out_shape=jax.ShapeDtypeStruct((rows, width), out_type),
+        compiler_params=grid_params(),
+    )(*lefts, *rights)
+
+
+def project(a, parts, layer):
+    widths = [v.shape[-1] for v in parts]
+
+    def body(left, *refs):
+        out = refs[-1]
+        at = 0
+        for right, width in zip(refs[:-1], widths):
+            out[:, at : at + width] = nn(left[...], right[...])
+            at += width
+
+    return pl.pallas_call(
+        body,
+        grid=(a.shape[0] // ROWS_BLK,),
+        in_specs=[row_spec(a)] + [layer_spec(v, layer) for v in parts],
+        out_specs=pl.BlockSpec((ROWS_BLK, sum(widths)), lambda i: (i, 0)),
+        out_shape=jax.ShapeDtypeStruct((a.shape[0], sum(widths)), f32),
+        compiler_params=grid_params(),
+    )(a, *parts)
+
+
+def ff_forward(m, w_gate, w_up, far, layer, ffp):
+    ff = w_gate.shape[-1]
+
+    def body(m_ref, gate_w, up_w, far_w, gate_ref, up_ref, product_ref):
+        m = m_ref[...]
+        both = nn(m, far_w[...])
+        values = ((nn(m, gate_w[...]), nn(m, up_w[...])), (both[:, :ff], both[:, ff:]))
+        for slot, (gate, up) in enumerate(values):
+            at = slot * ffp
+            gate_ref[:, at : at + ff] = gate.astype(bf16)
+            up_ref[:, at : at + ff] = up.astype(bf16)
+            product_ref[:, at : at + ff] = (gate * jax.nn.sigmoid(gate) * up).astype(bf16)
+
+    shape = (m.shape[0], 2 * ffp)
+    return pl.pallas_call(
+        body,
+        grid=(m.shape[0] // ROWS_BLK,),
+        in_specs=[row_spec(m), layer_spec(w_gate, layer), layer_spec(w_up, layer), layer_spec(far, layer)],
+        out_specs=[pl.BlockSpec((ROWS_BLK, 2 * ffp), lambda i: (i, 0))] * 3,
+        out_shape=[jax.ShapeDtypeStruct(shape, bf16)] * 3,
+        compiler_params=grid_params(),
+    )(m, w_gate, w_up, far)
+
+
+def ff_backward(m_all, g_all, gate, up, product, w_gate, w_up, w_down, down_far, layer, ffp):
+    ff = w_gate.shape[-1]
+    near = gate.shape[0] // ROWS_BLK
+
+    def pair(gate, up, dproduct):
+        sig = jax.nn.sigmoid(gate)
+        silu = gate * sig
+        dgate = dproduct * up * (sig + silu * (1.0 - sig))
+        return jnp.concatenate([dgate.astype(bf16), (dproduct * silu).astype(bf16)], axis=1), silu
+
+    def body(m_ref, g_ref, gate_ref, up_ref, product_ref, gate_w, up_w, down_w, far_w, own_ref, far_ref, all_ref):
+        step = pl.program_id(0)
+        g = g_ref[...]
+        dproduct = nt(g, down_w[...])
+
+        @pl.when(step < near)
+        def _():
+            own_ref[...] = pair(gate_ref[:, :ff].astype(f32), up_ref[:, :ff].astype(f32), dproduct)[0]
+            all_ref[...] = product_ref[:, :ff]
+            cols = slice(ffp, ffp + ff)
+            far_ref[...] = pair(
+                gate_ref[:, cols].astype(f32), up_ref[:, cols].astype(f32), nt(g, far_w[...])
+            )[0]
+
+        @pl.when(step >= near)
+        def _():
+            gate, up = nn(m_ref[...], gate_w[...]), nn(m_ref[...], up_w[...])
+            value, silu = pair(gate, up, dproduct)
+            own_ref[...] = value
+            all_ref[...] = (silu * up).astype(bf16)
+
+    rows = m_all.shape[0]
+    far_rows = gate.shape[0]
+    return pl.pallas_call(
+        body,
+        grid=(rows // ROWS_BLK,),
+        in_specs=[
+            pl.BlockSpec((ROWS_BLK, m_all.shape[1]), lambda i: (jnp.maximum(i, near), 0)),
+            row_spec(g_all),
+            row_spec(gate, 0, near - 1),
+            row_spec(up, 0, near - 1),
+            row_spec(product, 0, near - 1),
+            layer_spec(w_gate, layer),
+            layer_spec(w_up, layer),
+            layer_spec(w_down, layer),
+            layer_spec(down_far, layer),
+        ],
+        out_specs=[
+            pl.BlockSpec((ROWS_BLK, 2 * ff), lambda i: (i, 0)),
+            pl.BlockSpec((ROWS_BLK, 2 * ff), lambda i: (jnp.minimum(i, near - 1), 0)),
+            pl.BlockSpec((ROWS_BLK, ff), lambda i: (i, 0)),
+        ],
+        out_shape=[
+            jax.ShapeDtypeStruct((rows, 2 * ff), bf16),
+            jax.ShapeDtypeStruct((far_rows, 2 * ff), bf16),
+            jax.ShapeDtypeStruct((rows, ff), bf16),
+        ],
+        compiler_params=grid_params(),
+    )(m_all, g_all, gate, up, product, w_gate, w_up, w_down, down_far)
+
+
+def ring_place(index, n):
+    return jnp.where(index % 2 == 0, index // 2, n - 1 - index // 2)
+
+
+def ring_index(place, n):
+    return jnp.where(place < n // 2, 2 * place, 2 * (n - 1 - place) + 1)
+
+
+def ring_sum(n, data, out, slots, send, recv, out_send, out_recv):
+    me = ring_place(lax.axis_index("dp"), n)
+    peers = [ring_index(lax.rem(me + 1, n), n), ring_index(lax.rem(me + n - 1, n), n)]
+    rows = data.shape[0] // (2 * n)
+    signs = (1, -1)
+
+    def chunk(ref, way, back):
+        which = lax.rem(me + 2 * n - signs[way] * back, n)
+        return ref.at[pl.ds(pl.multiple_of((2 * which + way) * rows, 16), rows)]
+
+    def partial(way, source, step):
+        return pltpu.make_async_remote_copy(
+            src_ref=source, dst_ref=slots.at[way, step],
+            send_sem=send.at[way, step], recv_sem=recv.at[way, step],
+            device_id={"dp": peers[way]}, device_id_type=pl.DeviceIdType.MESH,
+        )
+
+    def final(way, step):
+        part = chunk(out, way, step - 1)
+        return pltpu.make_async_remote_copy(
+            src_ref=part, dst_ref=part,
+            send_sem=out_send.at[way, step], recv_sem=out_recv.at[way, step],
+            device_id={"dp": peers[way]}, device_id_type=pl.DeviceIdType.MESH,
+        )
+
+    def arrived(way, step):
+        part = chunk(out, way, step)
+        return pltpu.make_async_remote_copy(
+            src_ref=part, dst_ref=part,
+            send_sem=out_send.at[way, step], recv_sem=out_recv.at[way, step],
+            device_id={"dp": peers[way]}, device_id_type=pl.DeviceIdType.MESH,
+        )
+
+    for way in range(2):
+        partial(way, chunk(data, way, 0), 0).start()
+
+    def reduce_step(step, carry):
+        for way in range(2):
+            slot = slots.at[way, step]
+            partial(way, slot, step).wait_recv()
+            slot[...] = (slot[...].astype(f32) + chunk(data, way, step + 1)[...].astype(f32)).astype(bf16)
+
+            @pl.when(step < n - 2)
+            def _():
+                partial(way, slot, step + 1).start()
+
+        return carry
+
+    lax.fori_loop(0, n - 1, reduce_step, 0)
+    for way in range(2):
+        chunk(out, way, -1)[...] = slots[way, n - 2]
+        final(way, 0).start()
+
+    def gather_step(step, carry):
+        for way in range(2):
+            arrived(way, step).wait_recv()
+
+            @pl.when(step < n - 2)
+            def _():
+                final(way, step + 1).start()
+
+        return carry
+
+    lax.fori_loop(0, n - 1, gather_step, 0)
+
+    def sent_step(step, carry):
+        for way in range(2):
+            partial(way, slots.at[way, step], step).wait_send()
+            final(way, step).wait_send()
+        return carry
+
+    lax.fori_loop(0, n - 1, sent_step, 0)
+
+
+def mix_sum_kernel(n, done, own, far, out_done, out_own, came, total, slots, send, recv, out_send, out_recv, chip_send, chip_recv):
+    me = ring_place(lax.axis_index("dp"), n)
+    barrier = pltpu.get_barrier_semaphore()
+    for place in (lax.rem(me + 1, n), lax.rem(me + n - 1, n)):
+        pl.semaphore_signal(
+            barrier, inc=1, device_id={"dp": ring_index(place, n)}, device_id_type=pl.DeviceIdType.MESH
+        )
+    other = lax.axis_index("head") ^ 2
+    pl.semaphore_signal(barrier, inc=1, device_id={"head": other}, device_id_type=pl.DeviceIdType.MESH)
+    pl.semaphore_wait(barrier, 3)
+    swap = pltpu.make_async_remote_copy(
+        src_ref=far, dst_ref=came, send_sem=chip_send, recv_sem=chip_recv,
+        device_id={"head": other}, device_id_type=pl.DeviceIdType.MESH,
+    )
+    swap.start()
+    ring_sum(n, done, out_done, slots.at[0], send.at[0], recv.at[0], out_send.at[0], out_recv.at[0])
+    swap.wait()
+    total[...] = (own[...].astype(f32) + came[...].astype(f32)).astype(bf16)
+    ring_sum(n, total, out_own, slots.at[1], send.at[1], recv.at[1], out_send.at[1], out_recv.at[1])
+
+
+def mix_sum(done, own, far, n):
+    if n == 1:
+        return done, (own.astype(f32) + chip_swap(far).astype(f32)).astype(bf16)
+    rows, cols = own.shape
+
+    def body(*refs):
+        mix_sum_kernel(n, *refs)
+
+    vmem = pl.BlockSpec(memory_space=pltpu.VMEM)
+    return pl.pallas_call(
+        body,
+        in_specs=[vmem] * 3,
+        out_specs=[vmem] * 2,
+        out_shape=[jax.ShapeDtypeStruct((rows, cols), bf16)] * 2,
+        scratch_shapes=[
+            pltpu.VMEM((rows, cols), bf16),
+            pltpu.VMEM((rows, cols), bf16),
+            pltpu.VMEM((2, 2, n - 1, rows // (2 * n), cols), bf16),
+        ]
+        + [pltpu.SemaphoreType.DMA((2, 2, n - 1))] * 4
+        + [pltpu.SemaphoreType.DMA] * 2,
+        compiler_params=pltpu.CompilerParams(
+            collective_id=0, has_side_effects=True, vmem_limit_bytes=VMEM_LIMIT
+        ),
+    )(done, own, far)
+
+
 def norm_scale(hidden):
     return lax.rsqrt(jnp.mean(hidden * hidden, axis=-1, keepdims=True) + epsilon)
 
@@ -436,12 +722,33 @@
     return lax.ppermute(value, "head", [(i, i ^ 2) for i in range(4)])
 
 
-def pad_cols(value, width):
-    return jnp.pad(value, ((0, 0), (0, width - value.shape[1])))
-
-
-def pad_rows(value, height):
-    return jnp.pad(value, ((0, height - value.shape[0]), (0, 0)))
+def dp_swap(value, bit):
+    return lax.ppermute(value, "dp", [(i, i ^ (1 << bit)) for i in range(lax.axis_size("dp"))])
+
+
+def dp_bits():
+    return lax.axis_size("dp").bit_length() - 1
+
+
+def small_sum(value):
+    value = value + core_swap(value)
+    value = value + chip_swap(value)
+    for bit in range(dp_bits()):
+        value = value + dp_swap(value, bit)
+    return value
+
+
+def dp_slice(own):
+    rows = own.shape[0] // lax.axis_size("dp")
+    return lax.dynamic_slice_in_dim(own, lax.axis_index("dp") * rows, rows, 0)
+
+
+def dp_gather(part):
+    return lax.all_gather(part, "dp", axis=0, tiled=True)
+
+
+def after(value, *others):
+    return lax.optimization_barrier((value,) + others)[0]
 
 
 def per_device(
@@ -452,6 +759,7 @@
     ndoc = doc_starts.shape[1]
     ff = w_gate.shape[2]
     ffp = -(-ff // 128) * 128
+    rank = w_decay.shape[1]
     member = lax.axis_index("head")
     core = member % 2
     chip = member // 2
@@ -460,135 +768,159 @@
     )
     mixer = Mixer(meta, ndoc, 2 * shard_len)
 
+    def mix_pack(layer):
+        return jnp.concatenate(
+            [w_query[layer], w_key[layer], w_value[layer], w_outgate[layer]], axis=1
+        )
+
+    def ff_parts(layer, wait):
+        part = jnp.concatenate([dp_slice(w_gate[layer]), dp_slice(w_up[layer])], axis=1)
+        return chip_swap(after(part, wait)), chip_swap(after(dp_slice(w_down[layer]), wait))
+
+    def with_partner(local):
+        return jnp.concatenate([local, core_swap(local)], axis=0)
+
+    def settle(terms, layer):
+        sent = core_swap(sum_of_dots(terms, layer, shard_len, shard_len, bf16))
+        return sum_of_dots(terms, layer, 0, shard_len, f32) + sent.astype(f32)
+
     small = jnp.concatenate([w_decay.astype(f32), decay_bias[:, None, :]], axis=1)
     small = jnp.concatenate([small, chip_swap(small)], axis=2)
-    rank = w_decay.shape[1]
-
-    mix_w, out_w, in_w, down_w = [], [], [], []
-    for layer in range(LAYERS):
-        own = jnp.concatenate([w_query[layer], w_key[layer], w_value[layer], w_outgate[layer]], axis=1)
-        mix_w.append(jnp.concatenate([own, chip_swap(own), w_rank[layer]], axis=1))
-        out_w.append(jnp.concatenate([w_out[layer], chip_swap(w_out[layer])], axis=0))
-        own = jnp.concatenate([w_gate[layer], w_up[layer]], axis=1)
-        far = chip_swap(own)
-        in_w.append(
-            jnp.concatenate(
-                [
-                    pad_cols(part, ffp)
-                    for part in (own[:, :ff], far[:, :ff], own[:, ff:], far[:, ff:])
-                ],
-                axis=1,
-            )
-        )
-        far = chip_swap(w_down[layer])
-        down_w.append(jnp.concatenate([pad_rows(w_down[layer], ffp), pad_rows(far, ffp)], axis=0))
-
-    def with_partner(local):
-        return jnp.concatenate([local, core_swap(local)], axis=0)
-
-    def settle(dot, branch, weight):
-        sent = core_swap(dot(branch[shard_len:], weight).astype(bf16))
-        return dot(branch[:shard_len], weight) + sent.astype(f32)
-
+    in_part, down_part = ff_parts(0, meta)
+    in_far = dp_gather(in_part)
+    down_far = dp_gather(after(down_part, in_far))
+    mix_own = mix_pack(0)
+    mix_far = chip_swap(after(mix_own, in_part, down_part))
+    out_far = chip_swap(after(w_out[0], in_part, down_part))
+
+    grad = grad_out[0].astype(f32)
     hidden = tokens[0].astype(f32)
     saved = []
     for layer in range(LAYERS):
         hidden_in = hidden
         a = with_partner(norm_low(hidden, norm_one[layer]))
-        x = nn(a, mix_w[layer])
+        x = project(a, (mix_own, mix_far, w_rank), layer)
         wdec, bias = small[layer, :rank], small[layer, rank:]
         run, states, cum, final = mixer.states(x, wdec, bias)
-        first = chip_swap(final)[::-1] * chip.astype(bf16)
+        got = chip_swap(final)
+        first = got[::-1] * chip.astype(bf16)
         gain = group_gain[layer][None]
         gated, mixed = mixer.mix(x, run, states, cum, first, gain)
-        hidden_mid = hidden + settle(nn, gated, out_w[layer])
-        m = with_partner(norm_low(hidden_mid, norm_two[layer]))
-        both = nn(m, in_w[layer])
-        gate, up = both[:, : 2 * ffp], both[:, 2 * ffp :]
-        product = (jax.nn.silu(gate) * up).astype(bf16)
-        gate, up = gate.astype(bf16), up.astype(bf16)
-        hidden = hidden_mid + settle(nn, product, down_w[layer])
+        hidden_mid = hidden + settle([(gated, 0, w_out, False), (gated, HV, out_far, False)], layer)
+        if layer + 1 < LAYERS:
+            next_own = mix_pack(layer + 1)
+            next_mix = chip_swap(after(next_own, gated))
+            next_out = chip_swap(after(w_out[layer + 1], gated))
+            in_part, down_part = ff_parts(layer + 1, down_far)
+            next_in = dp_gather(in_part)
+            next_down = dp_gather(after(down_part, next_in))
+        m_own = norm_low(hidden_mid, norm_two[layer])
+        m = with_partner(m_own)
+        gate, up, product = ff_forward(m, w_gate, w_up, in_far, layer, ffp)
+        hidden = hidden_mid + settle([(product, 0, w_down, False), (product, ffp, down_far, False)], layer)
+        m_y = chip_swap(m_own)
+        m_all = jnp.concatenate([m, m_y, core_swap(m_y)], axis=0)
         saved.append(
-            (hidden_in, hidden_mid, a, m, x, run, states, cum, first, mixed, gated, gate, up, product)
-        )
+            (hidden_in, hidden_mid, a, m_all, x, run, states, cum, first, mixed, gated, gate, up, product,
+             mix_own, mix_far, out_far, in_far, down_far)
+        )
+        if layer + 1 < LAYERS:
+            mix_own, mix_far, out_far, in_far, down_far = next_own, next_mix, next_out, next_in, next_down
     result = hidden.astype(bf16)[None]
 
-    grad = grad_out[0].astype(f32)
-    split_grads = [None] * LAYERS
-    shared_grads = [None] * LAYERS
-
-    def gather_grad(own, far):
-        total = own.astype(f32) + chip_swap(far.astype(bf16)).astype(f32)
-        return lax.psum(total.astype(bf16), "dp")
-
+    ff_grads, misc_grads = [None] * LAYERS, [None] * LAYERS
     for layer in reversed(range(LAYERS)):
         (
-            hidden_in, hidden_mid, a, m, x, run, states, cum, first, mixed, gated, gate, up, product,
+            hidden_in, hidden_mid, a, m_all, x, run, states, cum, first, mixed, gated, gate, up, product,
+            mix_own, mix_far, out_far, in_far, down_far,
         ) = saved[layer]
         gain = group_gain[layer][None]
         wdec, bias = small[layer, :rank], small[layer, rank:]
-        g_out = with_partner(grad.astype(bf16))
-        dproduct = nt(g_out, down_w[layer])
-        gate, up = gate.astype(f32), up.astype(f32)
-        sig = jax.nn.sigmoid(gate)
-        dgate = (dproduct * up * sig * (1.0 + gate * (1.0 - sig))).astype(bf16)
-        dup = (dproduct * gate * sig).astype(bf16)
-        dboth = jnp.concatenate([dgate, dup], axis=1)
-        g_down = tn(product, g_out).astype(bf16)
-        down_grad = gather_grad(g_down[:ff], g_down[ffp : ffp + ff])
-        g_in = tn(m, dboth).astype(bf16)
-        in_grad = gather_grad(
-            jnp.concatenate([g_in[:, :ff], g_in[:, 2 * ffp : 2 * ffp + ff]], axis=1),
-            jnp.concatenate([g_in[:, ffp : ffp + ff], g_in[:, 3 * ffp : 3 * ffp + ff]], axis=1),
-        )
-        back_mid, gain_two = norm_back(hidden_mid, norm_two[layer], settle(nt, dboth, in_w[layer]))
+        g_own = grad.astype(bf16)
+        g_y = chip_swap(g_own)
+        if layer + 1 < LAYERS:
+            far_came = chip_swap(after(far, g_y))
+        g_all = jnp.concatenate([g_own, core_swap(g_own), g_y, core_swap(g_y)], axis=0)
+        dboth, dfar, product_all = ff_backward(
+            m_all, g_all, gate, up, product, w_gate, w_up, w_down, down_far, layer, ffp
+        )
+        in_grad = tn(dboth, m_all).astype(bf16)
+        down_grad = tn(product_all, g_all).astype(bf16)
+        back_mid, gain_two = norm_back(
+            hidden_mid,
+            norm_two[layer],
+            settle([(dboth, 0, w_gate, True), (dboth, ff, w_up, True), (dfar, 0, in_far, True)], layer),
+        )
         grad = grad + back_mid
         g_mix = with_partner(grad.astype(bf16))
-        dgated = nt(g_mix, out_w[layer])
         g_wout = tn(gated, g_mix).astype(bf16)
-        out_grad = gather_grad(g_wout[:HV], g_wout[HV:])
-        dmixed, doutgate, dstates, dcum, dfinal, dgain = mixer.back_states(x, run, mixed, dgated, gain)
-        dlast = chip_swap(dfinal)[::-1] * (1 - chip).astype(bf16)
+        dmixed, doutgate, dstates, dcum, dfinal, dgain = mixer.back_states(
+            x, run, mixed, g_mix, w_out[layer], out_far, gain
+        )
+        got = chip_swap(dfinal)
+        dlast = got[::-1] * (1 - chip).astype(bf16)
         dx, dwdec, dbias = mixer.back(
             x, run, states, cum, first, dmixed, doutgate, dstates, dcum, dlast, wdec, bias
         )
-        g_wmix = tn(a, dx)
-        mix_grad = gather_grad(g_wmix[:, :HEAD_COLS], g_wmix[:, HEAD_COLS : 2 * HEAD_COLS])
-        back_in, gain_one = norm_back(hidden_in, norm_one[layer], settle(nt, dx, mix_w[layer]))
-        grad = grad + back_in
-        split_grads[layer] = (mix_grad, out_grad, in_grad, down_grad)
-        shared_grads[layer] = (
-            gain_one,
-            g_wmix[:, 2 * HEAD_COLS :],
-            dgain[0],
-            gain_two,
-            jnp.concatenate([dwdec, dbias], axis=0),
-        )
-
-    def stacked(group, pick=lambda v: v):
-        return jnp.stack([pick(split_grads[layer][group]).astype(f32) for layer in range(LAYERS)])
-
-    shared = [jnp.stack([shared_grads[layer][i] for layer in range(LAYERS)]) for i in range(5)]
-    far_small = chip_swap(shared[4][:, :, HK:])
-    own_small = lax.psum(shared[4][:, :, :HK] + far_small, "dp")
-    shared = lax.psum(tuple(shared[:4]), ("dp", "head"))
+        g_wmix = tn(dx, a)
+        if layer + 1 < LAYERS:
+            done = (own.astype(f32) + after(far_came, dx).astype(f32)).astype(bf16)
+        far = jnp.concatenate([g_wmix[HEAD_COLS : 2 * HEAD_COLS].astype(bf16), g_wout[HV:]], axis=0)
+        own = jnp.concatenate([g_wmix[:HEAD_COLS].astype(bf16), g_wout[:HV]], axis=0)
+        back_first, gain_one = norm_back(hidden_in, norm_one[layer], settle(
+            [(dx, 0, mix_own, True), (dx, HEAD_COLS, mix_far, True), (dx, 2 * HEAD_COLS, w_rank, True)], layer
+        ))
+        grad = grad + back_first
+        if layer > 0:
+            ff_grads[layer] = lax.psum((in_grad, down_grad), "dp")
+        else:
+            in_grad, down_grad, _ = lax.optimization_barrier((in_grad, down_grad, ff_grads[1]))
+            ff_grads[layer] = lax.psum((in_grad, down_grad), "dp")
+            mix_grads = mix_sum(done, own, far, lax.axis_size("dp"))
+            mix_grads = [mix_grads[1], mix_grads[0]]
+        heads = jnp.concatenate([dwdec, dbias], axis=0)
+        places = lax.iota(jnp.int32, 4)[:, None, None]
+        heads = jnp.where(places == member, heads[None, :, :HK], 0.0) + jnp.where(
+            places == member ^ 2, heads[None, :, HK:], 0.0
+        )
+        misc_grads[layer] = jnp.concatenate(
+            [g_wmix[2 * HEAD_COLS :].reshape(-1), gain_one, gain_two, dgain[0], heads.reshape(-1)]
+        )
+
+    misc = jnp.stack(misc_grads)
+    misc = small_sum(misc.reshape(-1, 128)).reshape(LAYERS, -1)
+    sizes = (rank * width, width, width, HV, 4 * (rank + 1) * HK)
+    pieces, at = [], 0
+    for size in sizes:
+        pieces.append(misc[:, at : at + size])
+        at += size
+    heads = lax.dynamic_index_in_dim(
+        pieces[4].reshape(LAYERS, 4, rank + 1, HK), member, axis=1, keepdims=False
+    )
+
+    def rows_of(grads, start, stop):
+        return jnp.stack([g[start:stop].astype(f32) for g in grads])
+
+    def cols_of(grads, start, stop):
+        return jnp.stack([g[start:stop].T.astype(f32) for g in grads])
+
     return (
         result,
         grad[None],
-        shared[0],
-        stacked(0, lambda v: v[:, :HK]),
-        stacked(0, lambda v: v[:, HK : 2 * HK]),
-        stacked(0, lambda v: v[:, 2 * HK : 2 * HK + HV]),
-        stacked(0, lambda v: v[:, 2 * HK + HV :]),
-        shared[1],
-        own_small[:, :rank],
-        own_small[:, rank],
-        shared[2],
-        stacked(1),
-        shared[3],
-        stacked(2, lambda v: v[:, :ff]),
-        stacked(2, lambda v: v[:, ff:]),
-        stacked(3),
+        pieces[1],
+        cols_of(mix_grads, 0, HK),
+        cols_of(mix_grads, HK, 2 * HK),
+        cols_of(mix_grads, 2 * HK, 2 * HK + HV),
+        cols_of(mix_grads, 2 * HK + HV, HEAD_COLS),
+        jnp.swapaxes(pieces[0].reshape(LAYERS, rank, width), 1, 2),
+        heads[:, :rank],
+        heads[:, rank],
+        pieces[3],
+        rows_of(mix_grads, HEAD_COLS, HEAD_COLS + HV),
+        pieces[2],
+        cols_of([g[0] for g in ff_grads], 0, ff),
+        cols_of([g[0] for g in ff_grads], ff, 2 * ff),
+        rows_of([g[1] for g in ff_grads], 0, ff),
     )
 
 

time: 1290 us -> 975 us (0.76); the launches traced: 1290 us -> 957 us
  waiting for transfers between devices: 744 us -> 296 us
  Pallas kernels: 75 us -> 404 us
  matrix products: 199 us -> 49.1 us
  blocking collectives: 82.1 us -> 0 us
    pallas_call x0 -> x23, Pallas kernels: none -> 320 us  [the longest x1 186 us: mix_sum(): pl.pallas_call(body, in_specs=[vmem] * 3, out_specs=[vmem] * 2, out_shape...]
    psum x2, waiting for transfers between devices: 388 us -> 113 us  [per_device(): ff_grads[layer] = lax.psum((in_grad, down_grad), 'dp')]
    ppermute x22 -> x19, waiting for transfers between devices: 343 us -> 145 us  [chip_swap(): return lax.ppermute(value, 'head', [(i, i ^ 2) for i in range(4)])]
    dot_general x24 -> x0, matrix products: 151 us -> none  [the longest x12 76.9 us: nt(): lax.dot_general(left, right, (((1,), (1,)), ((), ())), preferred_element_...]
    psum x2 -> x0, blocking collectives: 82.1 us -> none  [the longest x1 41.9 us: per_device(): shared = lax.psum(tuple(shared[:4]), ('dp', 'head'))]
    all_gather x0 -> x4, waiting for transfers between devices: none -> 29.1 us  [dp_gather(): return lax.all_gather(part, 'dp', axis=0, tiled=True)]
    concatenate x6 -> x17, other arithmetic: 11.9 us -> 32.2 us  [the longest x6 8.58 us: with_partner(): return jnp.concatenate([local, core_swap(local)], axis=0)]
    unnamed x247 -> x329, local copies, waits for them, and re-layouts: 45.9 us -> 35.6 us
  transfers between devices with their start and end apart: 40 -> 49, of which waited for: 19 -> 15; matrix products, arithmetic and copies ran while one was open for 23% -> 19% of each run, Pallas kernels for 6% -> 39%
where the time goes in v2:
time: 975 us; the launch traced here: 957 us
  Pallas kernels  404 us (41%)
  waiting for transfers between devices  296 us (30%)
  other arithmetic  86.5 us (9%)
  local copies, waits for them, and re-layouts  75 us (8%)
  matrix products  49.1 us (5%)
  starting transfers between devices  30.3 us (3%)
  between operations  16.4 us (2%)
    pallas_call x1, Pallas kernels, mix_sum(): pl.pallas_call(body, in_specs=[vmem] * 3, out_specs=[vmem] * 2, out_shape...  186 us
    ppermute x19, waiting for transfers between devices, chip_swap(): return lax.ppermute(value, 'head', [(i, i ^ 2) for i in range(4)])  145 us
    psum x2, waiting for transfers between devices, per_device(): ff_grads[layer] = lax.psum((in_grad, down_grad), 'dp')  113 us
    pallas_call x8, Pallas kernels, call(): pl.pallas_call(body, grid_spec=pltpu.PrefetchScalarGridSpec(num_scalar_pr...  83.9 us
    pallas_call x16, Pallas kernels, sum_of_dots(): pl.pallas_call(body, grid=(rows // ROWS_BLK,), in_specs=[row_spec(v, firs...  62.3 us
    dot_general x8, matrix products, tn(): lax.dot_general(left, right, (((0,), (0,)), ((), ())), preferred_element_...  49.1 us
    pallas_call x2, Pallas kernels, ff_backward(): pl.pallas_call(body, grid=(rows // ROWS_BLK,), in_specs=[pl.BlockSpec((RO...  38.5 us
    unnamed x329, local copies, waits for them, and re-layouts  35.6 us
  transfers between devices with their start and end apart: 49, of which 15 were waited for; matrix products, arithmetic and copies ran while one was open for 19% of the time, Pallas kernels for 39%

profile of v2, /device:TPU:0, one launch (start us, length us, event | category | flops | bytes accessed | tf_op | source)
XLA Modules:
  0.0 957.3 jit_solution(5163446246090026774)
XLA Ops:
  17.6 8.4 collective-permute-done.1
  42.2 28.3 %collective-permute-done.4 = f32[2,17,128]{2,1,0:T(8,128)S(1)} collective-permute-done((f32[2,17,128]{2,1,0:T(8,128)S(1)}, f32[2,17,128]{2,1,0:T(8,128)S(1)}, u32[]{:S(2)}, u32[]{:S(2)}) %collective-permute-start.4) | collective-permute-done | bytes 17440 | tf_op jit(solution)/shard_map/ppermute | solution.py:722
  81.0 9.3 shard_map.289
  120.5 29.1 %all-gather.7.cloned.1.call-done.refs_2_.far_w = bf16[704,1024]{1,0:T(8,128)(2,1)} async-done(((bf16[88,1024]{1,0:T(8,128)(2,1)}), bf16[704,1024]{1,0:T(8,128)(2,1)}) %all-gather.7.cloned.1.call-update) | async-done | bytes 1441808 | tf_op jit(solution)/shard_map/all_gather | solution.py:747
  162.7 10.4 %shard_map.293 = (bf16[1024,1536]{1,0:T(8,128)(2,1)}, bf16[1024,1536]{1,0:T(8,128)(2,1)}, bf16[1024,1536]{1,0:T(8,128)(2,1)}) custom-call(bf16[1024,1024]{1,0:T(8,128)(2,1)S(1)} %pad_maximum_fusion.5.m_ref, bf16[2,1024,704]{2,1,0:T(8,128)(2,1)} %copy.99.gate_w.refs_2_, bf16[2,1024,704]{2,1,0:T(8,128)(2,1)} %copy.100.up_w.refs_3_, ...), custom_call_target="tpu_custom_call" | custom-call | tf_op jit(solution)/shard_map/pallas_call | solution.py:499
  189.5 26.7 %collective-permute-done.11.refs_1_.refs_2_ = bf16[1024,768]{1,0:T(8,128)(2,1)S(1)} collective-permute-done((bf16[1024,768]{1,0:T(8,128)(2,1)S(1)}, bf16[1024,768]{1,0:T(8,128)(2,1)S(1)}, u32[]{:S(2)}, u32[]{:S(2)}) %collective-permute-start.11) | collective-permute-done | bytes 1572896 | tf_op jit(solution)/shard_map/ppermute | solution.py:722
  222.1 9.3 shard_map.297
  236.5 7.7 shard_map.298
  251.6 23.5 %collective-permute-done.17 = bf16[88,1024]{1,0:T(8,128)(2,1)} collective-permute-done((bf16[88,1024]{1,0:T(8,128)(2,1)S(1)}, bf16[88,1024]{1,0:T(8,128)(2,1)}, u32[]{:S(2)}, u32[]{:S(2)}) %collective-permute-start.17) | collective-permute-done | bytes 180256 | tf_op jit(solution)/shard_map/ppermute | solution.py:722
  278.1 23.6 %collective-permute-done.19 = bf16[512,1024]{1,0:T(8,128)(2,1)S(1)} collective-permute-done((bf16[512,1024]{1,0:T(8,128)(2,1)S(1)}, bf16[512,1024]{1,0:T(8,128)(2,1)S(1)}, u32[]{:S(2)}, u32[]{:S(2)}) %collective-permute-start.19) | collective-permute-done | bytes 1048608 | tf_op jit(solution)/shard_map/ppermute | solution.py:722
  309.4 10.3 %shard_map.301 = (bf16[1024,1536]{1,0:T(8,128)(2,1)}, bf16[1024,1536]{1,0:T(8,128)(2,1)}, bf16[1024,1536]{1,0:T(8,128)(2,1)}) custom-call(bf16[1024,1024]{1,0:T(8,128)(2,1)S(1)} %pad_maximum_fusion.7.m_ref, bf16[2,1024,704]{2,1,0:T(8,128)(2,1)} %copy.99.gate_w.refs_2_, bf16[2,1024,704]{2,1,0:T(8,128)(2,1)} %copy.100.up_w.refs_3_, ...), custom_call_target="tpu_custom_call" | custom-call | tf_op jit(solution)/shard_map/pallas_call | solution.py:499
  321.0 19.3 %shard_map.304 = (bf16[2048,1408]{1,0:T(8,128)(2,1)}, bf16[1024,1408]{1,0:T(8,128)(2,1)S(1)}, bf16[2048,704]{1,0:T(8,128)(2,1)}) custom-call(bf16[2048,1024]{1,0:T(8,128)(2,1)} %pad_maximum_fusion.m_ref, bf16[2048,1024]{1,0:T(8,128)(2,1)} %pad_maximum_fusion.1.g_ref, bf16[1024,1536]{1,0:T(8,128)(2,1)} %get-tuple-element.96.gate_ref, ...), custom_call_target="tpu_custom_call" | custom-call | tf_op jit(solution)/shard_map/pallas_call | solution.py:542
  368.4 8.3 collective-permute-done.28
  379.8 12.6 %shard_map.307 = (bf16[1024,512]{1,0:T(8,128)(2,1)S(1)}, bf16[1024,512]{1,0:T(8,128)(2,1)S(1)}, bf16[8,2,256,128]{3,2,1,0:T(8,128)(2,1)S(1)}, f32[8,1,256]{2,1,0...) custom-call(s32[6]{0:T(128)S(1)} %copy-done.50, f32[1024,1552]{1,0:T(8,128)} %shard_map.296.refs_1_, ...), custom_call_target="tpu_custom_call" | custom-call | tf_op jit(solution)/shard_map/pallas_call | solution.py:282
  393.2 10.6 %convolution_convert_fusion = bf16[1408,1024]{1,0:T(8,128)(2,1)} fusion(bf16[2048,1408]{1,0:T(8,128)(2,1)} %get-tuple-element.98.refs_0_, bf16[512,1024]{1,0:T(8,128)(2,1)S(1)} %copy-done.119, bf16[512,1024]{1,0:T(8,128)(2,1)S(1)} %copy-done.117, bf16[512,1024]{1,0:T(8,128)(2,1)S(1)} %copy-done.94, bf16[512,1024]{1,0:T(8,128)(2,1)S(1)} %copy-done.82), kind=kOutput, calls=%fused_computation.11 | convolution fusion | flops 5923799040 | bytes 12845056 | tf_op jit(solution)/shard_map/dot_general | solution.py:31
  403.8 12.1 %shard_map.308 = (bf16[1024,1552]{1,0:T(8,128)(2,1)}, f32[16,256]{1,0:T(8,128)S(1)}, f32[1,256]{1,0:T(1,128)S(1)}) custom-call(s32[6]{0:T(128)S(1)} %copy-done.50, f32[1024,1552]{1,0:T(8,128)} %shard_map.296.refs_1_, f32[1024,256]{1,0:T(8,128)S(1)} %copy-done.22, bf16[8,2,256,128]{3,2,1,0:T(8,128)(2,1)S(1)} %copy-done.36, f32[8,1,256]{2,1,0:T(1,128)S(1)} %copy-done.55, ...), custom_call_target="tpu_custom_call" | custom-call | tf_op jit(solution)/shard_map/pallas_call | solution.py:282
  454.9 15.2 %collective-permute-done.31 = bf16[512,1024]{1,0:T(8,128)(2,1)} collective-permute-done((bf16[512,1024]{1,0:T(8,128)(2,1)S(1)}, bf16[512,1024]{1,0:T(8,128)(2,1)}, u32[]{:S(2)}, u32[]{:S(2)}) %collective-permute-start.31) | collective-permute-done | bytes 1048608 | tf_op jit(solution)/shard_map/ppermute | solution.py:722
  471.7 112.9 %all-reduce.7.cloned.1.call-done = (bf16[1408,1024]{1,0:T(8,128)(2,1)}, bf16[704,1024]{1,0:T(8,128)(2,1)}) async-done(((bf16[1408,1024]{1,0:T(8,128)(2,1)}, bf16[704,1024]{1,0:T(8,128)(2,1)}), (bf16[1408,1024]{1,0:T(8,128)(2,1)}, bf16[704,1024]{1,0:T(8,128)(2,1)})) %all-reduce.7.cloned.1.call-update) | async-done | bytes 4325392 | tf_op jit(solution)/shard_map/psum | solution.py:875
  593.5 19.2 %shard_map.311 = (bf16[2048,1408]{1,0:T(8,128)(2,1)}, bf16[1024,1408]{1,0:T(8,128)(2,1)S(1)}, bf16[2048,704]{1,0:T(8,128)(2,1)}) custom-call(bf16[2048,1024]{1,0:T(8,128)(2,1)} %pad_maximum_fusion.2.m_ref, bf16[2048,1024]{1,0:T(8,128)(2,1)} %pad_maximum_fusion.3.g_ref, bf16[1024,1536]{1,0:T(8,128)(2,1)} %get-tuple-element.107.gate_ref, ...), custom_call_target="tpu_custom_call" | custom-call | tf_op jit(solution)/shard_map/pallas_call | solution.py:542
  619.7 9.0 convolution_convert_fusion.1
  649.2 13.2 %shard_map.314 = (bf16[1024,512]{1,0:T(8,128)(2,1)S(1)}, bf16[1024,512]{1,0:T(8,128)(2,1)S(1)}, bf16[8,2,256,128]{3,2,1,0:T(8,128)(2,1)S(1)}, f32[8,1,256]{2,1,0...) custom-call(s32[6]{0:T(128)S(1)} %copy-done.51, f32[1024,1552]{1,0:T(8,128)} %shard_map.288.refs_1_, ...), custom_call_target="tpu_custom_call" | custom-call | tf_op jit(solution)/shard_map/pallas_call | solution.py:282
  668.6 12.1 %shard_map.315 = (bf16[1024,1552]{1,0:T(8,128)(2,1)}, f32[16,256]{1,0:T(8,128)S(1)}, f32[1,256]{1,0:T(1,128)S(1)}) custom-call(s32[6]{0:T(128)S(1)} %copy-done.51, f32[1024,1552]{1,0:T(8,128)} %shard_map.288.refs_1_, f32[1024,256]{1,0:T(8,128)S(1)} %copy-done.20, bf16[8,2,256,128]{3,2,1,0:T(8,128)(2,1)S(1)} %copy-done.34, f32[8,1,256]{2,1,0:T(1,128)S(1)} %copy-done.53, ...), custom_call_target="tpu_custom_call" | custom-call | tf_op jit(solution)/shard_map/pallas_call | solution.py:282
  685.6 7.8 fusion.30
  704.0 185.7 %shard_map.318 = (bf16[1024,1024]{1,0:T(8,128)(2,1)S(1)}, bf16[1024,1024]{1,0:T(8,128)(2,1)S(1)}) custom-call(bf16[1024,1024]{1,0:T(8,128)(2,1)} %add_convert_fusion.refs_0_, bf16[1024,1024]{1,0:T(8,128)(2,1)} %pad_maximum_fusion.11.refs_1_, bf16[1024,1024]{1,0:T(8,128)(2,1)} %pad_maximum_fusion.12.refs_2_), custom_call_target="tpu_custom_call" | custom-call | tf_op jit(solution)/shard_map/pallas_call | solution.py:682
  (564 shorter events, 316.5 us)
Async XLA Ops:
  7.2 97.9 %all-gather.5.cloned.1.call-start = ((), (), s32[]{:S(2)}) async-start(), calls=%async_computation | async-start | bytes 3244032 | tf_op jit(solution)/shard_map/all_gather | solution.py:747
  26.8 122.8 %all-gather.7.cloned.1.call-start = ((), (), s32[]{:S(2)}) async-start(), calls=%async_computation.1 | async-start | bytes 1622016 | tf_op jit(solution)/shard_map/all_gather | solution.py:747
  34.6 38.9 %collective-permute-start.3 = (bf16[1024,768]{1,0:T(8,128)(2,1)}, bf16[1024,768]{1,0:T(8,128)(2,1)}, u32[]{:S(2)}, u32[]{:S(2)}) collective-permute-start(bf16[1024,768]{1,0:T(8,128)(2,1)} %pad_maximum_fusion.13.refs_0_.refs_1_), channel_id=1, source_target_pairs={{0,2},{1,3},{2,0},{3,1},{4,6},{5,7},{6,4},{7,5},{8,10},{9,11},{10,... | collective-permute-start | bytes 4718600 | tf_op jit(solution)/shard_map/ppermute | solution.py:722
  38.8 32.9 %collective-permute-start = (bf16[512,1024]{1,0:T(8,128)(2,1)}, bf16[512,1024]{1,0:T(8,128)(2,1)}, u32[]{:S(2)}, u32[]{:S(2)}) collective-permute-start(bf16[512,1024]{1,0:T(8,128)(2,1)} %fusion.2), channel_id=1, source_target_pairs={{0,1},{1,0},{2,3},{3,2},{4,5},{5,4},{6,7},{7,6},{8,9},{9,8},{10,11... | collective-permute-start | bytes 3145736 | tf_op jit(solution)/shard_map/ppermute | solution.py:718
  38.8 31.6 %collective-permute-start.4 = (f32[2,17,128]{2,1,0:T(8,128)S(1)}, f32[2,17,128]{2,1,0:T(8,128)S(1)}, u32[]{:S(2)}, u32[]{:S(2)}) collective-permute-start(f32[2,17,128]{2,1,0:T(8,128)S(1)} %pad_maximum_fusion.19), channel_id=1, source_target_pairs={{0,2},{1,3},{2,0},{3,1},{4,6},{5,7},{6,4},{7,5},{8,10},{9,11},{10,... | collective-permute-start | bytes 52232 | tf_op jit(solution)/shard_map/ppermute | solution.py:722
  70.5 32.7 %collective-permute-start.6 = (bf16[256,1024]{1,0:T(8,128)(2,1)}, bf16[256,1024]{1,0:T(8,128)(2,1)S(1)}, u32[]{:S(2)}, u32[]{:S(2)}) collective-permute-start(bf16[256,1024]{1,0:T(8,128)(2,1)} %get-tuple-element.82.refs_5_), channel_id=1, source_target_pairs={{0,2},{1,3},{2,0},{3,1},{4,6},{5,7},{6,4},{7,5},{8,10},{9,11},{10,... | collective-permute-start | bytes 1572872 | tf_op jit(solution)/shard_map/ppermute | solution.py:722
  105.1 169.9 %all-gather.9.cloned.1.call-start = ((), (), s32[]{:S(2)}) async-start(), calls=%async_computation.2 | async-start | bytes 3244032 | tf_op jit(solution)/shard_map/all_gather | solution.py:747
  114.7 45.5 %collective-permute-start.8 = (bf16[512,1024]{1,0:T(8,128)(2,1)}, bf16[512,1024]{1,0:T(8,128)(2,1)}, u32[]{:S(2)}, u32[]{:S(2)}) collective-permute-start(bf16[512,1024]{1,0:T(8,128)(2,1)} %multiply_convert_fusion.2), channel_id=1, source_target_pairs={{0,1},{1,0},{2,3},{3,2},{4,5},{5,4},{6,7},{7,6},{8,9},{9,8},{10,11... | collective-permute-start | bytes 3145736 | tf_op jit(solution)/shard_map/ppermute | solution.py:718
  149.6 27.4 %collective-permute-start.16 = (bf16[128,1408]{1,0:T(8,128)(2,1)}, bf16[128,1408]{1,0:T(8,128)(2,1)}, u32[]{:S(2)}, u32[]{:S(2)}) collective-permute-start(bf16[128,1408]{1,0:T(8,128)(2,1)} %pad_maximum_fusion.16), channel_id=1, source_target_pairs={{0,2},{1,3},{2,0},{3,1},{4,6},{5,7},{6,4},{7,5},{8,10},{9,11},{10,... | collective-permute-start | bytes 1081352 | tf_op jit(solution)/shard_map/ppermute | solution.py:722
  177.1 142.6 %all-gather.11.cloned.1.call-start = ((), (), s32[]{:S(2)}) async-start(), calls=%async_computation.3 | async-start | bytes 1622016 | tf_op jit(solution)/shard_map/all_gather | solution.py:747
  178.9 37.3 %collective-permute-start.11 = (bf16[1024,768]{1,0:T(8,128)(2,1)S(1)}, bf16[1024,768]{1,0:T(8,128)(2,1)S(1)}, u32[]{:S(2)}, u32[]{:S(2)}) collective-permute-start(bf16[1024,768]{1,0:T(8,128)(2,1)S(1)} %pad_maximum_fusion.14.refs_0_.refs_1_), channel_id=1, source_target_pairs={{0,2},{1,3},{2,0},{3,1},{4,6},{5,7},{6,4},{7,5},{8,10},{9,11},{10,... | collective-permute-start | bytes 4718600 | tf_op jit(solution)/shard_map/ppermute | solution.py:722
  186.3 57.9 %collective-permute-start.13 = (bf16[256,1024]{1,0:T(8,128)(2,1)S(1)}, bf16[256,1024]{1,0:T(8,128)(2,1)S(1)}, u32[]{:S(2)}, u32[]{:S(2)}) collective-permute-start(bf16[256,1024]{1,0:T(8,128)(2,1)S(1)} %copy-done.38), channel_id=1, source_target_pairs={{0,2},{1,3},{2,0},{3,1},{4,6},{5,7},{6,4},{7,5},{8,10},{9,11},{10,... | collective-permute-start | bytes 1572872 | tf_op jit(solution)/shard_map/ppermute | solution.py:722
  245.3 32.3 %collective-permute-start.22 = (bf16[512,1024]{1,0:T(8,128)(2,1)}, bf16[512,1024]{1,0:T(8,128)(2,1)}, u32[]{:S(2)}, u32[]{:S(2)}) collective-permute-start(bf16[512,1024]{1,0:T(8,128)(2,1)} %bitcast.31), channel_id=1, source_target_pairs={{0,2},{1,3},{2,0},{3,1},{4,6},{5,7},{6,4},{7,5},{8,10},{9,11},{10,... | collective-permute-start | bytes 3145736 | tf_op jit(solution)/shard_map/ppermute | solution.py:722
  246.9 28.2 %collective-permute-start.17 = (bf16[88,1024]{1,0:T(8,128)(2,1)S(1)}, bf16[88,1024]{1,0:T(8,128)(2,1)}, u32[]{:S(2)}, u32[]{:S(2)}) collective-permute-start(bf16[88,1024]{1,0:T(8,128)(2,1)S(1)} %dynamic-slice_bitcast_fusion), channel_id=1, source_target_pairs={{0,2},{1,3},{2,0},{3,1},{4,6},{5,7},{6,4},{7,5},{8,10},{9,11},{10,... | collective-permute-start | bytes 540680 | tf_op jit(solution)/shard_map/ppermute | solution.py:722
  275.0 309.5 %all-reduce.7.cloned.1.call-start = ((), (), s32[]{:S(2)}) async-start(), calls=%async_computation.5 | async-start | bytes 8650752 | tf_op jit(solution)/shard_map/psum | solution.py:875
  278.1 27.9 %collective-permute-start.15 = (bf16[512,1024]{1,0:T(8,128)(2,1)S(1)}, bf16[512,1024]{1,0:T(8,128)(2,1)S(1)}, u32[]{:S(2)}, u32[]{:S(2)}) collective-permute-start(bf16[512,1024]{1,0:T(8,128)(2,1)S(1)} %multiply_convert_fusion), channel_id=1, source_target_pairs={{0,1},{1,0},{2,3},{3,2},{4,5},{5,4},{6,7},{7,6},{8,9},{9,8},{10,11... | collective-permute-start | bytes 3145736 | tf_op jit(solution)/shard_map/ppermute | solution.py:718
  350.9 25.8 %collective-permute-start.28 = (bf16[512,1024]{1,0:T(8,128)(2,1)}, bf16[512,1024]{1,0:T(8,128)(2,1)}, u32[]{:S(2)}, u32[]{:S(2)}) collective-permute-start(bf16[512,1024]{1,0:T(8,128)(2,1)} %multiply_convert_fusion.2), channel_id=1, source_target_pairs={{0,2},{1,3},{2,0},{3,1},{4,6},{5,7},{6,4},{7,5},{8,10},{9,11},{10,... | collective-permute-start | bytes 3145736 | tf_op jit(solution)/shard_map/ppermute | solution.py:722
  376.7 49.8 %collective-permute-start.29 = (bf16[512,1024]{1,0:T(8,128)(2,1)}, bf16[512,1024]{1,0:T(8,128)(2,1)}, u32[]{:S(2)}, u32[]{:S(2)}) collective-permute-start(bf16[512,1024]{1,0:T(8,128)(2,1)} %collective-permute-done.28), channel_id=1, source_target_pairs={{0,1},{1,0},{2,3},{3,2},{4,5},{5,4},{6,7},{7,6},{8,9},{9,8},{10,11... | collective-permute-start | bytes 3145736 | tf_op jit(solution)/shard_map/ppermute | solution.py:718
  426.5 509.3 %all-reduce.5.cloned.1.call-start = ((), (), s32[]{:S(2)}) async-start(), calls=%async_computation.4 | async-start | bytes 8650752 | tf_op jit(solution)/shard_map/psum | solution.py:878
  444.7 25.5 %collective-permute-start.31 = (bf16[512,1024]{1,0:T(8,128)(2,1)S(1)}, bf16[512,1024]{1,0:T(8,128)(2,1)}, u32[]{:S(2)}, u32[]{:S(2)}) collective-permute-start(bf16[512,1024]{1,0:T(8,128)(2,1)S(1)} %get-tuple-element.194), channel_id=1, source_target_pairs={{0,2},{1,3},{2,0},{3,1},{4,6},{5,7},{6,4},{7,5},{8,10},{9,11},{10,... | collective-permute-start | bytes 3145736 | tf_op jit(solution)/shard_map/ppermute | solution.py:722
  454.9 134.9 %collective-permute-start.30 = (bf16[512,1024]{1,0:T(8,128)(2,1)S(1)}, bf16[512,1024]{1,0:T(8,128)(2,1)}, u32[]{:S(2)}, u32[]{:S(2)}) collective-permute-start(bf16[512,1024]{1,0:T(8,128)(2,1)S(1)} %get-tuple-element.194), channel_id=1, source_target_pairs={{0,1},{1,0},{2,3},{3,2},{4,5},{5,4},{6,7},{7,6},{8,9},{9,8},{10,11... | collective-permute-start | bytes 3145736 | tf_op jit(solution)/shard_map/ppermute | solution.py:718
  470.1 119.6 %collective-permute-start.32 = (bf16[512,1024]{1,0:T(8,128)(2,1)}, bf16[512,1024]{1,0:T(8,128)(2,1)}, u32[]{:S(2)}, u32[]{:S(2)}) collective-permute-start(bf16[512,1024]{1,0:T(8,128)(2,1)} %collective-permute-done.31), channel_id=1, source_target_pairs={{0,1},{1,0},{2,3},{3,2},{4,5},{5,4},{6,7},{7,6},{8,9},{9,8},{10,11... | collective-permute-start | bytes 3145736 | tf_op jit(solution)/shard_map/ppermute | solution.py:718
  588.3 105.7 %collective-permute-start.42 = (bf16[1024,1024]{1,0:T(8,128)(2,1)}, bf16[1024,1024]{1,0:T(8,128)(2,1)}, u32[]{:S(2)}, u32[]{:S(2)}) collective-permute-start(bf16[1024,1024]{1,0:T(8,128)(2,1)} %pad_maximum_fusion.10), channel_id=1, source_target_pairs={{0,2},{1,3},{2,0},{3,1},{4,6},{5,7},{6,4},{7,5},{8,10},{9,11},{10,... | collective-permute-start | bytes 6291464 | tf_op jit(solution)/shard_map/ppermute | solution.py:722
  684.7 214.3 %collective-permute-start.36 = (bf16[512,1024]{1,0:T(8,128)(2,1)S(1)}, bf16[512,1024]{1,0:T(8,128)(2,1)}, u32[]{:S(2)}, u32[]{:S(2)}) collective-permute-start(bf16[512,1024]{1,0:T(8,128)(2,1)S(1)} %shard_map.317), channel_id=1, source_target_pairs={{0,1},{1,0},{2,3},{3,2},{4,5},{5,4},{6,7},{7,6},{8,9},{9,8},{10,11... | collective-permute-start | bytes 3145736 | tf_op jit(solution)/shard_map/ppermute | solution.py:718
  (178 other events, 1480.3 us)
Sparse Core Ops, SparseCore 0:
  26.9 59.1 all-gather.4
  105.2 44.3 all-gather.6
  177.2 54.9 all-gather.8
  275.2 40.4 all-gather.10
  426.6 157.9 all-reduce.6
  646.7 184.2 all-reduce.4

commit v3 on v2

--- a/solution.py
+++ b/solution.py
@@ -289,6 +289,7 @@
                 scratch_shapes=scratch,
             ),
             out_shape=[jax.ShapeDtypeStruct(s, d) for s, d in out_shape],
+            cost_estimate=NO_COST,
             compiler_params=kernel_params(),
         )(self.meta, *args)
 
@@ -416,32 +417,53 @@
 ROWS_BLK = 256
 
 
-def layer_spec(array, layer):
+def matrix_spec(part):
+    array, which = part
     if array.ndim == 3:
-        return pl.BlockSpec((None,) + array.shape[1:], lambda i: (layer, 0, 0))
-    return pl.BlockSpec(array.shape, lambda i: (0, 0))
-
-
-def row_spec(array, first=0, last=None):
-    def place(i):
-        at = i + first
-        return (at if last is None else jnp.minimum(at, last), 0)
-
-    return pl.BlockSpec((ROWS_BLK, array.shape[1]), place)
-
-
-def grid_params():
-    return pltpu.CompilerParams(dimension_semantics=("arbitrary",), vmem_limit_bytes=VMEM_LIMIT)
-
-
-def sum_of_dots(terms, layer, first_row, rows, out_type):
+        return pl.BlockSpec((None,) + array.shape[1:], lambda i: (which, 0, 0))
+    if which is None:
+        return pl.BlockSpec(array.shape, lambda i: (0, 0))
+    at, rows = which
+    return pl.BlockSpec((rows, array.shape[1]), lambda i: (at, 0))
+
+
+def matrix_shape(part):
+    array, which = part
+    if array.ndim == 3 or which is None:
+        return array.shape[-2:]
+    return which[1], array.shape[1]
+
+
+def row_spec(array, first=0):
+    return pl.BlockSpec((ROWS_BLK, array.shape[1]), lambda i: (i + first, 0))
+
+
+NO_COST = pl.CostEstimate(flops=0, bytes_accessed=0, transcendentals=0)
+
+
+def local_call(body, grid, in_specs, out_specs, out_shape, args, aliases=None):
+    return pl.pallas_call(
+        body,
+        grid=(grid,),
+        in_specs=in_specs,
+        out_specs=out_specs,
+        out_shape=out_shape,
+        input_output_aliases=aliases or {},
+        cost_estimate=NO_COST,
+        compiler_params=pltpu.CompilerParams(
+            dimension_semantics=("arbitrary",), vmem_limit_bytes=VMEM_LIMIT
+        ),
+    )(*args)
+
+
+def sum_of_dots(terms, first_row, rows, out_type):
     lefts = []
     for left, _, _, _ in terms:
         if not any(left is seen for seen in lefts):
             lefts.append(left)
     which = [next(i for i, seen in enumerate(lefts) if seen is left) for left, _, _, _ in terms]
     rights = [right for _, _, right, _ in terms]
-    width = rights[0].shape[-2] if terms[0][3] else rights[0].shape[-1]
+    width = matrix_shape(rights[0])[0 if terms[0][3] else 1]
 
     def body(*refs):
         left_refs, right_refs, out = refs[: len(lefts)], refs[len(lefts) : -1], refs[-1]
@@ -452,119 +474,120 @@
             total = part if total is None else total + part
         out[...] = total.astype(out_type)
 
-    return pl.pallas_call(
+    return local_call(
         body,
-        grid=(rows // ROWS_BLK,),
-        in_specs=[row_spec(v, first_row // ROWS_BLK) for v in lefts] + [layer_spec(v, layer) for v in rights],
-        out_specs=pl.BlockSpec((ROWS_BLK, width), lambda i: (i, 0)),
-        out_shape=jax.ShapeDtypeStruct((rows, width), out_type),
-        compiler_params=grid_params(),
-    )(*lefts, *rights)
-
-
-def project(a, parts, layer):
-    widths = [v.shape[-1] for v in parts]
+        rows // ROWS_BLK,
+        [row_spec(v, first_row // ROWS_BLK) for v in lefts] + [matrix_spec(v) for v in rights],
+        pl.BlockSpec((ROWS_BLK, width), lambda i: (i, 0)),
+        jax.ShapeDtypeStruct((rows, width), out_type),
+        lefts + [v[0] for v in rights],
+    )
+
+
+def project(a, parts):
+    widths = [matrix_shape(v)[1] for v in parts[:-1]] + [matrix_shape(parts[-1])[0]]
 
     def body(left, *refs):
         out = refs[-1]
         at = 0
         for right, width in zip(refs[:-1], widths):
-            out[:, at : at + width] = nn(left[...], right[...])
+            turned = at + width == out.shape[1]
+            out[:, at : at + width] = (nt if turned else nn)(left[...], right[...])
             at += width
 
-    return pl.pallas_call(
+    return local_call(
         body,
-        grid=(a.shape[0] // ROWS_BLK,),
-        in_specs=[row_spec(a)] + [layer_spec(v, layer) for v in parts],
-        out_specs=pl.BlockSpec((ROWS_BLK, sum(widths)), lambda i: (i, 0)),
-        out_shape=jax.ShapeDtypeStruct((a.shape[0], sum(widths)), f32),
-        compiler_params=grid_params(),
-    )(a, *parts)
-
-
-def ff_forward(m, w_gate, w_up, far, layer, ffp):
-    ff = w_gate.shape[-1]
-
-    def body(m_ref, gate_w, up_w, far_w, gate_ref, up_ref, product_ref):
+        a.shape[0] // ROWS_BLK,
+        [row_spec(a)] + [matrix_spec(v) for v in parts],
+        pl.BlockSpec((ROWS_BLK, sum(widths)), lambda i: (i, 0)),
+        jax.ShapeDtypeStruct((a.shape[0], sum(widths)), f32),
+        [a] + [v[0] for v in parts],
+    )
+
+
+def ff_forward(m, gate_w, up_w, far, ffp):
+    ff = matrix_shape(gate_w)[0]
+
+    def body(m_ref, gate_w, up_w, far_gate, far_up, gate_ref, up_ref, product_ref):
         m = m_ref[...]
-        both = nn(m, far_w[...])
-        values = ((nn(m, gate_w[...]), nn(m, up_w[...])), (both[:, :ff], both[:, ff:]))
-        for slot, (gate, up) in enumerate(values):
+        for slot, (gate_t, up_t) in enumerate(((gate_w, up_w), (far_gate, far_up))):
+            gate, up = nt(m, gate_t[...]), nt(m, up_t[...])
             at = slot * ffp
             gate_ref[:, at : at + ff] = gate.astype(bf16)
             up_ref[:, at : at + ff] = up.astype(bf16)
             product_ref[:, at : at + ff] = (gate * jax.nn.sigmoid(gate) * up).astype(bf16)
 
     shape = (m.shape[0], 2 * ffp)
-    return pl.pallas_call(
+    parts = [gate_w, up_w, (far, (0, ff)), (far, (1, ff))]
+    return local_call(
         body,
-        grid=(m.shape[0] // ROWS_BLK,),
-        in_specs=[row_spec(m), layer_spec(w_gate, layer), layer_spec(w_up, layer), layer_spec(far, layer)],
-        out_specs=[pl.BlockSpec((ROWS_BLK, 2 * ffp), lambda i: (i, 0))] * 3,
-        out_shape=[jax.ShapeDtypeStruct(shape, bf16)] * 3,
-        compiler_params=grid_params(),
-    )(m, w_gate, w_up, far)
-
-
-def ff_backward(m_all, g_all, gate, up, product, w_gate, w_up, w_down, down_far, layer, ffp):
-    ff = w_gate.shape[-1]
-    near = gate.shape[0] // ROWS_BLK
-
-    def pair(gate, up, dproduct):
-        sig = jax.nn.sigmoid(gate)
-        silu = gate * sig
-        dgate = dproduct * up * (sig + silu * (1.0 - sig))
-        return jnp.concatenate([dgate.astype(bf16), (dproduct * silu).astype(bf16)], axis=1), silu
-
-    def body(m_ref, g_ref, gate_ref, up_ref, product_ref, gate_w, up_w, down_w, far_w, own_ref, far_ref, all_ref):
-        step = pl.program_id(0)
+        m.shape[0] // ROWS_BLK,
+        [row_spec(m)] + [matrix_spec(v) for v in parts],
+        [pl.BlockSpec((ROWS_BLK, 2 * ffp), lambda i: (i, 0))] * 3,
+        [jax.ShapeDtypeStruct(shape, bf16)] * 3,
+        [m] + [v[0] for v in parts],
+    )
+
+
+def gate_pair(gate, up, dproduct):
+    sig = jax.nn.sigmoid(gate)
+    silu = gate * sig
+    dgate = dproduct * up * (sig + silu * (1.0 - sig))
+    return jnp.concatenate([dgate.astype(bf16), (dproduct * silu).astype(bf16)], axis=1), silu
+
+
+def ff_backward(g, gate, up, product, down_w, far, ffp):
+    ff = matrix_shape(down_w)[0]
+
+    def body(g_ref, gate_ref, up_ref, product_ref, down_ref, far_ref, own_out, far_out, product_out):
         g = g_ref[...]
-        dproduct = nt(g, down_w[...])
-
-        @pl.when(step < near)
-        def _():
-            own_ref[...] = pair(gate_ref[:, :ff].astype(f32), up_ref[:, :ff].astype(f32), dproduct)[0]
-            all_ref[...] = product_ref[:, :ff]
-            cols = slice(ffp, ffp + ff)
-            far_ref[...] = pair(
-                gate_ref[:, cols].astype(f32), up_ref[:, cols].astype(f32), nt(g, far_w[...])
+        for slot, (weight, out) in enumerate(((down_ref, own_out), (far_ref, far_out))):
+            cols = slice(slot * ffp, slot * ffp + ff)
+            out[...] = gate_pair(
+                gate_ref[:, cols].astype(f32), up_ref[:, cols].astype(f32), nt(g, weight[...])
             )[0]
-
-        @pl.when(step >= near)
-        def _():
-            gate, up = nn(m_ref[...], gate_w[...]), nn(m_ref[...], up_w[...])
-            value, silu = pair(gate, up, dproduct)
-            own_ref[...] = value
-            all_ref[...] = (silu * up).astype(bf16)
-
-    rows = m_all.shape[0]
-    far_rows = gate.shape[0]
-    return pl.pallas_call(
+        product_out[...] = product_ref[:, :ff]
+
+    rows = g.shape[0]
+    parts = [down_w, (far, (2, ff))]
+    return local_call(
         body,
-        grid=(rows // ROWS_BLK,),
-        in_specs=[
-            pl.BlockSpec((ROWS_BLK, m_all.shape[1]), lambda i: (jnp.maximum(i, near), 0)),
-            row_spec(g_all),
-            row_spec(gate, 0, near - 1),
-            row_spec(up, 0, near - 1),
-            row_spec(product, 0, near - 1),
-            layer_spec(w_gate, layer),
-            layer_spec(w_up, layer),
-            layer_spec(w_down, layer),
-            layer_spec(down_far, layer),
-        ],
-        out_specs=[
+        rows // ROWS_BLK,
+        [row_spec(v) for v in (g, gate, up, product)] + [matrix_spec(v) for v in parts],
+        [
             pl.BlockSpec((ROWS_BLK, 2 * ff), lambda i: (i, 0)),
-            pl.BlockSpec((ROWS_BLK, 2 * ff), lambda i: (jnp.minimum(i, near - 1), 0)),
+            pl.BlockSpec((ROWS_BLK, 2 * ff), lambda i: (i, 0)),
             pl.BlockSpec((ROWS_BLK, ff), lambda i: (i, 0)),
         ],
-        out_shape=[
+        [
+            jax.ShapeDtypeStruct((2 * rows, 2 * ff), bf16),
             jax.ShapeDtypeStruct((rows, 2 * ff), bf16),
-            jax.ShapeDtypeStruct((far_rows, 2 * ff), bf16),
-            jax.ShapeDtypeStruct((rows, ff), bf16),
+            jax.ShapeDtypeStruct((2 * rows, ff), bf16),
         ],
-        compiler_params=grid_params(),
-    )(m_all, g_all, gate, up, product, w_gate, w_up, w_down, down_far)
+        [g, gate, up, product] + [v[0] for v in parts],
+    )
+
+
+def ff_backward_far(m_all, g_all, dboth, product_all, gate_w, up_w, down_w):
+    def body(m_ref, g_ref, gate_t, up_t, down_ref, _, __, own_out, product_out):
+        gate, up = nt(m_ref[...], gate_t[...]), nt(m_ref[...], up_t[...])
+        value, silu = gate_pair(gate, up, nt(g_ref[...], down_ref[...]))
+        own_out[...] = value
+        product_out[...] = (silu * up).astype(bf16)
+
+    near = m_all.shape[0] // ROWS_BLK // 2
+    parts = [gate_w, up_w, down_w]
+    return local_call(
+        body,
+        near,
+        [row_spec(m_all, near), row_spec(g_all, near)]
+        + [matrix_spec(v) for v in parts]
+        + [pl.BlockSpec(memory_space=pl.ANY)] * 2,
+        [row_spec(dboth, near), row_spec(product_all, near)],
+        [jax.ShapeDtypeStruct(v.shape, bf16) for v in (dboth, product_all)],
+        [m_all, g_all] + [v[0] for v in parts] + [dboth, product_all],
+        {5: 0, 6: 1},
+    )
 
 
 def ring_place(index, n):
@@ -575,105 +598,157 @@
     return jnp.where(place < n // 2, 2 * place, 2 * (n - 1 - place) + 1)
 
 
-def ring_sum(n, data, out, slots, send, recv, out_send, out_recv):
-    me = ring_place(lax.axis_index("dp"), n)
-    peers = [ring_index(lax.rem(me + 1, n), n), ring_index(lax.rem(me + n - 1, n), n)]
-    rows = data.shape[0] // (2 * n)
-    signs = (1, -1)
-
-    def chunk(ref, way, back):
-        which = lax.rem(me + 2 * n - signs[way] * back, n)
-        return ref.at[pl.ds(pl.multiple_of((2 * which + way) * rows, 16), rows)]
-
-    def partial(way, source, step):
+MESH = pl.DeviceIdType.MESH
+
+
+class Ring:
+    def __init__(self, n, data, out, slots, sems):
+        self.n, self.data, self.out, self.slots = n, data, out, slots
+        self.send, self.recv, self.out_send, self.out_recv = sems
+        self.me = ring_place(lax.axis_index("dp"), n)
+        self.peers = [
+            ring_index(lax.rem(self.me + 1, n), n),
+            ring_index(lax.rem(self.me + n - 1, n), n),
+        ]
+        self.rows = data.shape[0] // (2 * n)
+
+    def chunk(self, ref, way, back):
+        which = lax.rem(self.me + 2 * self.n - (1, -1)[way] * back, self.n)
+        return ref.at[pl.ds(pl.multiple_of((2 * which + way) * self.rows, 16), self.rows)]
+
+    def partial(self, way, source, step):
         return pltpu.make_async_remote_copy(
-            src_ref=source, dst_ref=slots.at[way, step],
-            send_sem=send.at[way, step], recv_sem=recv.at[way, step],
-            device_id={"dp": peers[way]}, device_id_type=pl.DeviceIdType.MESH,
-        )
-
-    def final(way, step):
-        part = chunk(out, way, step - 1)
+            src_ref=source, dst_ref=self.slots.at[way, step],
+            send_sem=self.send.at[way, step], recv_sem=self.recv.at[way, step],
+            device_id={"dp": self.peers[way]}, device_id_type=MESH,
+        )
+
+    def final(self, way, step, back):
+        part = self.chunk(self.out, way, back)
         return pltpu.make_async_remote_copy(
             src_ref=part, dst_ref=part,
-            send_sem=out_send.at[way, step], recv_sem=out_recv.at[way, step],
-            device_id={"dp": peers[way]}, device_id_type=pl.DeviceIdType.MESH,
-        )
-
-    def arrived(way, step):
-        part = chunk(out, way, step)
+            send_sem=self.out_send.at[way, step], recv_sem=self.out_recv.at[way, step],
+            device_id={"dp": self.peers[way]}, device_id_type=MESH,
+        )
+
+    def start(self):
+        for way in range(2):
+            self.partial(way, self.chunk(self.data, way, 0), 0).start()
+
+    def reduce(self, step):
+        for way in range(2):
+            slot = self.slots.at[way, step]
+            self.partial(way, slot, step).wait_recv()
+            part = self.chunk(self.data, way, step + 1)
+            slot[...] = (slot[...].astype(f32) + part[...].astype(f32)).astype(bf16)
+
+            @pl.when(step < self.n - 2)
+            def _():
+                self.partial(way, slot, step + 1).start()
+
+    def turn(self):
+        for way in range(2):
+            self.chunk(self.out, way, -1)[...] = self.slots[way, self.n - 2]
+            self.final(way, 0, -1).start()
+
+    def gather(self, step):
+        for way in range(2):
+            self.final(way, step, step).wait_recv()
+
+            @pl.when(step < self.n - 2)
+            def _():
+                self.final(way, step + 1, step).start()
+
+    def sent(self, step):
+        for way in range(2):
+            self.partial(way, self.slots.at[way, step], step).wait_send()
+            self.final(way, step, step - 1).wait_send()
+
+
+def steps_of(lo, hi, *bodies):
+    def body(step, carry):
+        for each in bodies:
+            each(step)
+        return carry
+
+    lax.fori_loop(lo, hi, body, 0)
+
+
+def mix_sum_kernel(
+    n, done, own, far, misc, out_done, out_own, out_misc, came, total, slots,
+    send, recv, out_send, out_recv, chip_send, chip_recv, sums, misc_came, misc_send, misc_recv,
+):
+    me = ring_place(lax.axis_index("dp"), n)
+    member, row = lax.axis_index("head"), lax.axis_index("dp")
+    swaps = [{"head": member ^ 1}, {"head": member ^ 2}]
+    swaps += [{"dp": row ^ (1 << bit)} for bit in range(n.bit_length() - 1)]
+    peers = swaps + [
+        {"dp": ring_index(lax.rem(me + 1, n), n)},
+        {"dp": ring_index(lax.rem(me + n - 1, n), n)},
+    ]
+    barrier = pltpu.get_barrier_semaphore()
+    for peer in peers:
+        pl.semaphore_signal(barrier, inc=1, device_id=peer, device_id_type=MESH)
+    pl.semaphore_wait(barrier, len(peers))
+
+    def small(step):
         return pltpu.make_async_remote_copy(
-            src_ref=part, dst_ref=part,
-            send_sem=out_send.at[way, step], recv_sem=out_recv.at[way, step],
-            device_id={"dp": peers[way]}, device_id_type=pl.DeviceIdType.MESH,
-        )
-
-    for way in range(2):
-        partial(way, chunk(data, way, 0), 0).start()
-
-    def reduce_step(step, carry):
-        for way in range(2):
-            slot = slots.at[way, step]
-            partial(way, slot, step).wait_recv()
-            slot[...] = (slot[...].astype(f32) + chunk(data, way, step + 1)[...].astype(f32)).astype(bf16)
-
-            @pl.when(step < n - 2)
-            def _():
-                partial(way, slot, step + 1).start()
-
-        return carry
-
-    lax.fori_loop(0, n - 1, reduce_step, 0)
-    for way in range(2):
-        chunk(out, way, -1)[...] = slots[way, n - 2]
-        final(way, 0).start()
-
-    def gather_step(step, carry):
-        for way in range(2):
-            arrived(way, step).wait_recv()
-
-            @pl.when(step < n - 2)
-            def _():
-                final(way, step + 1).start()
-
-        return carry
-
-    lax.fori_loop(0, n - 1, gather_step, 0)
-
-    def sent_step(step, carry):
-        for way in range(2):
-            partial(way, slots.at[way, step], step).wait_send()
-            final(way, step).wait_send()
-        return carry
-
-    lax.fori_loop(0, n - 1, sent_step, 0)
-
-
-def mix_sum_kernel(n, done, own, far, out_done, out_own, came, total, slots, send, recv, out_send, out_recv, chip_send, chip_recv):
-    me = ring_place(lax.axis_index("dp"), n)
-    barrier = pltpu.get_barrier_semaphore()
-    for place in (lax.rem(me + 1, n), lax.rem(me + n - 1, n)):
-        pl.semaphore_signal(
-            barrier, inc=1, device_id={"dp": ring_index(place, n)}, device_id_type=pl.DeviceIdType.MESH
-        )
-    other = lax.axis_index("head") ^ 2
-    pl.semaphore_signal(barrier, inc=1, device_id={"head": other}, device_id_type=pl.DeviceIdType.MESH)
-    pl.semaphore_wait(barrier, 3)
+            src_ref=sums.at[step], dst_ref=misc_came.at[step],
+            send_sem=misc_send.at[step], recv_sem=misc_recv.at[step],
+            device_id=swaps[step], device_id_type=MESH,
+        )
+
+    taken = [0]
+
+    def small_step():
+        step = taken[0]
+        if step == len(swaps):
+            return
+        small(step).wait()
+        sums[step + 1] = sums[step] + misc_came[step]
+        taken[0] += 1
+        if step + 1 < len(swaps):
+            small(step + 1).start()
+
     swap = pltpu.make_async_remote_copy(
         src_ref=far, dst_ref=came, send_sem=chip_send, recv_sem=chip_recv,
-        device_id={"head": other}, device_id_type=pl.DeviceIdType.MESH,
+        device_id={"head": member ^ 2}, device_id_type=MESH,
     )
+    first = Ring(n, done, out_done, slots.at[0], [v.at[0] for v in (send, recv, out_send, out_recv)])
+    second = Ring(n, total, out_own, slots.at[1], [v.at[1] for v in (send, recv, out_send, out_recv)])
+    middle, last = (n - 1) // 2, n - 1
+    sums[0] = misc[...]
+    small(0).start()
     swap.start()
-    ring_sum(n, done, out_done, slots.at[0], send.at[0], recv.at[0], out_send.at[0], out_recv.at[0])
+    first.start()
+    steps_of(0, middle, first.reduce)
+    small_step()
+    steps_of(middle, last, first.reduce)
+    first.turn()
+    small_step()
     swap.wait()
     total[...] = (own[...].astype(f32) + came[...].astype(f32)).astype(bf16)
-    ring_sum(n, total, out_own, slots.at[1], send.at[1], recv.at[1], out_send.at[1], out_recv.at[1])
-
-
-def mix_sum(done, own, far, n):
+    second.start()
+    steps_of(0, middle, first.gather, second.reduce)
+    small_step()
+    steps_of(middle, last, first.gather, second.reduce)
+    second.turn()
+    small_step()
+    steps_of(0, middle, second.gather)
+    small_step()
+    steps_of(middle, last, second.gather)
+    for _ in swaps:
+        small_step()
+    out_misc[...] = sums[len(swaps)]
+    steps_of(0, last, first.sent, second.sent)
+
+
+def mix_sum(done, own, far, misc, n):
     if n == 1:
-        return done, (own.astype(f32) + chip_swap(far).astype(f32)).astype(bf16)
+        misc = misc + core_swap(misc)
+        return done, (own.astype(f32) + chip_swap(far).astype(f32)).astype(bf16), misc + chip_swap(misc)
     rows, cols = own.shape
+    swaps = 2 + n.bit_length() - 1
 
     def body(*refs):
         mix_sum_kernel(n, *refs)
@@ -681,20 +756,26 @@
     vmem = pl.BlockSpec(memory_space=pltpu.VMEM)
     return pl.pallas_call(
         body,
-        in_specs=[vmem] * 3,
-        out_specs=[vmem] * 2,
-        out_shape=[jax.ShapeDtypeStruct((rows, cols), bf16)] * 2,
+        in_specs=[vmem] * 4,
+        out_specs=[vmem] * 3,
+        out_shape=[jax.ShapeDtypeStruct((rows, cols), bf16)] * 2 + [jax.ShapeDtypeStruct(misc.shape, f32)],
         scratch_shapes=[
             pltpu.VMEM((rows, cols), bf16),
             pltpu.VMEM((rows, cols), bf16),
             pltpu.VMEM((2, 2, n - 1, rows // (2 * n), cols), bf16),
         ]
         + [pltpu.SemaphoreType.DMA((2, 2, n - 1))] * 4
-        + [pltpu.SemaphoreType.DMA] * 2,
+        + [pltpu.SemaphoreType.DMA] * 2
+        + [
+            pltpu.VMEM((swaps + 1,) + misc.shape, f32),
+            pltpu.VMEM((swaps,) + misc.shape, f32),
+            pltpu.SemaphoreType.DMA((swaps,)),
+            pltpu.SemaphoreType.DMA((swaps,)),
+        ],
         compiler_params=pltpu.CompilerParams(
             collective_id=0, has_side_effects=True, vmem_limit_bytes=VMEM_LIMIT
         ),
-    )(done, own, far)
+    )(done, own, far, misc)
 
 
 def norm_scale(hidden):
@@ -722,29 +803,14 @@
     return lax.ppermute(value, "head", [(i, i ^ 2) for i in range(4)])
 
 
-def dp_swap(value, bit):
-    return lax.ppermute(value, "dp", [(i, i ^ (1 << bit)) for i in range(lax.axis_size("dp"))])
-
-
-def dp_bits():
-    return lax.axis_size("dp").bit_length() - 1
-
-
-def small_sum(value):
-    value = value + core_swap(value)
-    value = value + chip_swap(value)
-    for bit in range(dp_bits()):
-        value = value + dp_swap(value, bit)
-    return value
-
-
 def dp_slice(own):
     rows = own.shape[0] // lax.axis_size("dp")
     return lax.dynamic_slice_in_dim(own, lax.axis_index("dp") * rows, rows, 0)
 
 
-def dp_gather(part):
-    return lax.all_gather(part, "dp", axis=0, tiled=True)
+def dp_ring():
+    n = lax.axis_size("dp")
+    return list(range(0, n, 2)) + list(range(n - 1, 0, -2)) if n > 1 else [0]
 
 
 def after(value, *others):
@@ -773,25 +839,32 @@
             [w_query[layer], w_key[layer], w_value[layer], w_outgate[layer]], axis=1
         )
 
-    def ff_parts(layer, wait):
-        part = jnp.concatenate([dp_slice(w_gate[layer]), dp_slice(w_up[layer])], axis=1)
-        return chip_swap(after(part, wait)), chip_swap(after(dp_slice(w_down[layer]), wait))
+    gate_t, up_t, rank_t = (jnp.swapaxes(v, 1, 2) for v in (w_gate, w_up, w_rank))
+
+    def ff_slice(layer, wait):
+        part = jnp.concatenate([dp_slice(v[layer]) for v in (gate_t, up_t, w_down)], axis=0)
+        return chip_swap(after(part, wait))
+
+    def ff_gather(part):
+        dp = lax.axis_size("dp")
+        whole = lax.all_gather(part, "dp", axis=0, tiled=True)
+        return jnp.swapaxes(whole.reshape(dp, 3, ff // dp, width), 0, 1).reshape(3 * ff, width)
 
     def with_partner(local):
         return jnp.concatenate([local, core_swap(local)], axis=0)
 
-    def settle(terms, layer):
-        sent = core_swap(sum_of_dots(terms, layer, shard_len, shard_len, bf16))
-        return sum_of_dots(terms, layer, 0, shard_len, f32) + sent.astype(f32)
+    def settle(terms):
+        sent = core_swap(sum_of_dots(terms, shard_len, shard_len, bf16))
+        return sum_of_dots(terms, 0, shard_len, f32) + sent.astype(f32)
 
     small = jnp.concatenate([w_decay.astype(f32), decay_bias[:, None, :]], axis=1)
     small = jnp.concatenate([small, chip_swap(small)], axis=2)
-    in_part, down_part = ff_parts(0, meta)
-    in_far = dp_gather(in_part)
-    down_far = dp_gather(after(down_part, in_far))
+    ff_part = ff_slice(0, meta)
+    ff_far = ff_gather(ff_part)
     mix_own = mix_pack(0)
-    mix_far = chip_swap(after(mix_own, in_part, down_part))
-    out_far = chip_swap(after(w_out[0], in_part, down_part))
+    mix_far = chip_swap(after(mix_own, ff_part))
+    out_far = chip_swap(after(w_out[0], ff_part))
+    next_part = ff_slice(1, mix_far)
 
     grad = grad_out[0].astype(f32)
     hidden = tokens[0].astype(f32)
@@ -799,61 +872,75 @@
     for layer in range(LAYERS):
         hidden_in = hidden
         a = with_partner(norm_low(hidden, norm_one[layer]))
-        x = project(a, (mix_own, mix_far, w_rank), layer)
+        x = project(a if layer == 0 else after(a, g_y), ((mix_own, None), (mix_far, None), (rank_t, layer)))
         wdec, bias = small[layer, :rank], small[layer, rank:]
         run, states, cum, final = mixer.states(x, wdec, bias)
         got = chip_swap(final)
         first = got[::-1] * chip.astype(bf16)
         gain = group_gain[layer][None]
         gated, mixed = mixer.mix(x, run, states, cum, first, gain)
-        hidden_mid = hidden + settle([(gated, 0, w_out, False), (gated, HV, out_far, False)], layer)
         if layer + 1 < LAYERS:
             next_own = mix_pack(layer + 1)
-            next_mix = chip_swap(after(next_own, gated))
-            next_out = chip_swap(after(w_out[layer + 1], gated))
-            in_part, down_part = ff_parts(layer + 1, down_far)
-            next_in = dp_gather(in_part)
-            next_down = dp_gather(after(down_part, next_in))
+            next_mix = chip_swap(after(next_own, got))
+            next_out = chip_swap(after(w_out[layer + 1], got))
+            next_far = ff_gather(next_part)
+        hidden_mid = hidden + settle(
+            [(gated, 0, (w_out, layer), False), (gated, HV, (out_far, None), False)]
+        )
         m_own = norm_low(hidden_mid, norm_two[layer])
         m = with_partner(m_own)
-        gate, up, product = ff_forward(m, w_gate, w_up, in_far, layer, ffp)
-        hidden = hidden_mid + settle([(product, 0, w_down, False), (product, ffp, down_far, False)], layer)
+        gate, up, product = ff_forward(m, (gate_t, layer), (up_t, layer), ff_far, ffp)
+        if layer + 1 < LAYERS:
+            product = after(product, next_mix, next_out)
+        hidden = hidden_mid + settle(
+            [(product, 0, (w_down, layer), False), (product, ffp, (ff_far, (2, ff)), False)]
+        )
         m_y = chip_swap(m_own)
         m_all = jnp.concatenate([m, m_y, core_swap(m_y)], axis=0)
         saved.append(
             (hidden_in, hidden_mid, a, m_all, x, run, states, cum, first, mixed, gated, gate, up, product,
-             mix_own, mix_far, out_far, in_far, down_far)
+             mix_own, mix_far, out_far, ff_far)
         )
         if layer + 1 < LAYERS:
-            mix_own, mix_far, out_far, in_far, down_far = next_own, next_mix, next_out, next_in, next_down
+            mix_own, mix_far, out_far, ff_far = next_own, next_mix, next_out, next_far
+            g_own = grad_out[0]
+            g_y = chip_swap(after(g_own, next_mix))
     result = hidden.astype(bf16)[None]
 
     ff_grads, misc_grads = [None] * LAYERS, [None] * LAYERS
     for layer in reversed(range(LAYERS)):
         (
             hidden_in, hidden_mid, a, m_all, x, run, states, cum, first, mixed, gated, gate, up, product,
-            mix_own, mix_far, out_far, in_far, down_far,
+            mix_own, mix_far, out_far, ff_far,
         ) = saved[layer]
         gain = group_gain[layer][None]
         wdec, bias = small[layer, :rank], small[layer, rank:]
-        g_own = grad.astype(bf16)
-        g_y = chip_swap(g_own)
         if layer + 1 < LAYERS:
+            g_own = grad.astype(bf16)
+            g_y = chip_swap(g_own)
             far_came = chip_swap(after(far, g_y))
-        g_all = jnp.concatenate([g_own, core_swap(g_own), g_y, core_swap(g_y)], axis=0)
-        dboth, dfar, product_all = ff_backward(
-            m_all, g_all, gate, up, product, w_gate, w_up, w_down, down_far, layer, ffp
-        )
-        in_grad = tn(dboth, m_all).astype(bf16)
-        down_grad = tn(product_all, g_all).astype(bf16)
+        g = with_partner(g_own)
+        g_all = jnp.concatenate([g, g_y, core_swap(g_y)], axis=0)
+        dboth, dfar, product_all = ff_backward(g, gate, up, product, (w_down, layer), ff_far, ffp)
         back_mid, gain_two = norm_back(
             hidden_mid,
             norm_two[layer],
-            settle([(dboth, 0, w_gate, True), (dboth, ff, w_up, True), (dfar, 0, in_far, True)], layer),
-        )
+            settle(
+                [
+                    (dboth, 0, (gate_t, layer), False),
+                    (dboth, ff, (up_t, layer), False),
+                    (dfar, 0, (ff_far, (0, 2 * ff)), False),
+                ]
+            ),
+        )
+        dboth, product_all = ff_backward_far(
+            m_all, g_all, dboth, product_all, (gate_t, layer), (up_t, layer), (w_down, layer)
+        )
+        in_grad = tn(dboth, m_all).astype(bf16)
+        down_grad = tn(product_all, g_all).astype(bf16)
         grad = grad + back_mid
         g_mix = with_partner(grad.astype(bf16))
-        g_wout = tn(gated, g_mix).astype(bf16)
+        g_wout = tn(g_mix, gated).astype(bf16)
         dmixed, doutgate, dstates, dcum, dfinal, dgain = mixer.back_states(
             x, run, mixed, g_mix, w_out[layer], out_far, gain
         )
@@ -862,33 +949,40 @@
         dx, dwdec, dbias = mixer.back(
             x, run, states, cum, first, dmixed, doutgate, dstates, dcum, dlast, wdec, bias
         )
-        g_wmix = tn(dx, a)
+        g_wmix = tn(a, dx[:, : 2 * HEAD_COLS]).astype(bf16)
+        g_rank = tn(dx[:, 2 * HEAD_COLS :], a)
         if layer + 1 < LAYERS:
             done = (own.astype(f32) + after(far_came, dx).astype(f32)).astype(bf16)
-        far = jnp.concatenate([g_wmix[HEAD_COLS : 2 * HEAD_COLS].astype(bf16), g_wout[HV:]], axis=0)
-        own = jnp.concatenate([g_wmix[:HEAD_COLS].astype(bf16), g_wout[:HV]], axis=0)
+        far = jnp.concatenate([g_wmix[:, HEAD_COLS:], g_wout[:, HV:]], axis=1)
+        own = jnp.concatenate([g_wmix[:, :HEAD_COLS], g_wout[:, :HV]], axis=1)
         back_first, gain_one = norm_back(hidden_in, norm_one[layer], settle(
-            [(dx, 0, mix_own, True), (dx, HEAD_COLS, mix_far, True), (dx, 2 * HEAD_COLS, w_rank, True)], layer
+            [
+                (dx, 0, (mix_own, None), True),
+                (dx, HEAD_COLS, (mix_far, None), True),
+                (dx, 2 * HEAD_COLS, (rank_t, layer), False),
+            ]
         ))
         grad = grad + back_first
         if layer > 0:
             ff_grads[layer] = lax.psum((in_grad, down_grad), "dp")
         else:
-            in_grad, down_grad, _ = lax.optimization_barrier((in_grad, down_grad, ff_grads[1]))
-            ff_grads[layer] = lax.psum((in_grad, down_grad), "dp")
-            mix_grads = mix_sum(done, own, far, lax.axis_size("dp"))
-            mix_grads = [mix_grads[1], mix_grads[0]]
+            ff_grads[layer] = [lax.psum(v, "dp", axis_index_groups=[dp_ring()]) for v in (in_grad, down_grad)]
+            ff_grads[1] = after(ff_grads[1], grad)
         heads = jnp.concatenate([dwdec, dbias], axis=0)
         places = lax.iota(jnp.int32, 4)[:, None, None]
         heads = jnp.where(places == member, heads[None, :, :HK], 0.0) + jnp.where(
             places == member ^ 2, heads[None, :, HK:], 0.0
         )
         misc_grads[layer] = jnp.concatenate(
-            [g_wmix[2 * HEAD_COLS :].reshape(-1), gain_one, gain_two, dgain[0], heads.reshape(-1)]
+            [g_rank.reshape(-1), gain_one, gain_two, dgain[0], heads.reshape(-1)]
         )
 
     misc = jnp.stack(misc_grads)
-    misc = small_sum(misc.reshape(-1, 128)).reshape(LAYERS, -1)
+    length = misc.shape[1]
+    misc = jnp.pad(misc.reshape(-1), (0, -misc.size % 1024)).reshape(-1, 128)
+    later_mix, first_mix, misc = mix_sum(done, own, far, misc, lax.axis_size("dp"))
+    mix_grads = [first_mix, later_mix]
+    misc = misc.reshape(-1)[: LAYERS * length].reshape(LAYERS, length)
     sizes = (rank * width, width, width, HV, 4 * (rank + 1) * HK)
     pieces, at = [], 0
     for size in sizes:
@@ -901,8 +995,11 @@
     def rows_of(grads, start, stop):
         return jnp.stack([g[start:stop].astype(f32) for g in grads])
 
+    def turned(grads, start, stop):
+        return jnp.stack([g[start:stop].T.astype(f32) for g in grads])
+
     def cols_of(grads, start, stop):
-        return jnp.stack([g[start:stop].T.astype(f32) for g in grads])
+        return jnp.stack([g[:, start:stop].astype(f32) for g in grads])
 
     return (
         result,
@@ -916,10 +1013,10 @@
         heads[:, :rank],
         heads[:, rank],
         pieces[3],
-        rows_of(mix_grads, HEAD_COLS, HEAD_COLS + HV),
+        jnp.stack([g[:, HEAD_COLS:].T.astype(f32) for g in mix_grads]),
         pieces[2],
-        cols_of([g[0] for g in ff_grads], 0, ff),
-        cols_of([g[0] for g in ff_grads], ff, 2 * ff),
+        turned([g[0] for g in ff_grads], 0, ff),
+        turned([g[0] for g in ff_grads], ff, 2 * ff),
         rows_of([g[1] for g in ff_grads], 0, ff),
     )
 

time: 975 us -> 797 us (0.82)
  waiting for transfers between devices: 296 us -> 113 us
  Pallas kernels: 404 us -> 435 us
  local copies, waits for them, and re-layouts: 75 us -> 64.3 us
    psum x2 -> x1, waiting for transfers between devices: 113 us -> 0.01 us  [per_device(): ff_grads[layer] = lax.psum((in_grad, down_grad), 'dp')]
    ppermute x19 -> x16, waiting for transfers between devices: 145 us -> 111 us  [chip_swap(): return lax.ppermute(value, 'head', [(i, i ^ 2) for i in range(4)])]
    pallas_call x23 -> x25, Pallas kernels: 320 us -> 352 us  [the longest x1 207 us: mix_sum(): pl.pallas_call(body, in_specs=[vmem] * 4, out_specs=[vmem] * 3, out_shape...]
    all_gather x4 -> x2, waiting for transfers between devices: 29.1 us -> 0.01 us  [ff_gather(): whole = lax.all_gather(part, 'dp', axis=0, tiled=True)]
    unnamed x329 -> x257, local copies, waits for them, and re-layouts: 35.6 us -> 20.2 us
    transpose x0 -> x2, local copies, waits for them, and re-layouts: none -> 9.94 us  [ff_gather(): jnp.swapaxes(whole.reshape(dp, 3, ff // dp, width), 0, 1)]
    ppermute x19 -> x16, starting transfers between devices: 20.8 us -> 17.9 us  [chip_swap(): return lax.ppermute(value, 'head', [(i, i ^ 2) for i in range(4)])]
    dot_general x8 -> x10, matrix products: 49.1 us -> 48.6 us  [tn(): lax.dot_general(left, right, (((0,), (0,)), ((), ())), preferred_element_...]
  transfers between devices with their start and end apart: 49 -> 40, of which waited for: 15 -> 10; matrix products, arithmetic and copies ran while one was open for 19% -> 21% of each run, Pallas kernels for 39% -> 51%
where the time goes in v3:
time: 797 us; the launch traced here: 789 us
  Pallas kernels  435 us (55%)
  waiting for transfers between devices  113 us (14%)
  other arithmetic  90 us (11%)
  local copies, waits for them, and re-layouts  64.3 us (8%)
  matrix products  48.6 us (6%)
  starting transfers between devices  22 us (3%)
  between operations  15.7 us (2%)
    pallas_call x1, Pallas kernels, mix_sum(): pl.pallas_call(body, in_specs=[vmem] * 4, out_specs=[vmem] * 3, out_shape...  207 us
    pallas_call x24, Pallas kernels, local_call(): pl.pallas_call(body, grid=(grid,), in_specs=in_specs, out_specs=out_specs...  144 us
    ppermute x16, waiting for transfers between devices, chip_swap(): return lax.ppermute(value, 'head', [(i, i ^ 2) for i in range(4)])  111 us
    pallas_call x8, Pallas kernels, call(): pl.pallas_call(body, grid_spec=pltpu.PrefetchScalarGridSpec(num_scalar_pr...  83.3 us
    dot_general x10, matrix products, tn(): lax.dot_general(left, right, (((0,), (0,)), ((), ())), preferred_element_...  48.6 us
    unnamed x257, local copies, waits for them, and re-layouts  20.2 us
    ppermute x16, starting transfers between devices, chip_swap(): return lax.ppermute(value, 'head', [(i, i ^ 2) for i in range(4)])  17.9 us
  transfers between devices with their start and end apart: 40, of which 10 were waited for; matrix products, arithmetic and copies ran while one was open for 21% of the time, Pallas kernels for 51%

profile of v3, /device:TPU:0, one launch (start us, length us, event | category | flops | bytes accessed | tf_op | source)
XLA Modules:
  0.0 788.6 jit_solution(5059971788925944097)
XLA Ops:
  21.7 12.3 %collective-permute-done.1 = bf16[264,1024]{1,0:T(8,128)(2,1)S(1)} collective-permute-done((bf16[264,1024]{1,0:T(8,128)(2,1)S(1)}, bf16[264,1024]{1,0:T(8,128)(2,1)S(1)}, u32[]{:S(2)}, u32[]{:S(2)}) %collective-permute-start.1) | collective-permute-done | bytes 540704 | tf_op jit(solution)/shard_map/ppermute | solution.py:803
  45.1 31.4 %collective-permute-done.3 = f32[2,17,128]{2,1,0:T(8,128)S(1)} collective-permute-done((f32[2,17,128]{2,1,0:T(8,128)S(1)}, f32[2,17,128]{2,1,0:T(8,128)S(1)}, u32[]{:S(2)}, u32[]{:S(2)}) %collective-permute-start.3) | collective-permute-done | bytes 17440 | tf_op jit(solution)/shard_map/ppermute | solution.py:803
  79.8 7.8 shard_map.288.refs_1_
  87.7 9.3 %shard_map.289 = (f32[1024,256]{1,0:T(8,128)S(1)}, bf16[8,2,256,128]{3,2,1,0:T(8,128)(2,1)S(1)}, f32[8,1,256]{2,1,0:T(1,128)S(1)}, bf16[2,256,128]{2,1,0:T(8,128)(2,1)S(1)}) custom-call(s32[6]{0:T(128)S(1)} %pad_add_fusion.refs_0_, f32[1024,1552]{1,0:T(8,128)} %shard_map.288.refs_1_, f32[16,256]{1,0:T(8,128)S(1)} %get-tuple-element.254.refs_2_.refs_11_, ...), custom_call_target="tpu_custom_call" | custom-call | tf_op jit(solution)/shard_map/pallas_call | solution.py:282
  102.1 7.7 shard_map.290
  120.7 9.3 %collective-permute-done.16 = bf16[264,1024]{1,0:T(8,128)(2,1)} collective-permute-done((bf16[264,1024]{1,0:T(8,128)(2,1)S(1)}, bf16[264,1024]{1,0:T(8,128)(2,1)}, u32[]{:S(2)}, u32[]{:S(2)}) %collective-permute-start.16) | collective-permute-done | bytes 540704 | tf_op jit(solution)/shard_map/ppermute | solution.py:803
  138.8 11.3 %shard_map.293 = (bf16[1024,1536]{1,0:T(8,128)(2,1)}, bf16[1024,1536]{1,0:T(8,128)(2,1)}, bf16[1024,1536]{1,0:T(8,128)(2,1)}) custom-call(bf16[1024,1024]{1,0:T(8,128)(2,1)S(1)} %copy-done.17, bf16[2,704,1024]{2,1,0:T(8,128)(2,1)S(1)} %bitcast.151, bf16[2,704,1024]{2,1,0:T(8,128)(2,1)} %bitcast.156, bf16[2112,1024]{1,0:T(8,128)(2,1)} %bitcast.173, ...), custom_call_target="tpu_custom_call" | custom-call | tf_op jit(solution)/shard_map/pallas_call | solution.py:445
  150.1 23.9 %collective-permute-done.9.refs_2_.refs_6_ = bf16[256,1024]{1,0:T(8,128)(2,1)S(1)} collective-permute-done((bf16[256,1024]{1,0:T(8,128)(2,1)}, bf16[256,1024]{1,0:T(8,128)(2,1)S(1)}, u32[]{:S(2)}, u32[]{:S(2)}) %collective-permute-start.9) | collective-permute-done | bytes 524320 | tf_op jit(solution)/shard_map/ppermute | solution.py:803
  186.0 23.5 %collective-permute-done.12 = bf16[512,1024]{1,0:T(8,128)(2,1)} collective-permute-done((bf16[512,1024]{1,0:T(8,128)(2,1)S(1)}, bf16[512,1024]{1,0:T(8,128)(2,1)}, u32[]{:S(2)}, u32[]{:S(2)}) %collective-permute-start.12) | collective-permute-done | bytes 1048608 | tf_op jit(solution)/shard_map/ppermute | solution.py:803
  217.1 9.3 %shard_map.297 = (f32[1024,256]{1,0:T(8,128)S(1)}, bf16[8,2,256,128]{3,2,1,0:T(8,128)(2,1)S(1)}, f32[8,1,256]{2,1,0:T(1,128)S(1)}, bf16[2,256,128]{2,1,0:T(8,128)(2,1)S(1)}) custom-call(s32[6]{0:T(128)S(1)} %pad_add_fusion.refs_0_, f32[1024,1552]{1,0:T(8,128)} %shard_map.296.refs_1_, f32[16,256]{1,0:T(8,128)S(1)} %get-tuple-element.253.refs_2_.refs_11_, ...), custom_call_target="tpu_custom_call" | custom-call | tf_op jit(solution)/shard_map/pallas_call | solution.py:282
  231.5 7.7 shard_map.298
  257.7 11.0 %shard_map.301 = (bf16[1024,1536]{1,0:T(8,128)(2,1)}, bf16[1024,1536]{1,0:T(8,128)(2,1)}, bf16[1024,1536]{1,0:T(8,128)(2,1)}) custom-call(bf16[1024,1024]{1,0:T(8,128)(2,1)S(1)} %pad_maximum_fusion.7.m_ref, bf16[2,704,1024]{2,1,0:T(8,128)(2,1)S(1)} %bitcast.152, bf16[2,704,1024]{2,1,0:T(8,128)(2,1)} %bitcast.157, bf16[2112,1024]{1,0:T(8,128)(2,1)} %bitcast.180, ...), custom_call_target="tpu_custom_call" | custom-call | tf_op jit(solution)/shard_map/pallas_call | solution.py:445
  268.7 10.1 %shard_map.304 = (bf16[2048,1408]{1,0:T(8,128)(2,1)}, bf16[1024,1408]{1,0:T(8,128)(2,1)S(1)}, bf16[2048,704]{1,0:T(8,128)(2,1)}) custom-call(bf16[1024,1024]{1,0:T(8,128)(2,1)S(1)} %copy-done.16, bf16[1024,1536]{1,0:T(8,128)(2,1)} %get-tuple-element.99.gate_ref, bf16[1024,1536]{1,0:T(8,128)(2,1)} %get-tuple-element.100.up_ref, ...), custom_call_target="tpu_custom_call" | custom-call | tf_op jit(solution)/shard_map/pallas_call | solution.py:445
  278.7 9.1 %shard_map.306 = bf16[512,1024]{1,0:T(8,128)(2,1)} custom-call(bf16[2048,1408]{1,0:T(8,128)(2,1)} %get-tuple-element.101.refs_0_._, bf16[1024,1408]{1,0:T(8,128)(2,1)S(1)} %get-tuple-element.102.refs_1_, bf16[2,704,1024]{2,1,0:T(8,128)(2,1)} %bitcast.146, bf16[2,704,1024]{2,1,0:T(8,128)(2,1)} %bitcast.158, bf16[2112,1024]{1,0:T(8,128)(2,1)} %bitcast.183), custom_call_target="tpu_custom_call" | custom-call | tf_op jit(solution)/shard_map/pallas_call | solution.py:445
  325.6 9.1 %shard_map.320 = (bf16[2048,1408]{1,0:T(8,128)(2,1)}, bf16[2048,704]{1,0:T(8,128)(2,1)}) custom-call(bf16[2048,1024]{1,0:T(8,128)(2,1)} %pad_maximum_fusion.2.m_ref, bf16[2048,1024]{1,0:T(8,128)(2,1)} %pad_maximum_fusion.3.g_ref, bf16[2,704,1024]{2,1,0:T(8,128)(2,1)S(1)} %bitcast.153, ...), custom_call_target="tpu_custom_call", output_to_operand_aliasing={{0}: (5, {}), {1}: (6, {})} | custom-call | tf_op jit(solution)/shard_map/pallas_call | solution.py:445
  337.1 12.6 %shard_map.307 = (bf16[1024,512]{1,0:T(8,128)(2,1)S(1)}, bf16[1024,512]{1,0:T(8,128)(2,1)S(1)}, bf16[8,2,256,128]{3,2,1,0:T(8,128)(2,1)S(1)}, f32[8,1,256]{2,1,0...) custom-call(s32[6]{0:T(128)S(1)} %pad_add_fusion.refs_0_, f32[1024,1552]{1,0:T(8,128)} %shard_map.296.refs_1_, ...), custom_call_target="tpu_custom_call" | custom-call | tf_op jit(solution)/shard_map/pallas_call | solution.py:282
  350.4 9.2 %convolution_convert_fusion = bf16[1408,1024]{1,0:T(8,128)(2,1)} fusion(bf16[2048,1408]{1,0:T(8,128)(2,1)S(1)} %bitcast.188, bf16[512,1024]{1,0:T(8,128)(2,1)S(1)} %collective-permute-done.34, bf16[512,1024]{1,0:T(8,128)(2,1)} %collective-permute-done.33, bf16[512,1024]{1,0:T(8,128)(2,1)} %collective-permute-done.15, bf16[512,1024]{1,0:T(8,128)(2,1)} %multiply_convert_fusion), kind=kOutput, calls=%fused_computation.11 | convolution fusion | flops 5923799040 | bytes 12845056 | tf_op jit(solution)/shard_map/dot_general | solution.py:31
  359.6 12.2 %shard_map.308 = (bf16[1024,1552]{1,0:T(8,128)(2,1)}, f32[16,256]{1,0:T(8,128)S(1)}, f32[1,256]{1,0:T(1,128)S(1)}) custom-call(s32[6]{0:T(128)S(1)} %pad_add_fusion.refs_0_, f32[1024,1552]{1,0:T(8,128)} %shard_map.296.refs_1_, f32[1024,256]{1,0:T(8,128)S(1)} %copy-done.15, bf16[8,2,256,128]{3,2,1,0:T(8,128)(2,1)S(1)} %copy-done.27, ...), custom_call_target="tpu_custom_call" | custom-call | tf_op jit(solution)/shard_map/pallas_call | solution.py:282
  409.8 10.1 %shard_map.311 = (bf16[2048,1408]{1,0:T(8,128)(2,1)}, bf16[1024,1408]{1,0:T(8,128)(2,1)S(1)}, bf16[2048,704]{1,0:T(8,128)(2,1)}) custom-call(bf16[1024,1024]{1,0:T(8,128)(2,1)S(1)} %pad_maximum_fusion.10.g_ref, bf16[1024,1536]{1,0:T(8,128)(2,1)} %get-tuple-element.110.gate_ref, bf16[1024,1536]{1,0:T(8,128)(2,1)} %get-tuple-element.111.up_ref, ...), custom_call_target="tpu_custom_call" | custom-call | tf_op jit(solution)/shard_map/pallas_call | solution.py:445
  449.1 9.3 %shard_map.319 = (bf16[2048,1408]{1,0:T(8,128)(2,1)}, bf16[2048,704]{1,0:T(8,128)(2,1)}) custom-call(bf16[2048,1024]{1,0:T(8,128)(2,1)} %pad_maximum_fusion.m_ref, bf16[2048,1024]{1,0:T(8,128)(2,1)} %pad_maximum_fusion.1.g_ref, bf16[2,704,1024]{2,1,0:T(8,128)(2,1)S(1)} %bitcast.154, ...), custom_call_target="tpu_custom_call", output_to_operand_aliasing={{0}: (5, {}), {1}: (6, {})} | custom-call | tf_op jit(solution)/shard_map/pallas_call | solution.py:445
  458.5 10.8 %convolution_convert_fusion.1 = bf16[1408,1024]{1,0:T(8,128)(2,1)} fusion(bf16[2048,1408]{1,0:T(8,128)(2,1)} %get-tuple-element.133, bf16[512,1024]{1,0:T(8,128)(2,1)S(1)} %copy-done.97, bf16[512,1024]{1,0:T(8,128)(2,1)} %collective-permute-done.30, bf16[512,1024]{1,0:T(8,128)(2,1)} %collective-permute-done.7, bf16[512,1024]{1,0:T(8,128)(2,1)} %multiply_convert_fusion.2), kind=kOutput, calls=%fused_computation.12 | convolution fusion | flops 5923799040 | bytes 12845056 | tf_op jit(solution)/shard_map/dot_general | solution.py:31
  477.6 12.3 %shard_map.314 = (bf16[1024,512]{1,0:T(8,128)(2,1)S(1)}, bf16[1024,512]{1,0:T(8,128)(2,1)S(1)}, bf16[8,2,256,128]{3,2,1,0:T(8,128)(2,1)S(1)}, f32[8,1,256]{2,1,0...) custom-call(s32[6]{0:T(128)S(1)} %pad_add_fusion.refs_0_, f32[1024,1552]{1,0:T(8,128)} %shard_map.288.refs_1_, ...), custom_call_target="tpu_custom_call" | custom-call | tf_op jit(solution)/shard_map/pallas_call | solution.py:282
  495.9 12.2 %shard_map.315 = (bf16[1024,1552]{1,0:T(8,128)(2,1)}, f32[16,256]{1,0:T(8,128)S(1)}, f32[1,256]{1,0:T(1,128)S(1)}) custom-call(s32[6]{0:T(128)S(1)} %pad_add_fusion.refs_0_, f32[1024,1552]{1,0:T(8,128)} %shard_map.288.refs_1_, f32[1024,256]{1,0:T(8,128)S(1)} %copy-done.13, bf16[8,2,256,128]{3,2,1,0:T(8,128)(2,1)S(1)} %copy-done.25, ...), custom_call_target="tpu_custom_call" | custom-call | tf_op jit(solution)/shard_map/pallas_call | solution.py:282
  538.2 207.5 %shard_map.318 = (bf16[1024,1024]{1,0:T(8,128)(2,1)S(1)}, bf16[1024,1024]{1,0:T(8,128)(2,1)S(1)}, f32[432,128]{1,0:T(8,128)S(1)}) custom-call(bf16[1024,1024]{1,0:T(8,128)(2,1)} %add_convert_fusion.refs_0_, bf16[1024,1024]{1,0:T(8,128)(2,1)} %pad_maximum_fusion.13.refs_1_, bf16[1024,1024]{1,0:T(8,128)(2,1)} %pad_maximum_fusion.14.refs_2_, ...), custom_call_target="tpu_custom_call" | custom-call | tf_op jit(solution)/shard_map/pallas_call | solution.py:757
  (473 shorter events, 284.1 us)
Async XLA Ops:
  7.2 126.6 %all-gather.3.cloned.1.call-start = ((), (), s32[]{:S(2)}) async-start(), calls=%async_computation | async-start | bytes 4866048 | tf_op jit(solution)/shard_map/all_gather | solution.py:850
  18.6 15.3 %collective-permute-start.1 = (bf16[264,1024]{1,0:T(8,128)(2,1)S(1)}, bf16[264,1024]{1,0:T(8,128)(2,1)S(1)}, u32[]{:S(2)}, u32[]{:S(2)}) collective-permute-start(bf16[264,1024]{1,0:T(8,128)(2,1)S(1)} %pad_maximum_fusion.17), channel_id=1, source_target_pairs={{0,2},{1,3},{2,0},{3,1},{4,6},{5,7},{6,4},{7,5},{8,10},{9,11},{10,... | collective-permute-start | bytes 1622024 | tf_op jit(solution)/shard_map/ppermute | solution.py:803
  34.8 214.8 %all-gather.5.cloned.1.call-start = ((), (), s32[]{:S(2)}) async-start(), calls=%async_computation.1 | async-start | bytes 4866048 | tf_op jit(solution)/shard_map/all_gather | solution.py:850
  40.1 39.7 %collective-permute-start.2 = (bf16[1024,768]{1,0:T(8,128)(2,1)}, bf16[1024,768]{1,0:T(8,128)(2,1)}, u32[]{:S(2)}, u32[]{:S(2)}) collective-permute-start(bf16[1024,768]{1,0:T(8,128)(2,1)} %pad_maximum_fusion.15.refs_0_.refs_1_), channel_id=1, source_target_pairs={{0,2},{1,3},{2,0},{3,1},{4,6},{5,7},{6,4},{7,5},{8,10},{9,11},{10,... | collective-permute-start | bytes 4718600 | tf_op jit(solution)/shard_map/ppermute | solution.py:803
  43.8 34.2 %collective-permute-start = (bf16[512,1024]{1,0:T(8,128)(2,1)}, bf16[512,1024]{1,0:T(8,128)(2,1)}, u32[]{:S(2)}, u32[]{:S(2)}) collective-permute-start(bf16[512,1024]{1,0:T(8,128)(2,1)} %fusion.4), channel_id=1, source_target_pairs={{0,1},{1,0},{2,3},{3,2},{4,5},{5,4},{6,7},{7,6},{8,9},{9,8},{10,11... | collective-permute-start | bytes 3145736 | tf_op jit(solution)/shard_map/ppermute | solution.py:799
  43.8 32.7 %collective-permute-start.3 = (f32[2,17,128]{2,1,0:T(8,128)S(1)}, f32[2,17,128]{2,1,0:T(8,128)S(1)}, u32[]{:S(2)}, u32[]{:S(2)}) collective-permute-start(f32[2,17,128]{2,1,0:T(8,128)S(1)} %pad_maximum_fusion.21), channel_id=1, source_target_pairs={{0,2},{1,3},{2,0},{3,1},{4,6},{5,7},{6,4},{7,5},{8,10},{9,11},{10,... | collective-permute-start | bytes 52232 | tf_op jit(solution)/shard_map/ppermute | solution.py:803
  76.5 33.3 %collective-permute-start.5 = (bf16[256,1024]{1,0:T(8,128)(2,1)S(1)}, bf16[256,1024]{1,0:T(8,128)(2,1)S(1)}, u32[]{:S(2)}, u32[]{:S(2)}) collective-permute-start(bf16[256,1024]{1,0:T(8,128)(2,1)S(1)} %get-tuple-element.85.refs_5_), channel_id=1, source_target_pairs={{0,2},{1,3},{2,0},{3,1},{4,6},{5,7},{6,4},{7,5},{8,10},{9,11},{10,... | collective-permute-start | bytes 1572872 | tf_op jit(solution)/shard_map/ppermute | solution.py:803
  115.3 58.7 %collective-permute-start.8 = (bf16[1024,768]{1,0:T(8,128)(2,1)}, bf16[1024,768]{1,0:T(8,128)(2,1)}, u32[]{:S(2)}, u32[]{:S(2)}) collective-permute-start(bf16[1024,768]{1,0:T(8,128)(2,1)} %pad_maximum_fusion.16.refs_0_.refs_1_), channel_id=1, source_target_pairs={{0,2},{1,3},{2,0},{3,1},{4,6},{5,7},{6,4},{7,5},{8,10},{9,11},{10,... | collective-permute-start | bytes 4718600 | tf_op jit(solution)/shard_map/ppermute | solution.py:803
  130.0 632.3 %all-reduce.6.cloned.1.call-start = ((), (), s32[]{:S(2)}) async-start(), calls=%async_computation.2 | async-start | bytes 8650752 | tf_op jit(solution)/shard_map/psum | solution.py:967
  130.0 44.0 %collective-permute-start.9 = (bf16[256,1024]{1,0:T(8,128)(2,1)}, bf16[256,1024]{1,0:T(8,128)(2,1)S(1)}, u32[]{:S(2)}, u32[]{:S(2)}) collective-permute-start(bf16[256,1024]{1,0:T(8,128)(2,1)} %get-tuple-element.88.refs_5_), channel_id=1, source_target_pairs={{0,2},{1,3},{2,0},{3,1},{4,6},{5,7},{6,4},{7,5},{8,10},{9,11},{10,... | collective-permute-start | bytes 1572872 | tf_op jit(solution)/shard_map/ppermute | solution.py:803
  183.9 25.6 %collective-permute-start.12 = (bf16[512,1024]{1,0:T(8,128)(2,1)S(1)}, bf16[512,1024]{1,0:T(8,128)(2,1)}, u32[]{:S(2)}, u32[]{:S(2)}) collective-permute-start(bf16[512,1024]{1,0:T(8,128)(2,1)S(1)} %bitcast.189), channel_id=1, source_target_pairs={{0,2},{1,3},{2,0},{3,1},{4,6},{5,7},{6,4},{7,5},{8,10},{9,11},{10,... | collective-permute-start | bytes 3145736 | tf_op jit(solution)/shard_map/ppermute | solution.py:803
  249.0 44.2 %collective-permute-start.30 = (bf16[512,1024]{1,0:T(8,128)(2,1)}, bf16[512,1024]{1,0:T(8,128)(2,1)}, u32[]{:S(2)}, u32[]{:S(2)}) collective-permute-start(bf16[512,1024]{1,0:T(8,128)(2,1)} %multiply_convert_fusion.2), channel_id=1, source_target_pairs={{0,2},{1,3},{2,0},{3,1},{4,6},{5,7},{6,4},{7,5},{8,10},{9,11},{10,... | collective-permute-start | bytes 3145736 | tf_op jit(solution)/shard_map/ppermute | solution.py:803
  254.5 51.4 %collective-permute-start.33 = (bf16[512,1024]{1,0:T(8,128)(2,1)}, bf16[512,1024]{1,0:T(8,128)(2,1)}, u32[]{:S(2)}, u32[]{:S(2)}) collective-permute-start(bf16[512,1024]{1,0:T(8,128)(2,1)} %multiply_convert_fusion), channel_id=1, source_target_pairs={{0,2},{1,3},{2,0},{3,1},{4,6},{5,7},{6,4},{7,5},{8,10},{9,11},{10,... | collective-permute-start | bytes 3145736 | tf_op jit(solution)/shard_map/ppermute | solution.py:803
  287.8 18.3 %collective-permute-start.19 = (bf16[512,1024]{1,0:T(8,128)(2,1)}, bf16[512,1024]{1,0:T(8,128)(2,1)}, u32[]{:S(2)}, u32[]{:S(2)}) collective-permute-start(bf16[512,1024]{1,0:T(8,128)(2,1)} %shard_map.306), channel_id=1, source_target_pairs={{0,1},{1,0},{2,3},{3,2},{4,5},{5,4},{6,7},{7,6},{8,9},{9,8},{10,11... | collective-permute-start | bytes 3145736 | tf_op jit(solution)/shard_map/ppermute | solution.py:799
  292.2 15.9 %collective-permute-start.17 = (bf16[512,1024]{1,0:T(8,128)(2,1)}, bf16[512,1024]{1,0:T(8,128)(2,1)}, u32[]{:S(2)}, u32[]{:S(2)}) collective-permute-start(bf16[512,1024]{1,0:T(8,128)(2,1)} %shard_map.303), channel_id=1, source_target_pairs={{0,1},{1,0},{2,3},{3,2},{4,5},{5,4},{6,7},{7,6},{8,9},{9,8},{10,11... | collective-permute-start | bytes 3145736 | tf_op jit(solution)/shard_map/ppermute | solution.py:799
  293.2 19.4 %collective-permute-start.31 = (bf16[512,1024]{1,0:T(8,128)(2,1)}, bf16[512,1024]{1,0:T(8,128)(2,1)S(1)}, u32[]{:S(2)}, u32[]{:S(2)}) collective-permute-start(bf16[512,1024]{1,0:T(8,128)(2,1)} %collective-permute-done.30), channel_id=1, source_target_pairs={{0,1},{1,0},{2,3},{3,2},{4,5},{5,4},{6,7},{7,6},{8,9},{9,8},{10,11... | collective-permute-start | bytes 3145736 | tf_op jit(solution)/shard_map/ppermute | solution.py:799
  293.3 23.3 %collective-permute-start.35 = (bf16[512,1024]{1,0:T(8,128)(2,1)}, bf16[512,1024]{1,0:T(8,128)(2,1)S(1)}, u32[]{:S(2)}, u32[]{:S(2)}) collective-permute-start(bf16[512,1024]{1,0:T(8,128)(2,1)} %collective-permute-done.12), channel_id=1, source_target_pairs={{0,1},{1,0},{2,3},{3,2},{4,5},{5,4},{6,7},{7,6},{8,9},{9,8},{10,11... | collective-permute-start | bytes 3145736 | tf_op jit(solution)/shard_map/ppermute | solution.py:799
  312.3 22.4 %collective-permute-start.20 = (bf16[512,1024]{1,0:T(8,128)(2,1)S(1)}, bf16[512,1024]{1,0:T(8,128)(2,1)S(1)}, u32[]{:S(2)}, u32[]{:S(2)}) collective-permute-start(bf16[512,1024]{1,0:T(8,128)(2,1)S(1)} %get-tuple-element.204), channel_id=1, source_target_pairs={{0,1},{1,0},{2,3},{3,2},{4,5},{5,4},{6,7},{7,6},{8,9},{9,8},{10,11... | collective-permute-start | bytes 3145736 | tf_op jit(solution)/shard_map/ppermute | solution.py:799
  376.4 18.2 %collective-permute-start.22 = (bf16[512,1024]{1,0:T(8,128)(2,1)S(1)}, bf16[512,1024]{1,0:T(8,128)(2,1)}, u32[]{:S(2)}, u32[]{:S(2)}) collective-permute-start(bf16[512,1024]{1,0:T(8,128)(2,1)S(1)} %shard_map.310), channel_id=1, source_target_pairs={{0,1},{1,0},{2,3},{3,2},{4,5},{5,4},{6,7},{7,6},{8,9},{9,8},{10,11... | collective-permute-start | bytes 3145736 | tf_op jit(solution)/shard_map/ppermute | solution.py:799
  382.5 388.5 %all-reduce.8.cloned.1.call-start = ((), (), s32[]{:S(2)}) async-start(), calls=%async_computation.3 | async-start | bytes 8650752 | tf_op jit(solution)/shard_map/psum | solution.py:969
  406.5 31.6 %collective-permute-start.28 = (bf16[512,1024]{1,0:T(8,128)(2,1)}, bf16[512,1024]{1,0:T(8,128)(2,1)}, u32[]{:S(2)}, u32[]{:S(2)}) collective-permute-start(bf16[512,1024]{1,0:T(8,128)(2,1)} %get-tuple-element.202), channel_id=1, source_target_pairs={{0,2},{1,3},{2,0},{3,1},{4,6},{5,7},{6,4},{7,5},{8,10},{9,11},{10,... | collective-permute-start | bytes 3145736 | tf_op jit(solution)/shard_map/ppermute | solution.py:803
  438.1 74.8 %collective-permute-start.29 = (bf16[1024,1024]{1,0:T(8,128)(2,1)}, bf16[1024,1024]{1,0:T(8,128)(2,1)}, u32[]{:S(2)}, u32[]{:S(2)}) collective-permute-start(bf16[1024,1024]{1,0:T(8,128)(2,1)} %pad_maximum_fusion.12), channel_id=1, source_target_pairs={{0,2},{1,3},{2,0},{3,1},{4,6},{5,7},{6,4},{7,5},{8,10},{9,11},{10,... | collective-permute-start | bytes 6291464 | tf_op jit(solution)/shard_map/ppermute | solution.py:803
  444.2 31.1 %collective-permute-start.25 = (bf16[512,1024]{1,0:T(8,128)(2,1)S(1)}, bf16[512,1024]{1,0:T(8,128)(2,1)S(1)}, u32[]{:S(2)}, u32[]{:S(2)}) collective-permute-start(bf16[512,1024]{1,0:T(8,128)(2,1)S(1)} %get-tuple-element.200), channel_id=1, source_target_pairs={{0,1},{1,0},{2,3},{3,2},{4,5},{5,4},{6,7},{7,6},{8,9},{9,8},{10,11... | collective-permute-start | bytes 3145736 | tf_op jit(solution)/shard_map/ppermute | solution.py:799
  512.8 22.7 %collective-permute-start.27 = (bf16[512,1024]{1,0:T(8,128)(2,1)S(1)}, bf16[512,1024]{1,0:T(8,128)(2,1)}, u32[]{:S(2)}, u32[]{:S(2)}) collective-permute-start(bf16[512,1024]{1,0:T(8,128)(2,1)S(1)} %shard_map.317), channel_id=1, source_target_pairs={{0,1},{1,0},{2,3},{3,2},{4,5},{5,4},{6,7},{7,6},{8,9},{9,8},{10,11... | collective-permute-start | bytes 3145736 | tf_op jit(solution)/shard_map/ppermute | solution.py:799
  (137 other events, 838.9 us)
Sparse Core Ops, SparseCore 0:
  34.9 76.4 all-gather.2
  130.1 75.3 all-gather.4
  382.7 160.8 all-reduce.5
  547.7 212.0 all-reduce.7

commit v4 on v3

--- a/solution.py
+++ b/solution.py
@@ -11,6 +11,7 @@
 HEAD_COLS = 2 * HK + 2 * HV
 BLK = 128
 MID = BLK // 2 - 1
+SUB = 2
 epsilon = 1e-06
 highest = lax.Precision.HIGHEST
 VMEM_LIMIT = 48 * 1024 * 1024
@@ -78,14 +79,7 @@
     return jnp.dot(ranked, wdec_ref[...], precision=highest, preferred_element_type=f32) + bias_ref[...]
 
 
-def states_kernel(ndoc, meta, x_ref, wdec_ref, bias_ref, run_ref, state_ref, cum_ref, final_ref, state, cum):
-    block = pl.program_id(0)
-
-    @pl.when(block == 0)
-    def _():
-        state[...] = jnp.zeros_like(state)
-        cum[...] = jnp.ones_like(cum)
-
+def states_kernel(ndoc, block, meta, x_ref, wdec_ref, bias_ref, run_ref, state_ref, cum_ref, final_ref, state, cum):
     start = meta[ndoc] + block * BLK
     _, _, same, keep = block_masks(meta, ndoc, start)
     before = decay_before(x_ref, wdec_ref, bias_ref)
@@ -107,8 +101,7 @@
         final_ref[slot] = new.astype(bf16)
 
 
-def mix_kernel(ndoc, meta, x_ref, run_ref, state_ref, cum_ref, first_ref, gain_ref, gated_ref, mixed_ref):
-    block = pl.program_id(0)
+def mix_kernel(ndoc, block, meta, x_ref, run_ref, state_ref, cum_ref, first_ref, gain_ref, gated_ref, mixed_ref):
     start = meta[ndoc] + block * BLK
     allowed, carried, _, _ = block_masks(meta, ndoc, start)
     gain = gain_ref[...]
@@ -130,18 +123,10 @@
 
 
 def back_states_kernel(
-    ndoc, nblk, meta, x_ref, run_ref, mixed_ref, grad_ref, own_out_ref, far_out_ref, gain_ref,
+    ndoc, block, meta, x_ref, run_ref, mixed_ref, grad_ref, own_out_ref, far_out_ref, gain_ref,
     dmixed_ref, doutgate_ref, dstate_ref, cum_ref, final_ref, dgain_ref, state, cum,
 ):
-    step = pl.program_id(0)
-
-    @pl.when(step == 0)
-    def _():
-        state[...] = jnp.zeros_like(state)
-        cum[...] = jnp.ones_like(cum)
-        dgain_ref[...] = jnp.zeros_like(dgain_ref)
-
-    start = meta[ndoc] + (nblk - 1 - step) * BLK
+    start = meta[ndoc] + block * BLK
     _, carried, _, keep = block_masks(meta, ndoc, start)
     gain = gain_ref[...]
     running = run_ref[...]
@@ -175,16 +160,9 @@
 
 
 def back_kernel(
-    ndoc, meta, x_ref, run_ref, state_ref, cum_ref, first_ref, dmixed_ref, doutgate_ref,
+    ndoc, block, meta, x_ref, run_ref, state_ref, cum_ref, first_ref, dmixed_ref, doutgate_ref,
     dstate_ref, dcum_ref, dlast_ref, wdec_ref, bias_ref, dx_ref, dwdec_ref, dbias_ref,
 ):
-    block = pl.program_id(0)
-
-    @pl.when(block == 0)
-    def _():
-        dwdec_ref[...] = jnp.zeros_like(dwdec_ref)
-        dbias_ref[...] = jnp.zeros_like(dbias_ref)
-
     start = meta[ndoc] + block * BLK
     allowed, carried, same, keep = block_masks(meta, ndoc, start)
     last_row = lax.broadcasted_iota(jnp.int32, (BLK, HK), 0) == BLK - 1
@@ -250,40 +228,64 @@
     return pltpu.CompilerParams(dimension_semantics=("arbitrary",), vmem_limit_bytes=VMEM_LIMIT)
 
 
+def sub_blocks(kernel, ndoc, tokens, rows, blocks, reverse, starts):
+    steps = tokens // (BLK * SUB)
+
+    def body(meta, *refs):
+        step = pl.program_id(0)
+
+        @pl.when(step == 0)
+        def _():
+            for which, value in starts:
+                refs[which][...] = jnp.full_like(refs[which], value)
+
+        first = (steps - 1 - step if reverse else step) * SUB
+        for sub in reversed(range(SUB)) if reverse else range(SUB):
+            views = [
+                ref.at[sub * BLK : (sub + 1) * BLK] if i in rows
+                else ref.at[sub : sub + 1] if i in blocks
+                else ref
+                for i, ref in enumerate(refs)
+            ]
+            kernel(ndoc, first + sub, meta, *views)
+
+    return body
+
+
 class Mixer:
     def __init__(self, meta, ndoc, tokens):
         self.meta = meta
         self.ndoc = ndoc
         self.tokens = tokens
         self.nblk = tokens // BLK
-        self.half = self.nblk // 2
+        self.steps = self.nblk // SUB
 
     def rows(self, width, reverse=False):
-        nblk, half, core = self.nblk, self.half, self.ndoc + 1
+        steps, core = self.steps, self.ndoc + 1
 
         def place(step, meta):
-            time = nblk - 1 - step if reverse else step
-            return (lax.rem(time + meta[core] * half, nblk), 0)
-
-        return pl.BlockSpec((BLK, width), place)
+            time = steps - 1 - step if reverse else step
+            return (lax.rem(time + meta[core] * (steps // 2), steps), 0)
+
+        return pl.BlockSpec((BLK * SUB, width), place)
 
     def per_block(self, shape, reverse=False):
-        nblk = self.nblk
+        steps = self.steps
         zeros = (0,) * len(shape)
         return pl.BlockSpec(
-            (1,) + shape, lambda step, meta: ((nblk - 1 - step if reverse else step),) + zeros
+            (SUB,) + shape, lambda step, meta: ((steps - 1 - step if reverse else step),) + zeros
         )
 
     def whole(self, shape):
         zeros = (0,) * len(shape)
         return pl.BlockSpec(shape, lambda step, meta: zeros)
 
-    def call(self, body, in_specs, out_specs, out_shape, scratch, *args):
+    def call(self, kernel, layout, in_specs, out_specs, out_shape, scratch, *args):
         return pl.pallas_call(
-            body,
+            sub_blocks(kernel, self.ndoc, self.tokens, *layout),
             grid_spec=pltpu.PrefetchScalarGridSpec(
                 num_scalar_prefetch=1,
-                grid=(self.nblk,),
+                grid=(self.steps,),
                 in_specs=in_specs,
                 out_specs=out_specs,
                 scratch_shapes=scratch,
@@ -297,13 +299,10 @@
         return [pltpu.VMEM((2, HV, HK), f32), pltpu.VMEM((1, 2 * HK), f32)]
 
     def states(self, x, wdec, bias):
-        ndoc, n = self.ndoc, self.nblk
-
-        def body(*refs):
-            states_kernel(ndoc, *refs)
-
+        n = self.nblk
         return self.call(
-            body,
+            states_kernel,
+            ((0, 3), (4, 5), False, ((7, 0.0), (8, 1.0))),
             [self.rows(x.shape[1]), self.whole(wdec.shape), self.whole(bias.shape)],
             [
                 self.rows(2 * HK),
@@ -322,13 +321,9 @@
         )
 
     def mix(self, x, run, states, cum, first, gain):
-        ndoc = self.ndoc
-
-        def body(*refs):
-            mix_kernel(ndoc, *refs)
-
         return self.call(
-            body,
+            mix_kernel,
+            ((0, 1, 6, 7), (2, 3), False, ()),
             [
                 self.rows(x.shape[1]),
                 self.rows(2 * HK),
@@ -344,13 +339,10 @@
         )
 
     def back_states(self, x, run, mixed, grad, own_out, far_out, gain):
-        ndoc, n = self.ndoc, self.nblk
-
-        def body(*refs):
-            back_states_kernel(ndoc, n, *refs)
-
+        n = self.nblk
         return self.call(
-            body,
+            back_states_kernel,
+            ((0, 1, 2, 3, 7, 8), (9, 10), True, ((12, 0.0), (13, 0.0), (14, 1.0))),
             [
                 self.rows(x.shape[1], True),
                 self.rows(2 * HK, True),
@@ -381,14 +373,10 @@
         )
 
     def back(self, x, run, states, cum, first, dmixed, doutgate, dstates, dcum, dlast, wdec, bias):
-        ndoc = self.ndoc
         rank = wdec.shape[0]
-
-        def body(*refs):
-            back_kernel(ndoc, *refs)
-
         return self.call(
-            body,
+            back_kernel,
+            ((0, 1, 5, 6, 12), (2, 3, 7, 8), False, ((13, 0.0), (14, 0.0))),
             [
                 self.rows(x.shape[1]),
                 self.rows(2 * HK),
@@ -675,7 +663,7 @@
 
 
 def mix_sum_kernel(
-    n, done, own, far, misc, out_done, out_own, out_misc, came, total, slots,
+    n, done, own, far, misc, out_done, out_own, out_misc, came, total, done_slots, slots,
     send, recv, out_send, out_recv, chip_send, chip_recv, sums, misc_came, misc_send, misc_recv,
 ):
     me = ring_place(lax.axis_index("dp"), n)
@@ -714,8 +702,8 @@
         src_ref=far, dst_ref=came, send_sem=chip_send, recv_sem=chip_recv,
         device_id={"head": member ^ 2}, device_id_type=MESH,
     )
-    first = Ring(n, done, out_done, slots.at[0], [v.at[0] for v in (send, recv, out_send, out_recv)])
-    second = Ring(n, total, out_own, slots.at[1], [v.at[1] for v in (send, recv, out_send, out_recv)])
+    first = Ring(n, done, out_done, done_slots, [v.at[0] for v in (send, recv, out_send, out_recv)])
+    second = Ring(n, total, out_own, slots, [v.at[1] for v in (send, recv, out_send, out_recv)])
     middle, last = (n - 1) // 2, n - 1
     sums[0] = misc[...]
     small(0).start()
@@ -743,11 +731,16 @@
     steps_of(0, last, first.sent, second.sent)
 
 
-def mix_sum(done, own, far, misc, n):
+def mix_sum(parts, own, far, misc, n):
     if n == 1:
         misc = misc + core_swap(misc)
-        return done, (own.astype(f32) + chip_swap(far).astype(f32)).astype(bf16), misc + chip_swap(misc)
+        own = (own.astype(f32) + chip_swap(far).astype(f32)).astype(bf16)
+        return jnp.concatenate(parts, axis=0), own, misc + chip_swap(misc)
     rows, cols = own.shape
+    done_rows = sum(v.shape[0] for v in parts)
+    spare = -done_rows % (32 * n)
+    done_rows += spare
+    done = jnp.concatenate(list(parts) + ([jnp.zeros((spare, cols), bf16)] if spare else []), axis=0)
     swaps = 2 + n.bit_length() - 1
 
     def body(*refs):
@@ -758,11 +751,16 @@
         body,
         in_specs=[vmem] * 4,
         out_specs=[vmem] * 3,
-        out_shape=[jax.ShapeDtypeStruct((rows, cols), bf16)] * 2 + [jax.ShapeDtypeStruct(misc.shape, f32)],
+        out_shape=[
+            jax.ShapeDtypeStruct((done_rows, cols), bf16),
+            jax.ShapeDtypeStruct((rows, cols), bf16),
+        ]
+        + [jax.ShapeDtypeStruct(misc.shape, f32)],
         scratch_shapes=[
             pltpu.VMEM((rows, cols), bf16),
             pltpu.VMEM((rows, cols), bf16),
-            pltpu.VMEM((2, 2, n - 1, rows // (2 * n), cols), bf16),
+            pltpu.VMEM((2, n - 1, done_rows // (2 * n), cols), bf16),
+            pltpu.VMEM((2, n - 1, rows // (2 * n), cols), bf16),
         ]
         + [pltpu.SemaphoreType.DMA((2, 2, n - 1))] * 4
         + [pltpu.SemaphoreType.DMA] * 2
@@ -872,10 +870,10 @@
     for layer in range(LAYERS):
         hidden_in = hidden
         a = with_partner(norm_low(hidden, norm_one[layer]))
-        x = project(a if layer == 0 else after(a, g_y), ((mix_own, None), (mix_far, None), (rank_t, layer)))
+        x = project(a, ((mix_own, None), (mix_far, None), (rank_t, layer)))
         wdec, bias = small[layer, :rank], small[layer, rank:]
         run, states, cum, final = mixer.states(x, wdec, bias)
-        got = chip_swap(final)
+        got = chip_swap(after(final, next_part) if layer == 0 else after(final, g_y))
         first = got[::-1] * chip.astype(bf16)
         gain = group_gain[layer][None]
         gated, mixed = mixer.mix(x, run, states, cum, first, gain)
@@ -889,9 +887,11 @@
         )
         m_own = norm_low(hidden_mid, norm_two[layer])
         m = with_partner(m_own)
+        if layer + 1 < LAYERS:
+            m = after(m, next_mix)
         gate, up, product = ff_forward(m, (gate_t, layer), (up_t, layer), ff_far, ffp)
         if layer + 1 < LAYERS:
-            product = after(product, next_mix, next_out)
+            product = after(product, next_out)
         hidden = hidden_mid + settle(
             [(product, 0, (w_down, layer), False), (product, ffp, (ff_far, (2, ff)), False)]
         )
@@ -918,7 +918,8 @@
         if layer + 1 < LAYERS:
             g_own = grad.astype(bf16)
             g_y = chip_swap(g_own)
-            far_came = chip_swap(after(far, g_y))
+            mix_done = (own.astype(f32) + chip_swap(after(far, g_y)).astype(f32)).astype(bf16)
+            mix_done = lax.psum(mix_done, "dp", axis_index_groups=[dp_ring()])
         g = with_partner(g_own)
         g_all = jnp.concatenate([g, g_y, core_swap(g_y)], axis=0)
         dboth, dfar, product_all = ff_backward(g, gate, up, product, (w_down, layer), ff_far, ffp)
@@ -951,8 +952,6 @@
         )
         g_wmix = tn(a, dx[:, : 2 * HEAD_COLS]).astype(bf16)
         g_rank = tn(dx[:, 2 * HEAD_COLS :], a)
-        if layer + 1 < LAYERS:
-            done = (own.astype(f32) + after(far_came, dx).astype(f32)).astype(bf16)
         far = jnp.concatenate([g_wmix[:, HEAD_COLS:], g_wout[:, HV:]], axis=1)
         own = jnp.concatenate([g_wmix[:, :HEAD_COLS], g_wout[:, :HV]], axis=1)
         back_first, gain_one = norm_back(hidden_in, norm_one[layer], settle(
@@ -966,7 +965,7 @@
         if layer > 0:
             ff_grads[layer] = lax.psum((in_grad, down_grad), "dp")
         else:
-            ff_grads[layer] = [lax.psum(v, "dp", axis_index_groups=[dp_ring()]) for v in (in_grad, down_grad)]
+            ff_parts = (in_grad, down_grad)
             ff_grads[1] = after(ff_grads[1], grad)
         heads = jnp.concatenate([dwdec, dbias], axis=0)
         places = lax.iota(jnp.int32, 4)[:, None, None]
@@ -980,8 +979,9 @@
     misc = jnp.stack(misc_grads)
     length = misc.shape[1]
     misc = jnp.pad(misc.reshape(-1), (0, -misc.size % 1024)).reshape(-1, 128)
-    later_mix, first_mix, misc = mix_sum(done, own, far, misc, lax.axis_size("dp"))
-    mix_grads = [first_mix, later_mix]
+    ff_done, first_mix, misc = mix_sum(ff_parts, own, far, misc, lax.axis_size("dp"))
+    mix_grads = [first_mix, after(mix_done, grad)]
+    ff_grads[0] = (ff_done[: 2 * ff], ff_done[2 * ff : 3 * ff])
     misc = misc.reshape(-1)[: LAYERS * length].reshape(LAYERS, length)
     sizes = (rank * width, width, width, HV, 4 * (rank + 1) * HK)
     pieces, at = [], 0

time: 797 us -> 801 us (level)
  waiting for transfers between devices: 113 us -> 91.2 us
  local copies, waits for them, and re-layouts: 64.3 us -> 78.5 us
    ppermute x16, waiting for transfers between devices: 111 us -> 88.7 us  [chip_swap(): return lax.ppermute(value, 'head', [(i, i ^ 2) for i in range(4)])]
    pallas_call x1, Pallas kernels: 207 us -> 219 us  [mix_sum(): pl.pallas_call(body, in_specs=[vmem] * 4, out_specs=[vmem] * 3, out_shape...]
    unnamed x257 -> x263, local copies, waits for them, and re-layouts: 20.2 us -> 29.7 us
    pallas_call x8, Pallas kernels: 83.3 us -> 74.1 us  [call(): pl.pallas_call(sub_blocks(kernel, self.ndoc, self.tokens, *layout), grid_...]
  transfers between devices with their start and end apart: 40 -> 40, of which waited for: 10 -> 10; matrix products, arithmetic and copies ran while one was open for 21% -> 22% of each run, Pallas kernels for 51% -> 52%
where the time goes in v4:
time: 801 us; the launch traced here: 791 us
  Pallas kernels  440 us (55%)
  waiting for transfers between devices  91.2 us (11%)
  other arithmetic  90.7 us (11%)
  local copies, waits for them, and re-layouts  78.5 us (10%)
  matrix products  50.2 us (6%)
  starting transfers between devices  25.2 us (3%)
  between operations  15.6 us (2%)
    pallas_call x1, Pallas kernels, mix_sum(): pl.pallas_call(body, in_specs=[vmem] * 4, out_specs=[vmem] * 3, out_shape...  219 us
    pallas_call x24, Pallas kernels, local_call(): pl.pallas_call(body, grid=(grid,), in_specs=in_specs, out_specs=out_specs...  147 us
    ppermute x16, waiting for transfers between devices, chip_swap(): return lax.ppermute(value, 'head', [(i, i ^ 2) for i in range(4)])  88.7 us
    pallas_call x8, Pallas kernels, call(): pl.pallas_call(sub_blocks(kernel, self.ndoc, self.tokens, *layout), grid_...  74.1 us
    dot_general x10, matrix products, tn(): lax.dot_general(left, right, (((0,), (0,)), ((), ())), preferred_element_...  50.2 us
    unnamed x263, local copies, waits for them, and re-layouts  29.7 us
    ppermute x16, starting transfers between devices, chip_swap(): return lax.ppermute(value, 'head', [(i, i ^ 2) for i in range(4)])  20.9 us
  transfers between devices with their start and end apart: 40, of which 10 were waited for; matrix products, arithmetic and copies ran while one was open for 22% of the time, Pallas kernels for 52%

profile of v4, /device:TPU:0, one launch (start us, length us, event | category | flops | bytes accessed | tf_op | source)
XLA Modules:
  0.0 791.1 jit_solution(15546865954057285070)
XLA Ops:
  21.7 12.3 %collective-permute-done.1 = bf16[264,1024]{1,0:T(8,128)(2,1)S(1)} collective-permute-done((bf16[264,1024]{1,0:T(8,128)(2,1)S(1)}, bf16[264,1024]{1,0:T(8,128)(2,1)S(1)}, u32[]{:S(2)}, u32[]{:S(2)}) %collective-permute-start.1) | collective-permute-done | bytes 540704 | tf_op jit(solution)/shard_map/ppermute | solution.py:801
  47.8 27.8 %collective-permute-done.2.refs_1_.refs_2_ = bf16[1024,768]{1,0:T(8,128)(2,1)} collective-permute-done((bf16[1024,768]{1,0:T(8,128)(2,1)}, bf16[1024,768]{1,0:T(8,128)(2,1)}, u32[]{:S(2)}, u32[]{:S(2)}) %collective-permute-start.2) | collective-permute-done | bytes 1572896 | tf_op jit(solution)/shard_map/ppermute | solution.py:801
  79.5 7.8 shard_map.288.refs_0_
  87.4 8.0 %shard_map.289 = (f32[1024,256]{1,0:T(8,128)S(1)}, bf16[8,2,256,128]{3,2,1,0:T(8,128)(2,1)S(1)}, f32[8,1,256]{2,1,0:T(1,128)S(1)}, bf16[2,256,128]{2,1,0:T(8,128)(2,1)S(1)}) custom-call(s32[6]{0:T(128)S(1)} %pad_add_fusion.meta, f32[1024,1552]{1,0:T(8,128)} %shard_map.288.refs_0_, f32[16,256]{1,0:T(8,128)S(1)} %get-tuple-element.257.refs_1_.refs_10_, ...), custom_call_target="tpu_custom_call" | custom-call | tf_op jit(solution)/shard_map/pallas_call | solution.py:284
  126.8 26.2 %collective-permute-done.9.refs_1_.refs_2_ = bf16[1024,768]{1,0:T(8,128)(2,1)} collective-permute-done((bf16[1024,768]{1,0:T(8,128)(2,1)}, bf16[1024,768]{1,0:T(8,128)(2,1)}, u32[]{:S(2)}, u32[]{:S(2)}) %collective-permute-start.9) | collective-permute-done | bytes 1572896 | tf_op jit(solution)/shard_map/ppermute | solution.py:801
  158.1 10.9 %shard_map.293 = (bf16[1024,1536]{1,0:T(8,128)(2,1)}, bf16[1024,1536]{1,0:T(8,128)(2,1)}, bf16[1024,1536]{1,0:T(8,128)(2,1)}) custom-call(bf16[1024,1024]{1,0:T(8,128)(2,1)S(1)} %copy-done.10, bf16[2,704,1024]{2,1,0:T(8,128)(2,1)S(1)} %bitcast.152, bf16[2,704,1024]{2,1,0:T(8,128)(2,1)} %bitcast.157, bf16[2112,1024]{1,0:T(8,128)(2,1)} %bitcast.174, ...), custom_call_target="tpu_custom_call" | custom-call | tf_op jit(solution)/shard_map/pallas_call | solution.py:433
  181.3 7.9 shard_map.296.refs_0_
  189.2 8.0 %shard_map.297 = (f32[1024,256]{1,0:T(8,128)S(1)}, bf16[8,2,256,128]{3,2,1,0:T(8,128)(2,1)S(1)}, f32[8,1,256]{2,1,0:T(1,128)S(1)}, bf16[2,256,128]{2,1,0:T(8,128)(2,1)S(1)}) custom-call(s32[6]{0:T(128)S(1)} %pad_add_fusion.meta, f32[1024,1552]{1,0:T(8,128)} %shard_map.296.refs_0_, f32[16,256]{1,0:T(8,128)S(1)} %get-tuple-element.256.refs_1_.refs_10_, ...), custom_call_target="tpu_custom_call" | custom-call | tf_op jit(solution)/shard_map/pallas_call | solution.py:284
  234.8 11.0 %shard_map.301 = (bf16[1024,1536]{1,0:T(8,128)(2,1)}, bf16[1024,1536]{1,0:T(8,128)(2,1)}, bf16[1024,1536]{1,0:T(8,128)(2,1)}) custom-call(bf16[1024,1024]{1,0:T(8,128)(2,1)S(1)} %pad_maximum_fusion.6.m_ref, bf16[2,704,1024]{2,1,0:T(8,128)(2,1)S(1)} %bitcast.153, bf16[2,704,1024]{2,1,0:T(8,128)(2,1)} %bitcast.158, bf16[2112,1024]{1,0:T(8,128)(2,1)} %bitcast.181, ...), custom_call_target="tpu_custom_call" | custom-call | tf_op jit(solution)/shard_map/pallas_call | solution.py:433
  245.9 10.3 %shard_map.304 = (bf16[2048,1408]{1,0:T(8,128)(2,1)}, bf16[1024,1408]{1,0:T(8,128)(2,1)S(1)}, bf16[2048,704]{1,0:T(8,128)(2,1)}) custom-call(bf16[1024,1024]{1,0:T(8,128)(2,1)S(1)} %copy-done.19, bf16[1024,1536]{1,0:T(8,128)(2,1)} %get-tuple-element.103.gate_ref, bf16[1024,1536]{1,0:T(8,128)(2,1)} %get-tuple-element.104.up_ref, ...), custom_call_target="tpu_custom_call" | custom-call | tf_op jit(solution)/shard_map/pallas_call | solution.py:433
  256.2 8.5 %shard_map.306 = bf16[512,1024]{1,0:T(8,128)(2,1)} custom-call(bf16[2048,1408]{1,0:T(8,128)(2,1)} %get-tuple-element.105.refs_0_._, bf16[1024,1408]{1,0:T(8,128)(2,1)S(1)} %get-tuple-element.106.refs_1_, bf16[2,704,1024]{2,1,0:T(8,128)(2,1)} %bitcast.147, bf16[2,704,1024]{2,1,0:T(8,128)(2,1)} %bitcast.159, bf16[2112,1024]{1,0:T(8,128)(2,1)} %bitcast.184), custom_call_target="tpu_custom_call" | custom-call | tf_op jit(solution)/shard_map/pallas_call | solution.py:433
  304.5 9.1 %shard_map.320 = (bf16[2048,1408]{1,0:T(8,128)(2,1)}, bf16[2048,704]{1,0:T(8,128)(2,1)}) custom-call(bf16[2048,1024]{1,0:T(8,128)(2,1)} %pad_maximum_fusion.1.m_ref, bf16[2048,1024]{1,0:T(8,128)(2,1)} %pad_maximum_fusion.2.g_ref, bf16[2,704,1024]{2,1,0:T(8,128)(2,1)S(1)} %bitcast.154, ...), custom_call_target="tpu_custom_call", output_to_operand_aliasing={{0}: (5, {}), {1}: (6, {})} | custom-call | tf_op jit(solution)/shard_map/pallas_call | solution.py:433
  316.0 11.8 %shard_map.307 = (bf16[1024,512]{1,0:T(8,128)(2,1)S(1)}, bf16[1024,512]{1,0:T(8,128)(2,1)S(1)}, bf16[8,2,256,128]{3,2,1,0:T(8,128)(2,1)S(1)}, f32[8,1,256]{2,1,0...) custom-call(s32[6]{0:T(128)S(1)} %pad_add_fusion.meta, f32[1024,1552]{1,0:T(8,128)} %shard_map.296.refs_0_, ...), custom_call_target="tpu_custom_call" | custom-call | tf_op jit(solution)/shard_map/pallas_call | solution.py:284
  329.4 9.6 %convolution_convert_fusion = bf16[1408,1024]{1,0:T(8,128)(2,1)} fusion(bf16[2048,1408]{1,0:T(8,128)(2,1)S(1)} %bitcast.189, bf16[512,1024]{1,0:T(8,128)(2,1)S(1)} %copy-done.94, bf16[512,1024]{1,0:T(8,128)(2,1)} %collective-permute-done.33, bf16[512,1024]{1,0:T(8,128)(2,1)} %collective-permute-done.16, bf16[512,1024]{1,0:T(8,128)(2,1)} %multiply_convert_fusion), kind=kOutput, calls=%fused_computation.11 | convolution fusion | flops 5923799040 | bytes 12845056 | tf_op jit(solution)/shard_map/dot_general | solution.py:32
  339.0 11.6 %shard_map.308 = (bf16[1024,1552]{1,0:T(8,128)(2,1)}, f32[16,256]{1,0:T(8,128)S(1)}, f32[1,256]{1,0:T(1,128)S(1)}) custom-call(s32[6]{0:T(128)S(1)} %pad_add_fusion.meta, f32[1024,1552]{1,0:T(8,128)} %shard_map.296.refs_0_, f32[1024,256]{1,0:T(8,128)S(1)} %copy-done.18, bf16[8,2,256,128]{3,2,1,0:T(8,128)(2,1)S(1)} %copy-done.29, ...), custom_call_target="tpu_custom_call" | custom-call | tf_op jit(solution)/shard_map/pallas_call | solution.py:284
  388.1 10.2 %shard_map.311 = (bf16[2048,1408]{1,0:T(8,128)(2,1)}, bf16[1024,1408]{1,0:T(8,128)(2,1)S(1)}, bf16[2048,704]{1,0:T(8,128)(2,1)}) custom-call(bf16[1024,1024]{1,0:T(8,128)(2,1)S(1)} %pad_maximum_fusion.9.g_ref, bf16[1024,1536]{1,0:T(8,128)(2,1)} %get-tuple-element.114.gate_ref, bf16[1024,1536]{1,0:T(8,128)(2,1)} %get-tuple-element.115.up_ref, ...), custom_call_target="tpu_custom_call" | custom-call | tf_op jit(solution)/shard_map/pallas_call | solution.py:433
  398.3 7.5 shard_map.313
  427.9 9.5 %shard_map.318 = (bf16[2048,1408]{1,0:T(8,128)(2,1)}, bf16[2048,704]{1,0:T(8,128)(2,1)}) custom-call(bf16[2048,1024]{1,0:T(8,128)(2,1)} %constant_dynamic-update-slice_fusion.m_ref, bf16[2048,1024]{1,0:T(8,128)(2,1)} %pad_maximum_fusion.g_ref, bf16[2,704,1024]{2,1,0:T(8,128)(2,1)S(1)} %bitcast.155, ...), custom_call_target="tpu_custom_call", output_to_operand_aliasing={{0}: (5, {}), {1}: (6, {})} | custom-call | tf_op jit(solution)/shard_map/pallas_call | solution.py:433
  437.4 9.9 %convolution_convert_fusion.1 = bf16[1408,1024]{1,0:T(8,128)(2,1)S(1)} fusion(bf16[2048,1408]{1,0:T(8,128)(2,1)} %get-tuple-element.126, bf16[2048,1024]{1,0:T(8,128)(2,1)} %constant_dynamic-update-slice_fusion.m_ref), kind=kOutput, calls=%fused_computation.12 | convolution fusion | flops 5907021824 | bytes 12845056 | tf_op jit(solution)/shard_map/dot_general | solution.py:32
  456.6 7.9 %collective-permute-done.32 = bf16[1024,1024]{1,0:T(8,128)(2,1)S(1)} collective-permute-done((bf16[1024,1024]{1,0:T(8,128)(2,1)S(1)}, bf16[1024,1024]{1,0:T(8,128)(2,1)S(1)}, u32[]{:S(2)}, u32[]{:S(2)}) %collective-permute-start.32) | collective-permute-done | bytes 2097184 | tf_op jit(solution)/shard_map/ppermute | solution.py:801
  469.6 11.4 %shard_map.314 = (bf16[1024,512]{1,0:T(8,128)(2,1)S(1)}, bf16[1024,512]{1,0:T(8,128)(2,1)S(1)}, bf16[8,2,256,128]{3,2,1,0:T(8,128)(2,1)S(1)}, f32[8,1,256]{2,1,0...) custom-call(s32[6]{0:T(128)S(1)} %pad_add_fusion.meta, f32[1024,1552]{1,0:T(8,128)} %shard_map.288.refs_0_, ...), custom_call_target="tpu_custom_call" | custom-call | tf_op jit(solution)/shard_map/pallas_call | solution.py:284
  486.6 12.0 %shard_map.315 = (bf16[1024,1552]{1,0:T(8,128)(2,1)}, f32[16,256]{1,0:T(8,128)S(1)}, f32[1,256]{1,0:T(1,128)S(1)}) custom-call(s32[6]{0:T(128)S(1)} %pad_add_fusion.meta, f32[1024,1552]{1,0:T(8,128)} %shard_map.288.refs_0_, f32[1024,256]{1,0:T(8,128)S(1)} %copy-done.16, bf16[8,2,256,128]{3,2,1,0:T(8,128)(2,1)S(1)} %copy-done.27, ...), custom_call_target="tpu_custom_call" | custom-call | tf_op jit(solution)/shard_map/pallas_call | solution.py:284
  504.3 7.7 convolution_convert_fusion.3
  527.4 218.6 %shard_map.319 = (bf16[2304,1024]{1,0:T(8,128)(2,1)}, bf16[1024,1024]{1,0:T(8,128)(2,1)S(1)}, f32[432,128]{1,0:T(8,128)S(1)}) custom-call(bf16[2304,1024]{1,0:T(8,128)(2,1)} %maximum_maximum_fusion.refs_0_, bf16[1024,1024]{1,0:T(8,128)(2,1)S(1)} %copy-done.20, bf16[1024,1024]{1,0:T(8,128)(2,1)} %pad_maximum_fusion.12.refs_2_, ...), custom_call_target="tpu_custom_call" | custom-call | tf_op jit(solution)/shard_map/pallas_call | solution.py:750
  (482 shorter events, 299.9 us)
Async XLA Ops:
  7.2 145.8 %all-gather.3.cloned.1.call-start = ((), (), s32[]{:S(2)}) async-start(), calls=%async_computation | async-start | bytes 4866048 | tf_op jit(solution)/shard_map/all_gather | solution.py:848
  34.8 192.8 %all-gather.5.cloned.1.call-start = ((), (), s32[]{:S(2)}) async-start(), calls=%async_computation.1 | async-start | bytes 4866048 | tf_op jit(solution)/shard_map/all_gather | solution.py:848
  39.5 36.2 %collective-permute-start.2 = (bf16[1024,768]{1,0:T(8,128)(2,1)}, bf16[1024,768]{1,0:T(8,128)(2,1)}, u32[]{:S(2)}, u32[]{:S(2)}) collective-permute-start(bf16[1024,768]{1,0:T(8,128)(2,1)} %pad_maximum_fusion.14.refs_0_.refs_1_), channel_id=1, source_target_pairs={{0,2},{1,3},{2,0},{3,1},{4,6},{5,7},{6,4},{7,5},{8,10},{9,11},{10,... | collective-permute-start | bytes 4718600 | tf_op jit(solution)/shard_map/ppermute | solution.py:801
  43.4 34.4 %collective-permute-start = (bf16[512,1024]{1,0:T(8,128)(2,1)}, bf16[512,1024]{1,0:T(8,128)(2,1)}, u32[]{:S(2)}, u32[]{:S(2)}) collective-permute-start(bf16[512,1024]{1,0:T(8,128)(2,1)} %fusion.4), channel_id=1, source_target_pairs={{0,1},{1,0},{2,3},{3,2},{4,5},{5,4},{6,7},{7,6},{8,9},{9,8},{10,11... | collective-permute-start | bytes 3145736 | tf_op jit(solution)/shard_map/ppermute | solution.py:797
  43.4 33.6 %collective-permute-start.3 = (f32[2,17,128]{2,1,0:T(8,128)S(1)}, f32[2,17,128]{2,1,0:T(8,128)S(1)}, u32[]{:S(2)}, u32[]{:S(2)}) collective-permute-start(f32[2,17,128]{2,1,0:T(8,128)S(1)} %pad_maximum_fusion.20), channel_id=1, source_target_pairs={{0,2},{1,3},{2,0},{3,1},{4,6},{5,7},{6,4},{7,5},{8,10},{9,11},{10,... | collective-permute-start | bytes 52232 | tf_op jit(solution)/shard_map/ppermute | solution.py:801
  75.6 22.4 %collective-permute-start.4 = (bf16[264,1024]{1,0:T(8,128)(2,1)}, bf16[264,1024]{1,0:T(8,128)(2,1)}, u32[]{:S(2)}, u32[]{:S(2)}) collective-permute-start(bf16[264,1024]{1,0:T(8,128)(2,1)} %pad_maximum_fusion.17), channel_id=1, source_target_pairs={{0,2},{1,3},{2,0},{3,1},{4,6},{5,7},{6,4},{7,5},{8,10},{9,11},{10,... | collective-permute-start | bytes 1622024 | tf_op jit(solution)/shard_map/ppermute | solution.py:801
  77.1 35.2 %collective-permute-start.6 = (bf16[256,1024]{1,0:T(8,128)(2,1)}, bf16[256,1024]{1,0:T(8,128)(2,1)S(1)}, u32[]{:S(2)}, u32[]{:S(2)}) collective-permute-start(bf16[256,1024]{1,0:T(8,128)(2,1)} %get-tuple-element.89.refs_4_), channel_id=1, source_target_pairs={{0,2},{1,3},{2,0},{3,1},{4,6},{5,7},{6,4},{7,5},{8,10},{9,11},{10,... | collective-permute-start | bytes 1572872 | tf_op jit(solution)/shard_map/ppermute | solution.py:801
  115.4 37.7 %collective-permute-start.9 = (bf16[1024,768]{1,0:T(8,128)(2,1)}, bf16[1024,768]{1,0:T(8,128)(2,1)}, u32[]{:S(2)}, u32[]{:S(2)}) collective-permute-start(bf16[1024,768]{1,0:T(8,128)(2,1)} %pad_maximum_fusion.15.refs_0_.refs_1_), channel_id=1, source_target_pairs={{0,2},{1,3},{2,0},{3,1},{4,6},{5,7},{6,4},{7,5},{8,10},{9,11},{10,... | collective-permute-start | bytes 4718600 | tf_op jit(solution)/shard_map/ppermute | solution.py:801
  120.8 634.0 %all-reduce.7.cloned.1.call-start = ((), (), s32[]{:S(2)}) async-start(), calls=%async_computation.3 | async-start | bytes 8650752 | tf_op jit(solution)/shard_map/psum | solution.py:966
  121.0 48.0 %collective-permute-start.10 = (bf16[256,1024]{1,0:T(8,128)(2,1)}, bf16[256,1024]{1,0:T(8,128)(2,1)}, u32[]{:S(2)}, u32[]{:S(2)}) collective-permute-start(bf16[256,1024]{1,0:T(8,128)(2,1)} %get-tuple-element.93.refs_4_), channel_id=1, source_target_pairs={{0,2},{1,3},{2,0},{3,1},{4,6},{5,7},{6,4},{7,5},{8,10},{9,11},{10,... | collective-permute-start | bytes 1572872 | tf_op jit(solution)/shard_map/ppermute | solution.py:801
  178.9 25.4 %collective-permute-start.13 = (bf16[512,1024]{1,0:T(8,128)(2,1)S(1)}, bf16[512,1024]{1,0:T(8,128)(2,1)S(1)}, u32[]{:S(2)}, u32[]{:S(2)}) collective-permute-start(bf16[512,1024]{1,0:T(8,128)(2,1)S(1)} %bitcast.190), channel_id=1, source_target_pairs={{0,2},{1,3},{2,0},{3,1},{4,6},{5,7},{6,4},{7,5},{8,10},{9,11},{10,... | collective-permute-start | bytes 3145736 | tf_op jit(solution)/shard_map/ppermute | solution.py:801
  226.2 44.7 %collective-permute-start.28 = (bf16[512,1024]{1,0:T(8,128)(2,1)}, bf16[512,1024]{1,0:T(8,128)(2,1)}, u32[]{:S(2)}, u32[]{:S(2)}) collective-permute-start(bf16[512,1024]{1,0:T(8,128)(2,1)} %multiply_convert_fusion.2), channel_id=1, source_target_pairs={{0,2},{1,3},{2,0},{3,1},{4,6},{5,7},{6,4},{7,5},{8,10},{9,11},{10,... | collective-permute-start | bytes 3145736 | tf_op jit(solution)/shard_map/ppermute | solution.py:801
  232.5 51.0 %collective-permute-start.33 = (bf16[512,1024]{1,0:T(8,128)(2,1)}, bf16[512,1024]{1,0:T(8,128)(2,1)}, u32[]{:S(2)}, u32[]{:S(2)}) collective-permute-start(bf16[512,1024]{1,0:T(8,128)(2,1)} %multiply_convert_fusion), channel_id=1, source_target_pairs={{0,2},{1,3},{2,0},{3,1},{4,6},{5,7},{6,4},{7,5},{8,10},{9,11},{10,... | collective-permute-start | bytes 3145736 | tf_op jit(solution)/shard_map/ppermute | solution.py:801
  264.7 19.0 %collective-permute-start.19 = (bf16[512,1024]{1,0:T(8,128)(2,1)}, bf16[512,1024]{1,0:T(8,128)(2,1)}, u32[]{:S(2)}, u32[]{:S(2)}) collective-permute-start(bf16[512,1024]{1,0:T(8,128)(2,1)} %shard_map.306), channel_id=1, source_target_pairs={{0,1},{1,0},{2,3},{3,2},{4,5},{5,4},{6,7},{7,6},{8,9},{9,8},{10,11... | collective-permute-start | bytes 3145736 | tf_op jit(solution)/shard_map/ppermute | solution.py:797
  269.1 16.6 %collective-permute-start.17 = (bf16[512,1024]{1,0:T(8,128)(2,1)}, bf16[512,1024]{1,0:T(8,128)(2,1)}, u32[]{:S(2)}, u32[]{:S(2)}) collective-permute-start(bf16[512,1024]{1,0:T(8,128)(2,1)} %shard_map.303), channel_id=1, source_target_pairs={{0,1},{1,0},{2,3},{3,2},{4,5},{5,4},{6,7},{7,6},{8,9},{9,8},{10,11... | collective-permute-start | bytes 3145736 | tf_op jit(solution)/shard_map/ppermute | solution.py:797
  270.8 23.4 %collective-permute-start.29 = (bf16[512,1024]{1,0:T(8,128)(2,1)}, bf16[512,1024]{1,0:T(8,128)(2,1)S(1)}, u32[]{:S(2)}, u32[]{:S(2)}) collective-permute-start(bf16[512,1024]{1,0:T(8,128)(2,1)} %collective-permute-done.28), channel_id=1, source_target_pairs={{0,1},{1,0},{2,3},{3,2},{4,5},{5,4},{6,7},{7,6},{8,9},{9,8},{10,11... | collective-permute-start | bytes 3145736 | tf_op jit(solution)/shard_map/ppermute | solution.py:797
  270.9 24.4 %collective-permute-start.35 = (bf16[512,1024]{1,0:T(8,128)(2,1)}, bf16[512,1024]{1,0:T(8,128)(2,1)S(1)}, u32[]{:S(2)}, u32[]{:S(2)}) collective-permute-start(bf16[512,1024]{1,0:T(8,128)(2,1)} %copy-done.88), channel_id=1, source_target_pairs={{0,1},{1,0},{2,3},{3,2},{4,5},{5,4},{6,7},{7,6},{8,9},{9,8},{10,11... | collective-permute-start | bytes 3145736 | tf_op jit(solution)/shard_map/ppermute | solution.py:797
  290.0 23.6 %collective-permute-start.20 = (bf16[512,1024]{1,0:T(8,128)(2,1)S(1)}, bf16[512,1024]{1,0:T(8,128)(2,1)S(1)}, u32[]{:S(2)}, u32[]{:S(2)}) collective-permute-start(bf16[512,1024]{1,0:T(8,128)(2,1)S(1)} %get-tuple-element.206), channel_id=1, source_target_pairs={{0,1},{1,0},{2,3},{3,2},{4,5},{5,4},{6,7},{7,6},{8,9},{9,8},{10,11... | collective-permute-start | bytes 3145736 | tf_op jit(solution)/shard_map/ppermute | solution.py:797
  355.3 18.5 %collective-permute-start.22 = (bf16[512,1024]{1,0:T(8,128)(2,1)S(1)}, bf16[512,1024]{1,0:T(8,128)(2,1)}, u32[]{:S(2)}, u32[]{:S(2)}) collective-permute-start(bf16[512,1024]{1,0:T(8,128)(2,1)S(1)} %shard_map.310), channel_id=1, source_target_pairs={{0,1},{1,0},{2,3},{3,2},{4,5},{5,4},{6,7},{7,6},{8,9},{9,8},{10,11... | collective-permute-start | bytes 3145736 | tf_op jit(solution)/shard_map/ppermute | solution.py:797
  360.9 410.0 %all-reduce.5.cloned.1.call-start = ((), (), s32[]{:S(2)}) async-start(), calls=%async_computation.2 | async-start | bytes 4194304 | tf_op jit(solution)/shard_map/psum | solution.py:922
  385.8 30.7 %collective-permute-start.30 = (bf16[512,1024]{1,0:T(8,128)(2,1)}, bf16[512,1024]{1,0:T(8,128)(2,1)}, u32[]{:S(2)}, u32[]{:S(2)}) collective-permute-start(bf16[512,1024]{1,0:T(8,128)(2,1)} %get-tuple-element.204), channel_id=1, source_target_pairs={{0,2},{1,3},{2,0},{3,1},{4,6},{5,7},{6,4},{7,5},{8,10},{9,11},{10,... | collective-permute-start | bytes 3145736 | tf_op jit(solution)/shard_map/ppermute | solution.py:801
  416.6 48.0 %collective-permute-start.32 = (bf16[1024,1024]{1,0:T(8,128)(2,1)S(1)}, bf16[1024,1024]{1,0:T(8,128)(2,1)S(1)}, u32[]{:S(2)}, u32[]{:S(2)}) collective-permute-start(bf16[1024,1024]{1,0:T(8,128)(2,1)S(1)} %pad_maximum_fusion.13), channel_id=1, source_target_pairs={{0,2},{1,3},{2,0},{3,1},{4,6},{5,7},{6,4},{7,5},{8,10},{9,11},{10,... | collective-permute-start | bytes 6291464 | tf_op jit(solution)/shard_map/ppermute | solution.py:801
  423.6 43.1 %collective-permute-start.25 = (bf16[512,1024]{1,0:T(8,128)(2,1)S(1)}, bf16[512,1024]{1,0:T(8,128)(2,1)}, u32[]{:S(2)}, u32[]{:S(2)}) collective-permute-start(bf16[512,1024]{1,0:T(8,128)(2,1)S(1)} %get-tuple-element.202), channel_id=1, source_target_pairs={{0,1},{1,0},{2,3},{3,2},{4,5},{5,4},{6,7},{7,6},{8,9},{9,8},{10,11... | collective-permute-start | bytes 3145736 | tf_op jit(solution)/shard_map/ppermute | solution.py:797
  504.0 19.2 %collective-permute-start.27 = (bf16[512,1024]{1,0:T(8,128)(2,1)}, bf16[512,1024]{1,0:T(8,128)(2,1)}, u32[]{:S(2)}, u32[]{:S(2)}) collective-permute-start(bf16[512,1024]{1,0:T(8,128)(2,1)} %shard_map.317), channel_id=1, source_target_pairs={{0,1},{1,0},{2,3},{3,2},{4,5},{5,4},{6,7},{7,6},{8,9},{9,8},{10,11... | collective-permute-start | bytes 3145736 | tf_op jit(solution)/shard_map/ppermute | solution.py:797
  (139 other events, 1102.9 us)
Sparse Core Ops, SparseCore 0:
  34.9 76.4 all-gather.2
  120.9 75.4 all-gather.4
  361.1 160.0 all-reduce.6
  524.6 139.4 all-reduce.4

commit v5 on v4

--- a/solution.py
+++ b/solution.py
@@ -663,7 +663,7 @@
 
 
 def mix_sum_kernel(
-    n, done, own, far, misc, out_done, out_own, out_misc, came, total, done_slots, slots,
+    n, cuts, done, own, far, misc, out_done, out_own, out_misc, came, total, slot_a, slot_b, slot_c, slot_d,
     send, recv, out_send, out_recv, chip_send, chip_recv, sums, misc_came, misc_send, misc_recv,
 ):
     me = ring_place(lax.axis_index("dp"), n)
@@ -702,33 +702,52 @@
         src_ref=far, dst_ref=came, send_sem=chip_send, recv_sem=chip_recv,
         device_id={"head": member ^ 2}, device_id_type=MESH,
     )
-    first = Ring(n, done, out_done, done_slots, [v.at[0] for v in (send, recv, out_send, out_recv)])
-    second = Ring(n, total, out_own, slots, [v.at[1] for v in (send, recv, out_send, out_recv)])
+    def ring(which, data, out, cut, slots):
+        rows = slice(*cut)
+        sems = [v.at[which] for v in (send, recv, out_send, out_recv)]
+        return Ring(n, data.at[rows], out.at[rows], slots, sems)
+
+    rings = (
+        (0, done, out_done, cuts[0], slot_a),
+        (1, done, out_done, cuts[1], slot_b),
+        (2, total, out_own, cuts[2], slot_c),
+        (3, total, out_own, cuts[3], slot_d),
+    )
+    first, second = ([ring(*v) for v in pair if v[3][1] > v[3][0]] for pair in (rings[:2], rings[2:]))
+
+    def each(rings, name):
+        return [getattr(v, name) for v in rings]
+
+    def now(steps):
+        for step in steps:
+            step()
+
     middle, last = (n - 1) // 2, n - 1
     sums[0] = misc[...]
     small(0).start()
     swap.start()
-    first.start()
-    steps_of(0, middle, first.reduce)
+    now(each(first, "start"))
+    steps_of(0, middle, *each(first, "reduce"))
     small_step()
-    steps_of(middle, last, first.reduce)
-    first.turn()
+    steps_of(middle, last, *each(first, "reduce"))
+    now(each(first, "turn"))
     small_step()
     swap.wait()
     total[...] = (own[...].astype(f32) + came[...].astype(f32)).astype(bf16)
-    second.start()
-    steps_of(0, middle, first.gather, second.reduce)
+    now(each(second, "start"))
+    together = each(first, "gather") + each(second, "reduce")
+    steps_of(0, middle, *together)
     small_step()
-    steps_of(middle, last, first.gather, second.reduce)
-    second.turn()
+    steps_of(middle, last, *together)
+    now(each(second, "turn"))
     small_step()
-    steps_of(0, middle, second.gather)
+    steps_of(0, middle, *each(second, "gather"))
     small_step()
-    steps_of(middle, last, second.gather)
+    steps_of(middle, last, *each(second, "gather"))
     for _ in swaps:
         small_step()
     out_misc[...] = sums[len(swaps)]
-    steps_of(0, last, first.sent, second.sent)
+    steps_of(0, last, *each(first + second, "sent"))
 
 
 def mix_sum(parts, own, far, misc, n):
@@ -743,8 +762,15 @@
     done = jnp.concatenate(list(parts) + ([jnp.zeros((spare, cols), bf16)] if spare else []), axis=0)
     swaps = 2 + n.bit_length() - 1
 
+    def two(total):
+        lines = total // (32 * n)
+        cut = (lines + 1) // 2 * 32 * n
+        return (0, cut), (cut, total)
+
+    cuts = two(done_rows) + two(rows)
+
     def body(*refs):
-        mix_sum_kernel(n, *refs)
+        mix_sum_kernel(n, cuts, *refs)
 
     vmem = pl.BlockSpec(memory_space=pltpu.VMEM)
     return pl.pallas_call(
@@ -759,10 +785,11 @@
         scratch_shapes=[
             pltpu.VMEM((rows, cols), bf16),
             pltpu.VMEM((rows, cols), bf16),
-            pltpu.VMEM((2, n - 1, done_rows // (2 * n), cols), bf16),
-            pltpu.VMEM((2, n - 1, rows // (2 * n), cols), bf16),
         ]
-        + [pltpu.SemaphoreType.DMA((2, 2, n - 1))] * 4
+        + [
+            pltpu.VMEM((2, n - 1, max(16, (stop - at) // (2 * n)), cols), bf16) for at, stop in cuts
+        ]
+        + [pltpu.SemaphoreType.DMA((4, 2, n - 1))] * 4
         + [pltpu.SemaphoreType.DMA] * 2
         + [
             pltpu.VMEM((swaps + 1,) + misc.shape, f32),
@@ -802,8 +829,8 @@
 
 
 def dp_slice(own):
-    rows = own.shape[0] // lax.axis_size("dp")
-    return lax.dynamic_slice_in_dim(own, lax.axis_index("dp") * rows, rows, 0)
+    parts = own.reshape((lax.axis_size("dp"), -1) + own.shape[1:])
+    return lax.dynamic_index_in_dim(parts, lax.axis_index("dp"), 0, keepdims=False)
 
 
 def dp_ring():
@@ -873,7 +900,7 @@
         x = project(a, ((mix_own, None), (mix_far, None), (rank_t, layer)))
         wdec, bias = small[layer, :rank], small[layer, rank:]
         run, states, cum, final = mixer.states(x, wdec, bias)
-        got = chip_swap(after(final, next_part) if layer == 0 else after(final, g_y))
+        got = chip_swap(after(final, next_part) if layer == 0 else after(final, g_y, out_far))
         first = got[::-1] * chip.astype(bf16)
         gain = group_gain[layer][None]
         gated, mixed = mixer.mix(x, run, states, cum, first, gain)
@@ -887,18 +914,14 @@
         )
         m_own = norm_low(hidden_mid, norm_two[layer])
         m = with_partner(m_own)
-        if layer + 1 < LAYERS:
-            m = after(m, next_mix)
         gate, up, product = ff_forward(m, (gate_t, layer), (up_t, layer), ff_far, ffp)
         if layer + 1 < LAYERS:
-            product = after(product, next_out)
+            product = after(product, next_mix)
         hidden = hidden_mid + settle(
             [(product, 0, (w_down, layer), False), (product, ffp, (ff_far, (2, ff)), False)]
         )
-        m_y = chip_swap(m_own)
-        m_all = jnp.concatenate([m, m_y, core_swap(m_y)], axis=0)
         saved.append(
-            (hidden_in, hidden_mid, a, m_all, x, run, states, cum, first, mixed, gated, gate, up, product,
+            (hidden_in, hidden_mid, a, m_own, m, x, run, states, cum, first, mixed, gated, gate, up, product,
              mix_own, mix_far, out_far, ff_far)
         )
         if layer + 1 < LAYERS:
@@ -910,7 +933,7 @@
     ff_grads, misc_grads = [None] * LAYERS, [None] * LAYERS
     for layer in reversed(range(LAYERS)):
         (
-            hidden_in, hidden_mid, a, m_all, x, run, states, cum, first, mixed, gated, gate, up, product,
+            hidden_in, hidden_mid, a, m_own, m, x, run, states, cum, first, mixed, gated, gate, up, product,
             mix_own, mix_far, out_far, ff_far,
         ) = saved[layer]
         gain = group_gain[layer][None]
@@ -920,6 +943,8 @@
             g_y = chip_swap(g_own)
             mix_done = (own.astype(f32) + chip_swap(after(far, g_y)).astype(f32)).astype(bf16)
             mix_done = lax.psum(mix_done, "dp", axis_index_groups=[dp_ring()])
+        m_y = chip_swap(m_own if layer + 1 == LAYERS else after(m_own, dfar))
+        m_all = jnp.concatenate([m, m_y, core_swap(m_y)], axis=0)
         g = with_partner(g_own)
         g_all = jnp.concatenate([g, g_y, core_swap(g_y)], axis=0)
         dboth, dfar, product_all = ff_backward(g, gate, up, product, (w_down, layer), ff_far, ffp)
@@ -941,6 +966,8 @@
         down_grad = tn(product_all, g_all).astype(bf16)
         grad = grad + back_mid
         g_mix = with_partner(grad.astype(bf16))
+        if layer + 1 == LAYERS:
+            g_mix = after(g_mix, in_grad, down_grad)
         g_wout = tn(g_mix, gated).astype(bf16)
         dmixed, doutgate, dstates, dcum, dfinal, dgain = mixer.back_states(
             x, run, mixed, g_mix, w_out[layer], out_far, gain

time: 801 us -> 774 us (0.966)
  Pallas kernels: 440 us -> 408 us
    pallas_call x1, Pallas kernels: 219 us -> 192 us  [mix_sum(): pl.pallas_call(body, in_specs=[vmem] * 4, out_specs=[vmem] * 3, out_shape...]
    unnamed x263 -> x257, local copies, waits for them, and re-layouts: 29.7 us -> 31.5 us
  transfers between devices with their start and end apart: 40 -> 40, of which waited for: 10 -> 11; matrix products, arithmetic and copies ran while one was open for 22% -> 23% of each run, Pallas kernels for 52% -> 53%
where the time goes in v5:
time: 774 us; the launch traced here: 767 us
  Pallas kernels  408 us (53%)
  other arithmetic  95.2 us (12%)
  waiting for transfers between devices  91.7 us (12%)
  local copies, waits for them, and re-layouts  81.1 us (10%)
  matrix products  49.2 us (6%)
  starting transfers between devices  26.4 us (3%)
  between operations  15.5 us (2%)
    pallas_call x1, Pallas kernels, mix_sum(): pl.pallas_call(body, in_specs=[vmem] * 4, out_specs=[vmem] * 3, out_shape...  192 us
    pallas_call x24, Pallas kernels, local_call(): pl.pallas_call(body, grid=(grid,), in_specs=in_specs, out_specs=out_specs...  143 us
    ppermute x16, waiting for transfers between devices, chip_swap(): return lax.ppermute(value, 'head', [(i, i ^ 2) for i in range(4)])  86.8 us
    pallas_call x8, Pallas kernels, call(): pl.pallas_call(sub_blocks(kernel, self.ndoc, self.tokens, *layout), grid_...  73 us
    dot_general x10, matrix products, tn(): lax.dot_general(left, right, (((0,), (0,)), ((), ())), preferred_element_...  49.2 us
    unnamed x257, local copies, waits for them, and re-layouts  31.5 us
    ppermute x16, starting transfers between devices, chip_swap(): return lax.ppermute(value, 'head', [(i, i ^ 2) for i in range(4)])  20.7 us
    concatenate x8, other arithmetic, with_partner(): return jnp.concatenate([local, core_swap(local)], axis=0)  16 us
  transfers between devices with their start and end apart: 40, of which 11 were waited for; matrix products, arithmetic and copies ran while one was open for 23% of the time, Pallas kernels for 53%

profile of v5, /device:TPU:0, one launch (start us, length us, event | category | flops | bytes accessed | tf_op | source)
XLA Modules:
  0.0 766.6 jit_solution(6503758900264279920)
XLA Ops:
  21.7 12.3 %collective-permute-done.1 = bf16[264,1024]{1,0:T(8,128)(2,1)S(1)} collective-permute-done((bf16[264,1024]{1,0:T(8,128)(2,1)S(1)}, bf16[264,1024]{1,0:T(8,128)(2,1)S(1)}, u32[]{:S(2)}, u32[]{:S(2)}) %collective-permute-start.1) | collective-permute-done | bytes 540704 | tf_op jit(solution)/shard_map/ppermute | solution.py:828
  47.8 27.8 %collective-permute-done.2.refs_1_.refs_2_ = bf16[1024,768]{1,0:T(8,128)(2,1)} collective-permute-done((bf16[1024,768]{1,0:T(8,128)(2,1)}, bf16[1024,768]{1,0:T(8,128)(2,1)}, u32[]{:S(2)}, u32[]{:S(2)}) %collective-permute-start.2) | collective-permute-done | bytes 1572896 | tf_op jit(solution)/shard_map/ppermute | solution.py:828
  79.5 7.8 %shard_map.288.refs_0_ = f32[1024,1552]{1,0:T(8,128)} custom-call(bf16[1024,1024]{1,0:T(8,128)(2,1)S(1)} %pad_maximum_fusion.4.left, bf16[1024,768]{1,0:T(8,128)(2,1)} %pad_maximum_fusion.15.refs_0_.refs_1_, bf16[1024,768]{1,0:T(8,128)(2,1)} %collective-permute-done.2.refs_1_.refs_2_, bf16[2,16,1024]{2,1,0:T(8,128)(2,1)S(1)} %bitcast.171), custom_call_target="tpu_custom_call" | custom-call | tf_op jit(solution)/shard_map/pallas_call | solution.py:433
  87.3 8.0 %shard_map.289 = (f32[1024,256]{1,0:T(8,128)S(1)}, bf16[8,2,256,128]{3,2,1,0:T(8,128)(2,1)S(1)}, f32[8,1,256]{2,1,0:T(1,128)S(1)}, bf16[2,256,128]{2,1,0:T(8,128)(2,1)S(1)}) custom-call(s32[6]{0:T(128)S(1)} %pad_add_fusion.meta, f32[1024,1552]{1,0:T(8,128)} %shard_map.288.refs_0_, f32[16,256]{1,0:T(8,128)S(1)} %get-tuple-element.259.refs_1_.refs_10_, ...), custom_call_target="tpu_custom_call" | custom-call | tf_op jit(solution)/shard_map/pallas_call | solution.py:284
  132.1 11.0 %shard_map.293 = (bf16[1024,1536]{1,0:T(8,128)(2,1)}, bf16[1024,1536]{1,0:T(8,128)(2,1)}, bf16[1024,1536]{1,0:T(8,128)(2,1)}) custom-call(bf16[1024,1024]{1,0:T(8,128)(2,1)S(1)} %copy-done.17, bf16[2,704,1024]{2,1,0:T(8,128)(2,1)S(1)} %bitcast.158, bf16[2,704,1024]{2,1,0:T(8,128)(2,1)} %bitcast.163, bf16[2112,1024]{1,0:T(8,128)(2,1)} %bitcast.180, ...), custom_call_target="tpu_custom_call" | custom-call | tf_op jit(solution)/shard_map/pallas_call | solution.py:433
  143.1 8.8 %collective-permute-done.9.refs_1_.refs_2_ = bf16[1024,768]{1,0:T(8,128)(2,1)} collective-permute-done((bf16[1024,768]{1,0:T(8,128)(2,1)}, bf16[1024,768]{1,0:T(8,128)(2,1)}, u32[]{:S(2)}, u32[]{:S(2)}) %collective-permute-start.9) | collective-permute-done | bytes 1572896 | tf_op jit(solution)/shard_map/ppermute | solution.py:828
  164.0 7.8 %shard_map.296.refs_0_ = f32[1024,1552]{1,0:T(8,128)} custom-call(bf16[1024,1024]{1,0:T(8,128)(2,1)S(1)} %pad_maximum_fusion.6.left, bf16[1024,768]{1,0:T(8,128)(2,1)} %pad_maximum_fusion.16.refs_0_.refs_1_, bf16[1024,768]{1,0:T(8,128)(2,1)} %collective-permute-done.9.refs_1_.refs_2_, bf16[2,16,1024]{2,1,0:T(8,128)(2,1)S(1)} %bitcast.172), custom_call_target="tpu_custom_call" | custom-call | tf_op jit(solution)/shard_map/pallas_call | solution.py:433
  171.8 8.0 %shard_map.297 = (f32[1024,256]{1,0:T(8,128)S(1)}, bf16[8,2,256,128]{3,2,1,0:T(8,128)(2,1)S(1)}, f32[8,1,256]{2,1,0:T(1,128)S(1)}, bf16[2,256,128]{2,1,0:T(8,128)(2,1)S(1)}) custom-call(s32[6]{0:T(128)S(1)} %pad_add_fusion.meta, f32[1024,1552]{1,0:T(8,128)} %shard_map.296.refs_0_, f32[16,256]{1,0:T(8,128)S(1)} %get-tuple-element.258.refs_1_.refs_10_, ...), custom_call_target="tpu_custom_call" | custom-call | tf_op jit(solution)/shard_map/pallas_call | solution.py:284
  179.9 17.5 %collective-permute-done.13.refs_2_.refs_5_ = bf16[256,1024]{1,0:T(8,128)(2,1)S(1)} collective-permute-done((bf16[256,1024]{1,0:T(8,128)(2,1)S(1)}, bf16[256,1024]{1,0:T(8,128)(2,1)S(1)}, u32[]{:S(2)}, u32[]{:S(2)}) %collective-permute-start.13) | collective-permute-done | bytes 524320 | tf_op jit(solution)/shard_map/ppermute | solution.py:828
  229.3 11.0 %shard_map.301 = (bf16[1024,1536]{1,0:T(8,128)(2,1)}, bf16[1024,1536]{1,0:T(8,128)(2,1)}, bf16[1024,1536]{1,0:T(8,128)(2,1)}) custom-call(bf16[1024,1024]{1,0:T(8,128)(2,1)S(1)} %pad_maximum_fusion.7.m_ref, bf16[2,704,1024]{2,1,0:T(8,128)(2,1)S(1)} %bitcast.159, bf16[2,704,1024]{2,1,0:T(8,128)(2,1)} %bitcast.164, bf16[2112,1024]{1,0:T(8,128)(2,1)} %bitcast.187, ...), custom_call_target="tpu_custom_call" | custom-call | tf_op jit(solution)/shard_map/pallas_call | solution.py:433
  240.3 10.6 %shard_map.304 = (bf16[2048,1408]{1,0:T(8,128)(2,1)}, bf16[1024,1408]{1,0:T(8,128)(2,1)S(1)}, bf16[2048,704]{1,0:T(8,128)(2,1)}) custom-call(bf16[1024,1024]{1,0:T(8,128)(2,1)S(1)} %copy-done.15, bf16[1024,1536]{1,0:T(8,128)(2,1)} %get-tuple-element.103.gate_ref, bf16[1024,1536]{1,0:T(8,128)(2,1)} %get-tuple-element.104.up_ref, ...), custom_call_target="tpu_custom_call" | custom-call | tf_op jit(solution)/shard_map/pallas_call | solution.py:433
  285.9 9.2 %shard_map.307 = (bf16[2048,1408]{1,0:T(8,128)(2,1)}, bf16[2048,704]{1,0:T(8,128)(2,1)}) custom-call(bf16[2048,1024]{1,0:T(8,128)(2,1)} %pad_maximum_fusion.m_ref, bf16[2048,1024]{1,0:T(8,128)(2,1)} %pad_maximum_fusion.1.g_ref, bf16[2,704,1024]{2,1,0:T(8,128)(2,1)S(1)} %bitcast.160, ...), custom_call_target="tpu_custom_call", output_to_operand_aliasing={{0}: (5, {}), {1}: (6, {})} | custom-call | tf_op jit(solution)/shard_map/pallas_call | solution.py:433
  295.1 10.9 %convolution_convert_fusion.1 = bf16[1408,1024]{1,0:T(8,128)(2,1)} fusion(bf16[2048,1408]{1,0:T(8,128)(2,1)} %get-tuple-element.109, bf16[512,1024]{1,0:T(8,128)(2,1)S(1)} %collective-permute-done.22, bf16[512,1024]{1,0:T(8,128)(2,1)} %collective-permute-done.21, bf16[512,1024]{1,0:T(8,128)(2,1)} %collective-permute-done.16, ...), kind=kOutput, calls=%fused_computation.13 | convolution fusion | flops 5923799040 | bytes 12845056 | tf_op jit(solution)/shard_map/dot_general | solution.py:32
  316.5 11.1 %shard_map.308 = (bf16[1024,512]{1,0:T(8,128)(2,1)S(1)}, bf16[1024,512]{1,0:T(8,128)(2,1)S(1)}, bf16[8,2,256,128]{3,2,1,0:T(8,128)(2,1)S(1)}, f32[8,1,256]{2,1,0...) custom-call(s32[6]{0:T(128)S(1)} %pad_add_fusion.meta, f32[1024,1552]{1,0:T(8,128)} %shard_map.296.refs_0_, ...), custom_call_target="tpu_custom_call" | custom-call | tf_op jit(solution)/shard_map/pallas_call | solution.py:284
  340.0 11.9 %shard_map.309 = (bf16[1024,1552]{1,0:T(8,128)(2,1)}, f32[16,256]{1,0:T(8,128)S(1)}, f32[1,256]{1,0:T(1,128)S(1)}) custom-call(s32[6]{0:T(128)S(1)} %pad_add_fusion.meta, f32[1024,1552]{1,0:T(8,128)} %shard_map.296.refs_0_, f32[1024,256]{1,0:T(8,128)S(1)} %copy-done.14, bf16[8,2,256,128]{3,2,1,0:T(8,128)(2,1)S(1)} %copy-done.28, ...), custom_call_target="tpu_custom_call" | custom-call | tf_op jit(solution)/shard_map/pallas_call | solution.py:284
  384.0 10.1 %shard_map.312 = (bf16[2048,1408]{1,0:T(8,128)(2,1)}, bf16[1024,1408]{1,0:T(8,128)(2,1)S(1)}, bf16[2048,704]{1,0:T(8,128)(2,1)}) custom-call(bf16[1024,1024]{1,0:T(8,128)(2,1)S(1)} %pad_maximum_fusion.10.g_ref, bf16[1024,1536]{1,0:T(8,128)(2,1)} %get-tuple-element.118.gate_ref, bf16[1024,1536]{1,0:T(8,128)(2,1)} %get-tuple-element.119.up_ref, ...), custom_call_target="tpu_custom_call" | custom-call | tf_op jit(solution)/shard_map/pallas_call | solution.py:433
  394.2 7.6 shard_map.314
  426.8 9.3 %shard_map.319 = (bf16[2048,1408]{1,0:T(8,128)(2,1)}, bf16[2048,704]{1,0:T(8,128)(2,1)}) custom-call(bf16[2048,1024]{1,0:T(8,128)(2,1)} %pad_maximum_fusion.2.m_ref, bf16[2048,1024]{1,0:T(8,128)(2,1)} %pad_maximum_fusion.3.g_ref, bf16[2,704,1024]{2,1,0:T(8,128)(2,1)S(1)} %bitcast.161, ...), custom_call_target="tpu_custom_call", output_to_operand_aliasing={{0}: (5, {}), {1}: (6, {})} | custom-call | tf_op jit(solution)/shard_map/pallas_call | solution.py:433
  436.1 9.9 %convolution_convert_fusion = bf16[1408,1024]{1,0:T(8,128)(2,1)S(1)} fusion(bf16[2048,1408]{1,0:T(8,128)(2,1)} %get-tuple-element.131, bf16[512,1024]{1,0:T(8,128)(2,1)} %collective-permute-done.32, bf16[512,1024]{1,0:T(8,128)(2,1)} %collective-permute-done.31, bf16[512,1024]{1,0:T(8,128)(2,1)} %collective-permute-done.8, ...), kind=kOutput, calls=%fused_computation.12 | convolution fusion | flops 5923799040 | bytes 12845056 | tf_op jit(solution)/shard_map/dot_general | solution.py:32
  455.6 8.6 %collective-permute-done.35 = bf16[1024,1024]{1,0:T(8,128)(2,1)} collective-permute-done((bf16[1024,1024]{1,0:T(8,128)(2,1)}, bf16[1024,1024]{1,0:T(8,128)(2,1)}, u32[]{:S(2)}, u32[]{:S(2)}) %collective-permute-start.35) | collective-permute-done | bytes 2097184 | tf_op jit(solution)/shard_map/ppermute | solution.py:828
  470.5 11.2 %shard_map.315 = (bf16[1024,512]{1,0:T(8,128)(2,1)S(1)}, bf16[1024,512]{1,0:T(8,128)(2,1)S(1)}, bf16[8,2,256,128]{3,2,1,0:T(8,128)(2,1)S(1)}, f32[8,1,256]{2,1,0...) custom-call(s32[6]{0:T(128)S(1)} %pad_add_fusion.meta, f32[1024,1552]{1,0:T(8,128)} %shard_map.288.refs_0_, ...), custom_call_target="tpu_custom_call" | custom-call | tf_op jit(solution)/shard_map/pallas_call | solution.py:284
  486.7 11.7 %shard_map.316 = (bf16[1024,1552]{1,0:T(8,128)(2,1)}, f32[16,256]{1,0:T(8,128)S(1)}, f32[1,256]{1,0:T(1,128)S(1)}) custom-call(s32[6]{0:T(128)S(1)} %pad_add_fusion.meta, f32[1024,1552]{1,0:T(8,128)} %shard_map.288.refs_0_, f32[1024,256]{1,0:T(8,128)S(1)} %copy-done.12, bf16[8,2,256,128]{3,2,1,0:T(8,128)(2,1)S(1)} %copy-done.26, ...), custom_call_target="tpu_custom_call" | custom-call | tf_op jit(solution)/shard_map/pallas_call | solution.py:284
  506.3 7.7 %convolution_convert_fusion.3 = bf16[1024,1536]{1,0:T(8,128)(2,1)} fusion(bf16[1024,1552]{1,0:T(8,128)(2,1)} %get-tuple-element.128.refs_0_, bf16[512,1024]{1,0:T(8,128)(2,1)} %collective-permute-done, bf16[512,1024]{1,0:T(8,128)(2,1)} %fusion.4), kind=kOutput, calls=%fused_computation.15 | convolution fusion | flops 3226992640 | bytes 8388608 | tf_op jit(solution)/shard_map/dot_general | solution.py:32
  529.6 191.9 %shard_map.320 = (bf16[2304,1024]{1,0:T(8,128)(2,1)}, bf16[1024,1024]{1,0:T(8,128)(2,1)S(1)}, f32[432,128]{1,0:T(8,128)S(1)}) custom-call(bf16[2304,1024]{1,0:T(8,128)(2,1)} %maximum_maximum_fusion.refs_0_, bf16[1024,1024]{1,0:T(8,128)(2,1)S(1)} %copy-done.16, bf16[1024,1024]{1,0:T(8,128)(2,1)} %pad_maximum_fusion.13.refs_2_, ...), custom_call_target="tpu_custom_call" | custom-call | tf_op jit(solution)/shard_map/pallas_call | solution.py:776
  (475 shorter events, 309.7 us)
Async XLA Ops:
  7.2 119.7 %all-gather.3.cloned.1.call-start = ((), (), s32[]{:S(2)}) async-start(), calls=%async_computation | async-start | bytes 4866048 | tf_op jit(solution)/shard_map/all_gather | solution.py:875
  18.6 15.3 %collective-permute-start.1 = (bf16[264,1024]{1,0:T(8,128)(2,1)S(1)}, bf16[264,1024]{1,0:T(8,128)(2,1)S(1)}, u32[]{:S(2)}, u32[]{:S(2)}) collective-permute-start(bf16[264,1024]{1,0:T(8,128)(2,1)S(1)} %pad_maximum_fusion.17), channel_id=1, source_target_pairs={{0,2},{1,3},{2,0},{3,1},{4,6},{5,7},{6,4},{7,5},{8,10},{9,11},{10,... | collective-permute-start | bytes 1622024 | tf_op jit(solution)/shard_map/ppermute | solution.py:828
  34.8 186.3 %all-gather.5.cloned.1.call-start = ((), (), s32[]{:S(2)}) async-start(), calls=%async_computation.1 | async-start | bytes 4866048 | tf_op jit(solution)/shard_map/all_gather | solution.py:875
  39.4 36.2 %collective-permute-start.2 = (bf16[1024,768]{1,0:T(8,128)(2,1)}, bf16[1024,768]{1,0:T(8,128)(2,1)}, u32[]{:S(2)}, u32[]{:S(2)}) collective-permute-start(bf16[1024,768]{1,0:T(8,128)(2,1)} %pad_maximum_fusion.15.refs_0_.refs_1_), channel_id=1, source_target_pairs={{0,2},{1,3},{2,0},{3,1},{4,6},{5,7},{6,4},{7,5},{8,10},{9,11},{10,... | collective-permute-start | bytes 4718600 | tf_op jit(solution)/shard_map/ppermute | solution.py:828
  43.4 34.4 %collective-permute-start = (bf16[512,1024]{1,0:T(8,128)(2,1)}, bf16[512,1024]{1,0:T(8,128)(2,1)}, u32[]{:S(2)}, u32[]{:S(2)}) collective-permute-start(bf16[512,1024]{1,0:T(8,128)(2,1)} %fusion.4), channel_id=1, source_target_pairs={{0,1},{1,0},{2,3},{3,2},{4,5},{5,4},{6,7},{7,6},{8,9},{9,8},{10,11... | collective-permute-start | bytes 3145736 | tf_op jit(solution)/shard_map/ppermute | solution.py:824
  43.4 33.6 %collective-permute-start.3 = (f32[2,17,128]{2,1,0:T(8,128)S(1)}, f32[2,17,128]{2,1,0:T(8,128)S(1)}, u32[]{:S(2)}, u32[]{:S(2)}) collective-permute-start(f32[2,17,128]{2,1,0:T(8,128)S(1)} %pad_maximum_fusion.21), channel_id=1, source_target_pairs={{0,2},{1,3},{2,0},{3,1},{4,6},{5,7},{6,4},{7,5},{8,10},{9,11},{10,... | collective-permute-start | bytes 52232 | tf_op jit(solution)/shard_map/ppermute | solution.py:828
  75.6 22.4 %collective-permute-start.4 = (bf16[264,1024]{1,0:T(8,128)(2,1)}, bf16[264,1024]{1,0:T(8,128)(2,1)}, u32[]{:S(2)}, u32[]{:S(2)}) collective-permute-start(bf16[264,1024]{1,0:T(8,128)(2,1)} %pad_maximum_fusion.18), channel_id=1, source_target_pairs={{0,2},{1,3},{2,0},{3,1},{4,6},{5,7},{6,4},{7,5},{8,10},{9,11},{10,... | collective-permute-start | bytes 1622024 | tf_op jit(solution)/shard_map/ppermute | solution.py:828
  77.1 35.3 %collective-permute-start.6 = (bf16[256,1024]{1,0:T(8,128)(2,1)}, bf16[256,1024]{1,0:T(8,128)(2,1)S(1)}, u32[]{:S(2)}, u32[]{:S(2)}) collective-permute-start(bf16[256,1024]{1,0:T(8,128)(2,1)} %get-tuple-element.90.refs_4_), channel_id=1, source_target_pairs={{0,2},{1,3},{2,0},{3,1},{4,6},{5,7},{6,4},{7,5},{8,10},{9,11},{10,... | collective-permute-start | bytes 1572872 | tf_op jit(solution)/shard_map/ppermute | solution.py:828
  115.4 36.5 %collective-permute-start.9 = (bf16[1024,768]{1,0:T(8,128)(2,1)}, bf16[1024,768]{1,0:T(8,128)(2,1)}, u32[]{:S(2)}, u32[]{:S(2)}) collective-permute-start(bf16[1024,768]{1,0:T(8,128)(2,1)} %pad_maximum_fusion.16.refs_0_.refs_1_), channel_id=1, source_target_pairs={{0,2},{1,3},{2,0},{3,1},{4,6},{5,7},{6,4},{7,5},{8,10},{9,11},{10,... | collective-permute-start | bytes 4718600 | tf_op jit(solution)/shard_map/ppermute | solution.py:828
  120.9 609.4 %all-reduce.7.cloned.1.call-start = ((), (), s32[]{:S(2)}) async-start(), calls=%async_computation.3 | async-start | bytes 8650752 | tf_op jit(solution)/shard_map/psum | solution.py:993
  160.7 36.7 %collective-permute-start.12 = (bf16[512,1024]{1,0:T(8,128)(2,1)}, bf16[512,1024]{1,0:T(8,128)(2,1)}, u32[]{:S(2)}, u32[]{:S(2)}) collective-permute-start(bf16[512,1024]{1,0:T(8,128)(2,1)} %bitcast.40), channel_id=1, source_target_pairs={{0,2},{1,3},{2,0},{3,1},{4,6},{5,7},{6,4},{7,5},{8,10},{9,11},{10,... | collective-permute-start | bytes 3145736 | tf_op jit(solution)/shard_map/ppermute | solution.py:828
  162.2 35.2 %collective-permute-start.13 = (bf16[256,1024]{1,0:T(8,128)(2,1)S(1)}, bf16[256,1024]{1,0:T(8,128)(2,1)S(1)}, u32[]{:S(2)}, u32[]{:S(2)}) collective-permute-start(bf16[256,1024]{1,0:T(8,128)(2,1)S(1)} %copy-done.33), channel_id=1, source_target_pairs={{0,2},{1,3},{2,0},{3,1},{4,6},{5,7},{6,4},{7,5},{8,10},{9,11},{10,... | collective-permute-start | bytes 1572872 | tf_op jit(solution)/shard_map/ppermute | solution.py:828
  216.9 45.1 %collective-permute-start.23 = (bf16[512,1024]{1,0:T(8,128)(2,1)}, bf16[512,1024]{1,0:T(8,128)(2,1)}, u32[]{:S(2)}, u32[]{:S(2)}) collective-permute-start(bf16[512,1024]{1,0:T(8,128)(2,1)} %collective-permute-done.12), channel_id=1, source_target_pairs={{0,1},{1,0},{2,3},{3,2},{4,5},{5,4},{6,7},{7,6},{8,9},{9,8},{10,11... | collective-permute-start | bytes 3145736 | tf_op jit(solution)/shard_map/ppermute | solution.py:824
  226.0 50.5 %collective-permute-start.21 = (bf16[512,1024]{1,0:T(8,128)(2,1)}, bf16[512,1024]{1,0:T(8,128)(2,1)}, u32[]{:S(2)}, u32[]{:S(2)}) collective-permute-start(bf16[512,1024]{1,0:T(8,128)(2,1)} %multiply_convert_fusion), channel_id=1, source_target_pairs={{0,2},{1,3},{2,0},{3,1},{4,6},{5,7},{6,4},{7,5},{8,10},{9,11},{10,... | collective-permute-start | bytes 3145736 | tf_op jit(solution)/shard_map/ppermute | solution.py:828
  257.7 18.8 %collective-permute-start.19 = (bf16[512,1024]{1,0:T(8,128)(2,1)S(1)}, bf16[512,1024]{1,0:T(8,128)(2,1)S(1)}, u32[]{:S(2)}, u32[]{:S(2)}) collective-permute-start(bf16[512,1024]{1,0:T(8,128)(2,1)S(1)} %shard_map.306), channel_id=1, source_target_pairs={{0,1},{1,0},{2,3},{3,2},{4,5},{5,4},{6,7},{7,6},{8,9},{9,8},{10,11... | collective-permute-start | bytes 3145736 | tf_op jit(solution)/shard_map/ppermute | solution.py:824
  261.5 15.7 %collective-permute-start.17 = (bf16[512,1024]{1,0:T(8,128)(2,1)S(1)}, bf16[512,1024]{1,0:T(8,128)(2,1)S(1)}, u32[]{:S(2)}, u32[]{:S(2)}) collective-permute-start(bf16[512,1024]{1,0:T(8,128)(2,1)S(1)} %shard_map.303), channel_id=1, source_target_pairs={{0,1},{1,0},{2,3},{3,2},{4,5},{5,4},{6,7},{7,6},{8,9},{9,8},{10,11... | collective-permute-start | bytes 3145736 | tf_op jit(solution)/shard_map/ppermute | solution.py:824
  276.0 30.0 %collective-permute-start.31 = (bf16[512,1024]{1,0:T(8,128)(2,1)}, bf16[512,1024]{1,0:T(8,128)(2,1)}, u32[]{:S(2)}, u32[]{:S(2)}) collective-permute-start(bf16[512,1024]{1,0:T(8,128)(2,1)} %multiply_convert_fusion.2), channel_id=1, source_target_pairs={{0,2},{1,3},{2,0},{3,1},{4,6},{5,7},{6,4},{7,5},{8,10},{9,11},{10,... | collective-permute-start | bytes 3145736 | tf_op jit(solution)/shard_map/ppermute | solution.py:828
  281.4 31.8 %collective-permute-start.20 = (bf16[512,1024]{1,0:T(8,128)(2,1)}, bf16[512,1024]{1,0:T(8,128)(2,1)}, u32[]{:S(2)}, u32[]{:S(2)}) collective-permute-start(bf16[512,1024]{1,0:T(8,128)(2,1)} %get-tuple-element.208), channel_id=1, source_target_pairs={{0,1},{1,0},{2,3},{3,2},{4,5},{5,4},{6,7},{7,6},{8,9},{9,8},{10,11... | collective-permute-start | bytes 3145736 | tf_op jit(solution)/shard_map/ppermute | solution.py:824
  306.0 53.0 %collective-permute-start.32 = (bf16[512,1024]{1,0:T(8,128)(2,1)}, bf16[512,1024]{1,0:T(8,128)(2,1)}, u32[]{:S(2)}, u32[]{:S(2)}) collective-permute-start(bf16[512,1024]{1,0:T(8,128)(2,1)} %collective-permute-done.31), channel_id=1, source_target_pairs={{0,1},{1,0},{2,3},{3,2},{4,5},{5,4},{6,7},{7,6},{8,9},{9,8},{10,11... | collective-permute-start | bytes 3145736 | tf_op jit(solution)/shard_map/ppermute | solution.py:824
  333.5 413.0 %all-reduce.5.cloned.1.call-start = ((), (), s32[]{:S(2)}) async-start(), calls=%async_computation.2 | async-start | bytes 4194304 | tf_op jit(solution)/shard_map/psum | solution.py:945
  380.5 35.6 %collective-permute-start.33 = (bf16[512,1024]{1,0:T(8,128)(2,1)}, bf16[512,1024]{1,0:T(8,128)(2,1)}, u32[]{:S(2)}, u32[]{:S(2)}) collective-permute-start(bf16[512,1024]{1,0:T(8,128)(2,1)} %get-tuple-element.206), channel_id=1, source_target_pairs={{0,2},{1,3},{2,0},{3,1},{4,6},{5,7},{6,4},{7,5},{8,10},{9,11},{10,... | collective-permute-start | bytes 3145736 | tf_op jit(solution)/shard_map/ppermute | solution.py:828
  416.1 48.1 %collective-permute-start.35 = (bf16[1024,1024]{1,0:T(8,128)(2,1)}, bf16[1024,1024]{1,0:T(8,128)(2,1)}, u32[]{:S(2)}, u32[]{:S(2)}) collective-permute-start(bf16[1024,1024]{1,0:T(8,128)(2,1)} %pad_maximum_fusion.14), channel_id=1, source_target_pairs={{0,2},{1,3},{2,0},{3,1},{4,6},{5,7},{6,4},{7,5},{8,10},{9,11},{10,... | collective-permute-start | bytes 6291464 | tf_op jit(solution)/shard_map/ppermute | solution.py:828
  422.2 45.8 %collective-permute-start.28 = (bf16[512,1024]{1,0:T(8,128)(2,1)S(1)}, bf16[512,1024]{1,0:T(8,128)(2,1)S(1)}, u32[]{:S(2)}, u32[]{:S(2)}) collective-permute-start(bf16[512,1024]{1,0:T(8,128)(2,1)S(1)} %get-tuple-element.204), channel_id=1, source_target_pairs={{0,1},{1,0},{2,3},{3,2},{4,5},{5,4},{6,7},{7,6},{8,9},{9,8},{10,11... | collective-permute-start | bytes 3145736 | tf_op jit(solution)/shard_map/ppermute | solution.py:824
  503.7 21.6 %collective-permute-start.30 = (bf16[512,1024]{1,0:T(8,128)(2,1)}, bf16[512,1024]{1,0:T(8,128)(2,1)}, u32[]{:S(2)}, u32[]{:S(2)}) collective-permute-start(bf16[512,1024]{1,0:T(8,128)(2,1)} %shard_map.318), channel_id=1, source_target_pairs={{0,1},{1,0},{2,3},{3,2},{4,5},{5,4},{6,7},{7,6},{8,9},{9,8},{10,11... | collective-permute-start | bytes 3145736 | tf_op jit(solution)/shard_map/ppermute | solution.py:824
  (137 other events, 914.7 us)
Sparse Core Ops, SparseCore 0:
  34.9 76.4 all-gather.2
  121.0 75.4 all-gather.4
  333.6 159.7 all-reduce.6
  496.9 118.3 all-reduce.4

commit v6 on v5

--- a/solution.py
+++ b/solution.py
@@ -429,14 +429,14 @@
 NO_COST = pl.CostEstimate(flops=0, bytes_accessed=0, transcendentals=0)
 
 
-def local_call(body, grid, in_specs, out_specs, out_shape, args, aliases=None):
+def local_call(body, grid, in_specs, out_specs, out_shape, args, scratch=()):
     return pl.pallas_call(
         body,
         grid=(grid,),
         in_specs=in_specs,
         out_specs=out_specs,
         out_shape=out_shape,
-        input_output_aliases=aliases or {},
+        scratch_shapes=list(scratch),
         cost_estimate=NO_COST,
         compiler_params=pltpu.CompilerParams(
             dimension_semantics=("arbitrary",), vmem_limit_bytes=VMEM_LIMIT
@@ -493,27 +493,48 @@
     )
 
 
-def ff_forward(m, gate_w, up_w, far, ffp):
+def piece_specs(pieces):
+    per = pieces[0].shape[0] // ROWS_BLK
+
+    def spec(which, piece):
+        return pl.BlockSpec(
+            (ROWS_BLK, piece.shape[1]), lambda i: (jnp.clip(i - which * per, 0, per - 1), 0)
+        )
+
+    return [spec(which, piece) for which, piece in enumerate(pieces)]
+
+
+def two_pieces(body, near, far):
+    step = pl.program_id(0)
+    half = pl.num_programs(0) // 2
+    pl.when(step < half)(lambda: body(near))
+    pl.when(step >= half)(lambda: body(far))
+
+
+def ff_forward(pieces, gate_w, up_w, far, ffp):
     ff = matrix_shape(gate_w)[0]
-
-    def body(m_ref, gate_w, up_w, far_gate, far_up, gate_ref, up_ref, product_ref):
-        m = m_ref[...]
-        for slot, (gate_t, up_t) in enumerate(((gate_w, up_w), (far_gate, far_up))):
-            gate, up = nt(m, gate_t[...]), nt(m, up_t[...])
-            at = slot * ffp
-            gate_ref[:, at : at + ff] = gate.astype(bf16)
-            up_ref[:, at : at + ff] = up.astype(bf16)
-            product_ref[:, at : at + ff] = (gate * jax.nn.sigmoid(gate) * up).astype(bf16)
-
-    shape = (m.shape[0], 2 * ffp)
+    rows = sum(v.shape[0] for v in pieces)
+
+    def body(near_ref, part_ref, gate_w, up_w, far_gate, far_up, gate_ref, up_ref, product_ref):
+        def work(m_ref):
+            m = m_ref[...]
+            for slot, (gate_t, up_t) in enumerate(((gate_w, up_w), (far_gate, far_up))):
+                gate, up = nt(m, gate_t[...]), nt(m, up_t[...])
+                at = slot * ffp
+                gate_ref[:, at : at + ff] = gate.astype(bf16)
+                up_ref[:, at : at + ff] = up.astype(bf16)
+                product_ref[:, at : at + ff] = (gate * jax.nn.sigmoid(gate) * up).astype(bf16)
+
+        two_pieces(work, near_ref, part_ref)
+
     parts = [gate_w, up_w, (far, (0, ff)), (far, (1, ff))]
     return local_call(
         body,
-        m.shape[0] // ROWS_BLK,
-        [row_spec(m)] + [matrix_spec(v) for v in parts],
+        rows // ROWS_BLK,
+        piece_specs(pieces) + [matrix_spec(v) for v in parts],
         [pl.BlockSpec((ROWS_BLK, 2 * ffp), lambda i: (i, 0))] * 3,
-        [jax.ShapeDtypeStruct(shape, bf16)] * 3,
-        [m] + [v[0] for v in parts],
+        [jax.ShapeDtypeStruct((rows, 2 * ffp), bf16)] * 3,
+        list(pieces) + [v[0] for v in parts],
     )
 
 
@@ -524,57 +545,89 @@
     return jnp.concatenate([dgate.astype(bf16), (dproduct * silu).astype(bf16)], axis=1), silu
 
 
-def ff_backward(g, gate, up, product, down_w, far, ffp):
+def ff_backward(pieces, gate, up, down_w, far, ffp):
     ff = matrix_shape(down_w)[0]
 
-    def body(g_ref, gate_ref, up_ref, product_ref, down_ref, far_ref, own_out, far_out, product_out):
-        g = g_ref[...]
-        for slot, (weight, out) in enumerate(((down_ref, own_out), (far_ref, far_out))):
-            cols = slice(slot * ffp, slot * ffp + ff)
-            out[...] = gate_pair(
-                gate_ref[:, cols].astype(f32), up_ref[:, cols].astype(f32), nt(g, weight[...])
-            )[0]
-        product_out[...] = product_ref[:, :ff]
-
-    rows = g.shape[0]
+    def body(near_ref, part_ref, gate_ref, up_ref, down_ref, far_ref, own_out, far_out):
+        def work(g_ref):
+            g = g_ref[...]
+            for slot, (weight, out) in enumerate(((down_ref, own_out), (far_ref, far_out))):
+                cols = slice(slot * ffp, slot * ffp + ff)
+                out[...] = gate_pair(
+                    gate_ref[:, cols].astype(f32), up_ref[:, cols].astype(f32), nt(g, weight[...])
+                )[0]
+
+        two_pieces(work, near_ref, part_ref)
+
+    rows = gate.shape[0]
     parts = [down_w, (far, (2, ff))]
     return local_call(
         body,
         rows // ROWS_BLK,
-        [row_spec(v) for v in (g, gate, up, product)] + [matrix_spec(v) for v in parts],
-        [
-            pl.BlockSpec((ROWS_BLK, 2 * ff), lambda i: (i, 0)),
-            pl.BlockSpec((ROWS_BLK, 2 * ff), lambda i: (i, 0)),
-            pl.BlockSpec((ROWS_BLK, ff), lambda i: (i, 0)),
-        ],
-        [
-            jax.ShapeDtypeStruct((2 * rows, 2 * ff), bf16),
-            jax.ShapeDtypeStruct((rows, 2 * ff), bf16),
-            jax.ShapeDtypeStruct((2 * rows, ff), bf16),
-        ],
-        [g, gate, up, product] + [v[0] for v in parts],
+        piece_specs(pieces) + [row_spec(gate), row_spec(up)] + [matrix_spec(v) for v in parts],
+        [pl.BlockSpec((ROWS_BLK, 2 * ff), lambda i: (i, 0))] * 2,
+        [jax.ShapeDtypeStruct((rows, 2 * ff), bf16)] * 2,
+        list(pieces) + [gate, up] + [v[0] for v in parts],
     )
 
 
-def ff_backward_far(m_all, g_all, dboth, product_all, gate_w, up_w, down_w):
-    def body(m_ref, g_ref, gate_t, up_t, down_ref, _, __, own_out, product_out):
-        gate, up = nt(m_ref[...], gate_t[...]), nt(m_ref[...], up_t[...])
-        value, silu = gate_pair(gate, up, nt(g_ref[...], down_ref[...]))
-        own_out[...] = value
-        product_out[...] = (silu * up).astype(bf16)
-
-    near = m_all.shape[0] // ROWS_BLK // 2
+def ff_weight_grads(m_pieces, g_pieces, dboth, product, gate_w, up_w, down_w, spare):
+    ff = matrix_shape(down_w)[0]
+    rows, width = m_pieces[0].shape
+
+    def body(m0, m1, m2, m3, g0, g1, g2, g3, both_ref, product_ref, gate_t, up_t, down_ref, out, total):
+        step = pl.program_id(0)
+
+        def add(both, product, m, g):
+            for at, left, right in ((0, both, m), (2 * ff, product, g)):
+                part = tn(left, right)
+                place = slice(at, at + left.shape[1])
+
+                @pl.when(step == 0)
+                def _():
+                    total[place] = part
+
+                @pl.when(step > 0)
+                def _():
+                    total[place] += part
+
+        def near(m_ref, g_ref):
+            add(both_ref[...], product_ref[:, :ff], m_ref[...], g_ref[...])
+
+        def far(m_ref, g_ref):
+            m, g = m_ref[...], g_ref[...]
+            gate, up = nt(m, gate_t[...]), nt(m, up_t[...])
+            both, silu = gate_pair(gate, up, nt(g, down_ref[...]))
+            add(both, (silu * up).astype(bf16), m, g)
+
+        for which, (work, m_ref, g_ref) in enumerate(
+            ((near, m0, g0), (near, m1, g1), (far, m2, g2), (far, m3, g3))
+        ):
+            pl.when(step == which)(lambda work=work, m_ref=m_ref, g_ref=g_ref: work(m_ref, g_ref))
+
+        @pl.when(step == 3)
+        def _():
+            out[: 3 * ff] = total[...].astype(bf16)
+            if spare:
+                out[3 * ff :] = jnp.zeros((spare, width), bf16)
+
     parts = [gate_w, up_w, down_w]
+    once = pl.Buffered(1)
+
+    def alone(spec):
+        return pl.BlockSpec(spec.block_shape, spec.index_map, pipeline_mode=once)
+
+    piece = pl.BlockSpec((rows, width), lambda i: (0, 0), pipeline_mode=once)
     return local_call(
         body,
-        near,
-        [row_spec(m_all, near), row_spec(g_all, near)]
-        + [matrix_spec(v) for v in parts]
-        + [pl.BlockSpec(memory_space=pl.ANY)] * 2,
-        [row_spec(dboth, near), row_spec(product_all, near)],
-        [jax.ShapeDtypeStruct(v.shape, bf16) for v in (dboth, product_all)],
-        [m_all, g_all] + [v[0] for v in parts] + [dboth, product_all],
-        {5: 0, 6: 1},
+        4,
+        [piece] * 8
+        + [pl.BlockSpec((rows, v.shape[1]), lambda i: (jnp.minimum(i, 1), 0)) for v in (dboth, product)]
+        + [alone(matrix_spec(v)) for v in parts],
+        pl.BlockSpec((3 * ff + spare, width), lambda i: (0, 0), pipeline_mode=once),
+        jax.ShapeDtypeStruct((3 * ff + spare, width), bf16),
+        list(m_pieces) + list(g_pieces) + [dboth, product] + [v[0] for v in parts],
+        scratch=[pltpu.VMEM((3 * ff, width), f32)],
     )
 
 
@@ -750,16 +803,13 @@
     steps_of(0, last, *each(first + second, "sent"))
 
 
-def mix_sum(parts, own, far, misc, n):
+def mix_sum(done, own, far, misc, n):
     if n == 1:
         misc = misc + core_swap(misc)
         own = (own.astype(f32) + chip_swap(far).astype(f32)).astype(bf16)
-        return jnp.concatenate(parts, axis=0), own, misc + chip_swap(misc)
+        return done, own, misc + chip_swap(misc)
     rows, cols = own.shape
-    done_rows = sum(v.shape[0] for v in parts)
-    spare = -done_rows % (32 * n)
-    done_rows += spare
-    done = jnp.concatenate(list(parts) + ([jnp.zeros((spare, cols), bf16)] if spare else []), axis=0)
+    done_rows = done.shape[0]
     swaps = 2 + n.bit_length() - 1
 
     def two(total):
@@ -884,12 +934,15 @@
 
     small = jnp.concatenate([w_decay.astype(f32), decay_bias[:, None, :]], axis=1)
     small = jnp.concatenate([small, chip_swap(small)], axis=2)
+    mix_own = mix_pack(0)
+    first_far = chip_swap(mix_own[:, : 2 * HK])
     ff_part = ff_slice(0, meta)
     ff_far = ff_gather(ff_part)
-    mix_own = mix_pack(0)
-    mix_far = chip_swap(after(mix_own, ff_part))
+    mix_far = (first_far, chip_swap(after(mix_own[:, 2 * HK :], ff_part)))
     out_far = chip_swap(after(w_out[0], ff_part))
-    next_part = ff_slice(1, mix_far)
+    next_part = ff_slice(1, mix_far[1])
+    next_own = mix_pack(1)
+    spare = -3 * ff % (32 * lax.axis_size("dp"))
 
     grad = grad_out[0].astype(f32)
     hidden = tokens[0].astype(f32)
@@ -897,43 +950,40 @@
     for layer in range(LAYERS):
         hidden_in = hidden
         a = with_partner(norm_low(hidden, norm_one[layer]))
-        x = project(a, ((mix_own, None), (mix_far, None), (rank_t, layer)))
+        x = project(a, ((mix_own, None),) + tuple((v, None) for v in mix_far) + ((rank_t, layer),))
         wdec, bias = small[layer, :rank], small[layer, rank:]
         run, states, cum, final = mixer.states(x, wdec, bias)
-        got = chip_swap(after(final, next_part) if layer == 0 else after(final, g_y, out_far))
+        got = chip_swap(after(final, next_part, next_own) if layer == 0 else after(final, out_far))
         first = got[::-1] * chip.astype(bf16)
         gain = group_gain[layer][None]
         gated, mixed = mixer.mix(x, run, states, cum, first, gain)
         if layer + 1 < LAYERS:
-            next_own = mix_pack(layer + 1)
-            next_mix = chip_swap(after(next_own, got))
+            next_mix = (chip_swap(after(next_own, got)),)
             next_out = chip_swap(after(w_out[layer + 1], got))
             next_far = ff_gather(next_part)
         hidden_mid = hidden + settle(
             [(gated, 0, (w_out, layer), False), (gated, HV, (out_far, None), False)]
         )
         m_own = norm_low(hidden_mid, norm_two[layer])
-        m = with_partner(m_own)
+        m = (m_own, core_swap(m_own))
         gate, up, product = ff_forward(m, (gate_t, layer), (up_t, layer), ff_far, ffp)
         if layer + 1 < LAYERS:
-            product = after(product, next_mix)
+            product = after(product, next_mix[0])
         hidden = hidden_mid + settle(
             [(product, 0, (w_down, layer), False), (product, ffp, (ff_far, (2, ff)), False)]
         )
         saved.append(
-            (hidden_in, hidden_mid, a, m_own, m, x, run, states, cum, first, mixed, gated, gate, up, product,
+            (hidden_in, hidden_mid, a, m, x, run, states, cum, first, mixed, gated, gate, up, product,
              mix_own, mix_far, out_far, ff_far)
         )
         if layer + 1 < LAYERS:
             mix_own, mix_far, out_far, ff_far = next_own, next_mix, next_out, next_far
-            g_own = grad_out[0]
-            g_y = chip_swap(after(g_own, next_mix))
     result = hidden.astype(bf16)[None]
 
     ff_grads, misc_grads = [None] * LAYERS, [None] * LAYERS
     for layer in reversed(range(LAYERS)):
         (
-            hidden_in, hidden_mid, a, m_own, m, x, run, states, cum, first, mixed, gated, gate, up, product,
+            hidden_in, hidden_mid, a, m, x, run, states, cum, first, mixed, gated, gate, up, product,
             mix_own, mix_far, out_far, ff_far,
         ) = saved[layer]
         gain = group_gain[layer][None]
@@ -941,13 +991,15 @@
         if layer + 1 < LAYERS:
             g_own = grad.astype(bf16)
             g_y = chip_swap(g_own)
+            m_y = chip_swap(after(m[0], dfar))
             mix_done = (own.astype(f32) + chip_swap(after(far, g_y)).astype(f32)).astype(bf16)
             mix_done = lax.psum(mix_done, "dp", axis_index_groups=[dp_ring()])
-        m_y = chip_swap(m_own if layer + 1 == LAYERS else after(m_own, dfar))
-        m_all = jnp.concatenate([m, m_y, core_swap(m_y)], axis=0)
-        g = with_partner(g_own)
-        g_all = jnp.concatenate([g, g_y, core_swap(g_y)], axis=0)
-        dboth, dfar, product_all = ff_backward(g, gate, up, product, (w_down, layer), ff_far, ffp)
+        else:
+            g_own = grad_out[0]
+            g_y = chip_swap(after(g_own, got))
+            m_y = chip_swap(after(m[0], g_y))
+        g = (g_own, core_swap(g_own))
+        dboth, dfar = ff_backward(g, gate, up, (w_down, layer), ff_far, ffp)
         back_mid, gain_two = norm_back(
             hidden_mid,
             norm_two[layer],
@@ -959,15 +1011,14 @@
                 ]
             ),
         )
-        dboth, product_all = ff_backward_far(
-            m_all, g_all, dboth, product_all, (gate_t, layer), (up_t, layer), (w_down, layer)
-        )
-        in_grad = tn(dboth, m_all).astype(bf16)
-        down_grad = tn(product_all, g_all).astype(bf16)
+        ff_grad = ff_weight_grads(
+            m + (m_y, core_swap(m_y)), g + (g_y, core_swap(g_y)), dboth, product,
+            (gate_t, layer), (up_t, layer), (w_down, layer), 0 if layer else spare,
+        )
         grad = grad + back_mid
         g_mix = with_partner(grad.astype(bf16))
         if layer + 1 == LAYERS:
-            g_mix = after(g_mix, in_grad, down_grad)
+            g_mix = after(g_mix, ff_grad)
         g_wout = tn(g_mix, gated).astype(bf16)
         dmixed, doutgate, dstates, dcum, dfinal, dgain = mixer.back_states(
             x, run, mixed, g_mix, w_out[layer], out_far, gain
@@ -981,18 +1032,21 @@
         g_rank = tn(dx[:, 2 * HEAD_COLS :], a)
         far = jnp.concatenate([g_wmix[:, HEAD_COLS:], g_wout[:, HV:]], axis=1)
         own = jnp.concatenate([g_wmix[:, :HEAD_COLS], g_wout[:, :HV]], axis=1)
+        far_terms, at = [], HEAD_COLS
+        for part in mix_far:
+            far_terms.append((dx, at, (part, None), True))
+            at += part.shape[1]
         back_first, gain_one = norm_back(hidden_in, norm_one[layer], settle(
             [
                 (dx, 0, (mix_own, None), True),
-                (dx, HEAD_COLS, (mix_far, None), True),
+                *far_terms,
                 (dx, 2 * HEAD_COLS, (rank_t, layer), False),
             ]
         ))
         grad = grad + back_first
         if layer > 0:
-            ff_grads[layer] = lax.psum((in_grad, down_grad), "dp")
+            ff_grads[layer] = lax.psum(ff_grad, "dp")
         else:
-            ff_parts = (in_grad, down_grad)
             ff_grads[1] = after(ff_grads[1], grad)
         heads = jnp.concatenate([dwdec, dbias], axis=0)
         places = lax.iota(jnp.int32, 4)[:, None, None]
@@ -1006,9 +1060,9 @@
     misc = jnp.stack(misc_grads)
     length = misc.shape[1]
     misc = jnp.pad(misc.reshape(-1), (0, -misc.size % 1024)).reshape(-1, 128)
-    ff_done, first_mix, misc = mix_sum(ff_parts, own, far, misc, lax.axis_size("dp"))
+    ff_done, first_mix, misc = mix_sum(ff_grad, own, far, misc, lax.axis_size("dp"))
     mix_grads = [first_mix, after(mix_done, grad)]
-    ff_grads[0] = (ff_done[: 2 * ff], ff_done[2 * ff : 3 * ff])
+    ff_grads[0] = ff_done
     misc = misc.reshape(-1)[: LAYERS * length].reshape(LAYERS, length)
     sizes = (rank * width, width, width, HV, 4 * (rank + 1) * HK)
     pieces, at = [], 0
@@ -1042,9 +1096,9 @@
         pieces[3],
         jnp.stack([g[:, HEAD_COLS:].T.astype(f32) for g in mix_grads]),
         pieces[2],
-        turned([g[0] for g in ff_grads], 0, ff),
-        turned([g[0] for g in ff_grads], ff, 2 * ff),
-        rows_of([g[1] for g in ff_grads], 0, ff),
+        turned(ff_grads, 0, ff),
+        turned(ff_grads, ff, 2 * ff),
+        rows_of(ff_grads, 2 * ff, 3 * ff),
     )
 
 

time: 774 us -> 792 us (1.023)
  Pallas kernels: 408 us -> 478 us
  matrix products: 49.2 us -> 19.4 us
  other arithmetic: 95.2 us -> 72.7 us
  waiting for transfers between devices: 91.7 us -> 99.9 us
    pallas_call x24, Pallas kernels: 143 us -> 181 us  [local_call(): pl.pallas_call(body, grid=(grid,), in_specs=in_specs, out_specs=out_specs...]
    pallas_call x1, Pallas kernels: 192 us -> 225 us  [mix_sum(): pl.pallas_call(body, in_specs=[vmem] * 4, out_specs=[vmem] * 3, out_shape...]
    dot_general x10 -> x6, matrix products: 49.2 us -> 19.4 us  [tn(): lax.dot_general(left, right, (((0,), (0,)), ((), ())), preferred_element_...]
    concatenate x5 -> x0, other arithmetic: 20 us -> none  [the longest x2 7.68 us: per_device(): m_all = jnp.concatenate([m, m_y, core_swap(m_y)], axis=0)]
    ppermute x16 -> x17, waiting for transfers between devices: 86.8 us -> 96.6 us  [chip_swap(): return lax.ppermute(value, 'head', [(i, i ^ 2) for i in range(4)])]
    concatenate x8 -> x4, other arithmetic: 16 us -> 8.03 us  [with_partner(): return jnp.concatenate([local, core_swap(local)], axis=0)]
    ppermute x16 -> x17, starting transfers between devices: 20.7 us -> 19.6 us  [chip_swap(): return lax.ppermute(value, 'head', [(i, i ^ 2) for i in range(4)])]
  transfers between devices with their start and end apart: 40 -> 41, of which waited for: 11 -> 13; matrix products, arithmetic and copies ran while one was open for 23% -> 14% of each run, Pallas kernels for 53% -> 58%
where the time goes in v6:
time: 792 us; the launch traced here: 785 us
  Pallas kernels  478 us (60%)
  waiting for transfers between devices  99.9 us (13%)
  local copies, waits for them, and re-layouts  75.5 us (10%)
  other arithmetic  72.7 us (9%)
  starting transfers between devices  23.4 us (3%)
  matrix products  19.4 us (2%)
  between operations  15.6 us (2%)
    pallas_call x1, Pallas kernels, mix_sum(): pl.pallas_call(body, in_specs=[vmem] * 4, out_specs=[vmem] * 3, out_shape...  225 us
    pallas_call x24, Pallas kernels, local_call(): pl.pallas_call(body, grid=(grid,), in_specs=in_specs, out_specs=out_specs...  181 us
    ppermute x17, waiting for transfers between devices, chip_swap(): return lax.ppermute(value, 'head', [(i, i ^ 2) for i in range(4)])  96.6 us
    pallas_call x8, Pallas kernels, call(): pl.pallas_call(sub_blocks(kernel, self.ndoc, self.tokens, *layout), grid_...  72.6 us
    unnamed x257, local copies, waits for them, and re-layouts  31.8 us
    ppermute x17, starting transfers between devices, chip_swap(): return lax.ppermute(value, 'head', [(i, i ^ 2) for i in range(4)])  19.6 us
    dot_general x6, matrix products, tn(): lax.dot_general(left, right, (((0,), (0,)), ((), ())), preferred_element_...  19.4 us
  transfers between devices with their start and end apart: 41, of which 13 were waited for; matrix products, arithmetic and copies ran while one was open for 14% of the time, Pallas kernels for 58%

profile of v6, /device:TPU:0, one launch (start us, length us, event | category | flops | bytes accessed | tf_op | source)
XLA Modules:
  0.0 784.8 jit_solution(17208521917504313488)
XLA Ops:
  21.7 12.3 %collective-permute-done.2 = bf16[264,1024]{1,0:T(8,128)(2,1)S(1)} collective-permute-done((bf16[264,1024]{1,0:T(8,128)(2,1)S(1)}, bf16[264,1024]{1,0:T(8,128)(2,1)S(1)}, u32[]{:S(2)}, u32[]{:S(2)}) %collective-permute-start.2) | collective-permute-done | bytes 540704 | tf_op jit(solution)/shard_map/ppermute | solution.py:878
  52.8 15.0 %collective-permute-done.3.refs_2_.refs_3_ = bf16[1024,512]{1,0:T(8,128)(2,1)} collective-permute-done((bf16[1024,512]{1,0:T(8,128)(2,1)}, bf16[1024,512]{1,0:T(8,128)(2,1)}, u32[]{:S(2)}, u32[]{:S(2)}) %collective-permute-start.3) | collective-permute-done | bytes 1048608 | tf_op jit(solution)/shard_map/ppermute | solution.py:878
  69.6 9.9 %collective-permute-done.4 = f32[2,17,128]{2,1,0:T(8,128)S(1)} collective-permute-done((f32[2,17,128]{2,1,0:T(8,128)S(1)}, f32[2,17,128]{2,1,0:T(8,128)S(1)}, u32[]{:S(2)}, u32[]{:S(2)}) %collective-permute-start.4) | collective-permute-done | bytes 17440 | tf_op jit(solution)/shard_map/ppermute | solution.py:878
  84.6 7.3 shard_map.288.refs_0_
  91.8 8.0 %shard_map.289 = (f32[1024,256]{1,0:T(8,128)S(1)}, bf16[8,2,256,128]{3,2,1,0:T(8,128)(2,1)S(1)}, f32[8,1,256]{2,1,0:T(1,128)S(1)}, bf16[2,256,128]{2,1,0:T(8,128)(2,1)S(1)}) custom-call(s32[6]{0:T(128)S(1)} %pad_add_fusion.meta, f32[1024,1552]{1,0:T(8,128)} %shard_map.288.refs_0_, f32[16,256]{1,0:T(8,128)S(1)} %get-tuple-element.246.refs_1_.refs_10_, ...), custom_call_target="tpu_custom_call" | custom-call | tf_op jit(solution)/shard_map/pallas_call | solution.py:284
  132.3 11.8 %shard_map.293 = (bf16[1024,1536]{1,0:T(8,128)(2,1)}, bf16[1024,1536]{1,0:T(8,128)(2,1)}, bf16[1024,1536]{1,0:T(8,128)(2,1)}) custom-call(bf16[512,1024]{1,0:T(8,128)(2,1)} %multiply_convert_fusion.2.near_ref.m0, bf16[512,1024]{1,0:T(8,128)(2,1)} %collective-permute-done.9.part_ref.m1, bf16[2,704,1024]{2,1,0:T(8,128)(2,1)S(1)} %bitcast.157, ...), custom_call_target="tpu_custom_call" | custom-call | tf_op jit(solution)/shard_map/pallas_call | solution.py:433
  144.1 11.7 %collective-permute-done.10.refs_1_.refs_2_ = bf16[1024,768]{1,0:T(8,128)(2,1)} collective-permute-done((bf16[1024,768]{1,0:T(8,128)(2,1)}, bf16[1024,768]{1,0:T(8,128)(2,1)}, u32[]{:S(2)}, u32[]{:S(2)}) %collective-permute-start.10) | collective-permute-done | bytes 1572896 | tf_op jit(solution)/shard_map/ppermute | solution.py:878
  168.2 7.3 shard_map.296.refs_0_
  175.5 8.0 %shard_map.297 = (f32[1024,256]{1,0:T(8,128)S(1)}, bf16[8,2,256,128]{3,2,1,0:T(8,128)(2,1)S(1)}, f32[8,1,256]{2,1,0:T(1,128)S(1)}, bf16[2,256,128]{2,1,0:T(8,128)(2,1)S(1)}) custom-call(s32[6]{0:T(128)S(1)} %pad_add_fusion.meta, f32[1024,1552]{1,0:T(8,128)} %shard_map.296.refs_0_, f32[16,256]{1,0:T(8,128)S(1)} %get-tuple-element.245.refs_1_.refs_10_, ...), custom_call_target="tpu_custom_call" | custom-call | tf_op jit(solution)/shard_map/pallas_call | solution.py:284
  207.1 14.9 %collective-permute-done.21.g2 = bf16[512,1024]{1,0:T(8,128)(2,1)} collective-permute-done((bf16[512,1024]{1,0:T(8,128)(2,1)}, bf16[512,1024]{1,0:T(8,128)(2,1)}, u32[]{:S(2)}, u32[]{:S(2)}) %collective-permute-start.21) | collective-permute-done | bytes 1048608 | tf_op jit(solution)/shard_map/ppermute | solution.py:878
  222.3 11.9 %shard_map.301 = (bf16[1024,1536]{1,0:T(8,128)(2,1)}, bf16[1024,1536]{1,0:T(8,128)(2,1)}, bf16[1024,1536]{1,0:T(8,128)(2,1)}) custom-call(bf16[512,1024]{1,0:T(8,128)(2,1)} %multiply_convert_fusion.near_ref.m0, bf16[512,1024]{1,0:T(8,128)(2,1)} %collective-permute-done.16.part_ref.m1, bf16[2,704,1024]{2,1,0:T(8,128)(2,1)S(1)} %bitcast.158, ...), custom_call_target="tpu_custom_call" | custom-call | tf_op jit(solution)/shard_map/pallas_call | solution.py:433
  234.2 9.7 %shard_map.304 = (bf16[1024,1408]{1,0:T(8,128)(2,1)S(1)}, bf16[1024,1408]{1,0:T(8,128)(2,1)}) custom-call(bf16[512,1024]{1,0:T(8,128)(2,1)} %bitcast.46.near_ref.g0, bf16[512,1024]{1,0:T(8,128)(2,1)} %collective-permute-done.18.part_ref.g1, bf16[1024,1536]{1,0:T(8,128)(2,1)} %get-tuple-element.96.gate_ref, bf16[1024,1536]{1,0:T(8,128)(2,1)} %get-tuple-element.97.up_ref, ...), custom_call_target="tpu_custom_call" | custom-call | tf_op jit(solution)/shard_map/pallas_call | solution.py:433
  243.9 7.7 shard_map.306
  272.7 28.4 %shard_map.307 = bf16[2112,1024]{1,0:T(8,128)(2,1)} custom-call(bf16[512,1024]{1,0:T(8,128)(2,1)} %multiply_convert_fusion.near_ref.m0, bf16[512,1024]{1,0:T(8,128)(2,1)} %collective-permute-done.16.part_ref.m1, bf16[512,1024]{1,0:T(8,128)(2,1)S(1)} %collective-permute-done.22.m2, bf16[512,1024]{1,0:T(8,128)(2,1)S(1)} %collective-permute-done.23.m3, ...), custom_call_target="tpu_custom_call" | custom-call | tf_op jit(solution)/shard_map/pallas_call | solution.py:433
  304.3 11.0 %shard_map.308 = (bf16[1024,512]{1,0:T(8,128)(2,1)S(1)}, bf16[1024,512]{1,0:T(8,128)(2,1)S(1)}, bf16[8,2,256,128]{3,2,1,0:T(8,128)(2,1)S(1)}, f32[8,1,256]{2,1,0...) custom-call(s32[6]{0:T(128)S(1)} %pad_add_fusion.meta, f32[1024,1552]{1,0:T(8,128)} %shard_map.296.refs_0_, ...), custom_call_target="tpu_custom_call" | custom-call | tf_op jit(solution)/shard_map/pallas_call | solution.py:284
  327.9 11.7 %shard_map.309 = (bf16[1024,1552]{1,0:T(8,128)(2,1)}, f32[16,256]{1,0:T(8,128)S(1)}, f32[1,256]{1,0:T(1,128)S(1)}) custom-call(s32[6]{0:T(128)S(1)} %pad_add_fusion.meta, f32[1024,1552]{1,0:T(8,128)} %shard_map.296.refs_0_, f32[1024,256]{1,0:T(8,128)S(1)} %copy-done.19, bf16[8,2,256,128]{3,2,1,0:T(8,128)(2,1)S(1)} %copy-done.32, ...), custom_call_target="tpu_custom_call" | custom-call | tf_op jit(solution)/shard_map/pallas_call | solution.py:284
  354.2 15.4 %collective-permute-done.32.m2 = bf16[512,1024]{1,0:T(8,128)(2,1)} collective-permute-done((bf16[512,1024]{1,0:T(8,128)(2,1)}, bf16[512,1024]{1,0:T(8,128)(2,1)}, u32[]{:S(2)}, u32[]{:S(2)}) %collective-permute-start.32) | collective-permute-done | bytes 1048608 | tf_op jit(solution)/shard_map/ppermute | solution.py:878
  377.7 9.8 %shard_map.312 = (bf16[1024,1408]{1,0:T(8,128)(2,1)S(1)}, bf16[1024,1408]{1,0:T(8,128)(2,1)}) custom-call(bf16[512,1024]{1,0:T(8,128)(2,1)} %get-tuple-element.192.near_ref.g0, bf16[512,1024]{1,0:T(8,128)(2,1)S(1)} %copy-done.34, bf16[1024,1536]{1,0:T(8,128)(2,1)} %get-tuple-element.110.gate_ref, bf16[1024,1536]{1,0:T(8,128)(2,1)} %get-tuple-element.111.up_ref, ...), custom_call_target="tpu_custom_call" | custom-call | tf_op jit(solution)/shard_map/pallas_call | solution.py:433
  387.5 8.6 %shard_map.314 = bf16[512,1024]{1,0:T(8,128)(2,1)} custom-call(bf16[1024,1408]{1,0:T(8,128)(2,1)S(1)} %get-tuple-element.112.refs_0_.both_ref, bf16[1024,1408]{1,0:T(8,128)(2,1)} %get-tuple-element.113.refs_1_, bf16[2,704,1024]{2,1,0:T(8,128)(2,1)} %bitcast.153, bf16[2,704,1024]{2,1,0:T(8,128)(2,1)} %bitcast.188, bf16[2112,1024]{1,0:T(8,128)(2,1)} %bitcast.173), custom_call_target="tpu_custom_call" | custom-call | tf_op jit(solution)/shard_map/pallas_call | solution.py:433
  419.5 29.2 %shard_map.319.refs_0_ = bf16[2304,1024]{1,0:T(8,128)(2,1)} custom-call(bf16[512,1024]{1,0:T(8,128)(2,1)} %multiply_convert_fusion.2.near_ref.m0, bf16[512,1024]{1,0:T(8,128)(2,1)} %collective-permute-done.9.part_ref.m1, bf16[512,1024]{1,0:T(8,128)(2,1)} %collective-permute-done.32.m2, bf16[512,1024]{1,0:T(8,128)(2,1)} %collective-permute-done.33.m3, ...), custom_call_target="tpu_custom_call" | custom-call | tf_op jit(solution)/shard_map/pallas_call | solution.py:433
  457.8 11.1 %shard_map.315 = (bf16[1024,512]{1,0:T(8,128)(2,1)S(1)}, bf16[1024,512]{1,0:T(8,128)(2,1)S(1)}, bf16[8,2,256,128]{3,2,1,0:T(8,128)(2,1)S(1)}, f32[8,1,256]{2,1,0...) custom-call(s32[6]{0:T(128)S(1)} %pad_add_fusion.meta, f32[1024,1552]{1,0:T(8,128)} %shard_map.288.refs_0_, ...), custom_call_target="tpu_custom_call" | custom-call | tf_op jit(solution)/shard_map/pallas_call | solution.py:284
  474.0 11.7 %shard_map.316 = (bf16[1024,1552]{1,0:T(8,128)(2,1)}, f32[16,256]{1,0:T(8,128)S(1)}, f32[1,256]{1,0:T(1,128)S(1)}) custom-call(s32[6]{0:T(128)S(1)} %pad_add_fusion.meta, f32[1024,1552]{1,0:T(8,128)} %shard_map.288.refs_0_, f32[1024,256]{1,0:T(8,128)S(1)} %copy-done.17, bf16[8,2,256,128]{3,2,1,0:T(8,128)(2,1)S(1)} %copy-done.30, ...), custom_call_target="tpu_custom_call" | custom-call | tf_op jit(solution)/shard_map/pallas_call | solution.py:284
  490.0 7.7 convolution_convert_fusion.1
  513.9 225.1 %shard_map.320 = (bf16[2304,1024]{1,0:T(8,128)(2,1)}, bf16[1024,1024]{1,0:T(8,128)(2,1)S(1)}, f32[432,128]{1,0:T(8,128)S(1)}) custom-call(bf16[2304,1024]{1,0:T(8,128)(2,1)} %shard_map.319.refs_0_, bf16[1024,1024]{1,0:T(8,128)(2,1)S(1)} %copy-done.20, bf16[1024,1024]{1,0:T(8,128)(2,1)} %pad_maximum_fusion.5.refs_2_, f32[432,128]{1,0:T(8,128)S(1)} %pad_bitcast_fusion.refs_3_), custom_call_target="tpu_custom_call" | custom-call | tf_op jit(solution)/shard_map/pallas_call | solution.py:826
  (466 shorter events, 264.1 us)
Async XLA Ops:
  7.2 120.0 %all-gather.3.cloned.1.call-start = ((), (), s32[]{:S(2)}) async-start(), calls=%async_computation | async-start | bytes 4866048 | tf_op jit(solution)/shard_map/all_gather | solution.py:925
  34.8 167.4 %all-gather.5.cloned.1.call-start = ((), (), s32[]{:S(2)}) async-start(), calls=%async_computation.1 | async-start | bytes 4866048 | tf_op jit(solution)/shard_map/all_gather | solution.py:925
  39.6 42.9 %collective-permute-start = (bf16[512,1024]{1,0:T(8,128)(2,1)}, bf16[512,1024]{1,0:T(8,128)(2,1)}, u32[]{:S(2)}, u32[]{:S(2)}) collective-permute-start(bf16[512,1024]{1,0:T(8,128)(2,1)} %fusion.4), channel_id=1, source_target_pairs={{0,1},{1,0},{2,3},{3,2},{4,5},{5,4},{6,7},{7,6},{8,9},{9,8},{10,11... | collective-permute-start | bytes 3145736 | tf_op jit(solution)/shard_map/ppermute | solution.py:874
  41.5 26.3 %collective-permute-start.3 = (bf16[1024,512]{1,0:T(8,128)(2,1)}, bf16[1024,512]{1,0:T(8,128)(2,1)}, u32[]{:S(2)}, u32[]{:S(2)}) collective-permute-start(bf16[1024,512]{1,0:T(8,128)(2,1)} %pad_maximum_fusion.9), channel_id=1, source_target_pairs={{0,2},{1,3},{2,0},{3,1},{4,6},{5,7},{6,4},{7,5},{8,10},{9,11},{10,... | collective-permute-start | bytes 3145736 | tf_op jit(solution)/shard_map/ppermute | solution.py:878
  44.1 40.2 %collective-permute-start.1 = (bf16[1024,256]{1,0:T(8,128)(2,1)}, bf16[1024,256]{1,0:T(8,128)(2,1)}, u32[]{:S(2)}, u32[]{:S(2)}) collective-permute-start(bf16[1024,256]{1,0:T(8,128)(2,1)} %pad_maximum_fusion.12), channel_id=1, source_target_pairs={{0,2},{1,3},{2,0},{3,1},{4,6},{5,7},{6,4},{7,5},{8,10},{9,11},{10,... | collective-permute-start | bytes 1572872 | tf_op jit(solution)/shard_map/ppermute | solution.py:878
  44.4 35.0 %collective-permute-start.4 = (f32[2,17,128]{2,1,0:T(8,128)S(1)}, f32[2,17,128]{2,1,0:T(8,128)S(1)}, u32[]{:S(2)}, u32[]{:S(2)}) collective-permute-start(f32[2,17,128]{2,1,0:T(8,128)S(1)} %pad_maximum_fusion.15), channel_id=1, source_target_pairs={{0,2},{1,3},{2,0},{3,1},{4,6},{5,7},{6,4},{7,5},{8,10},{9,11},{10,... | collective-permute-start | bytes 52232 | tf_op jit(solution)/shard_map/ppermute | solution.py:878
  67.8 34.7 %collective-permute-start.5 = (bf16[264,1024]{1,0:T(8,128)(2,1)}, bf16[264,1024]{1,0:T(8,128)(2,1)}, u32[]{:S(2)}, u32[]{:S(2)}) collective-permute-start(bf16[264,1024]{1,0:T(8,128)(2,1)} %pad_maximum_fusion.11), channel_id=1, source_target_pairs={{0,2},{1,3},{2,0},{3,1},{4,6},{5,7},{6,4},{7,5},{8,10},{9,11},{10,... | collective-permute-start | bytes 1622024 | tf_op jit(solution)/shard_map/ppermute | solution.py:878
  80.1 36.7 %collective-permute-start.7 = (bf16[256,1024]{1,0:T(8,128)(2,1)}, bf16[256,1024]{1,0:T(8,128)(2,1)S(1)}, u32[]{:S(2)}, u32[]{:S(2)}) collective-permute-start(bf16[256,1024]{1,0:T(8,128)(2,1)} %get-tuple-element.84.refs_4_), channel_id=1, source_target_pairs={{0,2},{1,3},{2,0},{3,1},{4,6},{5,7},{6,4},{7,5},{8,10},{9,11},{10,... | collective-permute-start | bytes 1572872 | tf_op jit(solution)/shard_map/ppermute | solution.py:878
  118.6 631.3 %all-reduce.6.cloned.1.call-start = ((), (), s32[]{:S(2)}) async-start(), calls=%async_computation.3 | async-start | bytes 8650752 | tf_op jit(solution)/shard_map/psum | solution.py:1048
  118.6 37.2 %collective-permute-start.10 = (bf16[1024,768]{1,0:T(8,128)(2,1)}, bf16[1024,768]{1,0:T(8,128)(2,1)}, u32[]{:S(2)}, u32[]{:S(2)}) collective-permute-start(bf16[1024,768]{1,0:T(8,128)(2,1)} %pad_maximum_fusion.8.refs_0_.refs_1_), channel_id=1, source_target_pairs={{0,2},{1,3},{2,0},{3,1},{4,6},{5,7},{6,4},{7,5},{8,10},{9,11},{10,... | collective-permute-start | bytes 4718600 | tf_op jit(solution)/shard_map/ppermute | solution.py:878
  165.1 18.4 %collective-permute-start.13 = (bf16[256,1024]{1,0:T(8,128)(2,1)S(1)}, bf16[256,1024]{1,0:T(8,128)(2,1)S(1)}, u32[]{:S(2)}, u32[]{:S(2)}) collective-permute-start(bf16[256,1024]{1,0:T(8,128)(2,1)S(1)} %copy-done.39), channel_id=1, source_target_pairs={{0,2},{1,3},{2,0},{3,1},{4,6},{5,7},{6,4},{7,5},{8,10},{9,11},{10,... | collective-permute-start | bytes 1572872 | tf_op jit(solution)/shard_map/ppermute | solution.py:878
  196.1 25.9 %collective-permute-start.21 = (bf16[512,1024]{1,0:T(8,128)(2,1)}, bf16[512,1024]{1,0:T(8,128)(2,1)}, u32[]{:S(2)}, u32[]{:S(2)}) collective-permute-start(bf16[512,1024]{1,0:T(8,128)(2,1)} %bitcast.46.near_ref.g0), channel_id=1, source_target_pairs={{0,2},{1,3},{2,0},{3,1},{4,6},{5,7},{6,4},{7,5},{8,10},{9,11},{10,... | collective-permute-start | bytes 3145736 | tf_op jit(solution)/shard_map/ppermute | solution.py:878
  201.7 20.6 %collective-permute-start.16 = (bf16[512,1024]{1,0:T(8,128)(2,1)}, bf16[512,1024]{1,0:T(8,128)(2,1)}, u32[]{:S(2)}, u32[]{:S(2)}) collective-permute-start(bf16[512,1024]{1,0:T(8,128)(2,1)} %multiply_convert_fusion.near_ref.m0), channel_id=1, source_target_pairs={{0,1},{1,0},{2,3},{3,2},{4,5},{5,4},{6,7},{7,6},{8,9},{9,8},{10,11... | collective-permute-start | bytes 3145736 | tf_op jit(solution)/shard_map/ppermute | solution.py:874
  201.8 32.4 %collective-permute-start.18 = (bf16[512,1024]{1,0:T(8,128)(2,1)}, bf16[512,1024]{1,0:T(8,128)(2,1)}, u32[]{:S(2)}, u32[]{:S(2)}) collective-permute-start(bf16[512,1024]{1,0:T(8,128)(2,1)} %bitcast.46.near_ref.g0), channel_id=1, source_target_pairs={{0,1},{1,0},{2,3},{3,2},{4,5},{5,4},{6,7},{7,6},{8,9},{9,8},{10,11... | collective-permute-start | bytes 3145736 | tf_op jit(solution)/shard_map/ppermute | solution.py:874
  222.0 44.4 %collective-permute-start.22 = (bf16[512,1024]{1,0:T(8,128)(2,1)}, bf16[512,1024]{1,0:T(8,128)(2,1)S(1)}, u32[]{:S(2)}, u32[]{:S(2)}) collective-permute-start(bf16[512,1024]{1,0:T(8,128)(2,1)} %multiply_convert_fusion.near_ref.m0), channel_id=1, source_target_pairs={{0,2},{1,3},{2,0},{3,1},{4,6},{5,7},{6,4},{7,5},{8,10},{9,11},{10,... | collective-permute-start | bytes 3145736 | tf_op jit(solution)/shard_map/ppermute | solution.py:878
  272.6 28.5 %collective-permute-start.20 = (bf16[512,1024]{1,0:T(8,128)(2,1)}, bf16[512,1024]{1,0:T(8,128)(2,1)}, u32[]{:S(2)}, u32[]{:S(2)}) collective-permute-start(bf16[512,1024]{1,0:T(8,128)(2,1)} %get-tuple-element.194), channel_id=1, source_target_pairs={{0,1},{1,0},{2,3},{3,2},{4,5},{5,4},{6,7},{7,6},{8,9},{9,8},{10,11... | collective-permute-start | bytes 3145736 | tf_op jit(solution)/shard_map/ppermute | solution.py:874
  343.7 25.9 %collective-permute-start.32 = (bf16[512,1024]{1,0:T(8,128)(2,1)}, bf16[512,1024]{1,0:T(8,128)(2,1)}, u32[]{:S(2)}, u32[]{:S(2)}) collective-permute-start(bf16[512,1024]{1,0:T(8,128)(2,1)} %multiply_convert_fusion.2.near_ref.m0), channel_id=1, source_target_pairs={{0,2},{1,3},{2,0},{3,1},{4,6},{5,7},{6,4},{7,5},{8,10},{9,11},{10,... | collective-permute-start | bytes 3145736 | tf_op jit(solution)/shard_map/ppermute | solution.py:878
  353.5 21.7 %collective-permute-start.27 = (bf16[512,1024]{1,0:T(8,128)(2,1)}, bf16[512,1024]{1,0:T(8,128)(2,1)S(1)}, u32[]{:S(2)}, u32[]{:S(2)}) collective-permute-start(bf16[512,1024]{1,0:T(8,128)(2,1)} %get-tuple-element.192.near_ref.g0), channel_id=1, source_target_pairs={{0,1},{1,0},{2,3},{3,2},{4,5},{5,4},{6,7},{7,6},{8,9},{9,8},{10,11... | collective-permute-start | bytes 3145736 | tf_op jit(solution)/shard_map/ppermute | solution.py:874
  369.6 48.9 %collective-permute-start.33 = (bf16[512,1024]{1,0:T(8,128)(2,1)}, bf16[512,1024]{1,0:T(8,128)(2,1)}, u32[]{:S(2)}, u32[]{:S(2)}) collective-permute-start(bf16[512,1024]{1,0:T(8,128)(2,1)} %collective-permute-done.32.m2), channel_id=1, source_target_pairs={{0,1},{1,0},{2,3},{3,2},{4,5},{5,4},{6,7},{7,6},{8,9},{9,8},{10,11... | collective-permute-start | bytes 3145736 | tf_op jit(solution)/shard_map/ppermute | solution.py:874
  369.6 395.0 %all-reduce.4.cloned.1.call-start = ((), (), s32[]{:S(2)}) async-start(), calls=%async_computation.2 | async-start | bytes 4194304 | tf_op jit(solution)/shard_map/psum | solution.py:996
  373.4 29.6 %collective-permute-start.34 = (bf16[512,1024]{1,0:T(8,128)(2,1)}, bf16[512,1024]{1,0:T(8,128)(2,1)S(1)}, u32[]{:S(2)}, u32[]{:S(2)}) collective-permute-start(bf16[512,1024]{1,0:T(8,128)(2,1)} %get-tuple-element.192.near_ref.g0), channel_id=1, source_target_pairs={{0,2},{1,3},{2,0},{3,1},{4,6},{5,7},{6,4},{7,5},{8,10},{9,11},{10,... | collective-permute-start | bytes 3145736 | tf_op jit(solution)/shard_map/ppermute | solution.py:878
  403.1 48.2 %collective-permute-start.36 = (bf16[1024,1024]{1,0:T(8,128)(2,1)}, bf16[1024,1024]{1,0:T(8,128)(2,1)}, u32[]{:S(2)}, u32[]{:S(2)}) collective-permute-start(bf16[1024,1024]{1,0:T(8,128)(2,1)} %pad_maximum_fusion.6), channel_id=1, source_target_pairs={{0,2},{1,3},{2,0},{3,1},{4,6},{5,7},{6,4},{7,5},{8,10},{9,11},{10,... | collective-permute-start | bytes 6291464 | tf_op jit(solution)/shard_map/ppermute | solution.py:878
  418.0 36.9 %collective-permute-start.29 = (bf16[512,1024]{1,0:T(8,128)(2,1)S(1)}, bf16[512,1024]{1,0:T(8,128)(2,1)}, u32[]{:S(2)}, u32[]{:S(2)}) collective-permute-start(bf16[512,1024]{1,0:T(8,128)(2,1)S(1)} %get-tuple-element.190), channel_id=1, source_target_pairs={{0,1},{1,0},{2,3},{3,2},{4,5},{5,4},{6,7},{7,6},{8,9},{9,8},{10,11... | collective-permute-start | bytes 3145736 | tf_op jit(solution)/shard_map/ppermute | solution.py:874
  489.7 19.9 %collective-permute-start.31 = (bf16[512,1024]{1,0:T(8,128)(2,1)S(1)}, bf16[512,1024]{1,0:T(8,128)(2,1)}, u32[]{:S(2)}, u32[]{:S(2)}) collective-permute-start(bf16[512,1024]{1,0:T(8,128)(2,1)S(1)} %shard_map.318), channel_id=1, source_target_pairs={{0,1},{1,0},{2,3},{3,2},{4,5},{5,4},{6,7},{7,6},{8,9},{9,8},{10,11... | collective-permute-start | bytes 3145736 | tf_op jit(solution)/shard_map/ppermute | solution.py:874
  (139 other events, 1228.7 us)
Sparse Core Ops, SparseCore 0:
  34.9 76.4 all-gather.2
  118.7 75.5 all-gather.4
  369.7 164.1 all-reduce.5
  537.4 156.6 all-reduce.3

commit v7 on v6

--- a/solution.py
+++ b/solution.py
@@ -631,6 +631,56 @@
     )
 
 
+def weight_outputs(mix_grads, ff_grads, ff):
+    rows, cols = mix_grads[0].shape
+    steps = 4
+    high, flat = rows // steps, ff // steps
+    widths = (HK, HK, HV, HV)
+
+    def body(*refs):
+        ins, outs = refs[: 4 * LAYERS], refs[4 * LAYERS :]
+
+        def work(mix, *parts):
+            at = 0
+            for ref, width in zip(outs, widths):
+                ref[0] = mix[:, at : at + width].astype(f32)
+                at += width
+            outs[4][0] = mix[:, at : at + HV].astype(f32).T
+            for ref, part in zip(outs[5:], parts):
+                ref[0] = part[...].astype(f32)
+
+        for layer in range(LAYERS):
+            mine = ins[4 * layer : 4 * layer + 4]
+            pl.when(pl.program_id(0) == layer)(lambda mine=mine: work(*mine))
+
+    def spec(layer, height, first):
+        def place(now, step):
+            held = jnp.where(now < layer, 0, steps - 1)
+            return (first + jnp.where(now == layer, step, held), 0)
+
+        return pl.BlockSpec((height, cols), place)
+
+    in_specs, args = [], []
+    for layer in range(LAYERS):
+        in_specs += [spec(layer, high, 0)] + [spec(layer, flat, part * steps) for part in range(3)]
+        args += [mix_grads[layer]] + [ff_grads[layer]] * 3
+    out_specs = [pl.BlockSpec((1, high, width), lambda now, step: (now, step, 0)) for width in widths]
+    out_specs += [pl.BlockSpec((1, HV, high), lambda now, step: (now, 0, step))]
+    out_specs += [pl.BlockSpec((1, flat, cols), lambda now, step: (now, step, 0))] * 3
+    shapes = [(LAYERS, rows, width) for width in widths] + [(LAYERS, HV, rows)] + [(LAYERS, ff, cols)] * 3
+    return pl.pallas_call(
+        body,
+        grid=(LAYERS, steps),
+        in_specs=in_specs,
+        out_specs=out_specs,
+        out_shape=[jax.ShapeDtypeStruct(v, f32) for v in shapes],
+        cost_estimate=NO_COST,
+        compiler_params=pltpu.CompilerParams(
+            dimension_semantics=("arbitrary", "arbitrary"), vmem_limit_bytes=VMEM_LIMIT
+        ),
+    )(*args)
+
+
 def ring_place(index, n):
     return jnp.where(index % 2 == 0, index // 2, n - 1 - index // 2)
 
@@ -716,7 +766,8 @@
 
 
 def mix_sum_kernel(
-    n, cuts, done, own, far, misc, out_done, out_own, out_misc, came, total, slot_a, slot_b, slot_c, slot_d,
+    n, cuts, done, late, own, far, misc, out_done, out_late, out_own, out_misc, came, total,
+    slot_a, slot_b, slot_c, slot_d, slot_e, slot_f,
     send, recv, out_send, out_recv, chip_send, chip_recv, sums, misc_came, misc_send, misc_recv,
 ):
     me = ring_place(lax.axis_index("dp"), n)
@@ -763,10 +814,12 @@
     rings = (
         (0, done, out_done, cuts[0], slot_a),
         (1, done, out_done, cuts[1], slot_b),
-        (2, total, out_own, cuts[2], slot_c),
-        (3, total, out_own, cuts[3], slot_d),
+        (2, late, out_late, cuts[2], slot_c),
+        (3, late, out_late, cuts[3], slot_d),
+        (4, total, out_own, cuts[4], slot_e),
+        (5, total, out_own, cuts[5], slot_f),
     )
-    first, second = ([ring(*v) for v in pair if v[3][1] > v[3][0]] for pair in (rings[:2], rings[2:]))
+    first, second = ([ring(*v) for v in pair if v[3][1] > v[3][0]] for pair in (rings[:4], rings[4:]))
 
     def each(rings, name):
         return [getattr(v, name) for v in rings]
@@ -803,11 +856,11 @@
     steps_of(0, last, *each(first + second, "sent"))
 
 
-def mix_sum(done, own, far, misc, n):
+def mix_sum(done, late, own, far, misc, n):
     if n == 1:
         misc = misc + core_swap(misc)
         own = (own.astype(f32) + chip_swap(far).astype(f32)).astype(bf16)
-        return done, own, misc + chip_swap(misc)
+        return done, late, own, misc + chip_swap(misc)
     rows, cols = own.shape
     done_rows = done.shape[0]
     swaps = 2 + n.bit_length() - 1
@@ -817,7 +870,7 @@
         cut = (lines + 1) // 2 * 32 * n
         return (0, cut), (cut, total)
 
-    cuts = two(done_rows) + two(rows)
+    cuts = two(done_rows) + two(rows) + two(rows)
 
     def body(*refs):
         mix_sum_kernel(n, cuts, *refs)
@@ -825,10 +878,11 @@
     vmem = pl.BlockSpec(memory_space=pltpu.VMEM)
     return pl.pallas_call(
         body,
-        in_specs=[vmem] * 4,
-        out_specs=[vmem] * 3,
+        in_specs=[vmem] * 5,
+        out_specs=[vmem] * 4,
         out_shape=[
             jax.ShapeDtypeStruct((done_rows, cols), bf16),
+            jax.ShapeDtypeStruct((rows, cols), bf16),
             jax.ShapeDtypeStruct((rows, cols), bf16),
         ]
         + [jax.ShapeDtypeStruct(misc.shape, f32)],
@@ -839,7 +893,7 @@
         + [
             pltpu.VMEM((2, n - 1, max(16, (stop - at) // (2 * n)), cols), bf16) for at, stop in cuts
         ]
-        + [pltpu.SemaphoreType.DMA((4, 2, n - 1))] * 4
+        + [pltpu.SemaphoreType.DMA((6, 2, n - 1))] * 4
         + [pltpu.SemaphoreType.DMA] * 2
         + [
             pltpu.VMEM((swaps + 1,) + misc.shape, f32),
@@ -850,7 +904,7 @@
         compiler_params=pltpu.CompilerParams(
             collective_id=0, has_side_effects=True, vmem_limit_bytes=VMEM_LIMIT
         ),
-    )(done, own, far, misc)
+    )(done, late, own, far, misc)
 
 
 def norm_scale(hidden):
@@ -991,13 +1045,12 @@
         if layer + 1 < LAYERS:
             g_own = grad.astype(bf16)
             g_y = chip_swap(g_own)
-            m_y = chip_swap(after(m[0], dfar))
-            mix_done = (own.astype(f32) + chip_swap(after(far, g_y)).astype(f32)).astype(bf16)
-            mix_done = lax.psum(mix_done, "dp", axis_index_groups=[dp_ring()])
+            mix_late = (own, chip_swap(after(far, g_y)))
         else:
             g_own = grad_out[0]
             g_y = chip_swap(after(g_own, got))
-            m_y = chip_swap(after(m[0], g_y))
+            m_y = chip_swap(jnp.concatenate([v[3][0] for v in saved], axis=0))
+            m_far = (m_y, core_swap(m_y))
         g = (g_own, core_swap(g_own))
         dboth, dfar = ff_backward(g, gate, up, (w_down, layer), ff_far, ffp)
         back_mid, gain_two = norm_back(
@@ -1012,7 +1065,7 @@
             ),
         )
         ff_grad = ff_weight_grads(
-            m + (m_y, core_swap(m_y)), g + (g_y, core_swap(g_y)), dboth, product,
+            m + tuple(v[layer * shard_len : (layer + 1) * shard_len] for v in m_far), g + (g_y, core_swap(g_y)), dboth, product,
             (gate_t, layer), (up_t, layer), (w_down, layer), 0 if layer else spare,
         )
         grad = grad + back_mid
@@ -1030,6 +1083,8 @@
         )
         g_wmix = tn(a, dx[:, : 2 * HEAD_COLS]).astype(bf16)
         g_rank = tn(dx[:, 2 * HEAD_COLS :], a)
+        if layer + 1 < LAYERS:
+            mix_late = (mix_late[0].astype(f32) + after(mix_late[1], dx).astype(f32)).astype(bf16)
         far = jnp.concatenate([g_wmix[:, HEAD_COLS:], g_wout[:, HV:]], axis=1)
         own = jnp.concatenate([g_wmix[:, :HEAD_COLS], g_wout[:, :HV]], axis=1)
         far_terms, at = [], HEAD_COLS
@@ -1046,8 +1101,6 @@
         grad = grad + back_first
         if layer > 0:
             ff_grads[layer] = lax.psum(ff_grad, "dp")
-        else:
-            ff_grads[1] = after(ff_grads[1], grad)
         heads = jnp.concatenate([dwdec, dbias], axis=0)
         places = lax.iota(jnp.int32, 4)[:, None, None]
         heads = jnp.where(places == member, heads[None, :, :HK], 0.0) + jnp.where(
@@ -1060,8 +1113,8 @@
     misc = jnp.stack(misc_grads)
     length = misc.shape[1]
     misc = jnp.pad(misc.reshape(-1), (0, -misc.size % 1024)).reshape(-1, 128)
-    ff_done, first_mix, misc = mix_sum(ff_grad, own, far, misc, lax.axis_size("dp"))
-    mix_grads = [first_mix, after(mix_done, grad)]
+    ff_done, late_mix, first_mix, misc = mix_sum(ff_grad, mix_late, own, far, misc, lax.axis_size("dp"))
+    mix_grads = [first_mix, late_mix]
     ff_grads[0] = ff_done
     misc = misc.reshape(-1)[: LAYERS * length].reshape(LAYERS, length)
     sizes = (rank * width, width, width, HV, 4 * (rank + 1) * HK)
@@ -1073,32 +1126,24 @@
         pieces[4].reshape(LAYERS, 4, rank + 1, HK), member, axis=1, keepdims=False
     )
 
-    def rows_of(grads, start, stop):
-        return jnp.stack([g[start:stop].astype(f32) for g in grads])
-
-    def turned(grads, start, stop):
-        return jnp.stack([g[start:stop].T.astype(f32) for g in grads])
-
-    def cols_of(grads, start, stop):
-        return jnp.stack([g[:, start:stop].astype(f32) for g in grads])
-
+    query, key, value, outgate, out, gate, up, down = weight_outputs(mix_grads, ff_grads, ff)
     return (
         result,
         grad[None],
         pieces[1],
-        cols_of(mix_grads, 0, HK),
-        cols_of(mix_grads, HK, 2 * HK),
-        cols_of(mix_grads, 2 * HK, 2 * HK + HV),
-        cols_of(mix_grads, 2 * HK + HV, HEAD_COLS),
+        query,
+        key,
+        value,
+        outgate,
         jnp.swapaxes(pieces[0].reshape(LAYERS, rank, width), 1, 2),
         heads[:, :rank],
         heads[:, rank],
         pieces[3],
-        jnp.stack([g[:, HEAD_COLS:].T.astype(f32) for g in mix_grads]),
+        out,
         pieces[2],
-        turned(ff_grads, 0, ff),
-        turned(ff_grads, ff, 2 * ff),
-        rows_of(ff_grads, 2 * ff, 3 * ff),
+        jnp.swapaxes(gate, 1, 2),
+        jnp.swapaxes(up, 1, 2),
+        down,
     )
 
 

time: 792 us -> 754 us (0.952)
  other arithmetic: 72.7 us -> 54.9 us
  waiting for transfers between devices: 99.9 us -> 87.7 us
    another operation x8 -> x0, other arithmetic: 15.9 us -> none  [the longest x4 7.09 us: cols_of(): return jnp.stack([g[:, start:stop].astype(f32) for g in grads])]
    ppermute x17 -> x16, waiting for transfers between devices: 96.6 us -> 82.7 us  [chip_swap(): return lax.ppermute(value, 'head', [(i, i ^ 2) for i in range(4)])]
    another operation x6 -> x0, local copies, waits for them, and re-layouts: 10.4 us -> none  [the longest x2 3.85 us: cols_of(): return jnp.stack([g[:, start:stop].astype(f32) for g in grads])]
    ppermute x17 -> x16, starting transfers between devices: 19.6 us -> 17.6 us  [chip_swap(): return lax.ppermute(value, 'head', [(i, i ^ 2) for i in range(4)])]
    pallas_call x1 -> x2, Pallas kernels: 225 us -> 227 us  [the longest x1 215 us: mix_sum(): pl.pallas_call(body, in_specs=[vmem] * 5, out_specs=[vmem] * 4, out_shape...]
    unnamed x257 -> x226, local copies, waits for them, and re-layouts: 31.8 us -> 32.9 us
  transfers between devices with their start and end apart: 41 -> 38, of which waited for: 13 -> 12; matrix products, arithmetic and copies ran while one was open for 14% -> 13% of each run, Pallas kernels for 58% -> 55%
where the time goes in v7:
time: 754 us; the launch traced here: 747 us
  Pallas kernels  480 us (64%)
  waiting for transfers between devices  87.7 us (12%)
  local copies, waits for them, and re-layouts  69.1 us (9%)
  other arithmetic  54.9 us (7%)
  starting transfers between devices  21.8 us (3%)
  matrix products  17.5 us (2%)
  between operations  15.4 us (2%)
    pallas_call x1, Pallas kernels, mix_sum(): pl.pallas_call(body, in_specs=[vmem] * 5, out_specs=[vmem] * 4, out_shape...  215 us
    pallas_call x24, Pallas kernels, local_call(): pl.pallas_call(body, grid=(grid,), in_specs=in_specs, out_specs=out_specs...  180 us
    ppermute x16, waiting for transfers between devices, chip_swap(): return lax.ppermute(value, 'head', [(i, i ^ 2) for i in range(4)])  82.7 us
    pallas_call x8, Pallas kernels, call(): pl.pallas_call(sub_blocks(kernel, self.ndoc, self.tokens, *layout), grid_...  73.2 us
    unnamed x226, local copies, waits for them, and re-layouts  32.9 us
    ppermute x16, starting transfers between devices, chip_swap(): return lax.ppermute(value, 'head', [(i, i ^ 2) for i in range(4)])  17.6 us
    dot_general x6, matrix products, tn(): lax.dot_general(left, right, (((0,), (0,)), ((), ())), preferred_element_...  17.5 us
  transfers between devices with their start and end apart: 38, of which 12 were waited for; matrix products, arithmetic and copies ran while one was open for 13% of the time, Pallas kernels for 55%

profile of v7, /device:TPU:0, one launch (start us, length us, event | category | flops | bytes accessed | tf_op | source)
XLA Modules:
  0.0 746.6 jit_solution(10391445993654982300)
XLA Ops:
  21.7 12.3 %collective-permute-done.2 = bf16[264,1024]{1,0:T(8,128)(2,1)S(1)} collective-permute-done((bf16[264,1024]{1,0:T(8,128)(2,1)S(1)}, bf16[264,1024]{1,0:T(8,128)(2,1)S(1)}, u32[]{:S(2)}, u32[]{:S(2)}) %collective-permute-start.2) | collective-permute-done | bytes 540704 | tf_op jit(solution)/shard_map/ppermute | solution.py:932
  52.8 15.1 %collective-permute-done.3.refs_2_.refs_3_ = bf16[1024,512]{1,0:T(8,128)(2,1)} collective-permute-done((bf16[1024,512]{1,0:T(8,128)(2,1)}, bf16[1024,512]{1,0:T(8,128)(2,1)}, u32[]{:S(2)}, u32[]{:S(2)}) %collective-permute-start.3) | collective-permute-done | bytes 1048608 | tf_op jit(solution)/shard_map/ppermute | solution.py:932
  69.6 9.9 %collective-permute-done.4 = f32[2,17,128]{2,1,0:T(8,128)S(1)} collective-permute-done((f32[2,17,128]{2,1,0:T(8,128)S(1)}, f32[2,17,128]{2,1,0:T(8,128)S(1)}, u32[]{:S(2)}, u32[]{:S(2)}) %collective-permute-start.4) | collective-permute-done | bytes 17440 | tf_op jit(solution)/shard_map/ppermute | solution.py:932
  84.6 7.3 shard_map.288.refs_0_
  91.9 8.0 %shard_map.289 = (f32[1024,256]{1,0:T(8,128)S(1)}, bf16[8,2,256,128]{3,2,1,0:T(8,128)(2,1)S(1)}, f32[8,1,256]{2,1,0:T(1,128)S(1)}, bf16[2,256,128]{2,1,0:T(8,128)(2,1)S(1)}) custom-call(s32[6]{0:T(128)S(1)} %pad_add_fusion.meta, f32[1024,1552]{1,0:T(8,128)} %shard_map.288.refs_0_, f32[16,256]{1,0:T(8,128)S(1)} %get-tuple-element.246.refs_1_.refs_10_, ...), custom_call_target="tpu_custom_call" | custom-call | tf_op jit(solution)/shard_map/pallas_call | solution.py:284
  128.8 11.8 %shard_map.293 = (bf16[1024,1536]{1,0:T(8,128)(2,1)}, bf16[1024,1536]{1,0:T(8,128)(2,1)}, bf16[1024,1536]{1,0:T(8,128)(2,1)}) custom-call(bf16[512,1024]{1,0:T(8,128)(2,1)} %multiply_convert_fusion.2.near_ref.m0, bf16[512,1024]{1,0:T(8,128)(2,1)} %collective-permute-done.9.part_ref.m1, bf16[2,704,1024]{2,1,0:T(8,128)(2,1)S(1)} %bitcast.116, ...), custom_call_target="tpu_custom_call" | custom-call | tf_op jit(solution)/shard_map/pallas_call | solution.py:433
  140.6 14.4 %collective-permute-done.10.refs_1_.refs_2_ = bf16[1024,768]{1,0:T(8,128)(2,1)} collective-permute-done((bf16[1024,768]{1,0:T(8,128)(2,1)}, bf16[1024,768]{1,0:T(8,128)(2,1)}, u32[]{:S(2)}, u32[]{:S(2)}) %collective-permute-start.10) | collective-permute-done | bytes 1572896 | tf_op jit(solution)/shard_map/ppermute | solution.py:932
  167.7 7.7 %shard_map.296.refs_0_ = f32[1024,1552]{1,0:T(8,128)} custom-call(bf16[1024,1024]{1,0:T(8,128)(2,1)S(1)} %pad_maximum_fusion.1.left, bf16[1024,768]{1,0:T(8,128)(2,1)} %pad_maximum_fusion.9.refs_0_.refs_1_, bf16[1024,768]{1,0:T(8,128)(2,1)} %collective-permute-done.10.refs_1_.refs_2_, bf16[2,16,1024]{2,1,0:T(8,128)(2,1)S(1)} %bitcast.119), custom_call_target="tpu_custom_call" | custom-call | tf_op jit(solution)/shard_map/pallas_call | solution.py:433
  175.4 8.0 %shard_map.297 = (f32[1024,256]{1,0:T(8,128)S(1)}, bf16[8,2,256,128]{3,2,1,0:T(8,128)(2,1)S(1)}, f32[8,1,256]{2,1,0:T(1,128)S(1)}, bf16[2,256,128]{2,1,0:T(8,128)(2,1)S(1)}) custom-call(s32[6]{0:T(128)S(1)} %pad_add_fusion.meta, f32[1024,1552]{1,0:T(8,128)} %shard_map.296.refs_0_, f32[16,256]{1,0:T(8,128)S(1)} %get-tuple-element.245.refs_1_.refs_10_, ...), custom_call_target="tpu_custom_call" | custom-call | tf_op jit(solution)/shard_map/pallas_call | solution.py:284
  210.3 12.0 %shard_map.301 = (bf16[1024,1536]{1,0:T(8,128)(2,1)}, bf16[1024,1536]{1,0:T(8,128)(2,1)}, bf16[1024,1536]{1,0:T(8,128)(2,1)}) custom-call(bf16[512,1024]{1,0:T(8,128)(2,1)} %multiply_convert_fusion.near_ref.m0, bf16[512,1024]{1,0:T(8,128)(2,1)} %collective-permute-done.16.part_ref.m1, bf16[2,704,1024]{2,1,0:T(8,128)(2,1)S(1)} %bitcast.117, ...), custom_call_target="tpu_custom_call" | custom-call | tf_op jit(solution)/shard_map/pallas_call | solution.py:433
  222.3 9.7 %shard_map.304 = (bf16[1024,1408]{1,0:T(8,128)(2,1)S(1)}, bf16[1024,1408]{1,0:T(8,128)(2,1)}) custom-call(bf16[512,1024]{1,0:T(8,128)(2,1)} %bitcast.46.near_ref.g0, bf16[512,1024]{1,0:T(8,128)(2,1)} %collective-permute-done.18.part_ref.g1, bf16[1024,1536]{1,0:T(8,128)(2,1)} %get-tuple-element.102.gate_ref, bf16[1024,1536]{1,0:T(8,128)(2,1)} %get-tuple-element.103.up_ref, ...), custom_call_target="tpu_custom_call" | custom-call | tf_op jit(solution)/shard_map/pallas_call | solution.py:433
  232.1 7.7 %shard_map.306 = bf16[512,1024]{1,0:T(8,128)(2,1)S(1)} custom-call(bf16[1024,1408]{1,0:T(8,128)(2,1)S(1)} %get-tuple-element.104.refs_0_.both_ref, bf16[1024,1408]{1,0:T(8,128)(2,1)} %get-tuple-element.105.refs_1_, bf16[2,704,1024]{2,1,0:T(8,128)(2,1)} %bitcast.109, bf16[2,704,1024]{2,1,0:T(8,128)(2,1)} %bitcast.144, bf16[2112,1024]{1,0:T(8,128)(2,1)} %bitcast.137), custom_call_target="tpu_custom_call" | custom-call | tf_op jit(solution)/shard_map/pallas_call | solution.py:433
  261.0 14.5 %collective-permute-done.23.g2 = bf16[512,1024]{1,0:T(8,128)(2,1)S(1)} collective-permute-done((bf16[512,1024]{1,0:T(8,128)(2,1)}, bf16[512,1024]{1,0:T(8,128)(2,1)S(1)}, u32[]{:S(2)}, u32[]{:S(2)}) %collective-permute-start.23) | collective-permute-done | bytes 1048608 | tf_op jit(solution)/shard_map/ppermute | solution.py:932
  282.2 28.4 %shard_map.307 = bf16[2112,1024]{1,0:T(8,128)(2,1)} custom-call(bf16[512,1024]{1,0:T(8,128)(2,1)} %multiply_convert_fusion.near_ref.m0, bf16[512,1024]{1,0:T(8,128)(2,1)} %collective-permute-done.16.part_ref.m1, bf16[512,1024]{1,0:T(8,128)(2,1)S(1)} %get-tuple-element.227.m2, bf16[512,1024]{1,0:T(8,128)(2,1)S(1)} %get-tuple-element.225.m3, ...), custom_call_target="tpu_custom_call" | custom-call | tf_op jit(solution)/shard_map/pallas_call | solution.py:433
  311.6 11.7 %shard_map.308 = (bf16[1024,512]{1,0:T(8,128)(2,1)S(1)}, bf16[1024,512]{1,0:T(8,128)(2,1)S(1)}, bf16[8,2,256,128]{3,2,1,0:T(8,128)(2,1)S(1)}, f32[8,1,256]{2,1,0...) custom-call(s32[6]{0:T(128)S(1)} %pad_add_fusion.meta, f32[1024,1552]{1,0:T(8,128)} %shard_map.296.refs_0_, ...), custom_call_target="tpu_custom_call" | custom-call | tf_op jit(solution)/shard_map/pallas_call | solution.py:284
  335.7 11.7 %shard_map.309 = (bf16[1024,1552]{1,0:T(8,128)(2,1)}, f32[16,256]{1,0:T(8,128)S(1)}, f32[1,256]{1,0:T(1,128)S(1)}) custom-call(s32[6]{0:T(128)S(1)} %pad_add_fusion.meta, f32[1024,1552]{1,0:T(8,128)} %shard_map.296.refs_0_, f32[1024,256]{1,0:T(8,128)S(1)} %copy-done.16, bf16[8,2,256,128]{3,2,1,0:T(8,128)(2,1)S(1)} %copy-done.27, ...), custom_call_target="tpu_custom_call" | custom-call | tf_op jit(solution)/shard_map/pallas_call | solution.py:284
  368.7 9.6 %shard_map.312 = (bf16[1024,1408]{1,0:T(8,128)(2,1)S(1)}, bf16[1024,1408]{1,0:T(8,128)(2,1)}) custom-call(bf16[512,1024]{1,0:T(8,128)(2,1)} %get-tuple-element.204.near_ref.g0, bf16[512,1024]{1,0:T(8,128)(2,1)S(1)} %copy-done.31, bf16[1024,1536]{1,0:T(8,128)(2,1)} %get-tuple-element.115.gate_ref, bf16[1024,1536]{1,0:T(8,128)(2,1)} %get-tuple-element.116.up_ref, ...), custom_call_target="tpu_custom_call" | custom-call | tf_op jit(solution)/shard_map/pallas_call | solution.py:433
  378.3 7.7 %shard_map.314 = bf16[512,1024]{1,0:T(8,128)(2,1)S(1)} custom-call(bf16[1024,1408]{1,0:T(8,128)(2,1)S(1)} %get-tuple-element.117.refs_0_.both_ref, bf16[1024,1408]{1,0:T(8,128)(2,1)} %get-tuple-element.118.refs_1_, bf16[2,704,1024]{2,1,0:T(8,128)(2,1)} %bitcast.112, bf16[2,704,1024]{2,1,0:T(8,128)(2,1)} %bitcast.147, bf16[2112,1024]{1,0:T(8,128)(2,1)} %bitcast.132), custom_call_target="tpu_custom_call" | custom-call | tf_op jit(solution)/shard_map/pallas_call | solution.py:433
  393.2 6.9 shard_map.313
  409.2 28.5 %shard_map.319.refs_0_ = bf16[2304,1024]{1,0:T(8,128)(2,1)} custom-call(bf16[512,1024]{1,0:T(8,128)(2,1)} %multiply_convert_fusion.2.near_ref.m0, bf16[512,1024]{1,0:T(8,128)(2,1)} %collective-permute-done.9.part_ref.m1, bf16[512,1024]{1,0:T(8,128)(2,1)S(1)} %copy-done.28, bf16[512,1024]{1,0:T(8,128)(2,1)S(1)} %copy-done.29, ...), custom_call_target="tpu_custom_call" | custom-call | tf_op jit(solution)/shard_map/pallas_call | solution.py:433
  440.9 11.1 %shard_map.315 = (bf16[1024,512]{1,0:T(8,128)(2,1)S(1)}, bf16[1024,512]{1,0:T(8,128)(2,1)S(1)}, bf16[8,2,256,128]{3,2,1,0:T(8,128)(2,1)S(1)}, f32[8,1,256]{2,1,0...) custom-call(s32[6]{0:T(128)S(1)} %pad_add_fusion.meta, f32[1024,1552]{1,0:T(8,128)} %shard_map.288.refs_0_, ...), custom_call_target="tpu_custom_call" | custom-call | tf_op jit(solution)/shard_map/pallas_call | solution.py:284
  457.8 11.7 %shard_map.316 = (bf16[1024,1552]{1,0:T(8,128)(2,1)}, f32[16,256]{1,0:T(8,128)S(1)}, f32[1,256]{1,0:T(1,128)S(1)}) custom-call(s32[6]{0:T(128)S(1)} %pad_add_fusion.meta, f32[1024,1552]{1,0:T(8,128)} %shard_map.288.refs_0_, f32[1024,256]{1,0:T(8,128)S(1)} %copy-done.14, bf16[8,2,256,128]{3,2,1,0:T(8,128)(2,1)S(1)} %copy-done.25, ...), custom_call_target="tpu_custom_call" | custom-call | tf_op jit(solution)/shard_map/pallas_call | solution.py:284
  499.6 214.6 %shard_map.320 = (bf16[2304,1024]{1,0:T(8,128)(2,1)}, bf16[1024,1024]{1,0:T(8,128)(2,1)S(1)}, bf16[1024,1024]{1,0:T(8,128)(2,1)S(1)}, f32[432,128]{1,0:T(8,128)S(1)}) custom-call(bf16[2304,1024]{1,0:T(8,128)(2,1)} %shard_map.319.refs_0_, bf16[1024,1024]{1,0:T(8,128)(2,1)} %add_convert_fusion.refs_1_, bf16[1024,1024]{1,0:T(8,128)(2,1)} %pad_maximum_fusion.6.refs_2_, ...), custom_call_target="tpu_custom_call" | custom-call | tf_op jit(solution)/shard_map/pallas_call | solution.py:879
  727.5 12.4 %shard_map.321 = (f32[2,1024,128]{2,1,0:T(8,128)}, f32[2,1024,128]{2,1,0:T(8,128)}, f32[2,1024,256]{2,1,0:T(8,128)}, f32[2,1024,256]{2,1,0:T(8,128)}, f32[2,256,...) custom-call(bf16[1024,1024]{1,0:T(8,128)(2,1)S(1)} %copy-done.39, ...), custom_call_target="tpu_custom_call" | custom-call | tf_op jit(solution)/shard_map/pallas_call | solution.py:671
  (416 shorter events, 238.7 us)
Async XLA Ops:
  7.2 116.7 %all-gather.3.cloned.1.call-start = ((), (), s32[]{:S(2)}) async-start(), calls=%async_computation | async-start | bytes 4866048 | tf_op jit(solution)/shard_map/all_gather | solution.py:979
  18.7 15.3 %collective-permute-start.2 = (bf16[264,1024]{1,0:T(8,128)(2,1)S(1)}, bf16[264,1024]{1,0:T(8,128)(2,1)S(1)}, u32[]{:S(2)}, u32[]{:S(2)}) collective-permute-start(bf16[264,1024]{1,0:T(8,128)(2,1)S(1)} %pad_maximum_fusion.11), channel_id=1, source_target_pairs={{0,2},{1,3},{2,0},{3,1},{4,6},{5,7},{6,4},{7,5},{8,10},{9,11},{10,... | collective-permute-start | bytes 1622024 | tf_op jit(solution)/shard_map/ppermute | solution.py:932
  34.8 170.6 %all-gather.5.cloned.1.call-start = ((), (), s32[]{:S(2)}) async-start(), calls=%async_computation.1 | async-start | bytes 4866048 | tf_op jit(solution)/shard_map/all_gather | solution.py:979
  39.7 42.9 %collective-permute-start = (bf16[512,1024]{1,0:T(8,128)(2,1)}, bf16[512,1024]{1,0:T(8,128)(2,1)}, u32[]{:S(2)}, u32[]{:S(2)}) collective-permute-start(bf16[512,1024]{1,0:T(8,128)(2,1)} %fusion.4), channel_id=1, source_target_pairs={{0,1},{1,0},{2,3},{3,2},{4,5},{5,4},{6,7},{7,6},{8,9},{9,8},{10,11... | collective-permute-start | bytes 3145736 | tf_op jit(solution)/shard_map/ppermute | solution.py:928
  41.5 26.3 %collective-permute-start.3 = (bf16[1024,512]{1,0:T(8,128)(2,1)}, bf16[1024,512]{1,0:T(8,128)(2,1)}, u32[]{:S(2)}, u32[]{:S(2)}) collective-permute-start(bf16[1024,512]{1,0:T(8,128)(2,1)} %pad_maximum_fusion.10), channel_id=1, source_target_pairs={{0,2},{1,3},{2,0},{3,1},{4,6},{5,7},{6,4},{7,5},{8,10},{9,11},{10,... | collective-permute-start | bytes 3145736 | tf_op jit(solution)/shard_map/ppermute | solution.py:932
  44.1 40.2 %collective-permute-start.1 = (bf16[1024,256]{1,0:T(8,128)(2,1)}, bf16[1024,256]{1,0:T(8,128)(2,1)}, u32[]{:S(2)}, u32[]{:S(2)}) collective-permute-start(bf16[1024,256]{1,0:T(8,128)(2,1)} %pad_maximum_fusion.13), channel_id=1, source_target_pairs={{0,2},{1,3},{2,0},{3,1},{4,6},{5,7},{6,4},{7,5},{8,10},{9,11},{10,... | collective-permute-start | bytes 1572872 | tf_op jit(solution)/shard_map/ppermute | solution.py:932
  44.5 35.0 %collective-permute-start.4 = (f32[2,17,128]{2,1,0:T(8,128)S(1)}, f32[2,17,128]{2,1,0:T(8,128)S(1)}, u32[]{:S(2)}, u32[]{:S(2)}) collective-permute-start(f32[2,17,128]{2,1,0:T(8,128)S(1)} %pad_maximum_fusion.16), channel_id=1, source_target_pairs={{0,2},{1,3},{2,0},{3,1},{4,6},{5,7},{6,4},{7,5},{8,10},{9,11},{10,... | collective-permute-start | bytes 52232 | tf_op jit(solution)/shard_map/ppermute | solution.py:932
  67.8 34.7 %collective-permute-start.5 = (bf16[264,1024]{1,0:T(8,128)(2,1)}, bf16[264,1024]{1,0:T(8,128)(2,1)}, u32[]{:S(2)}, u32[]{:S(2)}) collective-permute-start(bf16[264,1024]{1,0:T(8,128)(2,1)} %pad_maximum_fusion.12), channel_id=1, source_target_pairs={{0,2},{1,3},{2,0},{3,1},{4,6},{5,7},{6,4},{7,5},{8,10},{9,11},{10,... | collective-permute-start | bytes 1622024 | tf_op jit(solution)/shard_map/ppermute | solution.py:932
  80.1 36.7 %collective-permute-start.7 = (bf16[256,1024]{1,0:T(8,128)(2,1)}, bf16[256,1024]{1,0:T(8,128)(2,1)S(1)}, u32[]{:S(2)}, u32[]{:S(2)}) collective-permute-start(bf16[256,1024]{1,0:T(8,128)(2,1)} %get-tuple-element.90.refs_4_), channel_id=1, source_target_pairs={{0,2},{1,3},{2,0},{3,1},{4,6},{5,7},{6,4},{7,5},{8,10},{9,11},{10,... | collective-permute-start | bytes 1572872 | tf_op jit(solution)/shard_map/ppermute | solution.py:932
  117.8 37.2 %collective-permute-start.10 = (bf16[1024,768]{1,0:T(8,128)(2,1)}, bf16[1024,768]{1,0:T(8,128)(2,1)}, u32[]{:S(2)}, u32[]{:S(2)}) collective-permute-start(bf16[1024,768]{1,0:T(8,128)(2,1)} %pad_maximum_fusion.9.refs_0_.refs_1_), channel_id=1, source_target_pairs={{0,2},{1,3},{2,0},{3,1},{4,6},{5,7},{6,4},{7,5},{8,10},{9,11},{10,... | collective-permute-start | bytes 4718600 | tf_op jit(solution)/shard_map/ppermute | solution.py:932
  123.6 600.7 %all-reduce.3.cloned.1.call-start = ((), (), s32[]{:S(2)}) async-start(), calls=%async_computation.2 | async-start | bytes 8650752 | tf_op jit(solution)/shard_map/psum | solution.py:1103
  164.4 19.1 %collective-permute-start.13 = (bf16[256,1024]{1,0:T(8,128)(2,1)S(1)}, bf16[256,1024]{1,0:T(8,128)(2,1)S(1)}, u32[]{:S(2)}, u32[]{:S(2)}) collective-permute-start(bf16[256,1024]{1,0:T(8,128)(2,1)S(1)} %copy-done.34), channel_id=1, source_target_pairs={{0,2},{1,3},{2,0},{3,1},{4,6},{5,7},{6,4},{7,5},{8,10},{9,11},{10,... | collective-permute-start | bytes 1572872 | tf_op jit(solution)/shard_map/ppermute | solution.py:932
  196.0 26.3 %collective-permute-start.18 = (bf16[512,1024]{1,0:T(8,128)(2,1)}, bf16[512,1024]{1,0:T(8,128)(2,1)}, u32[]{:S(2)}, u32[]{:S(2)}) collective-permute-start(bf16[512,1024]{1,0:T(8,128)(2,1)} %bitcast.46.near_ref.g0), channel_id=1, source_target_pairs={{0,1},{1,0},{2,3},{3,2},{4,5},{5,4},{6,7},{7,6},{8,9},{9,8},{10,11... | collective-permute-start | bytes 3145736 | tf_op jit(solution)/shard_map/ppermute | solution.py:928
  204.8 51.0 %collective-permute-start.21 = (bf16[1024,1024]{1,0:T(8,128)(2,1)}, bf16[1024,1024]{1,0:T(8,128)(2,1)}, u32[]{:S(2)}, u32[]{:S(2)}) collective-permute-start(bf16[1024,1024]{1,0:T(8,128)(2,1)} %pad_maximum_fusion.3), channel_id=1, source_target_pairs={{0,2},{1,3},{2,0},{3,1},{4,6},{5,7},{6,4},{7,5},{8,10},{9,11},{10,... | collective-permute-start | bytes 6291464 | tf_op jit(solution)/shard_map/ppermute | solution.py:932
  239.7 16.2 %collective-permute-start.19 = (bf16[512,1024]{1,0:T(8,128)(2,1)S(1)}, bf16[512,1024]{1,0:T(8,128)(2,1)S(1)}, u32[]{:S(2)}, u32[]{:S(2)}) collective-permute-start(bf16[512,1024]{1,0:T(8,128)(2,1)S(1)} %shard_map.306), channel_id=1, source_target_pairs={{0,1},{1,0},{2,3},{3,2},{4,5},{5,4},{6,7},{7,6},{8,9},{9,8},{10,11... | collective-permute-start | bytes 3145736 | tf_op jit(solution)/shard_map/ppermute | solution.py:928
  243.5 13.2 %collective-permute-start.17 = (bf16[512,1024]{1,0:T(8,128)(2,1)S(1)}, bf16[512,1024]{1,0:T(8,128)(2,1)S(1)}, u32[]{:S(2)}, u32[]{:S(2)}) collective-permute-start(bf16[512,1024]{1,0:T(8,128)(2,1)S(1)} %shard_map.303), channel_id=1, source_target_pairs={{0,1},{1,0},{2,3},{3,2},{4,5},{5,4},{6,7},{7,6},{8,9},{9,8},{10,11... | collective-permute-start | bytes 3145736 | tf_op jit(solution)/shard_map/ppermute | solution.py:928
  244.0 31.4 %collective-permute-start.23 = (bf16[512,1024]{1,0:T(8,128)(2,1)}, bf16[512,1024]{1,0:T(8,128)(2,1)S(1)}, u32[]{:S(2)}, u32[]{:S(2)}) collective-permute-start(bf16[512,1024]{1,0:T(8,128)(2,1)} %bitcast.46.near_ref.g0), channel_id=1, source_target_pairs={{0,2},{1,3},{2,0},{3,1},{4,6},{5,7},{6,4},{7,5},{8,10},{9,11},{10,... | collective-permute-start | bytes 3145736 | tf_op jit(solution)/shard_map/ppermute | solution.py:932
  255.8 24.2 %collective-permute-start.22 = (bf16[1024,1024]{1,0:T(8,128)(2,1)}, bf16[1024,1024]{1,0:T(8,128)(2,1)S(1)}, u32[]{:S(2)}, u32[]{:S(2)}) collective-permute-start(bf16[1024,1024]{1,0:T(8,128)(2,1)} %collective-permute-done.21), channel_id=1, source_target_pairs={{0,1},{1,0},{2,3},{3,2},{4,5},{5,4},{6,7},{7,6},{8,9},{9,8},{10,11... | collective-permute-start | bytes 6291464 | tf_op jit(solution)/shard_map/ppermute | solution.py:928
  260.5 18.0 %collective-permute-start.20 = (bf16[512,1024]{1,0:T(8,128)(2,1)S(1)}, bf16[512,1024]{1,0:T(8,128)(2,1)S(1)}, u32[]{:S(2)}, u32[]{:S(2)}) collective-permute-start(bf16[512,1024]{1,0:T(8,128)(2,1)S(1)} %get-tuple-element.206), channel_id=1, source_target_pairs={{0,1},{1,0},{2,3},{3,2},{4,5},{5,4},{6,7},{7,6},{8,9},{9,8},{10,11... | collective-permute-start | bytes 3145736 | tf_op jit(solution)/shard_map/ppermute | solution.py:928
  365.8 34.3 %collective-permute-start.32 = (bf16[512,1024]{1,0:T(8,128)(2,1)}, bf16[512,1024]{1,0:T(8,128)(2,1)}, u32[]{:S(2)}, u32[]{:S(2)}) collective-permute-start(bf16[512,1024]{1,0:T(8,128)(2,1)} %get-tuple-element.204.near_ref.g0), channel_id=1, source_target_pairs={{0,2},{1,3},{2,0},{3,1},{4,6},{5,7},{6,4},{7,5},{8,10},{9,11},{10,... | collective-permute-start | bytes 3145736 | tf_op jit(solution)/shard_map/ppermute | solution.py:932
  386.0 15.9 %collective-permute-start.28 = (bf16[512,1024]{1,0:T(8,128)(2,1)S(1)}, bf16[512,1024]{1,0:T(8,128)(2,1)}, u32[]{:S(2)}, u32[]{:S(2)}) collective-permute-start(bf16[512,1024]{1,0:T(8,128)(2,1)S(1)} %shard_map.314), channel_id=1, source_target_pairs={{0,1},{1,0},{2,3},{3,2},{4,5},{5,4},{6,7},{7,6},{8,9},{9,8},{10,11... | collective-permute-start | bytes 3145736 | tf_op jit(solution)/shard_map/ppermute | solution.py:928
  400.1 74.0 %collective-permute-start.34 = (bf16[1024,1024]{1,0:T(8,128)(2,1)}, bf16[1024,1024]{1,0:T(8,128)(2,1)}, u32[]{:S(2)}, u32[]{:S(2)}) collective-permute-start(bf16[1024,1024]{1,0:T(8,128)(2,1)} %pad_maximum_fusion.5), channel_id=1, source_target_pairs={{0,2},{1,3},{2,0},{3,1},{4,6},{5,7},{6,4},{7,5},{8,10},{9,11},{10,... | collective-permute-start | bytes 6291464 | tf_op jit(solution)/shard_map/ppermute | solution.py:932
  407.7 30.1 %collective-permute-start.29 = (bf16[512,1024]{1,0:T(8,128)(2,1)}, bf16[512,1024]{1,0:T(8,128)(2,1)}, u32[]{:S(2)}, u32[]{:S(2)}) collective-permute-start(bf16[512,1024]{1,0:T(8,128)(2,1)} %get-tuple-element.202), channel_id=1, source_target_pairs={{0,1},{1,0},{2,3},{3,2},{4,5},{5,4},{6,7},{7,6},{8,9},{9,8},{10,11... | collective-permute-start | bytes 3145736 | tf_op jit(solution)/shard_map/ppermute | solution.py:928
  474.1 22.8 %collective-permute-start.31 = (bf16[512,1024]{1,0:T(8,128)(2,1)S(1)}, bf16[512,1024]{1,0:T(8,128)(2,1)}, u32[]{:S(2)}, u32[]{:S(2)}) collective-permute-start(bf16[512,1024]{1,0:T(8,128)(2,1)S(1)} %shard_map.318), channel_id=1, source_target_pairs={{0,1},{1,0},{2,3},{3,2},{4,5},{5,4},{6,7},{7,6},{8,9},{9,8},{10,11... | collective-permute-start | bytes 3145736 | tf_op jit(solution)/shard_map/ppermute | solution.py:928
  (120 other events, 1070.0 us)
Sparse Core Ops, SparseCore 0:
  34.9 76.4 all-gather.2
  123.8 75.2 all-gather.4
  361.0 166.1 all-reduce.2

commit v8 on v7

--- a/solution.py
+++ b/solution.py
@@ -573,7 +573,7 @@
 
 def ff_weight_grads(m_pieces, g_pieces, dboth, product, gate_w, up_w, down_w, spare):
     ff = matrix_shape(down_w)[0]
-    rows, width = m_pieces[0].shape
+    rows, width = m_pieces[0][0].shape
 
     def body(m0, m1, m2, m3, g0, g1, g2, g3, both_ref, product_ref, gate_t, up_t, down_ref, out, total):
         step = pl.program_id(0)
@@ -617,16 +617,18 @@
     def alone(spec):
         return pl.BlockSpec(spec.block_shape, spec.index_map, pipeline_mode=once)
 
-    piece = pl.BlockSpec((rows, width), lambda i: (0, 0), pipeline_mode=once)
+    pieces = list(m_pieces) + list(g_pieces)
     return local_call(
         body,
         4,
-        [piece] * 8
+        [
+            pl.BlockSpec((rows, width), lambda i, at=at: (at, 0), pipeline_mode=once) for _, at in pieces
+        ]
         + [pl.BlockSpec((rows, v.shape[1]), lambda i: (jnp.minimum(i, 1), 0)) for v in (dboth, product)]
         + [alone(matrix_spec(v)) for v in parts],
         pl.BlockSpec((3 * ff + spare, width), lambda i: (0, 0), pipeline_mode=once),
         jax.ShapeDtypeStruct((3 * ff + spare, width), bf16),
-        list(m_pieces) + list(g_pieces) + [dboth, product] + [v[0] for v in parts],
+        [v for v, _ in pieces] + [dboth, product] + [v[0] for v in parts],
         scratch=[pltpu.VMEM((3 * ff, width), f32)],
     )
 
@@ -932,9 +934,27 @@
     return lax.ppermute(value, "head", [(i, i ^ 2) for i in range(4)])
 
 
-def dp_slice(own):
-    parts = own.reshape((lax.axis_size("dp"), -1) + own.shape[1:])
-    return lax.dynamic_index_in_dim(parts, lax.axis_index("dp"), 0, keepdims=False)
+def dp_slices(arrays, layer):
+    n = lax.axis_size("dp")
+    height, width = arrays[0].shape[1] // n, arrays[0].shape[2]
+    views = [v.reshape(v.shape[0], n, height, width) for v in arrays]
+
+    def body(at, *refs):
+        for which, ref in enumerate(refs[:-1]):
+            refs[-1][which] = ref[...]
+
+    return pl.pallas_call(
+        body,
+        grid_spec=pltpu.PrefetchScalarGridSpec(
+            num_scalar_prefetch=1,
+            grid=(1,),
+            in_specs=[pl.BlockSpec((None, None, height, width), lambda i, at: (layer, at[0], 0, 0))] * len(views),
+            out_specs=pl.BlockSpec((len(views), height, width), lambda i, at: (0, 0, 0)),
+        ),
+        out_shape=jax.ShapeDtypeStruct((len(views), height, width), bf16),
+        cost_estimate=NO_COST,
+        compiler_params=kernel_params(),
+    )(lax.axis_index("dp").astype(jnp.int32).reshape(1), *views)
 
 
 def dp_ring():
@@ -971,8 +991,7 @@
     gate_t, up_t, rank_t = (jnp.swapaxes(v, 1, 2) for v in (w_gate, w_up, w_rank))
 
     def ff_slice(layer, wait):
-        part = jnp.concatenate([dp_slice(v[layer]) for v in (gate_t, up_t, w_down)], axis=0)
-        return chip_swap(after(part, wait))
+        return chip_swap(after(dp_slices((gate_t, up_t, w_down), layer), wait))
 
     def ff_gather(part):
         dp = lax.axis_size("dp")
@@ -988,13 +1007,11 @@
 
     small = jnp.concatenate([w_decay.astype(f32), decay_bias[:, None, :]], axis=1)
     small = jnp.concatenate([small, chip_swap(small)], axis=2)
-    mix_own = mix_pack(0)
-    first_far = chip_swap(mix_own[:, : 2 * HK])
     ff_part = ff_slice(0, meta)
     ff_far = ff_gather(ff_part)
-    mix_far = (first_far, chip_swap(after(mix_own[:, 2 * HK :], ff_part)))
-    out_far = chip_swap(after(w_out[0], ff_part))
-    next_part = ff_slice(1, mix_far[1])
+    mix_own = mix_pack(0)
+    mix_far = chip_swap(after(mix_own, ff_part))
+    out_far = chip_swap(after(w_out[0], mix_far))
     next_own = mix_pack(1)
     spare = -3 * ff % (32 * lax.axis_size("dp"))
 
@@ -1004,7 +1021,9 @@
     for layer in range(LAYERS):
         hidden_in = hidden
         a = with_partner(norm_low(hidden, norm_one[layer]))
-        x = project(a, ((mix_own, None),) + tuple((v, None) for v in mix_far) + ((rank_t, layer),))
+        x = project(a, ((mix_own, None), (mix_far, None), (rank_t, layer)))
+        if layer == 0:
+            next_part = ff_slice(1, x)
         wdec, bias = small[layer, :rank], small[layer, rank:]
         run, states, cum, final = mixer.states(x, wdec, bias)
         got = chip_swap(after(final, next_part, next_own) if layer == 0 else after(final, out_far))
@@ -1012,9 +1031,11 @@
         gain = group_gain[layer][None]
         gated, mixed = mixer.mix(x, run, states, cum, first, gain)
         if layer + 1 < LAYERS:
-            next_mix = (chip_swap(after(next_own, got)),)
+            next_mix = chip_swap(after(next_own, got))
             next_out = chip_swap(after(w_out[layer + 1], got))
             next_far = ff_gather(next_part)
+        if layer > 0:
+            gated = after(gated, ff_far)
         hidden_mid = hidden + settle(
             [(gated, 0, (w_out, layer), False), (gated, HV, (out_far, None), False)]
         )
@@ -1022,7 +1043,7 @@
         m = (m_own, core_swap(m_own))
         gate, up, product = ff_forward(m, (gate_t, layer), (up_t, layer), ff_far, ffp)
         if layer + 1 < LAYERS:
-            product = after(product, next_mix[0])
+            product = after(product, next_mix)
         hidden = hidden_mid + settle(
             [(product, 0, (w_down, layer), False), (product, ffp, (ff_far, (2, ff)), False)]
         )
@@ -1045,12 +1066,13 @@
         if layer + 1 < LAYERS:
             g_own = grad.astype(bf16)
             g_y = chip_swap(g_own)
+            g_far = [(g_y, 0), (core_swap(g_y), 0)]
             mix_late = (own, chip_swap(after(far, g_y)))
         else:
             g_own = grad_out[0]
-            g_y = chip_swap(after(g_own, got))
-            m_y = chip_swap(jnp.concatenate([v[3][0] for v in saved], axis=0))
-            m_far = (m_y, core_swap(m_y))
+            came = chip_swap(jnp.concatenate([v[3][0] for v in saved] + [g_own], axis=0))
+            came = (came, core_swap(came))
+            g_far = [(v, LAYERS) for v in came]
         g = (g_own, core_swap(g_own))
         dboth, dfar = ff_backward(g, gate, up, (w_down, layer), ff_far, ffp)
         back_mid, gain_two = norm_back(
@@ -1065,7 +1087,7 @@
             ),
         )
         ff_grad = ff_weight_grads(
-            m + tuple(v[layer * shard_len : (layer + 1) * shard_len] for v in m_far), g + (g_y, core_swap(g_y)), dboth, product,
+            [(v, 0) for v in m] + [(v, layer) for v in came], [(v, 0) for v in g] + g_far, dboth, product,
             (gate_t, layer), (up_t, layer), (w_down, layer), 0 if layer else spare,
         )
         grad = grad + back_mid
@@ -1087,14 +1109,10 @@
             mix_late = (mix_late[0].astype(f32) + after(mix_late[1], dx).astype(f32)).astype(bf16)
         far = jnp.concatenate([g_wmix[:, HEAD_COLS:], g_wout[:, HV:]], axis=1)
         own = jnp.concatenate([g_wmix[:, :HEAD_COLS], g_wout[:, :HV]], axis=1)
-        far_terms, at = [], HEAD_COLS
-        for part in mix_far:
-            far_terms.append((dx, at, (part, None), True))
-            at += part.shape[1]
         back_first, gain_one = norm_back(hidden_in, norm_one[layer], settle(
             [
                 (dx, 0, (mix_own, None), True),
-                *far_terms,
+                (dx, HEAD_COLS, (mix_far, None), True),
                 (dx, 2 * HEAD_COLS, (rank_t, layer), False),
             ]
         ))

time: 754 us -> 771 us (1.023)
  waiting for transfers between devices: 87.7 us -> 125 us
  other arithmetic: 54.9 us -> 44.6 us
    ppermute x16 -> x14, waiting for transfers between devices: 82.7 us -> 116 us  [chip_swap(): return lax.ppermute(value, 'head', [(i, i ^ 2) for i in range(4)])]
    slice x5 -> x0, local copies, waits for them, and re-layouts: 13.5 us -> none  [the longest x3 9.29 us: ff_slice(): v[layer]]
    reshape x0 -> x2, local copies, waits for them, and re-layouts: none -> 9.96 us  [ff_gather(): whole.reshape(dp, 3, ff // dp, width)]
    transpose x2 -> x0, local copies, waits for them, and re-layouts: 9.79 us -> none  [ff_gather(): jnp.swapaxes(whole.reshape(dp, 3, ff // dp, width), 0, 1)]
    unnamed x226 -> x216, local copies, waits for them, and re-layouts: 32.9 us -> 36 us
    ppermute x16 -> x14, starting transfers between devices: 17.6 us -> 17.2 us  [chip_swap(): return lax.ppermute(value, 'head', [(i, i ^ 2) for i in range(4)])]
  transfers between devices with their start and end apart: 38 -> 35, of which waited for: 12 -> 15; matrix products, arithmetic and copies ran while one was open for 13% -> 10% of each run, Pallas kernels for 55% -> 53%
where the time goes in v8:
time: 771 us; the launch traced here: 766 us
  Pallas kernels  481 us (62%)
  waiting for transfers between devices  125 us (16%)
  local copies, waits for them, and re-layouts  62.9 us (8%)
  other arithmetic  44.6 us (6%)
  starting transfers between devices  20.7 us (3%)
  matrix products  15.8 us (2%)
  between operations  15.5 us (2%)
    pallas_call x1, Pallas kernels, mix_sum(): pl.pallas_call(body, in_specs=[vmem] * 5, out_specs=[vmem] * 4, out_shape...  216 us
    pallas_call x24, Pallas kernels, local_call(): pl.pallas_call(body, grid=(grid,), in_specs=in_specs, out_specs=out_specs...  176 us
    ppermute x14, waiting for transfers between devices, chip_swap(): return lax.ppermute(value, 'head', [(i, i ^ 2) for i in range(4)])  116 us
    pallas_call x8, Pallas kernels, call(): pl.pallas_call(sub_blocks(kernel, self.ndoc, self.tokens, *layout), grid_...  74.5 us
    unnamed x216, local copies, waits for them, and re-layouts  36 us
    ppermute x14, starting transfers between devices, chip_swap(): return lax.ppermute(value, 'head', [(i, i ^ 2) for i in range(4)])  17.2 us
    dot_general x6, matrix products, tn(): lax.dot_general(left, right, (((0,), (0,)), ((), ())), preferred_element_...  15.8 us
  transfers between devices with their start and end apart: 35, of which 15 were waited for; matrix products, arithmetic and copies ran while one was open for 10% of the time, Pallas kernels for 53%

profile of v8, /device:TPU:0, one launch (start us, length us, event | category | flops | bytes accessed | tf_op | source)
XLA Modules:
  0.0 765.7 jit_solution(1093311630551851819)
XLA Ops:
  13.9 12.4 %collective-permute-done.1 = bf16[3,88,1024]{2,1,0:T(8,128)(2,1)} collective-permute-done((bf16[3,88,1024]{2,1,0:T(8,128)(2,1)S(1)}, bf16[3,88,1024]{2,1,0:T(8,128)(2,1)}, u32[]{:S(2)}, u32[]{:S(2)}) %collective-permute-start.1) | collective-permute-done | bytes 540704 | tf_op jit(solution)/shard_map/ppermute | solution.py:934
  37.5 29.2 %collective-permute-done.2.refs_1_.refs_2_ = bf16[1024,768]{1,0:T(8,128)(2,1)S(1)} collective-permute-done((bf16[1024,768]{1,0:T(8,128)(2,1)S(1)}, bf16[1024,768]{1,0:T(8,128)(2,1)S(1)}, u32[]{:S(2)}, u32[]{:S(2)}) %collective-permute-start.2) | collective-permute-done | bytes 1572896 | tf_op jit(solution)/shard_map/ppermute | solution.py:934
  74.1 11.3 %collective-permute-done.4 = bf16[3,88,1024]{2,1,0:T(8,128)(2,1)} collective-permute-done((bf16[3,88,1024]{2,1,0:T(8,128)(2,1)S(1)}, bf16[3,88,1024]{2,1,0:T(8,128)(2,1)}, u32[]{:S(2)}, u32[]{:S(2)}) %collective-permute-start.4) | collective-permute-done | bytes 540704 | tf_op jit(solution)/shard_map/ppermute | solution.py:934
  92.7 8.2 %shard_map.290 = (f32[1024,256]{1,0:T(8,128)S(1)}, bf16[8,2,256,128]{3,2,1,0:T(8,128)(2,1)S(1)}, f32[8,1,256]{2,1,0:T(1,128)S(1)}, bf16[2,256,128]{2,1,0:T(8,128)(2,1)S(1)}) custom-call(s32[6]{0:T(128)S(1)} %pad_add_fusion.meta, f32[1024,1552]{1,0:T(8,128)} %shard_map.289.refs_0_, f32[16,256]{1,0:T(8,128)S(1)} %get-tuple-element.252.refs_1_.refs_10_, ...), custom_call_target="tpu_custom_call" | custom-call | tf_op jit(solution)/shard_map/pallas_call | solution.py:284
  123.6 11.8 %shard_map.295 = (bf16[1024,1536]{1,0:T(8,128)(2,1)}, bf16[1024,1536]{1,0:T(8,128)(2,1)}, bf16[1024,1536]{1,0:T(8,128)(2,1)}) custom-call(bf16[512,1024]{1,0:T(8,128)(2,1)} %multiply_convert_fusion.2.near_ref.m0, bf16[512,1024]{1,0:T(8,128)(2,1)} %collective-permute-done.8.part_ref.m1, bf16[2,704,1024]{2,1,0:T(8,128)(2,1)S(1)} %bitcast.105, ...), custom_call_target="tpu_custom_call" | custom-call | tf_op jit(solution)/shard_map/pallas_call | solution.py:433
  135.3 14.7 %collective-permute-done.9.refs_1_.refs_2_ = bf16[1024,768]{1,0:T(8,128)(2,1)} collective-permute-done((bf16[1024,768]{1,0:T(8,128)(2,1)}, bf16[1024,768]{1,0:T(8,128)(2,1)}, u32[]{:S(2)}, u32[]{:S(2)}) %collective-permute-start.9) | collective-permute-done | bytes 1572896 | tf_op jit(solution)/shard_map/ppermute | solution.py:934
  162.1 7.7 %shard_map.298.refs_0_ = f32[1024,1552]{1,0:T(8,128)} custom-call(bf16[1024,1024]{1,0:T(8,128)(2,1)S(1)} %pad_maximum_fusion.2.left, bf16[1024,768]{1,0:T(8,128)(2,1)} %pad_maximum_fusion.9.refs_0_.refs_1_, bf16[1024,768]{1,0:T(8,128)(2,1)} %collective-permute-done.9.refs_1_.refs_2_, bf16[2,16,1024]{2,1,0:T(8,128)(2,1)S(1)} %bitcast.114), custom_call_target="tpu_custom_call" | custom-call | tf_op jit(solution)/shard_map/pallas_call | solution.py:433
  169.8 8.7 %shard_map.299 = (f32[1024,256]{1,0:T(8,128)S(1)}, bf16[8,2,256,128]{3,2,1,0:T(8,128)(2,1)S(1)}, f32[8,1,256]{2,1,0:T(1,128)S(1)}, bf16[2,256,128]{2,1,0:T(8,128)(2,1)}) custom-call(s32[6]{0:T(128)S(1)} %pad_add_fusion.meta, f32[1024,1552]{1,0:T(8,128)} %shard_map.298.refs_0_, f32[16,256]{1,0:T(8,128)S(1)} %get-tuple-element.251.refs_1_.refs_10_, ...), custom_call_target="tpu_custom_call" | custom-call | tf_op jit(solution)/shard_map/pallas_call | solution.py:284
  207.1 11.1 %shard_map.303 = (bf16[1024,1536]{1,0:T(8,128)(2,1)}, bf16[1024,1536]{1,0:T(8,128)(2,1)}, bf16[1024,1536]{1,0:T(8,128)(2,1)}) custom-call(bf16[512,1024]{1,0:T(8,128)(2,1)S(1)} %multiply_convert_fusion.near_ref.m0, bf16[512,1024]{1,0:T(8,128)(2,1)S(1)} %collective-permute-done.15.part_ref.m1, bf16[2,704,1024]{2,1,0:T(8,128)(2,1)S(1)} %bitcast.106, ...), custom_call_target="tpu_custom_call" | custom-call | tf_op jit(solution)/shard_map/pallas_call | solution.py:433
  218.2 9.2 %shard_map.306 = (bf16[1024,1408]{1,0:T(8,128)(2,1)S(1)}, bf16[1024,1408]{1,0:T(8,128)(2,1)}) custom-call(bf16[512,1024]{1,0:T(8,128)(2,1)S(1)} %bitcast.111, bf16[512,1024]{1,0:T(8,128)(2,1)S(1)} %collective-permute-done.17.part_ref.g1, bf16[1024,1536]{1,0:T(8,128)(2,1)} %get-tuple-element.103.gate_ref, bf16[1024,1536]{1,0:T(8,128)(2,1)} %get-tuple-element.104.up_ref, ...), custom_call_target="tpu_custom_call" | custom-call | tf_op jit(solution)/shard_map/pallas_call | solution.py:433
  227.5 7.8 %shard_map.308 = bf16[512,1024]{1,0:T(8,128)(2,1)S(1)} custom-call(bf16[1024,1408]{1,0:T(8,128)(2,1)S(1)} %get-tuple-element.105.refs_0_.both_ref, bf16[1024,1408]{1,0:T(8,128)(2,1)} %get-tuple-element.106.refs_1_, bf16[2,704,1024]{2,1,0:T(8,128)(2,1)} %bitcast.97, bf16[2,704,1024]{2,1,0:T(8,128)(2,1)} %bitcast.126, bf16[2112,1024]{1,0:T(8,128)(2,1)} %bitcast.142), custom_call_target="tpu_custom_call" | custom-call | tf_op jit(solution)/shard_map/pallas_call | solution.py:433
  235.4 38.5 %collective-permute-done.20.m2.g2 = bf16[1536,1024]{1,0:T(8,128)(2,1)} collective-permute-done((bf16[1536,1024]{1,0:T(8,128)(2,1)}, bf16[1536,1024]{1,0:T(8,128)(2,1)}, u32[]{:S(2)}, u32[]{:S(2)}) %collective-permute-start.20) | collective-permute-done | bytes 3145760 | tf_op jit(solution)/shard_map/ppermute | solution.py:934
  278.1 6.7 shard_map.307
  299.0 27.9 %shard_map.309 = bf16[2112,1024]{1,0:T(8,128)(2,1)} custom-call(bf16[512,1024]{1,0:T(8,128)(2,1)S(1)} %multiply_convert_fusion.near_ref.m0, bf16[512,1024]{1,0:T(8,128)(2,1)S(1)} %collective-permute-done.15.part_ref.m1, bf16[1536,1024]{1,0:T(8,128)(2,1)} %collective-permute-done.20.m2.g2, bf16[1536,1024]{1,0:T(8,128)(2,1)} %collective-permute-done.21.m3.g3, ...), custom_call_target="tpu_custom_call" | custom-call | tf_op jit(solution)/shard_map/pallas_call | solution.py:433
  327.9 11.1 %shard_map.310 = (bf16[1024,512]{1,0:T(8,128)(2,1)S(1)}, bf16[1024,512]{1,0:T(8,128)(2,1)S(1)}, bf16[8,2,256,128]{3,2,1,0:T(8,128)(2,1)S(1)}, f32[8,1,256]{2,1,0...) custom-call(s32[6]{0:T(128)S(1)} %pad_add_fusion.meta, f32[1024,1552]{1,0:T(8,128)} %shard_map.298.refs_0_, ...), custom_call_target="tpu_custom_call" | custom-call | tf_op jit(solution)/shard_map/pallas_call | solution.py:284
  353.4 11.6 %shard_map.311 = (bf16[1024,1552]{1,0:T(8,128)(2,1)}, f32[16,256]{1,0:T(8,128)S(1)}, f32[1,256]{1,0:T(1,128)S(1)}) custom-call(s32[6]{0:T(128)S(1)} %pad_add_fusion.meta, f32[1024,1552]{1,0:T(8,128)} %shard_map.298.refs_0_, f32[1024,256]{1,0:T(8,128)S(1)} %copy-done.20, bf16[8,2,256,128]{3,2,1,0:T(8,128)(2,1)S(1)} %copy-done.32, ...), custom_call_target="tpu_custom_call" | custom-call | tf_op jit(solution)/shard_map/pallas_call | solution.py:284
  386.7 9.6 %shard_map.314 = (bf16[1024,1408]{1,0:T(8,128)(2,1)S(1)}, bf16[1024,1408]{1,0:T(8,128)(2,1)}) custom-call(bf16[512,1024]{1,0:T(8,128)(2,1)} %get-tuple-element.220.near_ref.g0, bf16[512,1024]{1,0:T(8,128)(2,1)S(1)} %copy-done.34, bf16[1024,1536]{1,0:T(8,128)(2,1)} %get-tuple-element.115.gate_ref, bf16[1024,1536]{1,0:T(8,128)(2,1)} %get-tuple-element.116.up_ref, ...), custom_call_target="tpu_custom_call" | custom-call | tf_op jit(solution)/shard_map/pallas_call | solution.py:433
  396.3 7.7 %shard_map.316 = bf16[512,1024]{1,0:T(8,128)(2,1)S(1)} custom-call(bf16[1024,1408]{1,0:T(8,128)(2,1)S(1)} %get-tuple-element.117.refs_0_.both_ref, bf16[1024,1408]{1,0:T(8,128)(2,1)} %get-tuple-element.118.refs_1_, bf16[2,704,1024]{2,1,0:T(8,128)(2,1)} %bitcast.100, bf16[2,704,1024]{2,1,0:T(8,128)(2,1)} %bitcast.129, bf16[2112,1024]{1,0:T(8,128)(2,1)} %bitcast.137), custom_call_target="tpu_custom_call" | custom-call | tf_op jit(solution)/shard_map/pallas_call | solution.py:433
  411.3 6.9 shard_map.315
  425.0 28.8 %shard_map.321.refs_0_ = bf16[2304,1024]{1,0:T(8,128)(2,1)} custom-call(bf16[512,1024]{1,0:T(8,128)(2,1)} %multiply_convert_fusion.2.near_ref.m0, bf16[512,1024]{1,0:T(8,128)(2,1)} %collective-permute-done.8.part_ref.m1, bf16[1536,1024]{1,0:T(8,128)(2,1)} %collective-permute-done.20.m2.g2, bf16[1536,1024]{1,0:T(8,128)(2,1)} %collective-permute-done.21.m3.g3, ...), custom_call_target="tpu_custom_call" | custom-call | tf_op jit(solution)/shard_map/pallas_call | solution.py:433
  457.0 11.1 %shard_map.317 = (bf16[1024,512]{1,0:T(8,128)(2,1)S(1)}, bf16[1024,512]{1,0:T(8,128)(2,1)S(1)}, bf16[8,2,256,128]{3,2,1,0:T(8,128)(2,1)S(1)}, f32[8,1,256]{2,1,0...) custom-call(s32[6]{0:T(128)S(1)} %pad_add_fusion.meta, f32[1024,1552]{1,0:T(8,128)} %shard_map.289.refs_0_, ...), custom_call_target="tpu_custom_call" | custom-call | tf_op jit(solution)/shard_map/pallas_call | solution.py:284
  473.9 12.0 %shard_map.318 = (bf16[1024,1552]{1,0:T(8,128)(2,1)}, f32[16,256]{1,0:T(8,128)S(1)}, f32[1,256]{1,0:T(1,128)S(1)}) custom-call(s32[6]{0:T(128)S(1)} %pad_add_fusion.meta, f32[1024,1552]{1,0:T(8,128)} %shard_map.289.refs_0_, f32[1024,256]{1,0:T(8,128)S(1)} %copy-done.17, bf16[8,2,256,128]{3,2,1,0:T(8,128)(2,1)S(1)} %copy-done.29, ...), custom_call_target="tpu_custom_call" | custom-call | tf_op jit(solution)/shard_map/pallas_call | solution.py:284
  515.9 216.2 %shard_map.322 = (bf16[2304,1024]{1,0:T(8,128)(2,1)}, bf16[1024,1024]{1,0:T(8,128)(2,1)S(1)}, bf16[1024,1024]{1,0:T(8,128)(2,1)S(1)}, f32[432,128]{1,0:T(8,128)S(1)}) custom-call(bf16[2304,1024]{1,0:T(8,128)(2,1)} %shard_map.321.refs_0_, bf16[1024,1024]{1,0:T(8,128)(2,1)} %add_convert_fusion.refs_1_, bf16[1024,1024]{1,0:T(8,128)(2,1)} %pad_maximum_fusion.6.refs_2_, ...), custom_call_target="tpu_custom_call" | custom-call | tf_op jit(solution)/shard_map/pallas_call | solution.py:881
  746.6 12.4 %shard_map.323 = (f32[2,1024,128]{2,1,0:T(8,128)}, f32[2,1024,128]{2,1,0:T(8,128)}, f32[2,1024,256]{2,1,0:T(8,128)}, f32[2,1024,256]{2,1,0:T(8,128)}, f32[2,256,...) custom-call(bf16[1024,1024]{1,0:T(8,128)(2,1)S(1)} %copy-done.41, ...), custom_call_target="tpu_custom_call" | custom-call | tf_op jit(solution)/shard_map/pallas_call | solution.py:673
  (389 shorter events, 217.6 us)
Async XLA Ops:
  7.2 111.5 %all-gather.3.cloned.1.call-start = ((), (), s32[]{:S(2)}) async-start(), calls=%async_computation | async-start | bytes 4866048 | tf_op jit(solution)/shard_map/all_gather | solution.py:998
  10.9 15.4 %collective-permute-start.1 = (bf16[3,88,1024]{2,1,0:T(8,128)(2,1)S(1)}, bf16[3,88,1024]{2,1,0:T(8,128)(2,1)}, u32[]{:S(2)}, u32[]{:S(2)}) collective-permute-start(bf16[3,88,1024]{2,1,0:T(8,128)(2,1)S(1)} %shard_map.288), channel_id=1, source_target_pairs={{0,2},{1,3},{2,0},{3,1},{4,6},{5,7},{6,4},{7,5},{8,10},{9,11},{10,... | collective-permute-start | bytes 1622024 | tf_op jit(solution)/shard_map/ppermute | solution.py:934
  26.3 155.9 %all-gather.5.cloned.1.call-start = ((), (), s32[]{:S(2)}) async-start(), calls=%async_computation.1 | async-start | bytes 4866048 | tf_op jit(solution)/shard_map/all_gather | solution.py:998
  31.1 35.6 %collective-permute-start.2 = (bf16[1024,768]{1,0:T(8,128)(2,1)S(1)}, bf16[1024,768]{1,0:T(8,128)(2,1)S(1)}, u32[]{:S(2)}, u32[]{:S(2)}) collective-permute-start(bf16[1024,768]{1,0:T(8,128)(2,1)S(1)} %pad_maximum_fusion.8.refs_0_.refs_1_), channel_id=1, source_target_pairs={{0,2},{1,3},{2,0},{3,1},{4,6},{5,7},{6,4},{7,5},{8,10},{9,11},{10,... | collective-permute-start | bytes 4718600 | tf_op jit(solution)/shard_map/ppermute | solution.py:934
  72.7 12.8 %collective-permute-start.4 = (bf16[3,88,1024]{2,1,0:T(8,128)(2,1)S(1)}, bf16[3,88,1024]{2,1,0:T(8,128)(2,1)}, u32[]{:S(2)}, u32[]{:S(2)}) collective-permute-start(bf16[3,88,1024]{2,1,0:T(8,128)(2,1)S(1)} %shard_map.291), channel_id=1, source_target_pairs={{0,2},{1,3},{2,0},{3,1},{4,6},{5,7},{6,4},{7,5},{8,10},{9,11},{10,... | collective-permute-start | bytes 1622024 | tf_op jit(solution)/shard_map/ppermute | solution.py:934
  85.4 659.6 %all-reduce.3.cloned.1.call-start = ((), (), s32[]{:S(2)}) async-start(), calls=%async_computation.2 | async-start | bytes 8650752 | tf_op jit(solution)/shard_map/psum | solution.py:1121
  85.5 6.0 collective-permute-start.3
  91.6 20.3 %collective-permute-start.6 = (bf16[256,1024]{1,0:T(8,128)(2,1)}, bf16[256,1024]{1,0:T(8,128)(2,1)S(1)}, u32[]{:S(2)}, u32[]{:S(2)}) collective-permute-start(bf16[256,1024]{1,0:T(8,128)(2,1)} %get-tuple-element.90.refs_4_), channel_id=1, source_target_pairs={{0,2},{1,3},{2,0},{3,1},{4,6},{5,7},{6,4},{7,5},{8,10},{9,11},{10,... | collective-permute-start | bytes 1572872 | tf_op jit(solution)/shard_map/ppermute | solution.py:934
  112.9 37.2 %collective-permute-start.9 = (bf16[1024,768]{1,0:T(8,128)(2,1)}, bf16[1024,768]{1,0:T(8,128)(2,1)}, u32[]{:S(2)}, u32[]{:S(2)}) collective-permute-start(bf16[1024,768]{1,0:T(8,128)(2,1)} %pad_maximum_fusion.9.refs_0_.refs_1_), channel_id=1, source_target_pairs={{0,2},{1,3},{2,0},{3,1},{4,6},{5,7},{6,4},{7,5},{8,10},{9,11},{10,... | collective-permute-start | bytes 4718600 | tf_op jit(solution)/shard_map/ppermute | solution.py:934
  159.4 21.1 %collective-permute-start.12 = (bf16[256,1024]{1,0:T(8,128)(2,1)S(1)}, bf16[256,1024]{1,0:T(8,128)(2,1)S(1)}, u32[]{:S(2)}, u32[]{:S(2)}) collective-permute-start(bf16[256,1024]{1,0:T(8,128)(2,1)S(1)} %copy-done.38), channel_id=1, source_target_pairs={{0,2},{1,3},{2,0},{3,1},{4,6},{5,7},{6,4},{7,5},{8,10},{9,11},{10,... | collective-permute-start | bytes 1572872 | tf_op jit(solution)/shard_map/ppermute | solution.py:934
  181.3 6.1 collective-permute-start.13
  203.5 70.5 %collective-permute-start.20 = (bf16[1536,1024]{1,0:T(8,128)(2,1)}, bf16[1536,1024]{1,0:T(8,128)(2,1)}, u32[]{:S(2)}, u32[]{:S(2)}) collective-permute-start(bf16[1536,1024]{1,0:T(8,128)(2,1)} %pad_maximum_fusion), channel_id=1, source_target_pairs={{0,2},{1,3},{2,0},{3,1},{4,6},{5,7},{6,4},{7,5},{8,10},{9,11},{10,... | collective-permute-start | bytes 9437192 | tf_op jit(solution)/shard_map/ppermute | solution.py:934
  204.4 13.8 %collective-permute-start.17 = (bf16[512,1024]{1,0:T(8,128)(2,1)S(1)}, bf16[512,1024]{1,0:T(8,128)(2,1)S(1)}, u32[]{:S(2)}, u32[]{:S(2)}) collective-permute-start(bf16[512,1024]{1,0:T(8,128)(2,1)S(1)} %bitcast.110), channel_id=1, source_target_pairs={{0,1},{1,0},{2,3},{3,2},{4,5},{5,4},{6,7},{7,6},{8,9},{9,8},{10,11... | collective-permute-start | bytes 3145736 | tf_op jit(solution)/shard_map/ppermute | solution.py:930
  235.2 53.2 %collective-permute-start.18 = (bf16[512,1024]{1,0:T(8,128)(2,1)S(1)}, bf16[512,1024]{1,0:T(8,128)(2,1)S(1)}, u32[]{:S(2)}, u32[]{:S(2)}) collective-permute-start(bf16[512,1024]{1,0:T(8,128)(2,1)S(1)} %shard_map.308), channel_id=1, source_target_pairs={{0,1},{1,0},{2,3},{3,2},{4,5},{5,4},{6,7},{7,6},{8,9},{9,8},{10,11... | collective-permute-start | bytes 3145736 | tf_op jit(solution)/shard_map/ppermute | solution.py:930
  273.9 25.1 %collective-permute-start.21 = (bf16[1536,1024]{1,0:T(8,128)(2,1)}, bf16[1536,1024]{1,0:T(8,128)(2,1)}, u32[]{:S(2)}, u32[]{:S(2)}) collective-permute-start(bf16[1536,1024]{1,0:T(8,128)(2,1)} %collective-permute-done.20.m2.g2), channel_id=1, source_target_pairs={{0,1},{1,0},{2,3},{3,2},{4,5},{5,4},{6,7},{7,6},{8,9},{9,8},{10,11... | collective-permute-start | bytes 9437192 | tf_op jit(solution)/shard_map/ppermute | solution.py:930
  277.6 13.4 %collective-permute-start.16 = (bf16[512,1024]{1,0:T(8,128)(2,1)S(1)}, bf16[512,1024]{1,0:T(8,128)(2,1)}, u32[]{:S(2)}, u32[]{:S(2)}) collective-permute-start(bf16[512,1024]{1,0:T(8,128)(2,1)S(1)} %shard_map.305), channel_id=1, source_target_pairs={{0,1},{1,0},{2,3},{3,2},{4,5},{5,4},{6,7},{7,6},{8,9},{9,8},{10,11... | collective-permute-start | bytes 3145736 | tf_op jit(solution)/shard_map/ppermute | solution.py:930
  342.0 5.5 collective-permute-start.22
  378.1 6.3 collective-permute-start.24
  383.5 34.8 %collective-permute-start.29 = (bf16[512,1024]{1,0:T(8,128)(2,1)}, bf16[512,1024]{1,0:T(8,128)(2,1)}, u32[]{:S(2)}, u32[]{:S(2)}) collective-permute-start(bf16[512,1024]{1,0:T(8,128)(2,1)} %get-tuple-element.220.near_ref.g0), channel_id=1, source_target_pairs={{0,2},{1,3},{2,0},{3,1},{4,6},{5,7},{6,4},{7,5},{8,10},{9,11},{10,... | collective-permute-start | bytes 3145736 | tf_op jit(solution)/shard_map/ppermute | solution.py:934
  404.1 15.7 %collective-permute-start.25 = (bf16[512,1024]{1,0:T(8,128)(2,1)S(1)}, bf16[512,1024]{1,0:T(8,128)(2,1)S(1)}, u32[]{:S(2)}, u32[]{:S(2)}) collective-permute-start(bf16[512,1024]{1,0:T(8,128)(2,1)S(1)} %shard_map.316), channel_id=1, source_target_pairs={{0,1},{1,0},{2,3},{3,2},{4,5},{5,4},{6,7},{7,6},{8,9},{9,8},{10,11... | collective-permute-start | bytes 3145736 | tf_op jit(solution)/shard_map/ppermute | solution.py:930
  418.3 71.5 %collective-permute-start.31 = (bf16[1024,1024]{1,0:T(8,128)(2,1)}, bf16[1024,1024]{1,0:T(8,128)(2,1)}, u32[]{:S(2)}, u32[]{:S(2)}) collective-permute-start(bf16[1024,1024]{1,0:T(8,128)(2,1)} %pad_maximum_fusion.5), channel_id=1, source_target_pairs={{0,2},{1,3},{2,0},{3,1},{4,6},{5,7},{6,4},{7,5},{8,10},{9,11},{10,... | collective-permute-start | bytes 6291464 | tf_op jit(solution)/shard_map/ppermute | solution.py:934
  422.9 30.9 %collective-permute-start.26 = (bf16[512,1024]{1,0:T(8,128)(2,1)}, bf16[512,1024]{1,0:T(8,128)(2,1)}, u32[]{:S(2)}, u32[]{:S(2)}) collective-permute-start(bf16[512,1024]{1,0:T(8,128)(2,1)} %get-tuple-element.218), channel_id=1, source_target_pairs={{0,1},{1,0},{2,3},{3,2},{4,5},{5,4},{6,7},{7,6},{8,9},{9,8},{10,11... | collective-permute-start | bytes 3145736 | tf_op jit(solution)/shard_map/ppermute | solution.py:930
  468.2 5.7 collective-permute-start.27
  489.7 23.5 %collective-permute-start.28 = (bf16[512,1024]{1,0:T(8,128)(2,1)S(1)}, bf16[512,1024]{1,0:T(8,128)(2,1)}, u32[]{:S(2)}, u32[]{:S(2)}) collective-permute-start(bf16[512,1024]{1,0:T(8,128)(2,1)S(1)} %shard_map.320), channel_id=1, source_target_pairs={{0,1},{1,0},{2,3},{3,2},{4,5},{5,4},{6,7},{7,6},{8,9},{9,8},{10,11... | collective-permute-start | bytes 3145736 | tf_op jit(solution)/shard_map/ppermute | solution.py:930
  (112 other events, 912.6 us)
Sparse Core Ops, SparseCore 0:
  26.4 76.4 all-gather.2
  105.1 73.2 all-gather.4
  378.6 168.4 all-reduce.2

commit v9 on v8

--- a/solution.py
+++ b/solution.py
@@ -1012,6 +1012,7 @@
     mix_own = mix_pack(0)
     mix_far = chip_swap(after(mix_own, ff_part))
     out_far = chip_swap(after(w_out[0], mix_far))
+    next_part = ff_slice(1, ff_part)
     next_own = mix_pack(1)
     spare = -3 * ff % (32 * lax.axis_size("dp"))
 
@@ -1022,11 +1023,9 @@
         hidden_in = hidden
         a = with_partner(norm_low(hidden, norm_one[layer]))
         x = project(a, ((mix_own, None), (mix_far, None), (rank_t, layer)))
-        if layer == 0:
-            next_part = ff_slice(1, x)
         wdec, bias = small[layer, :rank], small[layer, rank:]
         run, states, cum, final = mixer.states(x, wdec, bias)
-        got = chip_swap(after(final, next_part, next_own) if layer == 0 else after(final, out_far))
+        got = chip_swap(final if layer == 0 else after(final, out_far))
         first = got[::-1] * chip.astype(bf16)
         gain = group_gain[layer][None]
         gated, mixed = mixer.mix(x, run, states, cum, first, gain)
@@ -1070,9 +1069,10 @@
             mix_late = (own, chip_swap(after(far, g_y)))
         else:
             g_own = grad_out[0]
-            came = chip_swap(jnp.concatenate([v[3][0] for v in saved] + [g_own], axis=0))
+            g_y = chip_swap(after(g_own, got))
+            g_far = [(g_y, 0), (core_swap(g_y), 0)]
+            came = chip_swap(jnp.concatenate([v[3][0] for v in saved], axis=0))
             came = (came, core_swap(came))
-            g_far = [(v, LAYERS) for v in came]
         g = (g_own, core_swap(g_own))
         dboth, dfar = ff_backward(g, gate, up, (w_down, layer), ff_far, ffp)
         back_mid, gain_two = norm_back(
@@ -1092,14 +1092,14 @@
         )
         grad = grad + back_mid
         g_mix = with_partner(grad.astype(bf16))
-        if layer + 1 == LAYERS:
-            g_mix = after(g_mix, ff_grad)
         g_wout = tn(g_mix, gated).astype(bf16)
         dmixed, doutgate, dstates, dcum, dfinal, dgain = mixer.back_states(
             x, run, mixed, g_mix, w_out[layer], out_far, gain
         )
         got = chip_swap(dfinal)
         dlast = got[::-1] * (1 - chip).astype(bf16)
+        if layer + 1 == LAYERS:
+            dlast = after(dlast, ff_grad)
         dx, dwdec, dbias = mixer.back(
             x, run, states, cum, first, dmixed, doutgate, dstates, dcum, dlast, wdec, bias
         )

time: 771 us -> 766 us (level)
  waiting for transfers between devices: 125 us -> 102 us
  Pallas kernels: 481 us -> 490 us
    ppermute x14 -> x15, waiting for transfers between devices: 116 us -> 98.7 us  [chip_swap(): return lax.ppermute(value, 'head', [(i, i ^ 2) for i in range(4)])]
    unnamed x216 -> x264, local copies, waits for them, and re-layouts: 36 us -> 34.6 us
    ppermute x14 -> x15, starting transfers between devices: 17.2 us -> 16.8 us  [chip_swap(): return lax.ppermute(value, 'head', [(i, i ^ 2) for i in range(4)])]
  transfers between devices with their start and end apart: 35 -> 37, of which waited for: 15 -> 12; matrix products, arithmetic and copies ran while one was open for 10% -> 12% of each run, Pallas kernels for 53% -> 56%
where the time goes in v9:
time: 766 us; the launch traced here: 754 us
  Pallas kernels  490 us (64%)
  waiting for transfers between devices  102 us (13%)
  local copies, waits for them, and re-layouts  60.1 us (8%)
  other arithmetic  50 us (7%)
  starting transfers between devices  20.1 us (3%)
  matrix products  16.9 us (2%)
  between operations  15.8 us (2%)
    pallas_call x1, Pallas kernels, mix_sum(): pl.pallas_call(body, in_specs=[vmem] * 5, out_specs=[vmem] * 4, out_shape...  222 us
    pallas_call x24, Pallas kernels, local_call(): pl.pallas_call(body, grid=(grid,), in_specs=in_specs, out_specs=out_specs...  180 us
    ppermute x15, waiting for transfers between devices, chip_swap(): return lax.ppermute(value, 'head', [(i, i ^ 2) for i in range(4)])  98.7 us
    pallas_call x8, Pallas kernels, call(): pl.pallas_call(sub_blocks(kernel, self.ndoc, self.tokens, *layout), grid_...  73.4 us
    unnamed x264, local copies, waits for them, and re-layouts  34.6 us
    dot_general x6, matrix products, tn(): lax.dot_general(left, right, (((0,), (0,)), ((), ())), preferred_element_...  16.9 us
    ppermute x15, starting transfers between devices, chip_swap(): return lax.ppermute(value, 'head', [(i, i ^ 2) for i in range(4)])  16.8 us
  transfers between devices with their start and end apart: 37, of which 12 were waited for; matrix products, arithmetic and copies ran while one was open for 12% of the time, Pallas kernels for 56%

profile of v9, /device:TPU:0, one launch (start us, length us, event | category | flops | bytes accessed | tf_op | source)
XLA Modules:
  0.0 754.4 jit_solution(11245258294760764023)
XLA Ops:
  14.0 12.3 %collective-permute-done.1 = bf16[3,88,1024]{2,1,0:T(8,128)(2,1)S(1)} collective-permute-done((bf16[3,88,1024]{2,1,0:T(8,128)(2,1)S(1)}, bf16[3,88,1024]{2,1,0:T(8,128)(2,1)S(1)}, u32[]{:S(2)}, u32[]{:S(2)}) %collective-permute-start.1) | collective-permute-done | bytes 540704 | tf_op jit(solution)/shard_map/ppermute | solution.py:934
  37.0 43.1 %collective-permute-done.13 = bf16[3,88,1024]{2,1,0:T(8,128)(2,1)S(1)} collective-permute-done((bf16[3,88,1024]{2,1,0:T(8,128)(2,1)S(1)}, bf16[3,88,1024]{2,1,0:T(8,128)(2,1)S(1)}, u32[]{:S(2)}, u32[]{:S(2)}) %collective-permute-start.13) | collective-permute-done | bytes 540704 | tf_op jit(solution)/shard_map/ppermute | solution.py:934
  88.2 7.9 %shard_map.289.refs_0_ = f32[1024,1552]{1,0:T(8,128)} custom-call(bf16[1024,1024]{1,0:T(8,128)(2,1)S(1)} %pad_maximum_fusion.left, bf16[1024,768]{1,0:T(8,128)(2,1)} %pad_maximum_fusion.8.refs_0_.refs_1_, bf16[1024,768]{1,0:T(8,128)(2,1)} %collective-permute-done.2.refs_1_.refs_2_, bf16[2,16,1024]{2,1,0:T(8,128)(2,1)S(1)} %bitcast.112), custom_call_target="tpu_custom_call" | custom-call | tf_op jit(solution)/shard_map/pallas_call | solution.py:433
  96.1 8.0 %shard_map.290 = (f32[1024,256]{1,0:T(8,128)S(1)}, bf16[8,2,256,128]{3,2,1,0:T(8,128)(2,1)S(1)}, f32[8,1,256]{2,1,0:T(1,128)S(1)}, bf16[2,256,128]{2,1,0:T(8,128)(2,1)S(1)}) custom-call(s32[6]{0:T(128)S(1)} %pad_add_fusion.meta, f32[1024,1552]{1,0:T(8,128)} %shard_map.289.refs_0_, f32[16,256]{1,0:T(8,128)S(1)} %get-tuple-element.252.refs_1_.refs_10_, ...), custom_call_target="tpu_custom_call" | custom-call | tf_op jit(solution)/shard_map/pallas_call | solution.py:284
  128.0 11.7 %shard_map.294 = (bf16[1024,1536]{1,0:T(8,128)(2,1)}, bf16[1024,1536]{1,0:T(8,128)(2,1)}, bf16[1024,1536]{1,0:T(8,128)(2,1)}) custom-call(bf16[512,1024]{1,0:T(8,128)(2,1)} %multiply_convert_fusion.2.near_ref.m0, bf16[512,1024]{1,0:T(8,128)(2,1)} %collective-permute-done.7.part_ref.m1, bf16[2,704,1024]{2,1,0:T(8,128)(2,1)S(1)} %bitcast.104, ...), custom_call_target="tpu_custom_call" | custom-call | tf_op jit(solution)/shard_map/pallas_call | solution.py:433
  139.7 14.8 %collective-permute-done.8.refs_1_.refs_2_ = bf16[1024,768]{1,0:T(8,128)(2,1)} collective-permute-done((bf16[1024,768]{1,0:T(8,128)(2,1)}, bf16[1024,768]{1,0:T(8,128)(2,1)}, u32[]{:S(2)}, u32[]{:S(2)}) %collective-permute-start.8) | collective-permute-done | bytes 1572896 | tf_op jit(solution)/shard_map/ppermute | solution.py:934
  167.0 7.7 %shard_map.297.refs_0_ = f32[1024,1552]{1,0:T(8,128)} custom-call(bf16[1024,1024]{1,0:T(8,128)(2,1)S(1)} %pad_maximum_fusion.1.left, bf16[1024,768]{1,0:T(8,128)(2,1)} %pad_maximum_fusion.9.refs_0_.refs_1_, bf16[1024,768]{1,0:T(8,128)(2,1)} %collective-permute-done.8.refs_1_.refs_2_, bf16[2,16,1024]{2,1,0:T(8,128)(2,1)S(1)} %bitcast.113), custom_call_target="tpu_custom_call" | custom-call | tf_op jit(solution)/shard_map/pallas_call | solution.py:433
  174.7 8.9 %shard_map.298 = (f32[1024,256]{1,0:T(8,128)S(1)}, bf16[8,2,256,128]{3,2,1,0:T(8,128)(2,1)S(1)}, f32[8,1,256]{2,1,0:T(1,128)S(1)}, bf16[2,256,128]{2,1,0:T(8,128)(2,1)}) custom-call(s32[6]{0:T(128)S(1)} %pad_add_fusion.meta, f32[1024,1552]{1,0:T(8,128)} %shard_map.297.refs_0_, f32[16,256]{1,0:T(8,128)S(1)} %get-tuple-element.251.refs_1_.refs_10_, ...), custom_call_target="tpu_custom_call" | custom-call | tf_op jit(solution)/shard_map/pallas_call | solution.py:284
  209.4 11.5 %shard_map.303 = (bf16[1024,1536]{1,0:T(8,128)(2,1)}, bf16[1024,1536]{1,0:T(8,128)(2,1)}, bf16[1024,1536]{1,0:T(8,128)(2,1)}) custom-call(bf16[512,1024]{1,0:T(8,128)(2,1)S(1)} %multiply_convert_fusion.near_ref.m0, bf16[512,1024]{1,0:T(8,128)(2,1)S(1)} %collective-permute-done.15.part_ref.m1, bf16[2,704,1024]{2,1,0:T(8,128)(2,1)S(1)} %bitcast.105, ...), custom_call_target="tpu_custom_call" | custom-call | tf_op jit(solution)/shard_map/pallas_call | solution.py:433
  220.9 9.6 %shard_map.306 = (bf16[1024,1408]{1,0:T(8,128)(2,1)S(1)}, bf16[1024,1408]{1,0:T(8,128)(2,1)}) custom-call(bf16[512,1024]{1,0:T(8,128)(2,1)S(1)} %bitcast.109, bf16[512,1024]{1,0:T(8,128)(2,1)S(1)} %collective-permute-done.17.part_ref.g1, bf16[1024,1536]{1,0:T(8,128)(2,1)} %get-tuple-element.102.gate_ref, bf16[1024,1536]{1,0:T(8,128)(2,1)} %get-tuple-element.103.up_ref, ...), custom_call_target="tpu_custom_call" | custom-call | tf_op jit(solution)/shard_map/pallas_call | solution.py:433
  230.5 7.7 %shard_map.308 = bf16[512,1024]{1,0:T(8,128)(2,1)S(1)} custom-call(bf16[1024,1408]{1,0:T(8,128)(2,1)S(1)} %get-tuple-element.104.refs_0_.both_ref, bf16[1024,1408]{1,0:T(8,128)(2,1)} %get-tuple-element.105.refs_1_, bf16[2,704,1024]{2,1,0:T(8,128)(2,1)} %bitcast.96, bf16[2,704,1024]{2,1,0:T(8,128)(2,1)} %bitcast.125, bf16[2112,1024]{1,0:T(8,128)(2,1)} %bitcast.141), custom_call_target="tpu_custom_call" | custom-call | tf_op jit(solution)/shard_map/pallas_call | solution.py:433
  243.5 7.1 shard_map.307
  264.4 14.4 %collective-permute-done.23.g2 = bf16[512,1024]{1,0:T(8,128)(2,1)} collective-permute-done((bf16[512,1024]{1,0:T(8,128)(2,1)S(1)}, bf16[512,1024]{1,0:T(8,128)(2,1)}, u32[]{:S(2)}, u32[]{:S(2)}) %collective-permute-start.23) | collective-permute-done | bytes 1048608 | tf_op jit(solution)/shard_map/ppermute | solution.py:934
  280.5 11.0 %shard_map.309 = (bf16[1024,512]{1,0:T(8,128)(2,1)S(1)}, bf16[1024,512]{1,0:T(8,128)(2,1)S(1)}, bf16[8,2,256,128]{3,2,1,0:T(8,128)(2,1)S(1)}, f32[8,1,256]{2,1,0...) custom-call(s32[6]{0:T(128)S(1)} %pad_add_fusion.meta, f32[1024,1552]{1,0:T(8,128)} %shard_map.297.refs_0_, ...), custom_call_target="tpu_custom_call" | custom-call | tf_op jit(solution)/shard_map/pallas_call | solution.py:284
  303.1 27.7 %shard_map.310 = bf16[2112,1024]{1,0:T(8,128)(2,1)} custom-call(bf16[512,1024]{1,0:T(8,128)(2,1)S(1)} %copy-done.9, bf16[512,1024]{1,0:T(8,128)(2,1)S(1)} %copy-done.22, bf16[1024,1024]{1,0:T(8,128)(2,1)} %collective-permute-done.21.m2, bf16[1024,1024]{1,0:T(8,128)(2,1)} %collective-permute-done.22.m3, bf16[512,1024]{1,0:T(8,128)(2,1)S(1)} %bitcast.111, ...), custom_call_target="tpu_custom_call" | custom-call | tf_op jit(solution)/shard_map/pallas_call | solution.py:433
  335.7 11.6 %shard_map.311 = (bf16[1024,1552]{1,0:T(8,128)(2,1)}, f32[16,256]{1,0:T(8,128)S(1)}, f32[1,256]{1,0:T(1,128)S(1)}) custom-call(s32[6]{0:T(128)S(1)} %pad_add_fusion.meta, f32[1024,1552]{1,0:T(8,128)} %shard_map.297.refs_0_, f32[1024,256]{1,0:T(8,128)S(1)} %copy-done.14, bf16[8,2,256,128]{3,2,1,0:T(8,128)(2,1)S(1)} %copy-done.31, ...), custom_call_target="tpu_custom_call" | custom-call | tf_op jit(solution)/shard_map/pallas_call | solution.py:284
  368.3 9.6 %shard_map.314 = (bf16[1024,1408]{1,0:T(8,128)(2,1)S(1)}, bf16[1024,1408]{1,0:T(8,128)(2,1)}) custom-call(bf16[512,1024]{1,0:T(8,128)(2,1)} %get-tuple-element.220.near_ref.g0, bf16[512,1024]{1,0:T(8,128)(2,1)S(1)} %copy-done.35, bf16[1024,1536]{1,0:T(8,128)(2,1)} %get-tuple-element.115.gate_ref, bf16[1024,1536]{1,0:T(8,128)(2,1)} %get-tuple-element.116.up_ref, ...), custom_call_target="tpu_custom_call" | custom-call | tf_op jit(solution)/shard_map/pallas_call | solution.py:433
  377.9 7.7 %shard_map.316 = bf16[512,1024]{1,0:T(8,128)(2,1)S(1)} custom-call(bf16[1024,1408]{1,0:T(8,128)(2,1)S(1)} %get-tuple-element.117.refs_0_.both_ref, bf16[1024,1408]{1,0:T(8,128)(2,1)} %get-tuple-element.118.refs_1_, bf16[2,704,1024]{2,1,0:T(8,128)(2,1)} %bitcast.99, bf16[2,704,1024]{2,1,0:T(8,128)(2,1)} %bitcast.128, bf16[2112,1024]{1,0:T(8,128)(2,1)} %bitcast.136), custom_call_target="tpu_custom_call" | custom-call | tf_op jit(solution)/shard_map/pallas_call | solution.py:433
  392.6 6.8 shard_map.315
  405.7 28.7 %shard_map.321.refs_0_ = bf16[2304,1024]{1,0:T(8,128)(2,1)} custom-call(bf16[512,1024]{1,0:T(8,128)(2,1)} %multiply_convert_fusion.2.near_ref.m0, bf16[512,1024]{1,0:T(8,128)(2,1)} %collective-permute-done.7.part_ref.m1, bf16[1024,1024]{1,0:T(8,128)(2,1)} %collective-permute-done.21.m2, bf16[1024,1024]{1,0:T(8,128)(2,1)} %collective-permute-done.22.m3, ...), custom_call_target="tpu_custom_call" | custom-call | tf_op jit(solution)/shard_map/pallas_call | solution.py:433
  437.3 11.1 %shard_map.317 = (bf16[1024,512]{1,0:T(8,128)(2,1)S(1)}, bf16[1024,512]{1,0:T(8,128)(2,1)S(1)}, bf16[8,2,256,128]{3,2,1,0:T(8,128)(2,1)S(1)}, f32[8,1,256]{2,1,0...) custom-call(s32[6]{0:T(128)S(1)} %pad_add_fusion.meta, f32[1024,1552]{1,0:T(8,128)} %shard_map.289.refs_0_, ...), custom_call_target="tpu_custom_call" | custom-call | tf_op jit(solution)/shard_map/pallas_call | solution.py:284
  454.2 11.7 %shard_map.318 = (bf16[1024,1552]{1,0:T(8,128)(2,1)}, f32[16,256]{1,0:T(8,128)S(1)}, f32[1,256]{1,0:T(1,128)S(1)}) custom-call(s32[6]{0:T(128)S(1)} %pad_add_fusion.meta, f32[1024,1552]{1,0:T(8,128)} %shard_map.289.refs_0_, f32[1024,256]{1,0:T(8,128)S(1)} %copy-done.11, bf16[8,2,256,128]{3,2,1,0:T(8,128)(2,1)S(1)} %copy-done.28, ...), custom_call_target="tpu_custom_call" | custom-call | tf_op jit(solution)/shard_map/pallas_call | solution.py:284
  496.6 221.7 %shard_map.322 = (bf16[2304,1024]{1,0:T(8,128)(2,1)}, bf16[1024,1024]{1,0:T(8,128)(2,1)S(1)}, bf16[1024,1024]{1,0:T(8,128)(2,1)S(1)}, f32[432,128]{1,0:T(8,128)S(1)}) custom-call(bf16[2304,1024]{1,0:T(8,128)(2,1)} %shard_map.321.refs_0_, bf16[1024,1024]{1,0:T(8,128)(2,1)} %add_convert_fusion.refs_1_, bf16[1024,1024]{1,0:T(8,128)(2,1)} %pad_maximum_fusion.6.refs_2_, ...), custom_call_target="tpu_custom_call" | custom-call | tf_op jit(solution)/shard_map/pallas_call | solution.py:881
  735.1 12.4 %shard_map.323 = (f32[2,1024,128]{2,1,0:T(8,128)}, f32[2,1024,128]{2,1,0:T(8,128)}, f32[2,1024,256]{2,1,0:T(8,128)}, f32[2,1024,256]{2,1,0:T(8,128)}, f32[2,256,...) custom-call(bf16[1024,1024]{1,0:T(8,128)(2,1)S(1)} %copy-done.45, ...), custom_call_target="tpu_custom_call" | custom-call | tf_op jit(solution)/shard_map/pallas_call | solution.py:673
  (441 shorter events, 214.2 us)
Async XLA Ops:
  7.2 115.9 %all-gather.3.cloned.1.call-start = ((), (), s32[]{:S(2)}) async-start(), calls=%async_computation | async-start | bytes 4866048 | tf_op jit(solution)/shard_map/all_gather | solution.py:998
  11.0 15.3 %collective-permute-start.1 = (bf16[3,88,1024]{2,1,0:T(8,128)(2,1)S(1)}, bf16[3,88,1024]{2,1,0:T(8,128)(2,1)S(1)}, u32[]{:S(2)}, u32[]{:S(2)}) collective-permute-start(bf16[3,88,1024]{2,1,0:T(8,128)(2,1)S(1)} %shard_map.288), channel_id=1, source_target_pairs={{0,2},{1,3},{2,0},{3,1},{4,6},{5,7},{6,4},{7,5},{8,10},{9,11},{10,... | collective-permute-start | bytes 1622024 | tf_op jit(solution)/shard_map/ppermute | solution.py:934
  27.1 158.9 %all-gather.5.cloned.1.call-start = ((), (), s32[]{:S(2)}) async-start(), calls=%async_computation.1 | async-start | bytes 4866048 | tf_op jit(solution)/shard_map/all_gather | solution.py:998
  32.7 52.3 %collective-permute-start.2 = (bf16[1024,768]{1,0:T(8,128)(2,1)}, bf16[1024,768]{1,0:T(8,128)(2,1)}, u32[]{:S(2)}, u32[]{:S(2)}) collective-permute-start(bf16[1024,768]{1,0:T(8,128)(2,1)} %pad_maximum_fusion.8.refs_0_.refs_1_), channel_id=1, source_target_pairs={{0,2},{1,3},{2,0},{3,1},{4,6},{5,7},{6,4},{7,5},{8,10},{9,11},{10,... | collective-permute-start | bytes 4718600 | tf_op jit(solution)/shard_map/ppermute | solution.py:934
  34.7 45.4 %collective-permute-start.13 = (bf16[3,88,1024]{2,1,0:T(8,128)(2,1)S(1)}, bf16[3,88,1024]{2,1,0:T(8,128)(2,1)S(1)}, u32[]{:S(2)}, u32[]{:S(2)}) collective-permute-start(bf16[3,88,1024]{2,1,0:T(8,128)(2,1)S(1)} %shard_map.300), channel_id=1, source_target_pairs={{0,2},{1,3},{2,0},{3,1},{4,6},{5,7},{6,4},{7,5},{8,10},{9,11},{10,... | collective-permute-start | bytes 1622024 | tf_op jit(solution)/shard_map/ppermute | solution.py:934
  37.0 49.4 %collective-permute-start = (bf16[512,1024]{1,0:T(8,128)(2,1)}, bf16[512,1024]{1,0:T(8,128)(2,1)}, u32[]{:S(2)}, u32[]{:S(2)}) collective-permute-start(bf16[512,1024]{1,0:T(8,128)(2,1)} %fusion.4), channel_id=1, source_target_pairs={{0,1},{1,0},{2,3},{3,2},{4,5},{5,4},{6,7},{7,6},{8,9},{9,8},{10,11... | collective-permute-start | bytes 3145736 | tf_op jit(solution)/shard_map/ppermute | solution.py:930
  80.9 651.0 %all-reduce.3.cloned.1.call-start = ((), (), s32[]{:S(2)}) async-start(), calls=%async_computation.2 | async-start | bytes 8650752 | tf_op jit(solution)/shard_map/psum | solution.py:1121
  84.9 30.0 %collective-permute-start.5 = (bf16[256,1024]{1,0:T(8,128)(2,1)S(1)}, bf16[256,1024]{1,0:T(8,128)(2,1)S(1)}, u32[]{:S(2)}, u32[]{:S(2)}) collective-permute-start(bf16[256,1024]{1,0:T(8,128)(2,1)S(1)} %get-tuple-element.88.refs_4_), channel_id=1, source_target_pairs={{0,2},{1,3},{2,0},{3,1},{4,6},{5,7},{6,4},{7,5},{8,10},{9,11},{10,... | collective-permute-start | bytes 1572872 | tf_op jit(solution)/shard_map/ppermute | solution.py:934
  118.5 36.0 %collective-permute-start.8 = (bf16[1024,768]{1,0:T(8,128)(2,1)}, bf16[1024,768]{1,0:T(8,128)(2,1)}, u32[]{:S(2)}, u32[]{:S(2)}) collective-permute-start(bf16[1024,768]{1,0:T(8,128)(2,1)} %pad_maximum_fusion.9.refs_0_.refs_1_), channel_id=1, source_target_pairs={{0,2},{1,3},{2,0},{3,1},{4,6},{5,7},{6,4},{7,5},{8,10},{9,11},{10,... | collective-permute-start | bytes 4718600 | tf_op jit(solution)/shard_map/ppermute | solution.py:934
  163.8 21.7 %collective-permute-start.11 = (bf16[256,1024]{1,0:T(8,128)(2,1)S(1)}, bf16[256,1024]{1,0:T(8,128)(2,1)S(1)}, u32[]{:S(2)}, u32[]{:S(2)}) collective-permute-start(bf16[256,1024]{1,0:T(8,128)(2,1)S(1)} %copy-done.40), channel_id=1, source_target_pairs={{0,2},{1,3},{2,0},{3,1},{4,6},{5,7},{6,4},{7,5},{8,10},{9,11},{10,... | collective-permute-start | bytes 1572872 | tf_op jit(solution)/shard_map/ppermute | solution.py:934
  185.5 6.1 collective-permute-start.12
  200.7 20.1 %collective-permute-start.17 = (bf16[512,1024]{1,0:T(8,128)(2,1)S(1)}, bf16[512,1024]{1,0:T(8,128)(2,1)S(1)}, u32[]{:S(2)}, u32[]{:S(2)}) collective-permute-start(bf16[512,1024]{1,0:T(8,128)(2,1)S(1)} %bitcast.108), channel_id=1, source_target_pairs={{0,1},{1,0},{2,3},{3,2},{4,5},{5,4},{6,7},{7,6},{8,9},{9,8},{10,11... | collective-permute-start | bytes 3145736 | tf_op jit(solution)/shard_map/ppermute | solution.py:930
  208.4 48.8 %collective-permute-start.21 = (bf16[1024,1024]{1,0:T(8,128)(2,1)}, bf16[1024,1024]{1,0:T(8,128)(2,1)}, u32[]{:S(2)}, u32[]{:S(2)}) collective-permute-start(bf16[1024,1024]{1,0:T(8,128)(2,1)} %pad_maximum_fusion.3), channel_id=1, source_target_pairs={{0,2},{1,3},{2,0},{3,1},{4,6},{5,7},{6,4},{7,5},{8,10},{9,11},{10,... | collective-permute-start | bytes 6291464 | tf_op jit(solution)/shard_map/ppermute | solution.py:934
  238.2 19.0 %collective-permute-start.18 = (bf16[512,1024]{1,0:T(8,128)(2,1)S(1)}, bf16[512,1024]{1,0:T(8,128)(2,1)}, u32[]{:S(2)}, u32[]{:S(2)}) collective-permute-start(bf16[512,1024]{1,0:T(8,128)(2,1)S(1)} %shard_map.308), channel_id=1, source_target_pairs={{0,1},{1,0},{2,3},{3,2},{4,5},{5,4},{6,7},{7,6},{8,9},{9,8},{10,11... | collective-permute-start | bytes 3145736 | tf_op jit(solution)/shard_map/ppermute | solution.py:930
  241.9 17.8 %collective-permute-start.16 = (bf16[512,1024]{1,0:T(8,128)(2,1)S(1)}, bf16[512,1024]{1,0:T(8,128)(2,1)}, u32[]{:S(2)}, u32[]{:S(2)}) collective-permute-start(bf16[512,1024]{1,0:T(8,128)(2,1)S(1)} %shard_map.305), channel_id=1, source_target_pairs={{0,1},{1,0},{2,3},{3,2},{4,5},{5,4},{6,7},{7,6},{8,9},{9,8},{10,11... | collective-permute-start | bytes 3145736 | tf_op jit(solution)/shard_map/ppermute | solution.py:930
  242.4 36.4 %collective-permute-start.23 = (bf16[512,1024]{1,0:T(8,128)(2,1)S(1)}, bf16[512,1024]{1,0:T(8,128)(2,1)}, u32[]{:S(2)}, u32[]{:S(2)}) collective-permute-start(bf16[512,1024]{1,0:T(8,128)(2,1)S(1)} %bitcast.110), channel_id=1, source_target_pairs={{0,2},{1,3},{2,0},{3,1},{4,6},{5,7},{6,4},{7,5},{8,10},{9,11},{10,... | collective-permute-start | bytes 3145736 | tf_op jit(solution)/shard_map/ppermute | solution.py:934
  257.2 43.3 %collective-permute-start.22 = (bf16[1024,1024]{1,0:T(8,128)(2,1)}, bf16[1024,1024]{1,0:T(8,128)(2,1)}, u32[]{:S(2)}, u32[]{:S(2)}) collective-permute-start(bf16[1024,1024]{1,0:T(8,128)(2,1)} %collective-permute-done.21.m2), channel_id=1, source_target_pairs={{0,1},{1,0},{2,3},{3,2},{4,5},{5,4},{6,7},{7,6},{8,9},{9,8},{10,11... | collective-permute-start | bytes 6291464 | tf_op jit(solution)/shard_map/ppermute | solution.py:930
  263.8 15.0 %collective-permute-start.19 = (bf16[512,1024]{1,0:T(8,128)(2,1)S(1)}, bf16[512,1024]{1,0:T(8,128)(2,1)S(1)}, u32[]{:S(2)}, u32[]{:S(2)}) collective-permute-start(bf16[512,1024]{1,0:T(8,128)(2,1)S(1)} %get-tuple-element.222), channel_id=1, source_target_pairs={{0,1},{1,0},{2,3},{3,2},{4,5},{5,4},{6,7},{7,6},{8,9},{9,8},{10,11... | collective-permute-start | bytes 3145736 | tf_op jit(solution)/shard_map/ppermute | solution.py:930
  278.8 21.7 %collective-permute-start.24 = (bf16[512,1024]{1,0:T(8,128)(2,1)}, bf16[512,1024]{1,0:T(8,128)(2,1)}, u32[]{:S(2)}, u32[]{:S(2)}) collective-permute-start(bf16[512,1024]{1,0:T(8,128)(2,1)} %collective-permute-done.23.g2), channel_id=1, source_target_pairs={{0,1},{1,0},{2,3},{3,2},{4,5},{5,4},{6,7},{7,6},{8,9},{9,8},{10,11... | collective-permute-start | bytes 3145736 | tf_op jit(solution)/shard_map/ppermute | solution.py:930
  365.1 34.3 %collective-permute-start.31 = (bf16[512,1024]{1,0:T(8,128)(2,1)}, bf16[512,1024]{1,0:T(8,128)(2,1)}, u32[]{:S(2)}, u32[]{:S(2)}) collective-permute-start(bf16[512,1024]{1,0:T(8,128)(2,1)} %get-tuple-element.220.near_ref.g0), channel_id=1, source_target_pairs={{0,2},{1,3},{2,0},{3,1},{4,6},{5,7},{6,4},{7,5},{8,10},{9,11},{10,... | collective-permute-start | bytes 3145736 | tf_op jit(solution)/shard_map/ppermute | solution.py:934
  385.7 15.1 %collective-permute-start.27 = (bf16[512,1024]{1,0:T(8,128)(2,1)S(1)}, bf16[512,1024]{1,0:T(8,128)(2,1)S(1)}, u32[]{:S(2)}, u32[]{:S(2)}) collective-permute-start(bf16[512,1024]{1,0:T(8,128)(2,1)S(1)} %shard_map.316), channel_id=1, source_target_pairs={{0,1},{1,0},{2,3},{3,2},{4,5},{5,4},{6,7},{7,6},{8,9},{9,8},{10,11... | collective-permute-start | bytes 3145736 | tf_op jit(solution)/shard_map/ppermute | solution.py:930
  399.4 71.2 %collective-permute-start.33 = (bf16[1024,1024]{1,0:T(8,128)(2,1)}, bf16[1024,1024]{1,0:T(8,128)(2,1)}, u32[]{:S(2)}, u32[]{:S(2)}) collective-permute-start(bf16[1024,1024]{1,0:T(8,128)(2,1)} %pad_maximum_fusion.5), channel_id=1, source_target_pairs={{0,2},{1,3},{2,0},{3,1},{4,6},{5,7},{6,4},{7,5},{8,10},{9,11},{10,... | collective-permute-start | bytes 6291464 | tf_op jit(solution)/shard_map/ppermute | solution.py:934
  403.9 30.5 %collective-permute-start.28 = (bf16[512,1024]{1,0:T(8,128)(2,1)S(1)}, bf16[512,1024]{1,0:T(8,128)(2,1)}, u32[]{:S(2)}, u32[]{:S(2)}) collective-permute-start(bf16[512,1024]{1,0:T(8,128)(2,1)S(1)} %get-tuple-element.218), channel_id=1, source_target_pairs={{0,1},{1,0},{2,3},{3,2},{4,5},{5,4},{6,7},{7,6},{8,9},{9,8},{10,11... | collective-permute-start | bytes 3145736 | tf_op jit(solution)/shard_map/ppermute | solution.py:930
  470.5 23.4 %collective-permute-start.30 = (bf16[512,1024]{1,0:T(8,128)(2,1)S(1)}, bf16[512,1024]{1,0:T(8,128)(2,1)}, u32[]{:S(2)}, u32[]{:S(2)}) collective-permute-start(bf16[512,1024]{1,0:T(8,128)(2,1)S(1)} %shard_map.320), channel_id=1, source_target_pairs={{0,1},{1,0},{2,3},{3,2},{4,5},{5,4},{6,7},{7,6},{8,9},{9,8},{10,11... | collective-permute-start | bytes 3145736 | tf_op jit(solution)/shard_map/ppermute | solution.py:930
  (138 other events, 1104.5 us)
Sparse Core Ops, SparseCore 0:
  27.2 76.4 all-gather.2
  106.5 73.2 all-gather.4
  365.2 173.5 all-reduce.2

commit v10 on v8

--- a/solution.py
+++ b/solution.py
@@ -1007,11 +1007,13 @@
 
     small = jnp.concatenate([w_decay.astype(f32), decay_bias[:, None, :]], axis=1)
     small = jnp.concatenate([small, chip_swap(small)], axis=2)
+    mix_own = mix_pack(0)
+    first_far = chip_swap(mix_own[:, : 2 * HK])
     ff_part = ff_slice(0, meta)
     ff_far = ff_gather(ff_part)
-    mix_own = mix_pack(0)
-    mix_far = chip_swap(after(mix_own, ff_part))
-    out_far = chip_swap(after(w_out[0], mix_far))
+    mix_far = (first_far, chip_swap(after(mix_own[:, 2 * HK :], ff_part)))
+    out_far = chip_swap(after(w_out[0], ff_part))
+    next_part = ff_slice(1, mix_far[1])
     next_own = mix_pack(1)
     spare = -3 * ff % (32 * lax.axis_size("dp"))
 
@@ -1021,9 +1023,7 @@
     for layer in range(LAYERS):
         hidden_in = hidden
         a = with_partner(norm_low(hidden, norm_one[layer]))
-        x = project(a, ((mix_own, None), (mix_far, None), (rank_t, layer)))
-        if layer == 0:
-            next_part = ff_slice(1, x)
+        x = project(a, ((mix_own, None),) + tuple((v, None) for v in mix_far) + ((rank_t, layer),))
         wdec, bias = small[layer, :rank], small[layer, rank:]
         run, states, cum, final = mixer.states(x, wdec, bias)
         got = chip_swap(after(final, next_part, next_own) if layer == 0 else after(final, out_far))
@@ -1031,11 +1031,9 @@
         gain = group_gain[layer][None]
         gated, mixed = mixer.mix(x, run, states, cum, first, gain)
         if layer + 1 < LAYERS:
-            next_mix = chip_swap(after(next_own, got))
+            next_mix = (chip_swap(after(next_own, got)),)
             next_out = chip_swap(after(w_out[layer + 1], got))
             next_far = ff_gather(next_part)
-        if layer > 0:
-            gated = after(gated, ff_far)
         hidden_mid = hidden + settle(
             [(gated, 0, (w_out, layer), False), (gated, HV, (out_far, None), False)]
         )
@@ -1043,7 +1041,7 @@
         m = (m_own, core_swap(m_own))
         gate, up, product = ff_forward(m, (gate_t, layer), (up_t, layer), ff_far, ffp)
         if layer + 1 < LAYERS:
-            product = after(product, next_mix)
+            product = after(product, next_mix[0])
         hidden = hidden_mid + settle(
             [(product, 0, (w_down, layer), False), (product, ffp, (ff_far, (2, ff)), False)]
         )
@@ -1065,14 +1063,15 @@
         wdec, bias = small[layer, :rank], small[layer, rank:]
         if layer + 1 < LAYERS:
             g_own = grad.astype(bf16)
-            g_y = chip_swap(g_own)
-            g_far = [(g_y, 0), (core_swap(g_y), 0)]
+            g_y = chip_swap(jnp.concatenate([g_own, m[0]], axis=0))
+            came = (g_y, core_swap(g_y))
+            g_far, m_far = [(v, 0) for v in came], [(v, 1) for v in came]
             mix_late = (own, chip_swap(after(far, g_y)))
         else:
             g_own = grad_out[0]
-            came = chip_swap(jnp.concatenate([v[3][0] for v in saved] + [g_own], axis=0))
-            came = (came, core_swap(came))
-            g_far = [(v, LAYERS) for v in came]
+            g_y = chip_swap(after(g_own, got))
+            m_y = chip_swap(m[0])
+            m_far, g_far = ([(v, 0), (core_swap(v), 0)] for v in (m_y, g_y))
         g = (g_own, core_swap(g_own))
         dboth, dfar = ff_backward(g, gate, up, (w_down, layer), ff_far, ffp)
         back_mid, gain_two = norm_back(
@@ -1087,7 +1086,7 @@
             ),
         )
         ff_grad = ff_weight_grads(
-            [(v, 0) for v in m] + [(v, layer) for v in came], [(v, 0) for v in g] + g_far, dboth, product,
+            [(v, 0) for v in m] + m_far, [(v, 0) for v in g] + g_far, dboth, product,
             (gate_t, layer), (up_t, layer), (w_down, layer), 0 if layer else spare,
         )
         grad = grad + back_mid
@@ -1109,10 +1108,14 @@
             mix_late = (mix_late[0].astype(f32) + after(mix_late[1], dx).astype(f32)).astype(bf16)
         far = jnp.concatenate([g_wmix[:, HEAD_COLS:], g_wout[:, HV:]], axis=1)
         own = jnp.concatenate([g_wmix[:, :HEAD_COLS], g_wout[:, :HV]], axis=1)
+        far_terms, at = [], HEAD_COLS
+        for part in mix_far:
+            far_terms.append((dx, at, (part, None), True))
+            at += part.shape[1]
         back_first, gain_one = norm_back(hidden_in, norm_one[layer], settle(
             [
                 (dx, 0, (mix_own, None), True),
-                (dx, HEAD_COLS, (mix_far, None), True),
+                *far_terms,
                 (dx, 2 * HEAD_COLS, (rank_t, layer), False),
             ]
         ))

time: 771 us -> 776 us (level)
  Pallas kernels: 481 us -> 473 us
  waiting for transfers between devices: 125 us -> 133 us
    ppermute x14 -> x16, waiting for transfers between devices: 116 us -> 130 us  [chip_swap(): return lax.ppermute(value, 'head', [(i, i ^ 2) for i in range(4)])]
    pallas_call x1, Pallas kernels: 216 us -> 205 us  [mix_sum(): pl.pallas_call(body, in_specs=[vmem] * 5, out_specs=[vmem] * 4, out_shape...]
    unnamed x216 -> x222, local copies, waits for them, and re-layouts: 36 us -> 33.6 us
    ppermute x14 -> x16, starting transfers between devices: 17.2 us -> 17.3 us  [chip_swap(): return lax.ppermute(value, 'head', [(i, i ^ 2) for i in range(4)])]
  transfers between devices with their start and end apart: 35 -> 38, of which waited for: 15 -> 12; matrix products, arithmetic and copies ran while one was open for 10% -> 12% of each run, Pallas kernels for 53% -> 56%
where the time goes in v10:
time: 776 us; the launch traced here: 770 us
  Pallas kernels  473 us (61%)
  waiting for transfers between devices  133 us (17%)
  local copies, waits for them, and re-layouts  58 us (7%)
  other arithmetic  52.2 us (7%)
  starting transfers between devices  20.5 us (3%)
  matrix products  17.8 us (2%)
  between operations  15.5 us (2%)
    pallas_call x1, Pallas kernels, mix_sum(): pl.pallas_call(body, in_specs=[vmem] * 5, out_specs=[vmem] * 4, out_shape...  205 us
    pallas_call x24, Pallas kernels, local_call(): pl.pallas_call(body, grid=(grid,), in_specs=in_specs, out_specs=out_specs...  179 us
    ppermute x16, waiting for transfers between devices, chip_swap(): return lax.ppermute(value, 'head', [(i, i ^ 2) for i in range(4)])  130 us
    pallas_call x8, Pallas kernels, call(): pl.pallas_call(sub_blocks(kernel, self.ndoc, self.tokens, *layout), grid_...  72.9 us
    unnamed x222, local copies, waits for them, and re-layouts  33.6 us
    dot_general x6, matrix products, tn(): lax.dot_general(left, right, (((0,), (0,)), ((), ())), preferred_element_...  17.8 us
    ppermute x16, starting transfers between devices, chip_swap(): return lax.ppermute(value, 'head', [(i, i ^ 2) for i in range(4)])  17.3 us
  transfers between devices with their start and end apart: 38, of which 12 were waited for; matrix products, arithmetic and copies ran while one was open for 12% of the time, Pallas kernels for 56%

profile of v10, /device:TPU:0, one launch (start us, length us, event | category | flops | bytes accessed | tf_op | source)
XLA Modules:
  0.0 769.8 jit_solution(16825688010081958431)
XLA Ops:
  14.0 12.4 %collective-permute-done.2 = bf16[3,88,1024]{2,1,0:T(8,128)(2,1)} collective-permute-done((bf16[3,88,1024]{2,1,0:T(8,128)(2,1)S(1)}, bf16[3,88,1024]{2,1,0:T(8,128)(2,1)}, u32[]{:S(2)}, u32[]{:S(2)}) %collective-permute-start.2) | collective-permute-done | bytes 540704 | tf_op jit(solution)/shard_map/ppermute | solution.py:934
  41.3 14.9 %collective-permute-done.3.refs_2_.refs_3_ = bf16[1024,512]{1,0:T(8,128)(2,1)} collective-permute-done((bf16[1024,512]{1,0:T(8,128)(2,1)}, bf16[1024,512]{1,0:T(8,128)(2,1)}, u32[]{:S(2)}, u32[]{:S(2)}) %collective-permute-start.3) | collective-permute-done | bytes 1048608 | tf_op jit(solution)/shard_map/ppermute | solution.py:934
  57.9 9.9 %collective-permute-done.4 = f32[2,17,128]{2,1,0:T(8,128)S(1)} collective-permute-done((f32[2,17,128]{2,1,0:T(8,128)S(1)}, f32[2,17,128]{2,1,0:T(8,128)S(1)}, u32[]{:S(2)}, u32[]{:S(2)}) %collective-permute-start.4) | collective-permute-done | bytes 17440 | tf_op jit(solution)/shard_map/ppermute | solution.py:934
  71.7 7.2 shard_map.289.refs_0_
  78.9 8.0 %shard_map.290 = (f32[1024,256]{1,0:T(8,128)S(1)}, bf16[8,2,256,128]{3,2,1,0:T(8,128)(2,1)S(1)}, f32[8,1,256]{2,1,0:T(1,128)S(1)}, bf16[2,256,128]{2,1,0:T(8,128)(2,1)S(1)}) custom-call(s32[6]{0:T(128)S(1)} %pad_add_fusion.meta, f32[1024,1552]{1,0:T(8,128)} %shard_map.289.refs_0_, f32[16,256]{1,0:T(8,128)S(1)} %get-tuple-element.252.refs_1_.refs_10_, ...), custom_call_target="tpu_custom_call" | custom-call | tf_op jit(solution)/shard_map/pallas_call | solution.py:284
  119.3 11.7 %shard_map.295 = (bf16[1024,1536]{1,0:T(8,128)(2,1)}, bf16[1024,1536]{1,0:T(8,128)(2,1)}, bf16[1024,1536]{1,0:T(8,128)(2,1)}) custom-call(bf16[512,1024]{1,0:T(8,128)(2,1)} %multiply_convert_fusion.2.near_ref.m0, bf16[512,1024]{1,0:T(8,128)(2,1)} %collective-permute-done.9.part_ref.m1, bf16[2,704,1024]{2,1,0:T(8,128)(2,1)S(1)} %bitcast.105, ...), custom_call_target="tpu_custom_call" | custom-call | tf_op jit(solution)/shard_map/pallas_call | solution.py:433
  131.1 11.8 %collective-permute-done.10.refs_1_.refs_2_ = bf16[1024,768]{1,0:T(8,128)(2,1)} collective-permute-done((bf16[1024,768]{1,0:T(8,128)(2,1)}, bf16[1024,768]{1,0:T(8,128)(2,1)}, u32[]{:S(2)}, u32[]{:S(2)}) %collective-permute-start.10) | collective-permute-done | bytes 1572896 | tf_op jit(solution)/shard_map/ppermute | solution.py:934
  155.3 7.2 shard_map.298.refs_0_
  162.5 8.0 %shard_map.299 = (f32[1024,256]{1,0:T(8,128)S(1)}, bf16[8,2,256,128]{3,2,1,0:T(8,128)(2,1)S(1)}, f32[8,1,256]{2,1,0:T(1,128)S(1)}, bf16[2,256,128]{2,1,0:T(8,128)(2,1)S(1)}) custom-call(s32[6]{0:T(128)S(1)} %pad_add_fusion.meta, f32[1024,1552]{1,0:T(8,128)} %shard_map.298.refs_0_, f32[16,256]{1,0:T(8,128)S(1)} %get-tuple-element.251.refs_1_.refs_10_, ...), custom_call_target="tpu_custom_call" | custom-call | tf_op jit(solution)/shard_map/pallas_call | solution.py:284
  196.2 11.9 %shard_map.303 = (bf16[1024,1536]{1,0:T(8,128)(2,1)}, bf16[1024,1536]{1,0:T(8,128)(2,1)}, bf16[1024,1536]{1,0:T(8,128)(2,1)}) custom-call(bf16[512,1024]{1,0:T(8,128)(2,1)} %multiply_convert_fusion.near_ref.m0, bf16[512,1024]{1,0:T(8,128)(2,1)} %collective-permute-done.16.part_ref.m1, bf16[2,704,1024]{2,1,0:T(8,128)(2,1)S(1)} %bitcast.106, ...), custom_call_target="tpu_custom_call" | custom-call | tf_op jit(solution)/shard_map/pallas_call | solution.py:433
  208.1 9.7 %shard_map.306 = (bf16[1024,1408]{1,0:T(8,128)(2,1)S(1)}, bf16[1024,1408]{1,0:T(8,128)(2,1)}) custom-call(bf16[512,1024]{1,0:T(8,128)(2,1)} %bitcast.42.near_ref.g0, bf16[512,1024]{1,0:T(8,128)(2,1)} %collective-permute-done.18.part_ref.g1, bf16[1024,1536]{1,0:T(8,128)(2,1)} %get-tuple-element.102.gate_ref, bf16[1024,1536]{1,0:T(8,128)(2,1)} %get-tuple-element.103.up_ref, ...), custom_call_target="tpu_custom_call" | custom-call | tf_op jit(solution)/shard_map/pallas_call | solution.py:433
  217.8 7.7 shard_map.308
  247.8 28.3 %shard_map.309 = bf16[2112,1024]{1,0:T(8,128)(2,1)} custom-call(bf16[512,1024]{1,0:T(8,128)(2,1)} %multiply_convert_fusion.near_ref.m0, bf16[512,1024]{1,0:T(8,128)(2,1)} %collective-permute-done.16.part_ref.m1, bf16[512,1024]{1,0:T(8,128)(2,1)S(1)} %collective-permute-done.21.m2, bf16[512,1024]{1,0:T(8,128)(2,1)S(1)} %collective-permute-done.22.m3, ...), custom_call_target="tpu_custom_call" | custom-call | tf_op jit(solution)/shard_map/pallas_call | solution.py:433
  279.0 11.0 %shard_map.310 = (bf16[1024,512]{1,0:T(8,128)(2,1)S(1)}, bf16[1024,512]{1,0:T(8,128)(2,1)S(1)}, bf16[8,2,256,128]{3,2,1,0:T(8,128)(2,1)S(1)}, f32[8,1,256]{2,1,0...) custom-call(s32[6]{0:T(128)S(1)} %pad_add_fusion.meta, f32[1024,1552]{1,0:T(8,128)} %shard_map.298.refs_0_, ...), custom_call_target="tpu_custom_call" | custom-call | tf_op jit(solution)/shard_map/pallas_call | solution.py:284
  302.2 11.6 %shard_map.311 = (bf16[1024,1552]{1,0:T(8,128)(2,1)}, f32[16,256]{1,0:T(8,128)S(1)}, f32[1,256]{1,0:T(1,128)S(1)}) custom-call(s32[6]{0:T(128)S(1)} %pad_add_fusion.meta, f32[1024,1552]{1,0:T(8,128)} %shard_map.298.refs_0_, f32[1024,256]{1,0:T(8,128)S(1)} %copy-done.20, bf16[8,2,256,128]{3,2,1,0:T(8,128)(2,1)S(1)} %copy-done.32, ...), custom_call_target="tpu_custom_call" | custom-call | tf_op jit(solution)/shard_map/pallas_call | solution.py:284
  333.1 9.8 %shard_map.314 = (bf16[1024,1408]{1,0:T(8,128)(2,1)S(1)}, bf16[1024,1408]{1,0:T(8,128)(2,1)}) custom-call(bf16[512,1024]{1,0:T(8,128)(2,1)S(1)} %get-tuple-element.220.near_ref.g0, bf16[512,1024]{1,0:T(8,128)(2,1)} %collective-permute-done.27.part_ref.g1, bf16[1024,1536]{1,0:T(8,128)(2,1)} %get-tuple-element.115.gate_ref, ...), custom_call_target="tpu_custom_call" | custom-call | tf_op jit(solution)/shard_map/pallas_call | solution.py:433
  342.9 7.7 shard_map.316
  374.2 33.2 %collective-permute-done.32.m2.g2 = bf16[1024,1024]{1,0:T(8,128)(2,1)} collective-permute-done((bf16[1024,1024]{1,0:T(8,128)(2,1)}, bf16[1024,1024]{1,0:T(8,128)(2,1)}, u32[]{:S(2)}, u32[]{:S(2)}) %collective-permute-start.32) | collective-permute-done | bytes 2097184 | tf_op jit(solution)/shard_map/ppermute | solution.py:934
  411.2 11.6 %shard_map.317 = (bf16[1024,512]{1,0:T(8,128)(2,1)S(1)}, bf16[1024,512]{1,0:T(8,128)(2,1)S(1)}, bf16[8,2,256,128]{3,2,1,0:T(8,128)(2,1)S(1)}, f32[8,1,256]{2,1,0...) custom-call(s32[6]{0:T(128)S(1)} %pad_add_fusion.meta, f32[1024,1552]{1,0:T(8,128)} %shard_map.289.refs_0_, ...), custom_call_target="tpu_custom_call" | custom-call | tf_op jit(solution)/shard_map/pallas_call | solution.py:284
  427.4 30.3 %collective-permute-done.30 = bf16[2,256,128]{2,1,0:T(8,128)(2,1)S(1)} collective-permute-done((bf16[2,256,128]{2,1,0:T(8,128)(2,1)S(1)}, bf16[2,256,128]{2,1,0:T(8,128)(2,1)S(1)}, u32[]{:S(2)}, u32[]{:S(2)}) %collective-permute-start.30) | collective-permute-done | bytes 131104 | tf_op jit(solution)/shard_map/ppermute | solution.py:934
  457.7 11.6 %shard_map.318 = (bf16[1024,1552]{1,0:T(8,128)(2,1)}, f32[16,256]{1,0:T(8,128)S(1)}, f32[1,256]{1,0:T(1,128)S(1)}) custom-call(s32[6]{0:T(128)S(1)} %pad_add_fusion.meta, f32[1024,1552]{1,0:T(8,128)} %shard_map.289.refs_0_, f32[1024,256]{1,0:T(8,128)S(1)} %copy-done.18, bf16[8,2,256,128]{3,2,1,0:T(8,128)(2,1)S(1)} %copy-done.30, ...), custom_call_target="tpu_custom_call" | custom-call | tf_op jit(solution)/shard_map/pallas_call | solution.py:284
  493.8 28.7 %shard_map.321.refs_0_ = bf16[2304,1024]{1,0:T(8,128)(2,1)} custom-call(bf16[512,1024]{1,0:T(8,128)(2,1)} %multiply_convert_fusion.2.near_ref.m0, bf16[512,1024]{1,0:T(8,128)(2,1)} %collective-permute-done.9.part_ref.m1, bf16[1024,1024]{1,0:T(8,128)(2,1)} %collective-permute-done.32.m2.g2, bf16[1024,1024]{1,0:T(8,128)(2,1)} %collective-permute-done.33.m3.g3, ...), custom_call_target="tpu_custom_call" | custom-call | tf_op jit(solution)/shard_map/pallas_call | solution.py:433
  529.0 204.8 %shard_map.322 = (bf16[2304,1024]{1,0:T(8,128)(2,1)}, bf16[1024,1024]{1,0:T(8,128)(2,1)S(1)}, bf16[1024,1024]{1,0:T(8,128)(2,1)S(1)}, f32[432,128]{1,0:T(8,128)S(1)}) custom-call(bf16[2304,1024]{1,0:T(8,128)(2,1)} %shard_map.321.refs_0_, bf16[1024,1024]{1,0:T(8,128)(2,1)} %add_convert_fusion.refs_1_, bf16[1024,1024]{1,0:T(8,128)(2,1)} %pad_maximum_fusion.6.refs_2_, ...), custom_call_target="tpu_custom_call" | custom-call | tf_op jit(solution)/shard_map/pallas_call | solution.py:881
  750.7 12.4 %shard_map.323 = (f32[2,1024,128]{2,1,0:T(8,128)}, f32[2,1024,128]{2,1,0:T(8,128)}, f32[2,1024,256]{2,1,0:T(8,128)}, f32[2,1024,256]{2,1,0:T(8,128)}, f32[2,256,...) custom-call(bf16[1024,1024]{1,0:T(8,128)(2,1)S(1)} %copy-done.40, ...), custom_call_target="tpu_custom_call" | custom-call | tf_op jit(solution)/shard_map/pallas_call | solution.py:673
  (403 shorter events, 232.9 us)
Async XLA Ops:
  7.2 107.1 %all-gather.3.cloned.1.call-start = ((), (), s32[]{:S(2)}) async-start(), calls=%async_computation | async-start | bytes 4866048 | tf_op jit(solution)/shard_map/all_gather | solution.py:998
  26.4 162.9 %all-gather.5.cloned.1.call-start = ((), (), s32[]{:S(2)}) async-start(), calls=%async_computation.1 | async-start | bytes 4866048 | tf_op jit(solution)/shard_map/all_gather | solution.py:998
  28.6 41.0 %collective-permute-start = (bf16[512,1024]{1,0:T(8,128)(2,1)}, bf16[512,1024]{1,0:T(8,128)(2,1)}, u32[]{:S(2)}, u32[]{:S(2)}) collective-permute-start(bf16[512,1024]{1,0:T(8,128)(2,1)} %fusion.4), channel_id=1, source_target_pairs={{0,1},{1,0},{2,3},{3,2},{4,5},{5,4},{6,7},{7,6},{8,9},{9,8},{10,11... | collective-permute-start | bytes 3145736 | tf_op jit(solution)/shard_map/ppermute | solution.py:930
  29.9 26.3 %collective-permute-start.3 = (bf16[1024,512]{1,0:T(8,128)(2,1)}, bf16[1024,512]{1,0:T(8,128)(2,1)}, u32[]{:S(2)}, u32[]{:S(2)}) collective-permute-start(bf16[1024,512]{1,0:T(8,128)(2,1)} %pad_maximum_fusion.10), channel_id=1, source_target_pairs={{0,2},{1,3},{2,0},{3,1},{4,6},{5,7},{6,4},{7,5},{8,10},{9,11},{10,... | collective-permute-start | bytes 3145736 | tf_op jit(solution)/shard_map/ppermute | solution.py:934
  32.6 38.9 %collective-permute-start.1 = (bf16[1024,256]{1,0:T(8,128)(2,1)}, bf16[1024,256]{1,0:T(8,128)(2,1)}, u32[]{:S(2)}, u32[]{:S(2)}) collective-permute-start(bf16[1024,256]{1,0:T(8,128)(2,1)} %pad_maximum_fusion.11), channel_id=1, source_target_pairs={{0,2},{1,3},{2,0},{3,1},{4,6},{5,7},{6,4},{7,5},{8,10},{9,11},{10,... | collective-permute-start | bytes 1572872 | tf_op jit(solution)/shard_map/ppermute | solution.py:934
  33.1 34.7 %collective-permute-start.4 = (f32[2,17,128]{2,1,0:T(8,128)S(1)}, f32[2,17,128]{2,1,0:T(8,128)S(1)}, u32[]{:S(2)}, u32[]{:S(2)}) collective-permute-start(f32[2,17,128]{2,1,0:T(8,128)S(1)} %pad_maximum_fusion.14), channel_id=1, source_target_pairs={{0,2},{1,3},{2,0},{3,1},{4,6},{5,7},{6,4},{7,5},{8,10},{9,11},{10,... | collective-permute-start | bytes 52232 | tf_op jit(solution)/shard_map/ppermute | solution.py:934
  56.2 33.4 %collective-permute-start.5 = (bf16[3,88,1024]{2,1,0:T(8,128)(2,1)}, bf16[3,88,1024]{2,1,0:T(8,128)(2,1)}, u32[]{:S(2)}, u32[]{:S(2)}) collective-permute-start(bf16[3,88,1024]{2,1,0:T(8,128)(2,1)} %shard_map.291), channel_id=1, source_target_pairs={{0,2},{1,3},{2,0},{3,1},{4,6},{5,7},{6,4},{7,5},{8,10},{9,11},{10,... | collective-permute-start | bytes 1622024 | tf_op jit(solution)/shard_map/ppermute | solution.py:934
  67.8 36.0 %collective-permute-start.7 = (bf16[256,1024]{1,0:T(8,128)(2,1)}, bf16[256,1024]{1,0:T(8,128)(2,1)S(1)}, u32[]{:S(2)}, u32[]{:S(2)}) collective-permute-start(bf16[256,1024]{1,0:T(8,128)(2,1)} %get-tuple-element.90.refs_4_), channel_id=1, source_target_pairs={{0,2},{1,3},{2,0},{3,1},{4,6},{5,7},{6,4},{7,5},{8,10},{9,11},{10,... | collective-permute-start | bytes 1572872 | tf_op jit(solution)/shard_map/ppermute | solution.py:934
  105.7 641.9 %all-reduce.3.cloned.1.call-start = ((), (), s32[]{:S(2)}) async-start(), calls=%async_computation.2 | async-start | bytes 8650752 | tf_op jit(solution)/shard_map/psum | solution.py:1124
  105.7 37.2 %collective-permute-start.10 = (bf16[1024,768]{1,0:T(8,128)(2,1)}, bf16[1024,768]{1,0:T(8,128)(2,1)}, u32[]{:S(2)}, u32[]{:S(2)}) collective-permute-start(bf16[1024,768]{1,0:T(8,128)(2,1)} %pad_maximum_fusion.9.refs_0_.refs_1_), channel_id=1, source_target_pairs={{0,2},{1,3},{2,0},{3,1},{4,6},{5,7},{6,4},{7,5},{8,10},{9,11},{10,... | collective-permute-start | bytes 4718600 | tf_op jit(solution)/shard_map/ppermute | solution.py:934
  152.2 18.4 %collective-permute-start.13 = (bf16[256,1024]{1,0:T(8,128)(2,1)S(1)}, bf16[256,1024]{1,0:T(8,128)(2,1)S(1)}, u32[]{:S(2)}, u32[]{:S(2)}) collective-permute-start(bf16[256,1024]{1,0:T(8,128)(2,1)S(1)} %copy-done.35), channel_id=1, source_target_pairs={{0,2},{1,3},{2,0},{3,1},{4,6},{5,7},{6,4},{7,5},{8,10},{9,11},{10,... | collective-permute-start | bytes 1572872 | tf_op jit(solution)/shard_map/ppermute | solution.py:934
  188.9 19.2 %collective-permute-start.18 = (bf16[512,1024]{1,0:T(8,128)(2,1)}, bf16[512,1024]{1,0:T(8,128)(2,1)}, u32[]{:S(2)}, u32[]{:S(2)}) collective-permute-start(bf16[512,1024]{1,0:T(8,128)(2,1)} %bitcast.42.near_ref.g0), channel_id=1, source_target_pairs={{0,1},{1,0},{2,3},{3,2},{4,5},{5,4},{6,7},{7,6},{8,9},{9,8},{10,11... | collective-permute-start | bytes 3145736 | tf_op jit(solution)/shard_map/ppermute | solution.py:930
  194.2 35.6 %collective-permute-start.23 = (bf16[512,1024]{1,0:T(8,128)(2,1)}, bf16[512,1024]{1,0:T(8,128)(2,1)}, u32[]{:S(2)}, u32[]{:S(2)}) collective-permute-start(bf16[512,1024]{1,0:T(8,128)(2,1)} %bitcast.42.near_ref.g0), channel_id=1, source_target_pairs={{0,2},{1,3},{2,0},{3,1},{4,6},{5,7},{6,4},{7,5},{8,10},{9,11},{10,... | collective-permute-start | bytes 3145736 | tf_op jit(solution)/shard_map/ppermute | solution.py:934
  194.4 47.6 %collective-permute-start.21 = (bf16[512,1024]{1,0:T(8,128)(2,1)}, bf16[512,1024]{1,0:T(8,128)(2,1)S(1)}, u32[]{:S(2)}, u32[]{:S(2)}) collective-permute-start(bf16[512,1024]{1,0:T(8,128)(2,1)} %multiply_convert_fusion.near_ref.m0), channel_id=1, source_target_pairs={{0,2},{1,3},{2,0},{3,1},{4,6},{5,7},{6,4},{7,5},{8,10},{9,11},{10,... | collective-permute-start | bytes 3145736 | tf_op jit(solution)/shard_map/ppermute | solution.py:934
  225.5 16.5 %collective-permute-start.19 = (bf16[512,1024]{1,0:T(8,128)(2,1)S(1)}, bf16[512,1024]{1,0:T(8,128)(2,1)S(1)}, u32[]{:S(2)}, u32[]{:S(2)}) collective-permute-start(bf16[512,1024]{1,0:T(8,128)(2,1)S(1)} %shard_map.308), channel_id=1, source_target_pairs={{0,1},{1,0},{2,3},{3,2},{4,5},{5,4},{6,7},{7,6},{8,9},{9,8},{10,11... | collective-permute-start | bytes 3145736 | tf_op jit(solution)/shard_map/ppermute | solution.py:930
  229.8 18.0 %collective-permute-start.24 = (bf16[512,1024]{1,0:T(8,128)(2,1)}, bf16[512,1024]{1,0:T(8,128)(2,1)}, u32[]{:S(2)}, u32[]{:S(2)}) collective-permute-start(bf16[512,1024]{1,0:T(8,128)(2,1)} %collective-permute-done.23.g2), channel_id=1, source_target_pairs={{0,1},{1,0},{2,3},{3,2},{4,5},{5,4},{6,7},{7,6},{8,9},{9,8},{10,11... | collective-permute-start | bytes 3145736 | tf_op jit(solution)/shard_map/ppermute | solution.py:930
  247.3 28.9 %collective-permute-start.20 = (bf16[512,1024]{1,0:T(8,128)(2,1)}, bf16[512,1024]{1,0:T(8,128)(2,1)S(1)}, u32[]{:S(2)}, u32[]{:S(2)}) collective-permute-start(bf16[512,1024]{1,0:T(8,128)(2,1)} %get-tuple-element.222), channel_id=1, source_target_pairs={{0,1},{1,0},{2,3},{3,2},{4,5},{5,4},{6,7},{7,6},{8,9},{9,8},{10,11... | collective-permute-start | bytes 3145736 | tf_op jit(solution)/shard_map/ppermute | solution.py:930
  350.6 16.3 %collective-permute-start.28 = (bf16[512,1024]{1,0:T(8,128)(2,1)S(1)}, bf16[512,1024]{1,0:T(8,128)(2,1)S(1)}, u32[]{:S(2)}, u32[]{:S(2)}) collective-permute-start(bf16[512,1024]{1,0:T(8,128)(2,1)S(1)} %shard_map.316), channel_id=1, source_target_pairs={{0,1},{1,0},{2,3},{3,2},{4,5},{5,4},{6,7},{7,6},{8,9},{9,8},{10,11... | collective-permute-start | bytes 3145736 | tf_op jit(solution)/shard_map/ppermute | solution.py:930
  359.1 48.3 %collective-permute-start.32 = (bf16[1024,1024]{1,0:T(8,128)(2,1)}, bf16[1024,1024]{1,0:T(8,128)(2,1)}, u32[]{:S(2)}, u32[]{:S(2)}) collective-permute-start(bf16[1024,1024]{1,0:T(8,128)(2,1)} %pad_maximum_fusion.4), channel_id=1, source_target_pairs={{0,2},{1,3},{2,0},{3,1},{4,6},{5,7},{6,4},{7,5},{8,10},{9,11},{10,... | collective-permute-start | bytes 6291464 | tf_op jit(solution)/shard_map/ppermute | solution.py:934
  370.4 38.0 %collective-permute-start.29 = (bf16[512,1024]{1,0:T(8,128)(2,1)S(1)}, bf16[512,1024]{1,0:T(8,128)(2,1)}, u32[]{:S(2)}, u32[]{:S(2)}) collective-permute-start(bf16[512,1024]{1,0:T(8,128)(2,1)S(1)} %get-tuple-element.218), channel_id=1, source_target_pairs={{0,1},{1,0},{2,3},{3,2},{4,5},{5,4},{6,7},{7,6},{8,9},{9,8},{10,11... | collective-permute-start | bytes 3145736 | tf_op jit(solution)/shard_map/ppermute | solution.py:930
  407.4 86.4 %collective-permute-start.34 = (bf16[1024,1024]{1,0:T(8,128)(2,1)}, bf16[1024,1024]{1,0:T(8,128)(2,1)}, u32[]{:S(2)}, u32[]{:S(2)}) collective-permute-start(bf16[1024,1024]{1,0:T(8,128)(2,1)} %pad_maximum_fusion.5), channel_id=1, source_target_pairs={{0,2},{1,3},{2,0},{3,1},{4,6},{5,7},{6,4},{7,5},{8,10},{9,11},{10,... | collective-permute-start | bytes 6291464 | tf_op jit(solution)/shard_map/ppermute | solution.py:934
  408.4 85.4 %collective-permute-start.33 = (bf16[1024,1024]{1,0:T(8,128)(2,1)}, bf16[1024,1024]{1,0:T(8,128)(2,1)}, u32[]{:S(2)}, u32[]{:S(2)}) collective-permute-start(bf16[1024,1024]{1,0:T(8,128)(2,1)} %collective-permute-done.32.m2.g2), channel_id=1, source_target_pairs={{0,1},{1,0},{2,3},{3,2},{4,5},{5,4},{6,7},{7,6},{8,9},{9,8},{10,11... | collective-permute-start | bytes 6291464 | tf_op jit(solution)/shard_map/ppermute | solution.py:930
  422.7 34.9 %collective-permute-start.30 = (bf16[2,256,128]{2,1,0:T(8,128)(2,1)S(1)}, bf16[2,256,128]{2,1,0:T(8,128)(2,1)S(1)}, u32[]{:S(2)}, u32[]{:S(2)}) collective-permute-start(bf16[2,256,128]{2,1,0:T(8,128)(2,1)S(1)} %get-tuple-element.124), channel_id=1, source_target_pairs={{0,2},{1,3},{2,0},{3,1},{4,6},{5,7},{6,4},{7,5},{8,10},{9,11},{10,... | collective-permute-start | bytes 393224 | tf_op jit(solution)/shard_map/ppermute | solution.py:934
  474.1 52.1 %collective-permute-start.31 = (bf16[512,1024]{1,0:T(8,128)(2,1)}, bf16[512,1024]{1,0:T(8,128)(2,1)}, u32[]{:S(2)}, u32[]{:S(2)}) collective-permute-start(bf16[512,1024]{1,0:T(8,128)(2,1)} %shard_map.320), channel_id=1, source_target_pairs={{0,1},{1,0},{2,3},{3,2},{4,5},{5,4},{6,7},{7,6},{8,9},{9,8},{10,11... | collective-permute-start | bytes 3145736 | tf_op jit(solution)/shard_map/ppermute | solution.py:930
  (118 other events, 1249.2 us)
Sparse Core Ops, SparseCore 0:
  26.5 76.4 all-gather.2
  105.8 75.5 all-gather.4
  326.6 159.5 all-reduce.2
